TPU v7x, 32 devices: a whole 2x2x4 slice. The times are simulated.
32 devices in a mesh: row: 8 (over z, core), col: 4 (over y, x).
Axes of the slice: x: 2, y: 2, z: 4, core: 2. Of those that a mesh axis runs over, the one named last changes fastest.
Arguments:
- layer_input: bfloat16 [4, 4096, 2048], P('col', 'row'), may hold values from -6 to 6
- out_grad: bfloat16 [4, 4096, 2048], P('col', 'row'), may hold values from -6 to 6
- routes: int32 [4, 4096, 8], P('col', 'row'), may hold values from 0 to 31, all different within a row; in each aligned block of 512 rows (0 to 511, 512 to 1023, ..., all dimensions but the last counted through in order) at most 128 rows name the same one
- positions: int32 [4, 4096], P(None, 'row'), may hold values from 0 to 6398, as said below
- w_q: bfloat16 [2048, 4096], P('row', 'col'), may hold values from -0.125 to 0.125
- key_value_weight: bfloat16 [2048, 1024], P('row'), may hold values from -0.125 to 0.125
- w_out: bfloat16 [4096, 2048], P('col', 'row'), may hold values from -1.5 to 1.5
- router: bfloat16 [2048, 32], P('row'), may hold values from -0.0625 to 0.0625
- ln_attn: bfloat16 [2048], P('row'), may hold values from 0.5 to 1.5
- ln_moe: bfloat16 [2048], P('row'), may hold values from 0.5 to 1.5
- q_gain: bfloat16 [128], P('row'), may hold values from 0.5 to 1.5
- k_gain: bfloat16 [128], P('row'), may hold values from 0.5 to 1.5
- w_gate: bfloat16 [32, 2048, 768], P(('row', 'col')), may hold values from -0.125 to 0.125
- w_up: bfloat16 [32, 2048, 768], P(('row', 'col')), may hold values from -0.125 to 0.125
- w_down: bfloat16 [32, 768, 2048], P(('row', 'col')), may hold values from -1.25 to 1.25
Outputs:
- layer_output: bfloat16 [4, 4096, 2048], P('col', 'row')
- aux_loss: float32 [], replicated
- input_grad: float32 [4, 4096, 2048], P('col', 'row')
- grad_q: float32 [2048, 4096], P('row', 'col')
- grad_kv: float32 [2048, 1024], P(('row', 'col'))
- grad_out: float32 [4096, 2048], P('col', 'row')
- grad_router: float32 [2048, 32], P(('row', 'col'))
- grad_ln_attn: float32 [2048], P(('row', 'col'))
- grad_ln_moe: float32 [2048], P(('row', 'col'))
- grad_q_gain: float32 [128], P(('row', 'col'))
- grad_k_gain: float32 [128], P(('row', 'col'))
- grad_gate: float32 [32, 2048, 768], P(('row', 'col'))
- grad_up: float32 [32, 2048, 768], P(('row', 'col'))
- grad_down: float32 [32, 768, 2048], P(('row', 'col'))
- expert_load: float32 [2, 32], replicated
Inputs may be any that keep to these rules, and one draw needn't show every extreme that they name: `routes`: within the 512 rows of one device no expert is named more than 128 times; in every draw some device names some expert exactly 128 times. `positions`: in each group, for one offset b of 0 to 4095, the prompt's place t has position b + t and a continuation's place t has position b + 2048 + (t - 2048) % 256; in every draw some group has offset 0 and another offset 4095.
All inputs are finite; a program needn't handle non-finite values.
Results may differ from a plain program's by a relative error of at most 0.025.
Values may be sent and summed in bfloat16 or wider, within the bound.
No kernel may reach another device: no remote copies, remote signals or barrier semaphores. Data moves between devices by JAX's collectives and lax.ppermute only.
A program may use at most 448 MiB of HBM per device.

v0:
```python
from functools import partial
import math

import jax
import jax.numpy as jnp
from jax import lax
from jax.sharding import PartitionSpec as P

QUERY_HEADS = 32
KEY_VALUE_HEADS = 4
HEAD_SIZE = 128
TOPK = 8
CONTINUATION_LEN = 256
PROMPT_TOKENS = 2048
GROUP_TOKENS = 4096


EPS = 1e-06
THETA = 1000000.0
AUX_COEF = 0.001


def row_norm(vector, scale_gain):
    return vector * lax.rsqrt(jnp.mean(vector * vector, axis=-1, keepdims=True) + EPS) * scale_gain


def apply_rotation(vector, places):
    half_dim = vector.shape[-1] // 2
    inv_freq = THETA ** (-2.0 * jnp.arange(half_dim, dtype=jnp.float32) / vector.shape[-1])
    angles = places.astype(jnp.float32)[:, None] * inv_freq[None, :]
    cos_part = jnp.cos(angles)[:, None, :]
    sin_part = jnp.sin(angles)[:, None, :]
    lower_half = vector[..., :half_dim]
    upper_half = vector[..., half_dim:]
    return jnp.concatenate(
        [
            lower_half * cos_part - upper_half * sin_part,
            upper_half * cos_part + lower_half * sin_part,
        ],
        axis=-1,
    )


def head_prep(raw_heads, scale_gain, places):
    return apply_rotation(row_norm(raw_heads, scale_gain), places)


def key_scores(query_part, key_part, allowed, score_scale):
    scores = (
        jnp.einsum("tgd,kd->tgk", query_part, key_part, preferred_element_type=jnp.float32)
        * score_scale
    )
    return jnp.where(allowed[:, None, :], scores, -jnp.inf)


def fetch_weights(w_q, w_out, key_value_weight, router, ln_attn, ln_moe, q_gain, k_gain):
    return (
        lax.all_gather(w_q, "row", axis=0, tiled=True),
        lax.all_gather(w_out, "row", axis=1, tiled=True),
        lax.all_gather(key_value_weight, "row", axis=0, tiled=True),
        lax.all_gather(router, "row", axis=0, tiled=True),
        lax.all_gather(ln_attn, "row", axis=0, tiled=True),
        lax.all_gather(ln_moe, "row", axis=0, tiled=True),
        lax.all_gather(q_gain, "row", axis=0, tiled=True),
        lax.all_gather(k_gain, "row", axis=0, tiled=True),
    )


def select_heads(key_value_every, key_value_leading, key_value_local):
    key_cols = lax.dynamic_slice_in_dim(
        key_value_every, key_value_leading * HEAD_SIZE, key_value_local * HEAD_SIZE, 1
    )
    value_columns = lax.dynamic_slice_in_dim(
        key_value_every,
        KEY_VALUE_HEADS * HEAD_SIZE + key_value_leading * HEAD_SIZE,
        key_value_local * HEAD_SIZE,
        1,
    )
    return jnp.concatenate([key_cols, value_columns], axis=1)


def attend_forward(packed, allowed, score_scale):
    query_grp, key_grp, value_grp = packed
    scores = key_scores(query_grp[:, 0], key_grp[:, 0], allowed, score_scale)
    row_max = jnp.max(scores, axis=-1, keepdims=True)
    weights = jnp.exp(scores - row_max)
    row_total = jnp.sum(weights, axis=-1, keepdims=True)
    lse_parts = [row_max + jnp.log(row_total)]
    outputs = [
        jnp.einsum(
            "tgk,kd->tgd",
            (weights / row_total).astype(jnp.bfloat16),
            value_grp[:, 0],
            preferred_element_type=jnp.float32,
        )
    ]
    return (jnp.stack(outputs, axis=1).astype(jnp.bfloat16), jnp.stack(lse_parts, axis=1))


def attend_backward(packed, allowed, score_scale):
    query_grp, key_grp, value_grp, mix_grp, lse_grp = packed
    scores = key_scores(query_grp[:, 0], key_grp[:, 0], allowed, score_scale)
    attn_probs = jnp.exp(scores - lse_grp[:, 0])
    prob_grad = jnp.einsum(
        "tgd,kd->tgk", mix_grp[:, 0], value_grp[:, 0], preferred_element_type=jnp.float32
    )
    center = jnp.sum(attn_probs * prob_grad, axis=-1, keepdims=True)
    score_low = (attn_probs * (prob_grad - center)).astype(jnp.bfloat16)
    query_parts = [
        jnp.einsum("tgk,kd->tgd", score_low, key_grp[:, 0], preferred_element_type=jnp.float32)
        * score_scale
    ]
    key_parts = [
        jnp.einsum("tgk,tgd->kd", score_low, query_grp[:, 0], preferred_element_type=jnp.float32)
        * score_scale
    ]
    value_parts = [
        jnp.einsum(
            "tgk,tgd->kd",
            attn_probs.astype(jnp.bfloat16),
            mix_grp[:, 0],
            preferred_element_type=jnp.float32,
        )
    ]
    return (
        jnp.stack(query_parts, axis=1),
        jnp.stack(key_parts, axis=1),
        jnp.stack(value_parts, axis=1),
    )


def per_device(
    layer_input,
    out_grad,
    routes,
    positions,
    w_q,
    key_value_weight,
    w_out,
    router,
    ln_attn,
    ln_moe,
    q_gain,
    k_gain,
    w_gate,
    w_up,
    w_down,
):
    rows_dev = layer_input.shape[1]
    width_model = layer_input.shape[2]
    row_count = lax.axis_size("row")
    col_count = lax.axis_size("col")
    row_index = lax.axis_index("row")
    col_index = lax.axis_index("col")
    device_count = row_count * col_count
    local_experts = w_gate.shape[0]
    expert_total = local_experts * device_count
    capacity = max(2, (rows_dev * TOPK + expert_total - 1) // expert_total)
    token_count = rows_dev * device_count
    flat_rows = col_count * rows_dev
    head_cols = w_q.shape[1]
    heads_mine = head_cols // HEAD_SIZE
    group_length = QUERY_HEADS // KEY_VALUE_HEADS
    key_value_local = max(1, heads_mine // group_length)
    per_kv = heads_mine // key_value_local
    key_value_columns = key_value_local * HEAD_SIZE
    key_value_leading = col_index * heads_mine // group_length
    score_scale = 1.0 / math.sqrt(HEAD_SIZE)
    residual = layer_input[0].astype(jnp.float32)
    upstream = out_grad[0].astype(jnp.float32)
    chosen_ids = routes[0]
    places = positions.reshape(flat_rows)
    q_all, out_all, key_value_every, router_all, gain_one, gain_two, gain_q, key_gain = (
        fetch_weights(w_q, w_out, key_value_weight, router, ln_attn, ln_moe, q_gain, k_gain)
    )
    kv_pick = select_heads(key_value_every, key_value_leading, key_value_local)
    normed_one, norm_one_back = jax.vjp(row_norm, residual, gain_one.astype(jnp.float32))
    normed_one_low = normed_one.astype(jnp.bfloat16)
    normed_all = lax.all_gather(normed_one_low[None], "col", axis=0, tiled=True)
    normed_flat = normed_all.reshape(flat_rows, width_model)
    raw_query = jnp.dot(normed_flat, q_all, preferred_element_type=jnp.float32).reshape(
        flat_rows, heads_mine, HEAD_SIZE
    )
    raw_kv = jnp.dot(normed_flat, kv_pick, preferred_element_type=jnp.float32)
    raw_key = raw_kv[:, :key_value_columns].reshape(flat_rows, key_value_local, HEAD_SIZE)
    query_rows, query_back = jax.vjp(
        partial(head_prep, places=places), raw_query, gain_q.astype(jnp.float32)
    )
    key_rows, key_back = jax.vjp(
        partial(head_prep, places=places), raw_key, key_gain.astype(jnp.float32)
    )
    query_heads = query_rows.astype(jnp.bfloat16).reshape(
        col_count, rows_dev, key_value_local, per_kv, HEAD_SIZE
    )
    key_low = key_rows.astype(jnp.bfloat16).reshape(col_count, rows_dev, key_value_columns)
    value_low = (
        raw_kv[:, key_value_columns:]
        .astype(jnp.bfloat16)
        .reshape(col_count, rows_dev, key_value_columns)
    )
    group_pair = lax.all_gather(jnp.stack([key_low, value_low], axis=1), "row", axis=2, tiled=True)
    all_key = jnp.concatenate([group_pair[:, 0, :PROMPT_TOKENS], key_low], axis=1).reshape(
        col_count, PROMPT_TOKENS + rows_dev, key_value_local, HEAD_SIZE
    )
    all_value = jnp.concatenate([group_pair[:, 1, :PROMPT_TOKENS], value_low], axis=1).reshape(
        col_count, PROMPT_TOKENS + rows_dev, key_value_local, HEAD_SIZE
    )
    prompt_place = jnp.arange(PROMPT_TOKENS, dtype=jnp.int32)
    query_place = row_index * rows_dev + jnp.arange(rows_dev, dtype=jnp.int32)
    query_prompt = query_place < PROMPT_TOKENS
    allow_prompt = jnp.where(
        query_prompt[:, None], prompt_place[None, :] <= query_place[:, None], True
    )
    allow_local = (
        jnp.logical_not(query_prompt[:, None])
        & (query_place[None, :] // CONTINUATION_LEN == query_place[:, None] // CONTINUATION_LEN)
        & (query_place[None, :] <= query_place[:, None])
    )
    allowed = jnp.concatenate([allow_prompt, allow_local], axis=1)
    mixed_output, lse_all = lax.map(
        partial(attend_forward, allowed=allowed, score_scale=score_scale),
        (query_heads, all_key, all_value),
    )
    attn_low = mixed_output.reshape(col_count, rows_dev, head_cols)
    piece = lax.slice_in_dim(attn_low, 0, lax.axis_size("col") * 1, axis=0)
    attn_sum = lax.psum_scatter(
        jnp.einsum("gtc,cd->gtd", piece, out_all, preferred_element_type=jnp.float32),
        "col",
        scatter_dimension=0,
        tiled=True,
    )
    hidden = residual + attn_sum[0]
    normed_two, norm_two_back = jax.vjp(row_norm, hidden, gain_two.astype(jnp.float32))
    normed_two_low = normed_two.astype(jnp.bfloat16)
    logits = jnp.dot(normed_two_low, router_all, preferred_element_type=jnp.float32)
    router_probs = jax.nn.softmax(logits, axis=-1)
    expert_ids = jnp.arange(expert_total, dtype=jnp.int32)
    chosen = chosen_ids[:, :, None] == expert_ids[None, None, :]
    picked = jnp.sum(jnp.where(chosen, router_probs[:, None, :], 0.0), axis=-1)
    picked_sum = jnp.sum(picked, axis=-1, keepdims=True)
    gates = picked / picked_sum
    counts = jnp.sum(chosen.astype(jnp.float32), axis=(0, 1))
    prob_sums = jnp.sum(router_probs, axis=0)
    count_all, prob_all = lax.psum((counts, prob_sums), ("row", "col"))
    share = count_all / (token_count * TOPK)
    aux_loss = expert_total * jnp.sum(share * prob_all / token_count)
    expert_load = jnp.stack([expert_total * share, expert_total * (prob_all / token_count)], axis=0)
    pair_count = rows_dev * TOPK
    flat_ids = chosen_ids.reshape(pair_count)
    one_hot = (flat_ids[:, None] == expert_ids[None, :]).astype(jnp.int32)
    before = jnp.cumsum(one_hot, axis=0) - one_hot
    slot_of = jnp.sum(before * one_hot, axis=1)
    slot_dest = flat_ids * capacity + slot_of
    slot_pair = (
        jnp.full((expert_total * capacity,), pair_count, jnp.int32)
        .at[slot_dest]
        .set(jnp.arange(pair_count, dtype=jnp.int32))
    )
    padded_in = jnp.concatenate([normed_two_low, jnp.zeros((1, width_model), jnp.bfloat16)], axis=0)
    send_rows = padded_in[slot_pair // TOPK].reshape(
        device_count, local_experts * capacity, width_model
    )
    received = lax.all_to_all(send_rows, ("row", "col"), split_axis=0, concat_axis=0, tiled=True)
    expert_in = received.reshape(device_count, local_experts, capacity, width_model)
    gate_pre = jnp.einsum("sjcd,jdf->sjcf", expert_in, w_gate, preferred_element_type=jnp.float32)
    up_pre = jnp.einsum("sjcd,jdf->sjcf", expert_in, w_up, preferred_element_type=jnp.float32)
    sigma_gate = jax.nn.sigmoid(gate_pre)
    silu_gate = gate_pre * sigma_gate
    inner_low = (silu_gate * up_pre).astype(jnp.bfloat16)
    expert_out = jnp.einsum(
        "sjcf,jfd->sjcd", inner_low, w_down, preferred_element_type=jnp.float32
    ).astype(jnp.bfloat16)
    returned = lax.all_to_all(
        expert_out.reshape(device_count, local_experts * capacity, width_model),
        ("row", "col"),
        split_axis=0,
        concat_axis=0,
        tiled=True,
    )
    pair_out = (
        returned.reshape(expert_total * capacity, width_model)[slot_dest]
        .reshape(rows_dev, TOPK, width_model)
        .astype(jnp.float32)
    )
    moe_branch = jnp.sum(gates[:, :, None] * pair_out, axis=1)
    layer_output = (hidden + moe_branch).astype(jnp.bfloat16)
    q_all, out_all, key_value_every, router_all, gain_one, gain_two, gain_q, key_gain = (
        fetch_weights(w_q, w_out, key_value_weight, router, ln_attn, ln_moe, q_gain, k_gain)
    )
    kv_pick = select_heads(key_value_every, key_value_leading, key_value_local)
    gate_grad = jnp.sum(upstream[:, None, :] * pair_out, axis=-1)
    pair_grad = (
        (gates[:, :, None] * upstream[:, None, :])
        .reshape(pair_count, width_model)
        .astype(jnp.bfloat16)
    )
    padded_grad = jnp.concatenate([pair_grad, jnp.zeros((1, width_model), jnp.bfloat16)], axis=0)
    send_grad = padded_grad[slot_pair].reshape(device_count, local_experts * capacity, width_model)
    grad_in = lax.all_to_all(
        send_grad, ("row", "col"), split_axis=0, concat_axis=0, tiled=True
    ).reshape(device_count, local_experts, capacity, width_model)
    inner_grad = jnp.einsum("sjcd,jfd->sjcf", grad_in, w_down, preferred_element_type=jnp.float32)
    grad_down = jnp.einsum("sjcf,sjcd->jfd", inner_low, grad_in, preferred_element_type=jnp.float32)
    gate_grad_low = (
        inner_grad * up_pre * sigma_gate * (1.0 + gate_pre * (1.0 - sigma_gate))
    ).astype(jnp.bfloat16)
    up_grad_low = (inner_grad * silu_gate).astype(jnp.bfloat16)
    grad_gate = jnp.einsum(
        "sjcd,sjcf->jdf", expert_in, gate_grad_low, preferred_element_type=jnp.float32
    )
    grad_up = jnp.einsum(
        "sjcd,sjcf->jdf", expert_in, up_grad_low, preferred_element_type=jnp.float32
    )
    in_grad = jnp.einsum(
        "sjcf,jdf->sjcd", gate_grad_low, w_gate, preferred_element_type=jnp.float32
    ) + jnp.einsum("sjcf,jdf->sjcd", up_grad_low, w_up, preferred_element_type=jnp.float32)
    back_grad = lax.all_to_all(
        in_grad.astype(jnp.bfloat16).reshape(device_count, local_experts * capacity, width_model),
        ("row", "col"),
        split_axis=0,
        concat_axis=0,
        tiled=True,
    )
    pair_in_grad = back_grad.reshape(expert_total * capacity, width_model)[slot_dest].reshape(
        rows_dev, TOPK, width_model
    )
    moe_in_grad = jnp.sum(pair_in_grad.astype(jnp.float32), axis=1)
    weighted_sum = jnp.sum(gate_grad * gates, axis=-1, keepdims=True)
    picked_grad = (gate_grad - weighted_sum) / picked_sum
    prob_grad = (
        jnp.sum(jnp.where(chosen, picked_grad[:, :, None], 0.0), axis=1)
        + AUX_COEF * expert_total * share[None, :] / token_count
    )
    logit_grad = router_probs * (
        prob_grad - jnp.sum(router_probs * prob_grad, axis=-1, keepdims=True)
    )
    logit_low = logit_grad.astype(jnp.bfloat16)
    grad_router = jnp.dot(normed_two_low.T, logit_low, preferred_element_type=jnp.float32)
    normed_two_grad = moe_in_grad + jnp.dot(
        logit_low, router_all.T, preferred_element_type=jnp.float32
    )
    hidden_part, gain_two_grad = norm_two_back(normed_two_grad)
    hidden_grad = upstream + hidden_part
    branch_low = hidden_grad.astype(jnp.bfloat16)
    branch_all = lax.all_gather(branch_low[None], "col", axis=0, tiled=True)
    grad_out_mine = jnp.einsum(
        "gtc,gtd->cd", attn_low, branch_all, preferred_element_type=jnp.float32
    )
    mix_grad = (
        jnp.einsum("gtd,cd->gtc", branch_all, out_all, preferred_element_type=jnp.float32)
        .astype(jnp.bfloat16)
        .reshape(col_count, rows_dev, key_value_local, per_kv, HEAD_SIZE)
    )
    query_grad, key_grad_all, value_grad_all = lax.map(
        partial(attend_backward, allowed=allowed, score_scale=score_scale),
        (query_heads, all_key, all_value, mix_grad, lse_all),
    )
    pair_grads = jnp.stack([key_grad_all, value_grad_all], axis=1).reshape(
        col_count, 2, PROMPT_TOKENS + rows_dev, key_value_columns
    )
    prompt_term = jnp.concatenate(
        [
            pair_grads[:, :, :PROMPT_TOKENS],
            jnp.zeros((col_count, 2, GROUP_TOKENS - PROMPT_TOKENS, key_value_columns), jnp.float32),
        ],
        axis=2,
    )
    summed_pair = lax.psum_scatter(
        prompt_term.astype(jnp.bfloat16), "row", scatter_dimension=2, tiled=True
    ).astype(jnp.float32)
    own_pair = pair_grads[:, :, PROMPT_TOKENS:] + summed_pair
    raw_query_grad, gain_q_grad = query_back(query_grad.reshape(flat_rows, heads_mine, HEAD_SIZE))
    raw_key_grad, gain_k_grad = key_back(
        own_pair[:, 0].reshape(flat_rows, key_value_local, HEAD_SIZE)
    )
    query_low_grad = raw_query_grad.reshape(col_count, rows_dev, head_cols).astype(jnp.bfloat16)
    kv_grad = jnp.concatenate(
        [raw_key_grad.reshape(col_count, rows_dev, key_value_columns), own_pair[:, 1]], axis=2
    )
    grad_q_mine = jnp.dot(
        normed_flat.T,
        query_low_grad.reshape(flat_rows, head_cols),
        preferred_element_type=jnp.float32,
    )
    key_value_gradient_local = jnp.dot(
        normed_flat.astype(jnp.float32).T,
        kv_grad.reshape(flat_rows, 2 * key_value_columns),
        precision=lax.Precision.HIGHEST,
    )
    key_value_gradient_full = jnp.zeros((width_model, 2 * KEY_VALUE_HEADS * HEAD_SIZE), jnp.float32)
    key_value_gradient_full = lax.dynamic_update_slice_in_dim(
        key_value_gradient_full,
        key_value_gradient_local[:, :key_value_columns],
        key_value_leading * HEAD_SIZE,
        1,
    )
    key_value_gradient_full = lax.dynamic_update_slice_in_dim(
        key_value_gradient_full,
        key_value_gradient_local[:, key_value_columns:],
        KEY_VALUE_HEADS * HEAD_SIZE + key_value_leading * HEAD_SIZE,
        1,
    )
    kv_pick_wide = kv_pick.astype(jnp.float32)
    query_part = jnp.einsum(
        "gtc,dc->gtd", query_low_grad, q_all, preferred_element_type=jnp.float32
    )
    input_sum = lax.psum_scatter(
        (
            query_part
            + jnp.einsum("gtc,dc->gtd", kv_grad, kv_pick_wide, precision=lax.Precision.HIGHEST)
        ).astype(jnp.bfloat16),
        "col",
        scatter_dimension=0,
        tiled=True,
    ).astype(jnp.float32)
    input_part, gain_one_grad = norm_one_back(input_sum[0])
    input_grad = hidden_grad + input_part
    grad_q_part, grad_out_part = (
        lax.psum_scatter(
            grad_q_mine.astype(jnp.bfloat16), "row", scatter_dimension=0, tiled=True
        ).astype(jnp.float32),
        lax.psum_scatter(
            grad_out_mine.astype(jnp.bfloat16), "row", scatter_dimension=1, tiled=True
        ).astype(jnp.float32),
    )
    shared = (
        lax.psum_scatter(key_value_gradient_full, ("row", "col"), scatter_dimension=0, tiled=True),
        lax.psum_scatter(grad_router, ("row", "col"), scatter_dimension=0, tiled=True),
        lax.psum_scatter(gain_one_grad, ("row", "col"), scatter_dimension=0, tiled=True),
        lax.psum_scatter(gain_two_grad, ("row", "col"), scatter_dimension=0, tiled=True),
        lax.psum_scatter(gain_q_grad, ("row", "col"), scatter_dimension=0, tiled=True),
        lax.psum_scatter(gain_k_grad, ("row", "col"), scatter_dimension=0, tiled=True),
    )
    return (
        layer_output[None],
        aux_loss,
        input_grad[None],
        grad_q_part,
        shared[0],
        grad_out_part,
        shared[1],
        shared[2],
        shared[3],
        shared[4],
        shared[5],
        grad_gate,
        grad_up,
        grad_down,
        expert_load,
    )


def solution(mesh):
    in_specs = (
        P("col", "row", None),
        P("col", "row", None),
        P("col", "row", None),
        P(None, "row"),
        P("row", "col"),
        P("row", None),
        P("col", "row"),
        P("row", None),
        P("row"),
        P("row"),
        P("row"),
        P("row"),
        P(("row", "col"), None, None),
        P(("row", "col"), None, None),
        P(("row", "col"), None, None),
    )
    out_specs = (
        P("col", "row", None),
        P(),
        P("col", "row", None),
        P("row", "col"),
        P(("row", "col"), None),
        P("col", "row"),
        P(("row", "col"), None),
        P(("row", "col")),
        P(("row", "col")),
        P(("row", "col")),
        P(("row", "col")),
        P(("row", "col"), None, None),
        P(("row", "col"), None, None),
        P(("row", "col"), None, None),
        P(),
    )
    return jax.shard_map(
        per_device, mesh=mesh, in_specs=in_specs, out_specs=out_specs, check_vma=False
    )
```

profile of v0, /device:TPU:0, one launch (start us, length us, event | category | flops | bytes accessed | tf_op | source)
XLA Modules:
  0.0 3912.5 jit_solution(5676710209304580674)
XLA Ops:
  62.0 86.6 %all-gather.10.cloned.1.call-done = bf16[4,512,2048]{2,1,0:T(8,128)(2,1)} async-done(((bf16[1,512,2048]{2,1,0:T(8,128)(2,1)}), bf16[4,512,2048]{2,1,0:T(8,128)(2,1)}) %all-gather.10.cloned.1.call-update) | async-done | bytes 8388624 | tf_op jit(solution)/shard_map/all_gather | solution.py:179
  169.5 27.9 all-gather.12.cloned.1.call-done
  251.9 28.4 all-gather.16.cloned.1.call-done
  286.3 246.7 %while.26 = (s32[]{:T(128)}, bf16[4,512,1,8,128]{1,4,3,0,2:T(8,128)(2,1)}, f32[4,512,1,8,1]{1,3,4,2,0:T(8,128)}, pred[512,2560]{1,0:T(8,128)(4,1)}, bf16[4,512,1...) while((s32[]{:T(128)}, ...), condition=%wide.region_6.7_spmd, body=%wide.region_3.6_spmd.sunk | while | flops 5495058432 | bytes 142738560 | solution.py:220
  286.3 19.1 fusion.191
  305.4 18.9 fusion.192
  324.3 19.0 fusion.193
  348.4 18.7 fusion.191
  367.1 18.7 fusion.192
  385.8 19.0 fusion.193
  410.0 18.7 fusion.191
  428.6 18.7 fusion.192
  447.3 19.0 fusion.193
  471.5 18.7 fusion.191
  490.2 18.7 fusion.192
  508.9 19.0 fusion.193
  559.7 18.1 reduce-window.6
  597.6 103.2 %reduce-scatter.24.cloned.1.call-done = f32[1,512,2048]{2,1,0:T(8,128)} async-done(((f32[4,512,2048]{2,1,0:T(8,128)}), f32[1,512,2048]{2,1,0:T(8,128)}) %reduce-scatter.24.cloned.1.call-update) | async-done | bytes 4194320
  709.1 33.2 gather_fusion
  747.1 387.5 %all_gather.46 = bf16[2048,32]{0,1:T(8,128)(2,1)S(1)} all-gather(bf16[256,32]{0,1:T(8,128)(2,1)S(1)} %copy-done.84), channel_id=1, replica_groups=mesh['row'=8,'col'=4] {'row'}, dimensions={0}, use_global_device_ids=true | all-gather | bytes 147456 | tf_op jit(solution)/shard_map/all_gather | solution.py:61
  1154.7 39.3 %gather_fusion.2 = bf16[4096,2048]{1,0:T(8,128)(2,1)} fusion(bf16[4097,2048]{1,0:T(8,128)(2,1)} %concatenate.79, s32[4096]{0:T(1024)S(1)} %get-tuple-element.240), kind=kCustom, calls=%fused_computation.2 | custom fusion | bytes 33570816 | tf_op jit(solution)/shard_map/gather | solution.py:298
  1199.2 20.4 fusion.91
  1219.5 362.4 %all-to-all-done.2 = bf16[32,128,2048]{2,1,0:T(8,128)(2,1)} async-done(((bf16[32,128,2048]{2,1,0:T(8,128)(2,1)}), bf16[32,128,2048]{2,1,0:T(8,128)(2,1)}, u32[]{:S(2)}, u32[]{:S(2)}) %all-to-all-start.2) | async-done | bytes 16777248 | tf_op jit(solution)/shard_map/all_to_all | solution.py:299
  1582.0 20.8 fusion.87
  1602.7 30.4 fusion.56
  1633.1 19.7 convolution_convert_fusion
  1656.9 20.0 fusion.59
  1676.9 26.2 add_convert_fusion
  1703.1 336.7 %all-to-all-done.1 = bf16[32,128,2048]{2,1,0:T(8,128)(2,1)} async-done(((bf16[32,128,2048]{2,1,0:T(8,128)(2,1)}), bf16[32,128,2048]{2,1,0:T(8,128)(2,1)}, u32[]{:S(2)}, u32[]{:S(2)}) %all-to-all-start.1) | async-done | bytes 16777248 | tf_op jit(solution)/shard_map/all_to_all | solution.py:273
  2043.7 39.8 %gather_fusion.1 = bf16[4096,2048]{1,0:T(8,128)(2,1)} fusion(bf16[4096,2048]{1,0:T(8,128)(2,1)} %bitcast.61, s32[4096]{0:T(1024)S(1)} %broadcast_clamp_fusion), kind=kCustom, calls=%fused_computation.1 | custom fusion | bytes 33570816 | tf_op jit(solution)/shard_map/gather | solution.py:281
  2083.6 17.0 fusion.43
  2100.9 344.9 %psum.14 = f32[32]{0:T(128)S(1)} all-reduce(f32[32]{0:T(128)S(1)} %get-tuple-element.177), channel_id=1, replica_groups=mesh['row'=8,'col'=4] {'row','col'}, use_global_device_ids=true, to_apply=%region_19.20 | all-reduce | flops 32 | bytes 256 | tf_op jit(solution)/shard_map/psum | solution.py:244
  2447.1 39.3 %gather_fusion.3 = bf16[4096,2048]{1,0:T(8,128)(2,1)} fusion(bf16[4096,2048]{1,0:T(8,128)(2,1)} %bitcast.77, s32[4096]{0:T(1024)S(1)} %broadcast_clamp_fusion), kind=kCustom, calls=%fused_computation.3 | custom fusion | bytes 33570816 | tf_op jit(solution)/shard_map/gather | solution.py:324
  2507.1 87.5 %all-gather.20.cloned.1.call-done = bf16[2048,2048]{1,0:T(8,128)(2,1)} async-done(((bf16[512,2048]{1,0:T(8,128)(2,1)}), bf16[2048,2048]{1,0:T(8,128)(2,1)}) %all-gather.20.cloned.1.call-update) | async-done | bytes 8388624 | tf_op jit(solution)/shard_map/all_gather | solution.py:345
  2610.3 676.7 %while.27 = (s32[]{:T(128)}, f32[4,512,1,8,128]{1,0,4,3,2:T(4,128)}, f32[4,2560,1,128]{3,1,2,0:T(8,128)}, f32[4,2560,1,128]{3,1,2,0:T(8,128)}, pred[512,2560]{1,...) while((s32[]{:T(128)}, ...), condition=%wide.region_31.32_spmd, body=%wide.region_29.31_spmd.sunk | while | flops 13516992512 | bytes 421218464 | solution.py:354
  2612.4 17.5 fusion.200
  2629.9 29.3 multiply_reduce_fusion.12
  2659.2 34.2 multiply_convert_fusion.4
  2693.4 17.0 fusion.202
  2738.5 41.0 %dynamic_update_slice.42 = f32[4,512,1,8,128]{1,0,4,3,2:T(4,128)} dynamic-update-slice(f32[4,512,1,8,128]{1,0,4,3,2:T(4,128)} %get-tuple-element.408, f32[1,512,1,8,128]{1,0,4,3,2:T(1,128)} %copy.193, s32[]{:T(128)S(6)} %copy.214, s32[]{:T(128)} %constant.154.clone.1..sunk, s32[]{:T(128)} %constant.154.clone.1..sunk, s32[]{:T(128)} %constant.154.clone.1..sunk, s32[]{:T(128)} %constant.154.clone.1..sunk) | dynamic-update-slice | bytes 4194308 | tf_op jit(solution)/shard_map/while/body/jit(dynamic_update_index_in_dim)/dynamic_update_slice | solution.py:354
  2781.5 17.5 fusion.200
  2799.0 29.2 multiply_reduce_fusion.12
  2828.2 34.2 multiply_convert_fusion.4
  2862.3 17.0 fusion.202
  2907.5 41.0 %dynamic_update_slice.42 = f32[4,512,1,8,128]{1,0,4,3,2:T(4,128)} dynamic-update-slice(f32[4,512,1,8,128]{1,0,4,3,2:T(4,128)} %get-tuple-element.408, f32[1,512,1,8,128]{1,0,4,3,2:T(1,128)} %copy.193, s32[]{:T(128)S(6)} %copy.214, s32[]{:T(128)} %constant.154.clone.1..sunk, s32[]{:T(128)} %constant.154.clone.1..sunk, s32[]{:T(128)} %constant.154.clone.1..sunk, s32[]{:T(128)} %constant.154.clone.1..sunk) | dynamic-update-slice | bytes 4194308 | tf_op jit(solution)/shard_map/while/body/jit(dynamic_update_index_in_dim)/dynamic_update_slice | solution.py:354
  2950.5 17.5 fusion.200
  2968.0 29.3 multiply_reduce_fusion.12
  2997.3 34.2 multiply_convert_fusion.4
  3031.4 17.0 fusion.202
  3076.5 41.0 %dynamic_update_slice.42 = f32[4,512,1,8,128]{1,0,4,3,2:T(4,128)} dynamic-update-slice(f32[4,512,1,8,128]{1,0,4,3,2:T(4,128)} %get-tuple-element.408, f32[1,512,1,8,128]{1,0,4,3,2:T(1,128)} %copy.193, s32[]{:T(128)S(6)} %copy.214, s32[]{:T(128)} %constant.154.clone.1..sunk, s32[]{:T(128)} %constant.154.clone.1..sunk, s32[]{:T(128)} %constant.154.clone.1..sunk, s32[]{:T(128)} %constant.154.clone.1..sunk) | dynamic-update-slice | bytes 4194308 | tf_op jit(solution)/shard_map/while/body/jit(dynamic_update_index_in_dim)/dynamic_update_slice | solution.py:354
  3119.5 17.5 fusion.200
  3137.0 29.3 multiply_reduce_fusion.12
  3166.3 34.2 multiply_convert_fusion.4
  3200.5 17.0 fusion.202
  3245.6 41.0 %dynamic_update_slice.42 = f32[4,512,1,8,128]{1,0,4,3,2:T(4,128)} dynamic-update-slice(f32[4,512,1,8,128]{1,0,4,3,2:T(4,128)} %get-tuple-element.408, f32[1,512,1,8,128]{1,0,4,3,2:T(1,128)} %copy.193, s32[]{:T(128)S(6)} %copy.214, s32[]{:T(128)} %constant.154.clone.1..sunk, s32[]{:T(128)} %constant.154.clone.1..sunk, s32[]{:T(128)} %constant.154.clone.1..sunk, s32[]{:T(128)} %constant.154.clone.1..sunk) | dynamic-update-slice | bytes 4194308 | tf_op jit(solution)/shard_map/while/body/jit(dynamic_update_index_in_dim)/dynamic_update_slice | solution.py:354
  3437.6 20.5 convolution_bitcast_fusion.1
  3458.1 21.4 convolution_bitcast_fusion.2
  3479.6 19.6 fusion.84
  3501.9 28.3 reduce-scatter.22.cloned.1.call-done
  3531.7 47.0 %reduce-scatter.20.cloned.1.call-done = bf16[1024,256]{1,0:T(8,128)(2,1)} async-done(((bf16[1024,2048]{1,0:T(8,128)(2,1)}), bf16[1024,256]{1,0:T(8,128)(2,1)}) %reduce-scatter.20.cloned.1.call-update) | async-done | bytes 524304 | tf_op jit(solution)/shard_map/reduce_scatter | solution.py:422
  3580.7 48.5 %reduce-scatter.16.cloned.1.call-done = bf16[256,1024]{1,0:T(8,128)(2,1)} async-done(((bf16[2048,1024]{1,0:T(8,128)(2,1)}), bf16[256,1024]{1,0:T(8,128)(2,1)}) %reduce-scatter.16.cloned.1.call-update) | async-done | bytes 524304 | tf_op jit(solution)/shard_map/reduce_scatter | solution.py:419
  3631.4 85.7 %reduce-scatter.26.cloned.1.call-done = bf16[1,512,2048]{2,1,0:T(8,128)(2,1)} async-done(((bf16[4,512,2048]{2,1,0:T(8,128)(2,1)}), bf16[1,512,2048]{2,1,0:T(8,128)(2,1)}) %reduce-scatter.26.cloned.1.call-update) | async-done | bytes 2097168
  3720.4 41.8 %all-reduce.15 = (f32[32]{0:T(128)S(1)}, f32[2048]{0:T(1024)S(1)}, f32[2048]{0:T(1024)S(1)}, f32[128]{0:T(128)S(1)}, f32[128]{0:T(128)S(1)}) all-reduce(f32[32]{0:T(128)S(1)} %copy-done.92, f32[2048]{0:T(1024)S(1)} %get-tuple-element.170, f32[2048]{0:T(1024)S(1)} %copy-done.71, ...), channel_id=1, replica_groups=mesh['row'=8,'col'=4] {'row','col'}, use_global_device_ids=true, to_apply=%region_21.22 | all-reduce | flops 4384 | bytes 35072 | tf_op jit(solution)/shard_map/psum | solution.py:244
  3774.8 129.9 %reduce-scatter.18.cloned.1.call-done = f32[64,1024]{1,0:T(8,128)} async-done(((f32[2048,1024]{1,0:T(8,128)}), f32[64,1024]{1,0:T(8,128)}) %reduce-scatter.18.cloned.1.call-update) | async-done | bytes 262160 | tf_op jit(solution)/shard_map/reduce_scatter | solution.py:427
  (422 shorter events, 580.3 us)
Async XLA Ops:
  7.2 1595.5 %copy-start = (bf16[1,2048,768]{2,1,0:T(8,128)(2,1)S(1)}, bf16[1,2048,768]{2,1,0:T(8,128)(2,1)}, u32[]{:S(2)}) copy-start(bf16[1,2048,768]{2,1,0:T(8,128)(2,1)} %param.31) | copy-start | bytes 9437188
  7.2 52.6 %all-gather.14.cloned.1.call-start = ((), (), s32[]{:S(2)}) async-start(), calls=%async_computation.13 | async-start | bytes 4718592 | tf_op jit(solution)/shard_map/all_gather | solution.py:60
  7.9 140.7 %all-gather.10.cloned.1.call-start = ((), (), s32[]{:S(2)}) async-start(), calls=%async_computation.11 | async-start | bytes 10485760 | tf_op jit(solution)/shard_map/all_gather | solution.py:179
  22.3 23.8 copy-start.85
  29.1 168.3 %all-gather.12.cloned.1.call-start = ((), (), s32[]{:S(2)}) async-start(), calls=%async_computation.12 | async-start | bytes 4718592 | tf_op jit(solution)/shard_map/all_gather | solution.py:58
  29.8 250.4 %all-gather.16.cloned.1.call-start = ((), (), s32[]{:S(2)}) async-start(), calls=%async_computation.14 | async-start | bytes 9437184 | tf_op jit(solution)/shard_map/all_gather | solution.py:201
  46.1 109.1 %copy-start.88 = (f32[128]{0:T(128)}, f32[128]{0:T(128)S(1)}, u32[]{:S(2)}) copy-start(f32[128]{0:T(128)S(1)} %convert_element_type.182) | copy-start | bytes 1540
  46.1 118.3 %copy-start.58 = (f32[1,4,4,128]{3,1,2,0:T(4,128)}, f32[1,4,4,128]{3,1,2,0:T(4,128)S(1)}, u32[]{:S(2)}) copy-start(f32[1,4,4,128]{3,1,2,0:T(4,128)S(1)} %copy.179) | copy-start | bytes 24580
  46.1 118.3 %copy-start.90 = (f32[64]{0:T(128)}, f32[64]{0:T(128)S(1)}, u32[]{:S(2)}) copy-start(f32[64]{0:T(128)S(1)} %multiply_power_fusion) | copy-start | bytes 772
  163.5 369.5 %all-gather.18.cloned.1.call-start = ((), (), s32[]{:S(2)}) async-start(), calls=%async_computation.15 | async-start | bytes 4718592 | tf_op jit(solution)/shard_map/all_gather | solution.py:59
  164.1 536.8 %reduce-scatter.24.cloned.1.call-start = ((), (), s32[]{:S(2)}) async-start(), calls=%async_computation.22 | async-start | bytes 20971520
  167.2 50.7 %copy-start.86 = (f32[128]{0:T(128)}, f32[128]{0:T(128)S(1)}, u32[]{:S(2)}) copy-start(f32[128]{0:T(128)S(1)} %convert_element_type.179) | copy-start | bytes 1540
  286.3 19.1 copy-start.2
  348.4 18.7 copy-start.2
  410.0 18.7 copy-start.2
  471.5 18.7 copy-start.2
  558.5 146.0 %copy-start.51 = (f32[8,1,256]{2,1,0:T(1,128)}, f32[8,1,256]{2,1,0:T(1,128)S(1)}, u32[]{:S(2)}) copy-start(f32[8,1,256]{2,1,0:T(1,128)S(1)} %convert_element_type.217) | copy-start | bytes 24580
  742.3 451.7 %all-to-all-start = ((bf16[32,128,2048]{2,1,0:T(8,128)(2,1)}), bf16[32,128,2048]{2,1,0:T(8,128)(2,1)}, u32[]{:S(2)}, u32[]{:S(2)}) async-start(bf16[32,128,2048]{2,1,0:T(8,128)(2,1)} %bitcast.425), calls=%async_computation | async-start | bytes 33554432 | tf_op jit(solution)/shard_map/all_to_all | solution.py:263
  747.1 391.7 %copy-start.14 = (bf16[512,2048]{1,0:T(8,128)(2,1)S(1)}, bf16[512,2048]{1,0:T(8,128)(2,1)}, u32[]{:S(2)}) copy-start(bf16[512,2048]{1,0:T(8,128)(2,1)} %copy-done.13) | copy-start | bytes 6291460
  1194.0 388.0 %all-to-all-start.2 = ((bf16[32,128,2048]{2,1,0:T(8,128)(2,1)}), bf16[32,128,2048]{2,1,0:T(8,128)(2,1)}, u32[]{:S(2)}, u32[]{:S(2)}) async-start(bf16[32,128,2048]{2,1,0:T(8,128)(2,1)} %bitcast.426), calls=%async_computation.2 | async-start | bytes 33554432 | tf_op jit(solution)/shard_map/all_to_all | solution.py:299
  1652.8 387.0 %all-to-all-start.1 = ((bf16[32,128,2048]{2,1,0:T(8,128)(2,1)}), bf16[32,128,2048]{2,1,0:T(8,128)(2,1)}, u32[]{:S(2)}, u32[]{:S(2)}) async-start(bf16[32,128,2048]{2,1,0:T(8,128)(2,1)} %convolution_convert_fusion), calls=%async_computation.1 | async-start | bytes 33554432 | tf_op jit(solution)/shard_map/all_to_all | solution.py:273
  1703.1 340.6 %copy-start.65 = (s32[4096,1]{0,1:T(1,128)S(1)}, s32[4096,1]{0,1:T(1,128)}, u32[]{:S(2)}) copy-start(s32[4096,1]{0,1:T(1,128)} %copy-done.64) | copy-start | bytes 49156
  2039.8 407.3 %all-to-all-start.3 = ((bf16[32,128,2048]{2,1,0:T(8,128)(2,1)}), bf16[32,128,2048]{2,1,0:T(8,128)(2,1)}, u32[]{:S(2)}, u32[]{:S(2)}) async-start(bf16[32,128,2048]{2,1,0:T(8,128)(2,1)} %add_convert_fusion), calls=%async_computation.3 | async-start | bytes 33554432 | tf_op jit(solution)/shard_map/all_to_all | solution.py:317
  2043.7 551.0 %all-gather.20.cloned.1.call-start = ((), (), s32[]{:S(2)}) async-start(), calls=%async_computation.20 | async-start | bytes 10485760 | tf_op jit(solution)/shard_map/all_gather | solution.py:345
  2043.7 39.8 %copy-start.36 = (f32[512,8]{1,0:T(8,128)S(1)}, f32[512,8]{1,0:T(8,128)}, u32[]{:S(2)}) copy-start(f32[512,8]{1,0:T(8,128)} %copy-done.35) | copy-start | bytes 49156
  2083.5 17.1 copy-start.55
  2083.5 17.1 copy-start.77
  2083.5 17.2 copy-start.50
  2083.5 362.8 %copy-start.40 = (f32[512,32]{0,1:T(8,128)S(1)}, f32[512,32]{0,1:T(8,128)}, u32[]{:S(2)}) copy-start(f32[512,32]{0,1:T(8,128)} %copy-done.39) | copy-start | bytes 196612
  2083.5 362.8 %copy-start.67 = (f32[512]{0:T(512)S(1)}, f32[512]{0:T(512)}, u32[]{:S(2)}) copy-start(f32[512]{0:T(512)} %copy-done.66) | copy-start | bytes 6148
  2083.5 362.8 %copy-start.75 = (f32[512]{0:T(512)S(1)}, f32[512]{0:T(512)}, u32[]{:S(2)}) copy-start(f32[512]{0:T(512)} %copy-done.74) | copy-start | bytes 6148
  2445.8 40.5 %copy-start.94 = (f32[32]{0:T(128)}, f32[32]{0:T(128)S(1)}, u32[]{:S(2)}) copy-start(f32[32]{0:T(128)S(1)} %psum.14) | copy-start | bytes 388
  2447.0 52.8 %copy-start.45 = (bf16[512,32]{0,1:T(8,128)(2,1)}, bf16[512,32]{0,1:T(8,128)(2,1)S(1)}, u32[]{:S(2)}) copy-start(bf16[512,32]{0,1:T(8,128)(2,1)S(1)} %multiply_convert_fusion.2) | copy-start | bytes 98308
  2486.3 13.6 copy-start.6
  2486.3 13.6 copy-start.9
  2486.3 13.6 copy-start.42
  2486.3 13.6 copy-start.52
  2486.4 13.6 copy-start.69
  2507.1 887.7 %reduce-scatter.14.cloned.1.call-start = ((), (), s32[]{:S(2)}) async-start(), calls=%async_computation.16 | async-start | bytes 9437184 | tf_op jit(solution)/shard_map/reduce_scatter | solution.py:368
  2710.4 13.9 copy-start.4
  2879.3 13.9 copy-start.4
  3048.4 13.9 copy-start.4
  3217.5 13.9 copy-start.4
  3305.0 225.3 %reduce-scatter.22.cloned.1.call-start = ((), (), s32[]{:S(2)}) async-start(), calls=%async_computation.21 | async-start | bytes 1081344
  3308.5 270.1 %reduce-scatter.20.cloned.1.call-start = ((), (), s32[]{:S(2)}) async-start(), calls=%async_computation.19 | async-start | bytes 4718592 | tf_op jit(solution)/shard_map/reduce_scatter | solution.py:422
  3323.2 306.0 %reduce-scatter.16.cloned.1.call-start = ((), (), s32[]{:S(2)}) async-start(), calls=%async_computation.17 | async-start | bytes 4718592 | tf_op jit(solution)/shard_map/reduce_scatter | solution.py:419
  3378.5 338.5 %reduce-scatter.26.cloned.1.call-start = ((), (), s32[]{:S(2)}) async-start(), calls=%async_computation.23 | async-start | bytes 10485760
  3417.4 487.2 %reduce-scatter.18.cloned.1.call-start = ((), (), s32[]{:S(2)}) async-start(), calls=%async_computation.18 | async-start | bytes 8650752 | tf_op jit(solution)/shard_map/reduce_scatter | solution.py:427
  3437.6 42.0 %slice-start.2 = ((s8[6291456]{0:T(1024)(128)(4,1)}), s8[4194304]{0:T(1024)(128)(4,1)S(1)}, s32[]{:S(2)}) async-start(s8[6291456]{0:T(1024)(128)(4,1)} %bitcast.465), calls=%async_computation.26 | async-start | bytes 8388608
  3458.1 21.4 slice-start.3
  3479.6 19.6 copy-start.7
  3479.6 19.6 copy-start.10
  3479.6 19.6 copy-start.18
  3499.2 217.8 %copy-start.57 = (f32[8,1,256]{2,1,0:T(1,128)S(1)}, f32[8,1,256]{2,1,0:T(1,128)}, u32[]{:S(2)}) copy-start(f32[8,1,256]{2,1,0:T(1,128)} %copy-done.56) | copy-start | bytes 24580
  3499.2 217.8 %copy-start.73 = (f32[512]{0:T(512)S(1)}, f32[512]{0:T(512)}, u32[]{:S(2)}) copy-start(f32[512]{0:T(512)} %copy-done.72) | copy-start | bytes 6148
  3501.9 218.5 %copy-start.71 = (f32[2048]{0:T(1024)S(1)}, f32[2048]{0:T(1024)}, u32[]{:S(2)}) copy-start(f32[2048]{0:T(1024)} %get-tuple-element.166) | copy-start | bytes 24580
  3501.9 218.5 %copy-start.92 = (f32[32]{0:T(128)S(1)}, f32[32]{0:T(128)}, u32[]{:S(2)}) copy-start(f32[32]{0:T(128)} %get-tuple-element.175) | copy-start | bytes 388
  3501.9 262.7 %copy-start.95 = (f32[32]{0:T(128)S(1)}, f32[32]{0:T(128)}, u32[]{:S(2)}) copy-start(f32[32]{0:T(128)} %copy-done.94) | copy-start | bytes 388
  3501.9 264.0 %copy-start.93 = (f32[1,32]{1,0:T(1,128)S(1)}, f32[1,32]{1,0:T(1,128)}, u32[]{:S(2)}) copy-start(f32[1,32]{1,0:T(1,128)} %get-tuple-element.244) | copy-start | bytes 388
  3501.9 264.6 %copy-start.79 = (f32[512]{0:T(512)S(1)}, f32[512]{0:T(512)}, u32[]{:S(2)}) copy-start(f32[512]{0:T(512)} %copy-done.78) | copy-start | bytes 6148
  3501.9 264.6 %copy-start.53 = (f32[8,1,256]{2,1,0:T(1,128)S(1)}, f32[8,1,256]{2,1,0:T(1,128)}, u32[]{:S(2)}) copy-start(f32[8,1,256]{2,1,0:T(1,128)} %copy-done.51) | copy-start | bytes 24580
  3501.9 264.6 %copy-start.70 = (f32[512]{0:T(512)S(1)}, f32[512]{0:T(512)}, u32[]{:S(2)}) copy-start(f32[512]{0:T(512)} %copy-done.68) | copy-start | bytes 6148
  3501.9 264.6 %copy-start.83 = (f32[512]{0:T(512)S(1)}, f32[512]{0:T(512)}, u32[]{:S(2)}) copy-start(f32[512]{0:T(512)} %copy-done.82) | copy-start | bytes 6148
  3766.5 138.2 %copy-start.1 = (bf16[1,2048,768]{2,1,0:T(8,128)(2,1)S(1)}, bf16[1,2048,768]{2,1,0:T(8,128)(2,1)}, u32[]{:S(2)}) copy-start(bf16[1,2048,768]{2,1,0:T(8,128)(2,1)} %param.31) | copy-start | bytes 9437188
  (63 other events, 235.8 us)
Sparse Core Ops, SparseCore 0:
  9.6 50.1 all-gather.13
  62.2 86.3 all-gather.9
  150.2 47.1 all-gather.11
  199.5 80.7 all-gather.15
  281.7 46.3 all-gather.17
  548.6 152.1 reduce-scatter.23
  2507.2 87.3 all-gather.19
  3305.1 89.6 reduce-scatter.13
  3397.0 133.1 reduce-scatter.21
  3532.5 46.1 reduce-scatter.19
  3581.1 48.1 reduce-scatter.15
  3632.5 84.5 reduce-scatter.25
  3719.9 184.6 reduce-scatter.17
where the time goes:
time: 3930 us; the launch traced here: 3910 us
  waiting for transfers between devices  1390 us (35%)
  blocking collectives  811 us (21%)
  matrix products  804 us (20%)
  local copies, waits for them, and re-layouts  508 us (13%)
  other arithmetic  364 us (9%)
    all_gather x1, blocking collectives, fetch_weights(): lax.all_gather(router, 'row', axis=0, tiled=True)  388 us
    psum x2, blocking collectives, per_device(): count_all, prob_all = lax.psum((counts, prob_sums), ('row', 'col'))  387 us
    all_to_all x1, waiting for transfers between devices, per_device(): lax.all_to_all(send_grad, ('row', 'col'), split_axis=0, concat_axis=0, ti...  362 us
    all_to_all x1, waiting for transfers between devices, per_device(): lax.all_to_all(expert_out.reshape(device_count, local_experts * capacity,...  337 us
    unnamed x16, waiting for transfers between devices  219 us
    dot_general x8, matrix products, key_scores(): jnp.einsum('tgd,kd->tgk', query_part, key_part, preferred_element_type=jn...  192 us
    dynamic_update_slice x8, local copies, waits for them, and re-layouts, per_device(): lax.map(partial(attend_backward, allowed=allowed, score_scale=score_scale...  188 us
    convert_element_type x4, other arithmetic, attend_backward(): score_low = (attn_probs * (prob_grad - center)).astype(jnp.bfloat16)  137 us
  transfers between devices with their start and end apart: 17, of which 14 were waited for; matrix products, arithmetic and copies ran while one was open for 20% of the time, Pallas kernels for 0%

commit v1 on v0

v1 whole, which is shorter than its diff:
```python
from functools import partial
import math

import jax
import jax.numpy as jnp
from jax import lax
from jax.experimental import pallas as pl
from jax.experimental.pallas import tpu as pltpu
from jax.sharding import PartitionSpec as P

QUERY_HEADS = 32
KEY_VALUE_HEADS = 4
HEAD = 128
TOPK = 8
CONT = 256
PROMPT_TOKENS = 2048

EPS = 1e-06
THETA = 1000000.0
AUX_COEF = 0.001
LN2 = math.log(2.0)
SCALE2 = 1.0 / (math.sqrt(HEAD) * LN2)
VMEM = 56 * 1024 * 1024

BF = jnp.bfloat16
F32 = jnp.float32


def dot_nn(a, b):
    return lax.dot_general(a, b, (((1,), (0,)), ((), ())), preferred_element_type=F32)


def dot_nt(a, b):
    return lax.dot_general(a, b, (((1,), (1,)), ((), ())), preferred_element_type=F32)


def dot_tn(a, b):
    return lax.dot_general(a, b, (((0,), (0,)), ((), ())), preferred_element_type=F32)


def call(body, name, grid, in_specs, out_specs, out_shape, scratch=(), flops=0, moved=0, prefetch=0):
    return pl.pallas_call(
        body,
        name=name,
        grid_spec=pltpu.PrefetchScalarGridSpec(
            num_scalar_prefetch=prefetch,
            grid=grid,
            in_specs=in_specs,
            out_specs=out_specs,
            scratch_shapes=list(scratch),
        ),
        out_shape=out_shape,
        cost_estimate=pl.CostEstimate(flops=int(flops), bytes_accessed=int(moved), transcendentals=0),
        compiler_params=pltpu.CompilerParams(
            dimension_semantics=("arbitrary",) * len(grid), vmem_limit_bytes=VMEM
        ),
    )


def struct(shape, dtype):
    return jax.ShapeDtypeStruct(shape, dtype)


def turn(v, cos, sin):
    return v * cos + pltpu.roll(v, HEAD // 2, 1) * sin


def turn_back(v, cos, sin):
    return v * cos + pltpu.roll(v * sin, HEAD // 2, 1)


def qkv_body(heads, x_ref, gain_ref, w_ref, cos_ref, sin_ref, qg_ref, kg_ref, q_ref, kv_ref, a_ref, r_ref):
    x = x_ref[...].astype(F32)
    normed = x * lax.rsqrt(jnp.mean(x * x, axis=-1, keepdims=True) + EPS) * gain_ref[...]
    low = normed.astype(BF)
    a_ref[...] = low
    raw = dot_nn(low, w_ref[...])
    cos = cos_ref[...]
    sin = sin_ref[...]
    lane = lax.broadcasted_iota(jnp.int32, (x.shape[0], HEAD), 1)
    scales = jnp.zeros((x.shape[0], HEAD), F32)
    for h in range(heads + 1):
        v = raw[:, h * HEAD : (h + 1) * HEAD]
        r = lax.rsqrt(jnp.mean(v * v, axis=-1, keepdims=True) + EPS)
        scales = jnp.where(lane == h, r, scales)
        if h < heads:
            q_ref[h] = (turn(v * r * qg_ref[...], cos, sin) * SCALE2).astype(BF)
        else:
            kv_ref[0] = turn(v * r * kg_ref[...], cos, sin).astype(BF)
    kv_ref[1] = raw[:, (heads + 1) * HEAD :].astype(BF)
    r_ref[...] = scales


def qkv(x, gain, w, cos, sin, qg, kg, heads):
    rows, width = x.shape
    cols = w.shape[1]
    tile = 256
    whole = lambda i: (0, 0)
    row = lambda i: (i, 0)
    return call(
        partial(qkv_body, heads),
        "qkv",
        (rows // tile,),
        [
            pl.BlockSpec((tile, width), row),
            pl.BlockSpec((1, width), whole),
            pl.BlockSpec((width, cols), whole),
            pl.BlockSpec((tile, HEAD), row),
            pl.BlockSpec((tile, HEAD), row),
            pl.BlockSpec((1, HEAD), whole),
            pl.BlockSpec((1, HEAD), whole),
        ],
        [
            pl.BlockSpec((heads, tile, HEAD), lambda i: (0, i, 0)),
            pl.BlockSpec((2, tile, HEAD), lambda i: (0, i, 0)),
            pl.BlockSpec((tile, width), row),
            pl.BlockSpec((tile, HEAD), row),
        ],
        [
            struct((heads, rows, HEAD), BF),
            struct((2, rows, HEAD), BF),
            struct((rows, width), BF),
            struct((rows, HEAD), F32),
        ],
        flops=2 * rows * width * cols,
        moved=2 * (2 * rows * width + width * cols + rows * cols),
    )(x, gain, w, cos, sin, qg, kg)


def causal(count):
    q_at = lax.broadcasted_iota(jnp.int32, (count, CONT, CONT), 1)
    k_at = lax.broadcasted_iota(jnp.int32, (count, CONT, CONT), 2)
    return (k_at <= q_at).reshape(count * CONT, CONT)


def attend_body(heads, per, blocks, rows, row_ref, q_ref, kp_ref, vp_ref, kv_ref, o_ref, l_ref, vp_one, vl_one, acc):
    at = pl.program_id(0)
    part = pl.program_id(1)
    row = row_ref[0]

    @pl.when((at == 0) & (part == 0))
    def _():
        for j in range(blocks):
            vp_one[j * rows : (j + 1) * rows, :HEAD] = vp_ref[j, 0, 0]
        vp_one[:, HEAD:] = jnp.ones((blocks * rows, HEAD), BF)
        vl_one[:, :HEAD] = kv_ref[1]
        vl_one[:, HEAD:] = jnp.ones((rows, HEAD), BF)

    q = q_ref[...].reshape(per * CONT, HEAD)
    here = pl.ds(pl.multiple_of(at * CONT, CONT), CONT)
    weights = jnp.where(causal(per), jnp.exp2(dot_nt(q, kv_ref[0, here, :])), 0.0).astype(BF)
    acc[...] = dot_nn(weights, vl_one[here, :])

    @pl.when(row < blocks)
    def _():
        for j in range(rows // CONT - 1):

            @pl.when(j < at)
            def _():
                piece = slice(j * CONT, (j + 1) * CONT)
                weights = jnp.exp2(dot_nt(q, kv_ref[0, piece, :])).astype(BF)
                acc[...] += dot_nn(weights, vl_one[piece, :])

    @pl.loop(0, jnp.minimum(row, blocks))
    def _(j):
        weights = jnp.exp2(dot_nt(q, kp_ref[j, 0, 0])).astype(BF)
        acc[...] += dot_nn(weights, vp_one[pl.ds(pl.multiple_of(j * rows, rows), rows), :])

    total = acc[:, HEAD:]
    out = (acc[:, :HEAD] / total).astype(BF)
    logs = jnp.log2(total)
    lane = lax.broadcasted_iota(jnp.int32, (CONT, HEAD), 1)

    @pl.when(part == 0)
    def _():
        l_ref[...] = jnp.zeros((CONT, HEAD), F32)

    held = l_ref[...]
    for p in range(per):
        o_ref[:, p * HEAD : (p + 1) * HEAD] = out[p * CONT : (p + 1) * CONT]
        held = jnp.where(lane == part * per + p, logs[p * CONT : (p + 1) * CONT], held)
    l_ref[...] = held


def attend(row, q, every, kv, slot, blocks):
    heads, rows, _ = q.shape
    per = 2
    keys = blocks * rows
    return call(
        partial(attend_body, heads, per, blocks, rows),
        "attend",
        (rows // CONT, heads // per),
        [
            pl.BlockSpec((per, CONT, HEAD), lambda i, h, s: (h, i, 0)),
            pl.BlockSpec((blocks, 1, 1, rows, HEAD), lambda i, h, s: (0, slot, 0, 0, 0)),
            pl.BlockSpec((blocks, 1, 1, rows, HEAD), lambda i, h, s: (0, slot, 1, 0, 0)),
            pl.BlockSpec((2, rows, HEAD), lambda i, h, s: (0, 0, 0)),
        ],
        [
            pl.BlockSpec((CONT, per * HEAD), lambda i, h, s: (i, h)),
            pl.BlockSpec((CONT, HEAD), lambda i, h, s: (i, 0)),
        ],
        [struct((rows, heads * HEAD), BF), struct((rows, HEAD), F32)],
        scratch=[
            pltpu.VMEM((keys, 2 * HEAD), BF),
            pltpu.VMEM((rows, 2 * HEAD), BF),
            pltpu.VMEM((per * CONT, 2 * HEAD), F32),
        ],
        flops=8 * rows * heads * (keys + CONT) * HEAD,
        moved=2 * HEAD * (2 * rows * heads + 2 * keys),
        prefetch=1,
    )(row, q, every, every, kv)


def attend_back_body(
    heads, per, blocks, rows,
    row_ref, q_ref, kp_ref, vp_ref, kv_ref, do_ref, o_ref, l_ref, r_ref, cos_ref, sin_ref, qg_ref,
    dq_ref, dp_ref, dl_ref, g_ref,
    dq, dkp, dvp,
):
    at = pl.program_id(0)
    part = pl.program_id(1)
    row = row_ref[0]

    @pl.when((at == 0) & (part == 0))
    def _():
        dkp[...] = jnp.zeros_like(dkp)
        dvp[...] = jnp.zeros_like(dvp)
        dl_ref[...] = jnp.zeros_like(dl_ref)
        g_ref[...] = jnp.zeros_like(g_ref)

    q = q_ref[...].reshape(per * CONT, HEAD)
    lane = lax.broadcasted_iota(jnp.int32, (CONT, HEAD), 1)
    do_parts, logs, centers, scales = [], [], [], []
    for p in range(per):
        do_part = do_ref[:, p * HEAD : (p + 1) * HEAD]
        do_parts.append(do_part)
        centers.append(
            jnp.sum(
                do_part.astype(F32) * o_ref[:, p * HEAD : (p + 1) * HEAD].astype(F32),
                axis=-1,
                keepdims=True,
            )
        )
        pick = lane == part * per + p
        logs.append(jnp.sum(jnp.where(pick, l_ref[...], 0.0), axis=-1, keepdims=True))
        scales.append(jnp.sum(jnp.where(pick, r_ref[...], 0.0), axis=-1, keepdims=True))
    do = jnp.concatenate(do_parts, axis=0)
    center = jnp.concatenate(centers, axis=0)
    log = jnp.concatenate(logs, axis=0)

    def block(k, v, mask):
        probs = jnp.exp2(dot_nt(q, k) - log)
        if mask is not None:
            probs = jnp.where(mask, probs, 0.0)
        ds = (probs * (dot_nt(do, v) - center)).astype(BF)
        return dot_nn(ds, k), dot_tn(ds, q), dot_tn(probs.astype(BF), do)

    here = pl.ds(pl.multiple_of(at * CONT, CONT), CONT)
    a, b, c = block(kv_ref[0, here, :], kv_ref[1, here, :], causal(per))
    dq[...] = a
    dl_ref[0, here, :] += b
    dl_ref[1, here, :] += c

    @pl.when(row < blocks)
    def _():
        for j in range(rows // CONT - 1):

            @pl.when(j < at)
            def _():
                piece = slice(j * CONT, (j + 1) * CONT)
                a, b, c = block(kv_ref[0, piece, :], kv_ref[1, piece, :], None)
                dq[...] += a
                dl_ref[0, piece, :] += b
                dl_ref[1, piece, :] += c

    @pl.loop(0, jnp.minimum(row, blocks))
    def _(j):
        a, b, c = block(kp_ref[j, 0, 0], vp_ref[j, 0, 0], None)
        piece = pl.ds(pl.multiple_of(j * rows, rows), rows)
        dq[...] += a
        dkp[piece, :] += b
        dvp[piece, :] += c

    cos = cos_ref[...]
    sin = sin_ref[...]
    gain = qg_ref[...]
    tally = jnp.zeros((1, HEAD), F32)
    for p in range(per):
        dy = turn_back(dq[p * CONT : (p + 1) * CONT, :] * (SCALE2 * LN2), cos, sin)
        hat = turn_back(q[p * CONT : (p + 1) * CONT].astype(F32), cos, sin) * (1.0 / SCALE2) / gain
        tally += jnp.sum(dy * hat, axis=0, keepdims=True)
        dyg = dy * gain
        raw = scales[p] * (dyg - hat * jnp.mean(dyg * hat, axis=-1, keepdims=True))
        dq_ref[:, p * HEAD : (p + 1) * HEAD] = raw.astype(BF)
    g_ref[0:1, :] += tally

    @pl.when((at == rows // CONT - 1) & (part == heads // per - 1))
    def _():
        dp_ref[0] = (dkp[...] * LN2).astype(BF)
        dp_ref[1] = dvp[...].astype(BF)
        dl_ref[0] = dl_ref[0] * LN2


def attend_back(row, q, every, kv, slot, blocks, do, o, logs, scales, cos, sin, qg):
    heads, rows, _ = q.shape
    per = 2
    keys = blocks * rows
    tile = lambda i, h, s: (i, 0)
    head = lambda i, h, s: (i, h)
    return call(
        partial(attend_back_body, heads, per, blocks, rows),
        "attend_back",
        (rows // CONT, heads // per),
        [
            pl.BlockSpec((per, CONT, HEAD), lambda i, h, s: (h, i, 0)),
            pl.BlockSpec((blocks, 1, 1, rows, HEAD), lambda i, h, s: (0, slot, 0, 0, 0)),
            pl.BlockSpec((blocks, 1, 1, rows, HEAD), lambda i, h, s: (0, slot, 1, 0, 0)),
            pl.BlockSpec((2, rows, HEAD), lambda i, h, s: (0, 0, 0)),
            pl.BlockSpec((CONT, per * HEAD), head),
            pl.BlockSpec((CONT, per * HEAD), head),
            pl.BlockSpec((CONT, HEAD), tile),
            pl.BlockSpec((CONT, HEAD), tile),
            pl.BlockSpec((CONT, HEAD), tile),
            pl.BlockSpec((CONT, HEAD), tile),
            pl.BlockSpec((1, HEAD), lambda i, h, s: (0, 0)),
        ],
        [
            pl.BlockSpec((CONT, per * HEAD), head),
            pl.BlockSpec((2, keys, HEAD), lambda i, h, s: (0, 0, 0)),
            pl.BlockSpec((2, rows, HEAD), lambda i, h, s: (0, 0, 0)),
            pl.BlockSpec((8, HEAD), lambda i, h, s: (0, 0)),
        ],
        [
            struct((rows, heads * HEAD), BF),
            struct((2, keys, HEAD), BF),
            struct((2, rows, HEAD), F32),
            struct((8, HEAD), F32),
        ],
        scratch=[
            pltpu.VMEM((per * CONT, HEAD), F32),
            pltpu.VMEM((keys, HEAD), F32),
            pltpu.VMEM((keys, HEAD), F32),
        ],
        flops=20 * rows * heads * (keys + CONT) * HEAD,
        moved=2 * HEAD * (4 * rows * heads + 4 * keys),
        prefetch=1,
    )(row, q, every, every, kv, do, o, logs, scales, cos, sin, qg)


def dispatch_body(count, cap, rank_ref, rows_ref, out_ref):
    tokens = rows_ref.shape[1]
    slot = lax.broadcasted_iota(jnp.int32, (cap, tokens), 0)
    for d in range(count):
        hot = (rank_ref[0, d : d + 1, :] == slot).astype(F32).astype(BF)
        out_ref[d, 0] = dot_nn(hot, rows_ref[0]).astype(BF)


def dispatch(rank, rows, cap):
    sources, count, tokens = rank.shape
    width = rows.shape[2]
    return call(
        partial(dispatch_body, count, cap),
        "dispatch",
        (sources,),
        [
            pl.BlockSpec((1, count, tokens), lambda s: (s, 0, 0)),
            pl.BlockSpec((1, tokens, width), lambda s: (s, 0, 0)),
        ],
        pl.BlockSpec((count, 1, cap, width), lambda s: (0, s, 0, 0)),
        struct((count, sources, cap, width), BF),
        flops=2 * sources * count * cap * tokens * width,
        moved=2 * sources * width * (tokens + count * cap),
    )(rank, rows)


def combine_body(count, cap, rank_ref, *refs):
    tokens = rank_ref.shape[1]
    slot = lax.broadcasted_iota(jnp.int32, (tokens, cap), 1)
    total = None
    for d in range(count):
        hot = (rank_ref[0, :, d : d + 1] == slot).astype(F32).astype(BF)
        piece = dot_nn(hot, refs[d][0])
        total = piece if total is None else total + piece
    refs[-1][0] = total.astype(BF)


def combine(rank_t, parts):
    sources, tokens, count = rank_t.shape
    _, cap, width = parts[0].shape
    return call(
        partial(combine_body, count, cap),
        "combine",
        (sources,),
        [pl.BlockSpec((1, tokens, count), lambda s: (s, 0, 0))]
        + [pl.BlockSpec((1, cap, width), lambda s: (s, 0, 0))] * count,
        pl.BlockSpec((1, tokens, width), lambda s: (s, 0, 0)),
        struct((sources, tokens, width), BF),
        flops=2 * sources * count * cap * tokens * width,
        moved=2 * sources * width * (tokens + count * cap),
    )(rank_t, *parts)


def expert_body(
    x_ref, up_ref, gate_ref, wg_ref, wu_ref, wd_ref,
    y_ref, db_ref, m_ref, du_ref, dw_ref, dg_ref,
):
    x = x_ref[0]
    gate = gate_ref[...]
    u = dot_nn(x, wg_ref[0])
    w = dot_nn(x, wu_ref[0])
    sigma = 1.0 / (1.0 + jnp.exp(-u))
    silu = u * sigma
    inner = silu * w
    low = inner.astype(BF)
    y_ref[...] = (dot_nn(low, wd_ref[0]) * gate).astype(BF)
    m_ref[...] = (inner * gate).astype(BF)
    back = dot_nt(up_ref[0], wd_ref[0])
    dg_ref[...] = jnp.sum(low.astype(F32) * back, axis=-1, keepdims=True)
    back = back * gate
    du = (back * w * sigma * (1.0 + u * (1.0 - sigma))).astype(BF)
    dw = (back * silu).astype(BF)
    du_ref[...] = du
    dw_ref[...] = dw
    db_ref[...] = (dot_nt(du, wg_ref[0]) + dot_nt(dw, wu_ref[0])).astype(BF)


def expert(slot, x, up, gate, wg, wu, wd):
    _, rows, width = x.shape
    hidden = wg.shape[2]
    tile = min(256, rows)
    at = lambda i: (i, 0)
    mine = lambda i: (slot, i, 0)
    whole = lambda i: (0, 0, 0)
    return call(
        expert_body,
        "expert",
        (rows // tile,),
        [
            pl.BlockSpec((1, tile, width), mine),
            pl.BlockSpec((1, tile, width), mine),
            pl.BlockSpec((tile, 1), at),
            pl.BlockSpec((1, width, hidden), whole),
            pl.BlockSpec((1, width, hidden), whole),
            pl.BlockSpec((1, hidden, width), whole),
        ],
        [
            pl.BlockSpec((tile, width), at),
            pl.BlockSpec((tile, width), at),
            pl.BlockSpec((tile, hidden), at),
            pl.BlockSpec((tile, hidden), at),
            pl.BlockSpec((tile, hidden), at),
            pl.BlockSpec((tile, 1), at),
        ],
        [
            struct((rows, width), BF),
            struct((rows, width), BF),
            struct((rows, hidden), BF),
            struct((rows, hidden), BF),
            struct((rows, hidden), BF),
            struct((rows, 1), F32),
        ],
        flops=12 * rows * width * hidden,
        moved=2 * (4 * rows * width + 3 * rows * hidden + 3 * width * hidden),
    )(x, up, gate, wg, wu, wd)


def swap(v, step, count):
    return lax.ppermute(v, "col", [(i, i ^ step) for i in range(count)])


def fetch(v, count):
    if count != 4:
        return [v] + [swap(v, d, count) for d in range(1, count)]
    half = v.shape[1] // 2
    one, two = swap(v, 1, count), swap(v, 2, count)
    first = swap(one[:, :half], 2, count)
    second = swap(two[:, half:], 1, count)
    return [v, one, two, jnp.concatenate([first, second], axis=1)]


def deliver(parts, count):
    own = parts[0]
    low = [None] + [p.astype(BF) for p in parts[1:]]
    if count != 4:
        for d in range(1, count):
            own = own + swap(low[d], d, count).astype(F32)
        return own
    half = own.shape[0] // 2
    to_two = swap(low[3][:half], 1, count)
    to_one = swap(low[3][half:], 2, count)
    one = jnp.concatenate([low[1][:half], (parts[1][half:] + to_one.astype(F32)).astype(BF)], axis=0)
    two = jnp.concatenate([(parts[2][:half] + to_two.astype(F32)).astype(BF), low[2][half:]], axis=0)
    return own + swap(one, 1, count).astype(F32) + swap(two, 2, count).astype(F32)


def after(value, *earlier):
    return lax.optimization_barrier((value,) + earlier)[0]


def per_device(
    layer_input, out_grad, routes, positions, w_q, key_value_weight, w_out, router,
    ln_attn, ln_moe, q_gain, k_gain, w_gate, w_up, w_down,
):
    rows, width = layer_input.shape[1:]
    row_count, col_count = lax.axis_size("row"), lax.axis_size("col")
    row_at, col_at = lax.axis_index("row"), lax.axis_index("col")
    devices = row_count * col_count
    experts = w_gate.shape[0] * devices
    assert w_gate.shape[0] == 1
    cap = rows * TOPK // experts
    tokens = rows * devices
    heads = w_q.shape[1] // HEAD
    sharing = QUERY_HEADS // KEY_VALUE_HEADS // heads
    blocks = PROMPT_TOKENS // rows
    slots = range(col_count)
    members = [col_at ^ d for d in slots]
    row_word = row_at.astype(jnp.int32).reshape(1)

    x_own = layer_input[0]
    up_own = out_grad[0]

    key_head = col_at // sharing
    kv_cols = KEY_VALUE_HEADS * HEAD
    wkv_mine = jnp.concatenate(
        [
            lax.dynamic_slice_in_dim(key_value_weight, key_head * HEAD, HEAD, 1),
            lax.dynamic_slice_in_dim(key_value_weight, kv_cols + key_head * HEAD, HEAD, 1),
        ],
        axis=1,
    )
    wide = jnp.concatenate([w_q, wkv_mine], axis=1)
    small = jnp.concatenate([ln_attn, ln_moe, q_gain, k_gain, router.reshape(-1)])
    small_all = lax.all_gather(small, "row", axis=0)
    wqkv = lax.all_gather(wide, "row", axis=0, tiled=True)
    piece, head_piece = ln_attn.shape[0], q_gain.shape[0]
    cuts = [0, piece, 2 * piece, 2 * piece + head_piece, 2 * piece + 2 * head_piece, small.shape[0]]
    gain_one, gain_two, gain_q, gain_k, router_all = [
        small_all[:, a:b].reshape(-1) for a, b in zip(cuts[:-1], cuts[1:])
    ]
    gain_one, gain_two = gain_one.astype(F32)[None], gain_two.astype(F32)[None]
    gain_q, gain_k = gain_q.astype(F32)[None], gain_k.astype(F32)[None]
    router_all = router_all.reshape(width, experts)

    xs = [x_own] + [swap(x_own, d, col_count) for d in slots[1:]]
    wg, wu, wd = after((w_gate, w_up, w_down), xs[-1])
    wg_all, wu_all, wd_all = fetch(wg, col_count), fetch(wu, col_count), fetch(wd, col_count)

    routes_all = lax.all_gather(routes[0], "row", axis=0)
    expert_ids = jnp.arange(experts, dtype=jnp.int32)
    flat_routes = routes_all.reshape(row_count * rows, TOPK).T
    mask_all = jnp.any(flat_routes[:, None, :] == expert_ids[None, :, None], axis=0)
    mine_ids = [row_at * col_count + m for m in members]
    has = jnp.stack(
        [lax.dynamic_index_in_dim(mask_all, e, 0, keepdims=False) for e in mine_ids], axis=0
    ).reshape(col_count, row_count, rows)
    place = jnp.arange(rows)
    before = (place[:, None] <= place[None, :]).astype(BF)
    order = jnp.einsum("drt,tu->rdu", has.astype(BF), before, preferred_element_type=F32)
    rank = jnp.where(has.transpose(1, 0, 2), order.astype(jnp.int32) - 1, -1)
    rank_t = rank.transpose(0, 2, 1)

    inv_freq = THETA ** (-2.0 * jnp.arange(HEAD // 2, dtype=F32) / HEAD)
    coses, sines = [], []
    for m in members:
        spots = lax.dynamic_index_in_dim(positions, m, 0, keepdims=False).astype(F32)
        angles = spots[:, None] * inv_freq[None, :]
        cos, sin = jnp.cos(angles), jnp.sin(angles)
        coses.append(jnp.concatenate([cos, cos], axis=1))
        sines.append(jnp.concatenate([-sin, sin], axis=1))

    qs, kvs, normed, scales = [], [], [], []
    for d in slots:
        a, b, c, e = qkv(xs[d], gain_one, wqkv, coses[d], sines[d], gain_q, gain_k, heads)
        qs.append(a)
        kvs.append(b)
        normed.append(c)
        scales.append(e)
    every = lax.all_gather(jnp.stack(kvs, axis=0), "row", axis=0)
    out_all = lax.all_gather(after(w_out, every), "row", axis=1, tiled=True)
    up_all = lax.all_gather(after(up_own, out_all), "row", axis=0)
    mixes, logs = [None] * col_count, [None] * col_count
    hidden = x_own.astype(F32)
    for d in reversed(slots):
        mixes[d], logs[d] = attend(row_word, qs[d], every, kvs[d], d, blocks)
        share = jnp.dot(mixes[d], out_all, preferred_element_type=F32)
        hidden = hidden + (share if d == 0 else swap(share.astype(BF), d, col_count).astype(F32))

    spread = lax.rsqrt(jnp.mean(hidden * hidden, axis=-1, keepdims=True) + EPS)
    second = (hidden * spread * gain_two).astype(BF)
    second_all = lax.all_gather(second, "row", axis=0)

    def route(vectors, mask):
        logits = lax.dot_general(
            router_all, vectors, (((0,), (1,)), ((), ())), preferred_element_type=F32
        )
        probs = jax.nn.softmax(logits, axis=0)
        picked = jnp.where(mask, probs, 0.0)
        total = jnp.sum(picked, axis=0, keepdims=True)
        return probs, total, picked / total

    probs_all, _, gates_all = route(second_all.reshape(row_count * rows, width), mask_all)
    sums = jnp.stack([jnp.sum(mask_all.astype(F32), axis=1), jnp.sum(probs_all, axis=1)])
    step = 1
    while step < col_count:
        sums = sums + swap(sums, step, col_count)
        step *= 2
    load = sums[0] / (tokens * TOPK)
    mean_probs = sums[1] / tokens
    aux_loss = experts * jnp.sum(load * mean_probs)
    expert_load = jnp.stack([experts * load, experts * mean_probs])

    expert_in = dispatch(rank, second_all, cap)
    expert_up = dispatch(rank, up_all, cap).reshape(col_count, row_count * cap, width)
    gates_mine = jnp.stack(
        [lax.dynamic_index_in_dim(gates_all, e, 0, keepdims=False) for e in mine_ids], axis=0
    ).reshape(col_count, row_count, rows)
    slot_ids = jnp.arange(cap, dtype=jnp.int32)
    hot = rank.transpose(1, 0, 2)[:, :, None, :] == slot_ids[None, None, :, None]
    gate_pairs = jnp.sum(jnp.where(hot, gates_mine[:, :, None, :], 0.0), axis=-1)
    gate_pairs = gate_pairs.reshape(col_count, row_count * cap, 1)
    expert_in = expert_in.reshape(col_count, row_count * cap, width)
    ys, dbs, ms, dus, dws, dgs = [], [], [], [], [], []
    for d in slots:
        got = expert(d, expert_in, expert_up, gate_pairs[d], wg_all[d], wu_all[d], wd_all[d])
        for kept, value in zip((ys, dbs, ms, dus, dws, dgs), got):
            kept.append(value)
    cut = lambda parts: [p.reshape(row_count, cap, width) for p in parts]
    db_sum = lax.psum_scatter(combine(rank_t, cut(dbs)), "row", scatter_dimension=0)
    pair_scores = jnp.stack(dgs, axis=0).reshape(col_count, row_count, cap, 1)
    score_grads = jnp.sum(jnp.where(hot, pair_scores, 0.0), axis=2)
    score_grads = lax.all_to_all(
        score_grads.transpose(1, 0, 2), "row", split_axis=0, concat_axis=0, tiled=True
    )
    y_sum = lax.psum_scatter(
        after(combine(rank_t, cut(ys)), db_sum), "row", scatter_dimension=0
    )
    layer_output = (hidden + y_sum.astype(F32)).astype(BF)

    grad_down = deliver(
        [dot_tn(ms[d], expert_up[d]) for d in slots], col_count
    )
    grad_gate = deliver([dot_tn(expert_in[d], dus[d]) for d in slots], col_count)
    grad_up = deliver([dot_tn(expert_in[d], dws[d]) for d in slots], col_count)

    mask_own = jnp.any(routes[0].T[:, None, :] == expert_ids[None, :, None], axis=0)
    probs, total, gates = route(second, mask_own)
    to_member = jnp.stack(members)[:, None] == jnp.arange(col_count)[None, :]
    gate_grad = jnp.sum(
        jnp.where(to_member[None, :, :, None], score_grads[:, :, None, :], 0.0), axis=1
    ).reshape(experts, rows)
    weighted = jnp.sum(gate_grad * gates, axis=0, keepdims=True)
    prob_grad = (
        jnp.where(mask_own, (gate_grad - weighted) / total, 0.0)
        + AUX_COEF * experts * load[:, None] / tokens
    )
    logit_low = (probs * (prob_grad - jnp.sum(probs * prob_grad, axis=0, keepdims=True))).astype(BF)
    grad_router = lax.dot_general(
        second, logit_low, (((0,), (1,)), ((), ())), preferred_element_type=F32
    )
    second_grad = db_sum.astype(F32) + lax.dot_general(
        logit_low, router_all, (((0,), (1,)), ((), ())), preferred_element_type=F32
    )

    def norm_back(grad, hat, spread, gain):
        scaled = grad * gain
        return spread * (scaled - hat * jnp.mean(scaled * hat, axis=-1, keepdims=True))

    hat = hidden * spread
    gain_two_grad = jnp.sum(second_grad * hat, axis=0)
    hidden_grad = up_own.astype(F32) + norm_back(second_grad, hat, spread, gain_two)
    branch = hidden_grad.astype(BF)
    early = jnp.concatenate(
        [grad_router.reshape(devices, -1), gain_two_grad.reshape(devices, -1)], axis=1
    )
    early = lax.psum_scatter(early, ("row", "col"), scatter_dimension=0)

    branches = [branch] + [swap(branch, d, col_count) for d in slots[1:]]
    grad_qs, grad_prompts, grad_locals, gain_q_grad = [], [], [], 0.0
    for d in slots:
        mix_grad = dot_nt(branches[d], out_all).astype(BF)
        a, b, c, e = attend_back(
            row_word, qs[d], every, kvs[d], d, blocks, mix_grad, mixes[d], logs[d], scales[d],
            coses[d], sines[d], gain_q,
        )
        grad_qs.append(a)
        grad_prompts.append(b)
        grad_locals.append(c)
        gain_q_grad = gain_q_grad + e[0]
    prompt = lax.psum_scatter(
        jnp.stack(grad_prompts, axis=0), "row", scatter_dimension=2, tiled=True
    )
    chunk = prompt.shape[2]
    prompt = jnp.concatenate(
        [
            lax.ppermute(prompt, "row", [(rows // chunk * i + a, i) for i in range(blocks)])
            for a in range(rows // chunk)
        ],
        axis=2,
    )
    pair = jnp.stack(grad_locals, axis=0) + prompt.astype(F32)
    cos, sin = jnp.stack(coses), jnp.stack(sines)

    def back_turn(v):
        moved = v * sin
        half = HEAD // 2
        return v * cos + jnp.concatenate([moved[..., half:], moved[..., :half]], axis=-1)

    key_dy = back_turn(pair[:, 0])
    key_hat = back_turn(jnp.stack([kv[0] for kv in kvs]).astype(F32)) / gain_k
    gain_k_grad = jnp.sum(key_dy * key_hat, axis=(0, 1))
    key_spread = jnp.stack([s[:, heads : heads + 1] for s in scales])
    key_raw = norm_back(key_dy, key_hat, key_spread, gain_k)
    all_grads = jnp.concatenate(
        [jnp.stack(grad_qs, axis=0), key_raw.astype(BF), pair[:, 1].astype(BF)], axis=2
    )
    input_sum = None
    for d in reversed(slots):
        share = dot_nt(all_grads[d], wqkv)
        share = share if d == 0 else swap(share.astype(BF), d, col_count).astype(F32)
        input_sum = share if input_sum is None else input_sum + share
    grad_wide = lax.dot_general(
        jnp.stack(normed, axis=0), all_grads, (((0, 1), (0, 1)), ((), ())), preferred_element_type=F32
    )
    grad_wide = lax.psum_scatter(grad_wide.astype(BF), "row", scatter_dimension=0, tiled=True)
    grad_out = lax.dot_general(
        jnp.stack(mixes, axis=0),
        jnp.stack(branches, axis=0),
        (((0, 1), (0, 1)), ((), ())),
        preferred_element_type=F32,
    )
    grad_out = lax.psum_scatter(grad_out.astype(BF), "row", scatter_dimension=1, tiled=True)
    x_wide = x_own.astype(F32)
    x_spread = lax.rsqrt(jnp.mean(x_wide * x_wide, axis=-1, keepdims=True) + EPS)
    x_hat = x_wide * x_spread
    gain_one_grad = jnp.sum(input_sum * x_hat, axis=0)
    input_grad = hidden_grad + norm_back(input_sum, x_hat, x_spread, gain_one)

    late = jnp.concatenate(
        [v.reshape(devices, -1) for v in (gain_one_grad, gain_q_grad, gain_k_grad)], axis=1
    )
    late = lax.psum_scatter(late, ("row", "col"), scatter_dimension=0)
    per_one, per_q = gain_one_grad.size // devices, gain_q_grad.size // devices

    grad_kv = grad_wide[:, heads * HEAD :].astype(F32).reshape(col_count, -1, 2 * HEAD)
    grad_kv = lax.all_to_all(grad_kv, "col", split_axis=0, concat_axis=0, tiled=True)
    grad_kv = grad_kv.reshape(KEY_VALUE_HEADS, sharing, -1, 2, HEAD).sum(axis=1)
    grad_kv = grad_kv.transpose(1, 2, 0, 3).reshape(-1, 2 * kv_cols)

    return (
        layer_output[None],
        aux_loss,
        input_grad[None],
        grad_wide[:, : heads * HEAD].astype(F32),
        grad_kv,
        grad_out.astype(F32),
        early[: -(width // devices)].reshape(width // devices, experts),
        late[:per_one],
        early[-(width // devices) :],
        late[per_one : per_one + per_q],
        late[per_one + per_q :],
        grad_gate[None],
        grad_up[None],
        grad_down[None],
        expert_load,
    )


def solution(mesh):
    in_specs = (
        P("col", "row", None),
        P("col", "row", None),
        P("col", "row", None),
        P(None, "row"),
        P("row", "col"),
        P("row", None),
        P("col", "row"),
        P("row", None),
        P("row"),
        P("row"),
        P("row"),
        P("row"),
        P(("row", "col"), None, None),
        P(("row", "col"), None, None),
        P(("row", "col"), None, None),
    )
    out_specs = (
        P("col", "row", None),
        P(),
        P("col", "row", None),
        P("row", "col"),
        P(("row", "col"), None),
        P("col", "row"),
        P(("row", "col"), None),
        P(("row", "col")),
        P(("row", "col")),
        P(("row", "col")),
        P(("row", "col")),
        P(("row", "col"), None, None),
        P(("row", "col"), None, None),
        P(("row", "col"), None, None),
        P(),
    )
    return jax.shard_map(
        per_device, mesh=mesh, in_specs=in_specs, out_specs=out_specs, check_vma=False
    )
```

time: 3930 us -> 1910 us (0.49)
  blocking collectives: 811 us -> 166 us
  matrix products: 804 us -> 167 us
  waiting for transfers between devices: 1390 us -> 914 us
  local copies, waits for them, and re-layouts: 508 us -> 96.6 us
  Pallas kernels: 0 us -> 338 us
  other arithmetic: 364 us -> 112 us
  starting transfers between devices: 18.6 us -> 93.9 us
    all_to_all x4 -> x2, waiting for transfers between devices: 699 us -> 9.02 us  [the longest x1 5.77 us: per_device(): lax.all_to_all(score_grads.transpose(1, 0, 2), 'row', split_axis=0, conca...]
    dot_general x48 -> x31, matrix products: 802 us -> 167 us  [the longest x12 52 us: dot_tn(): lax.dot_general(a, b, (((0,), (0,)), ((), ())), preferred_element_type=F32)]
    ppermute x0 -> x40, waiting for transfers between devices: none -> 535 us  [the longest x38 535 us: swap(): return lax.ppermute(v, 'col', [(i, i ^ step) for i in range(count)])]
    psum x2 -> x0, blocking collectives: 387 us -> none  [per_device(): count_all, prob_all = lax.psum((counts, prob_sums), ('row', 'col'))]
    all_gather x3 -> x1, blocking collectives: 410 us -> 63.5 us  [per_device(): routes_all = lax.all_gather(routes[0], 'row', axis=0)]
    pallas_call x0 -> x20, Pallas kernels: none -> 338 us  [the longest x4 119 us: expert(): call(expert_body, 'expert', (rows // tile,), [pl.BlockSpec((1, tile, widt...]
    dynamic_update_slice x18 -> x0, local copies, waits for them, and re-layouts: 208 us -> none  [the longest x8 188 us: per_device(): lax.map(partial(attend_backward, allowed=allowed, score_scale=score_scale...]
    unnamed x16 -> x14, waiting for transfers between devices: 219 us -> 38.6 us
  transfers between devices with their start and end apart: 17 -> 54, of which waited for: 14 -> 22; matrix products, arithmetic and copies ran while one was open for 20% -> 16% of each run, Pallas kernels for 0% -> 8%
where the time goes in v1:
time: 1910 us
  waiting for transfers between devices  914 us (48%)
  Pallas kernels  338 us (18%)
  matrix products  167 us (9%)
  blocking collectives  166 us (9%)
  other arithmetic  112 us (6%)
  local copies, waits for them, and re-layouts  96.6 us (5%)
  starting transfers between devices  93.9 us (5%)
    ppermute x38, waiting for transfers between devices, swap(): return lax.ppermute(v, 'col', [(i, i ^ step) for i in range(count)])  535 us
    reduce_scatter x1, waiting for transfers between devices, per_device(): lax.psum_scatter(combine(rank_t, cut(dbs)), 'row', scatter_dimension=0)  146 us
    pallas_call x4, Pallas kernels, expert(): call(expert_body, 'expert', (rows // tile,), [pl.BlockSpec((1, tile, widt...  119 us
    unnamed x1, blocking collectives  103 us
    all_gather x1, waiting for transfers between devices, per_device(): every = lax.all_gather(jnp.stack(kvs, axis=0), 'row', axis=0)  80.9 us
    pallas_call x4, Pallas kernels, attend_back(): call(partial(attend_back_body, heads, per, blocks, rows), 'attend_back',...  68 us
    all_gather x1, blocking collectives, per_device(): routes_all = lax.all_gather(routes[0], 'row', axis=0)  63.5 us
    all_gather x1, waiting for transfers between devices, per_device(): wqkv = lax.all_gather(wide, 'row', axis=0, tiled=True)  56.2 us
  transfers between devices with their start and end apart: 54, of which 22 were waited for; matrix products, arithmetic and copies ran while one was open for 16% of the time, Pallas kernels for 8%

profile of v1, /device:TPU:0, one launch (start us, length us, event | category | flops | bytes accessed | tf_op | source)
XLA Modules:
  0.0 1905.3 jit_solution(5550269345133129840)
XLA Ops:
  30.5 38.4 %all-reduce.6.cloned.1.call-done = bf16[69888]{0:T(1024)(128)(2,1)} async-done(((bf16[69888]{0:T(1024)(128)(2,1)}), bf16[69888]{0:T(1024)(128)(2,1)}) %all-reduce.6.cloned.1.call-update) | async-done | bytes 139792
  72.5 56.2 %all-gather.10.cloned.1.call-done.w_ref = bf16[2048,1280]{1,0:T(8,128)(2,1)} async-done(((bf16[256,1280]{1,0:T(8,128)(2,1)}), bf16[2048,1280]{1,0:T(8,128)(2,1)}) %all-gather.10.cloned.1.call-update) | async-done | bytes 5242896 | tf_op jit(solution)/shard_map/all_gather | solution.py:535
  128.8 8.5 qkv.5
  137.3 8.3 qkv.7
  145.6 8.2 qkv.4
  155.2 8.3 qkv.6
  165.6 80.9 %all-gather.14.cloned.1.call-done = bf16[32,2,512,128]{3,2,1,0:T(8,128)(2,1)} async-done(((bf16[4,2,512,128]{3,2,1,0:T(8,128)(2,1)}), bf16[32,2,512,128]{3,2,1,0:T(8,128)(2,1)}) %all-gather.14.cloned.1.call-update) | async-done | bytes 8388624 | tf_op jit(solution)/shard_map/all_gather | solution.py:579
  246.6 47.8 %all-gather.12.cloned.1.call-done = bf16[1024,2048]{1,0:T(8,128)(2,1)} async-done(((bf16[1024,256]{1,0:T(8,128)(2,1)}), bf16[1024,2048]{1,0:T(8,128)(2,1)}) %all-gather.12.cloned.1.call-update) | async-done | bytes 4194320 | tf_op jit(solution)/shard_map/all_gather | solution.py:580
  294.5 9.4 attend.4
  303.9 9.3 attend.5
  313.2 9.3 attend.6
  337.0 9.7 attend.7
  346.7 19.0 collective-permute-done.3
  365.8 55.0 %collective-permute-done.4 = bf16[512,2048]{1,0:T(8,128)(2,1)} collective-permute-done((bf16[512,2048]{1,0:T(8,128)(2,1)}, bf16[512,2048]{1,0:T(8,128)(2,1)}, u32[]{:S(2)}, u32[]{:S(2)}) %collective-permute-start.4) | collective-permute-done | bytes 2097184 | tf_op jit(solution)/shard_map/ppermute | solution.py:469
  420.8 7.1 multiply_reduce_fusion.2
  437.3 65.5 %collective-permute-done.6.wg_ref = bf16[1,2048,768]{2,1,0:T(8,128)(2,1)S(1)} collective-permute-done((bf16[1,2048,768]{2,1,0:T(8,128)(2,1)}, bf16[1,2048,768]{2,1,0:T(8,128)(2,1)S(1)}, u32[]{:S(2)}, u32[]{:S(2)}) %collective-permute-start.6) | collective-permute-done | bytes 3145760 | tf_op jit(solution)/shard_map/ppermute | solution.py:469
  506.1 63.5 %all_gather.39 = s32[8,512,8]{1,2,0:T(8,128)S(1)} all-gather(s32[1,512,8]{1,2,0:T(8,128)S(1)} %copy-done.74), channel_id=1, replica_groups=mesh['row'=8,'col'=4] {'row'}, dimensions={0}, use_global_device_ids=true | all-gather | bytes 147456 | tf_op jit(solution)/shard_map/all_gather | solution.py:549
  579.7 58.0 %collective-permute-done.8.wd_ref = bf16[1,768,2048]{2,1,0:T(8,128)(2,1)} collective-permute-done((bf16[1,768,2048]{2,1,0:T(8,128)(2,1)}, bf16[1,768,2048]{2,1,0:T(8,128)(2,1)}, u32[]{:S(2)}, u32[]{:S(2)}) %collective-permute-start.8) | collective-permute-done | bytes 3145760 | tf_op jit(solution)/shard_map/ppermute | solution.py:469
  647.3 25.8 %collective-permute-done.12 = bf16[1,1024,768]{2,1,0:T(8,128)(2,1)} collective-permute-done((bf16[1,1024,768]{2,1,0:T(8,128)(2,1)S(1)}, bf16[1,1024,768]{2,1,0:T(8,128)(2,1)}, u32[]{:S(2)}, u32[]{:S(2)}) %collective-permute-start.12) | collective-permute-done | bytes 1572896 | tf_op jit(solution)/shard_map/ppermute | solution.py:469
  688.8 18.0 collective-permute-done.14
  710.5 29.0 %collective-permute-done.16 = bf16[1,384,2048]{2,1,0:T(8,128)(2,1)} collective-permute-done((bf16[1,384,2048]{2,1,0:T(8,128)(2,1)}, bf16[1,384,2048]{2,1,0:T(8,128)(2,1)}, u32[]{:S(2)}, u32[]{:S(2)}) %collective-permute-start.16) | collective-permute-done | bytes 1572896 | tf_op jit(solution)/shard_map/ppermute | solution.py:469
  743.5 17.3 dispatch.3
  760.8 11.0 fusion.88
  774.5 17.2 dispatch.2
  794.8 29.9 %expert.4 = (bf16[1024,2048]{1,0:T(8,128)(2,1)}, bf16[1024,2048]{1,0:T(8,128)(2,1)}, bf16[1024,768]{1,0:T(8,128)(2,1)}, bf16[1024,768]{1,0:T(8,128)(2,1)}, bf16[1024,768]{1,0:T(8,128)(2,1)}, /*index=5*/f32[1024,1]{1,0:T(8,128)}) custom-call(bf16[4,1024,2048]{2,1,0:T(8,128)(2,1)} %bitcast.256, bf16[4,1024,2048]{2,1,0:T(8,128)(2,1)} %bitcast.252, ...), custom_call_target="tpu_custom_call" | custom-call | flops 19327352832 | bytes 30932992 | tf_op jit(solution)/shard_map/expert/pallas_call | solution.py:435
  824.7 29.7 %expert.7 = (bf16[1024,2048]{1,0:T(8,128)(2,1)}, bf16[1024,2048]{1,0:T(8,128)(2,1)}, bf16[1024,768]{1,0:T(8,128)(2,1)}, bf16[1024,768]{1,0:T(8,128)(2,1)}, bf16[1024,768]{1,0:T(8,128)(2,1)}, /*index=5*/f32[1024,1]{1,0:T(8,128)}) custom-call(bf16[4,1024,2048]{2,1,0:T(8,128)(2,1)} %bitcast.257, bf16[4,1024,2048]{2,1,0:T(8,128)(2,1)} %bitcast.253, ...), custom_call_target="tpu_custom_call" | custom-call | flops 19327352832 | bytes 30932992 | tf_op jit(solution)/shard_map/expert/pallas_call | solution.py:435
  854.4 30.1 %expert.5 = (bf16[1024,2048]{1,0:T(8,128)(2,1)}, bf16[1024,2048]{1,0:T(8,128)(2,1)}, bf16[1024,768]{1,0:T(8,128)(2,1)}, bf16[1024,768]{1,0:T(8,128)(2,1)}, bf16[1024,768]{1,0:T(8,128)(2,1)}, /*index=5*/f32[1024,1]{1,0:T(8,128)}) custom-call(bf16[4,1024,2048]{2,1,0:T(8,128)(2,1)} %bitcast.258, bf16[4,1024,2048]{2,1,0:T(8,128)(2,1)} %bitcast.254, ...), custom_call_target="tpu_custom_call" | custom-call | flops 19327352832 | bytes 30932992 | tf_op jit(solution)/shard_map/expert/pallas_call | solution.py:435
  884.5 29.7 %expert.6 = (bf16[1024,2048]{1,0:T(8,128)(2,1)}, bf16[1024,2048]{1,0:T(8,128)(2,1)}, bf16[1024,768]{1,0:T(8,128)(2,1)}, bf16[1024,768]{1,0:T(8,128)(2,1)}, bf16[1024,768]{1,0:T(8,128)(2,1)}, /*index=5*/f32[1024,1]{1,0:T(8,128)}) custom-call(bf16[4,1024,2048]{2,1,0:T(8,128)(2,1)} %bitcast.259, bf16[4,1024,2048]{2,1,0:T(8,128)(2,1)} %bitcast.255, ...), custom_call_target="tpu_custom_call" | custom-call | flops 19327352832 | bytes 30932992 | tf_op jit(solution)/shard_map/expert/pallas_call | solution.py:435
  914.2 22.4 %combine.3 = bf16[8,512,2048]{2,1,0:T(8,128)(2,1)} custom-call(s32[8,512,4]{2,1,0:T(8,128)} %bitcast_select_fusion.2.rank_ref, bf16[8,128,2048]{2,1,0:T(8,128)(2,1)} %bitcast.282, bf16[8,128,2048]{2,1,0:T(8,128)(2,1)} %bitcast.284, bf16[8,128,2048]{2,1,0:T(8,128)(2,1)} %bitcast.285, bf16[8,128,2048]{2,1,0:T(8,128)(2,1)} %bitcast.283), custom_call_target="tpu_custom_call" | custom-call | flops 8589934592 | bytes 33554432 | tf_op jit(solution)/shard_map/combine/pallas_call | solution.py:391
  948.3 46.4 %all-to-all-start = ((f32[8,4,512]{2,1,0:T(4,128)}), f32[8,4,512]{2,1,0:T(4,128)S(1)}, u32[]{:S(2)}, u32[]{:S(2)}) async-start(f32[8,4,512]{2,1,0:T(4,128)} %copy.100), calls=%async_computation.2 | async-start | bytes 131072 | tf_op jit(solution)/shard_map/all_to_all | solution.py:632
  996.0 5.8 all-to-all-done
  1002.1 145.8 %reduce-scatter.6.cloned.1.call-done = bf16[1,512,2048]{2,1,0:T(8,128)(2,1)} async-done(((bf16[8,512,2048]{2,1,0:T(8,128)(2,1)}), bf16[1,512,2048]{2,1,0:T(8,128)(2,1)}) %reduce-scatter.6.cloned.1.call-update) | async-done | bytes 2097168 | tf_op jit(solution)/shard_map/reduce_scatter | solution.py:629
  1147.9 4.6 multiply_reduce_fusion
  1161.5 17.0 attend_back.4
  1178.5 24.7 %collective-permute-done.20 = bf16[512,2048]{1,0:T(8,128)(2,1)S(1)} collective-permute-done((bf16[512,2048]{1,0:T(8,128)(2,1)S(1)}, bf16[512,2048]{1,0:T(8,128)(2,1)S(1)}, u32[]{:S(2)}, u32[]{:S(2)}) %collective-permute-start.20) | collective-permute-done | bytes 2097184 | tf_op jit(solution)/shard_map/ppermute | solution.py:469
  1203.2 6.3 convolution_convert_fusion.11.do_ref
  1209.5 16.8 attend_back.5
  1226.3 19.8 %collective-permute-done.21 = bf16[512,2048]{1,0:T(8,128)(2,1)} collective-permute-done((bf16[512,2048]{1,0:T(8,128)(2,1)S(1)}, bf16[512,2048]{1,0:T(8,128)(2,1)}, u32[]{:S(2)}, u32[]{:S(2)}) %collective-permute-start.21) | collective-permute-done | bytes 2097184 | tf_op jit(solution)/shard_map/ppermute | solution.py:469
  1246.1 6.2 convolution_convert_fusion.10.do_ref
  1252.2 17.2 attend_back.6
  1269.5 6.2 convolution_convert_fusion.9.do_ref
  1275.6 17.0 attend_back.7
  1298.4 15.7 bitcast_convert_fusion.1
  1314.2 22.3 %combine.2 = bf16[8,512,2048]{2,1,0:T(8,128)(2,1)} custom-call(s32[8,512,4]{2,1,0:T(8,128)} %bitcast_select_fusion.2.rank_ref, bf16[8,128,2048]{2,1,0:T(8,128)(2,1)} %bitcast.278, bf16[8,128,2048]{2,1,0:T(8,128)(2,1)} %bitcast.280, bf16[8,128,2048]{2,1,0:T(8,128)(2,1)} %bitcast.281, bf16[8,128,2048]{2,1,0:T(8,128)(2,1)} %bitcast.279), custom_call_target="tpu_custom_call" | custom-call | flops 8589934592 | bytes 33554432 | tf_op jit(solution)/shard_map/combine/pallas_call | solution.py:391
  1340.2 9.6 fusion.80
  1371.9 6.4 fusion.81
  1378.4 5.8 convolution_convert_fusion.1
  1418.6 5.5 fusion.94
  1424.1 5.7 fusion.91
  1429.8 5.5 fusion.97
  1469.9 15.8 bitcast_convert_fusion
  1502.7 40.4 %collective-permute-done.37 = bf16[768,2048]{1,0:T(8,128)(2,1)} collective-permute-done((bf16[768,2048]{1,0:T(8,128)(2,1)}, bf16[768,2048]{1,0:T(8,128)(2,1)}, u32[]{:S(2)}, u32[]{:S(2)}) %collective-permute-start.37) | collective-permute-done | bytes 3145760 | tf_op jit(solution)/shard_map/ppermute | solution.py:469
  1544.5 4.2 convolution_convert_fusion.7
  1553.2 57.4 %collective-permute-done.33 = bf16[2048,768]{1,0:T(8,128)(2,1)} collective-permute-done((bf16[2048,768]{1,0:T(8,128)(2,1)}, bf16[2048,768]{1,0:T(8,128)(2,1)}, u32[]{:S(2)}, u32[]{:S(2)}) %collective-permute-start.33) | collective-permute-done | bytes 3145760 | tf_op jit(solution)/shard_map/ppermute | solution.py:469
  1612.2 7.4 add_bitcast_fusion
  1619.6 7.1 add_bitcast_fusion.1
  1626.7 51.1 %collective-permute-done.29 = bf16[2048,768]{1,0:T(8,128)(2,1)S(1)} collective-permute-done((bf16[2048,768]{1,0:T(8,128)(2,1)}, bf16[2048,768]{1,0:T(8,128)(2,1)S(1)}, u32[]{:S(2)}, u32[]{:S(2)}) %collective-permute-start.29) | collective-permute-done | bytes 3145760 | tf_op jit(solution)/shard_map/ppermute | solution.py:469
  1677.8 5.7 add_bitcast_fusion.2
  1689.5 34.3 %collective-permute-done.25 = bf16[512,2048]{1,0:T(8,128)(2,1)} collective-permute-done((bf16[512,2048]{1,0:T(8,128)(2,1)}, bf16[512,2048]{1,0:T(8,128)(2,1)}, u32[]{:S(2)}, u32[]{:S(2)}) %collective-permute-start.25) | collective-permute-done | bytes 2097184 | tf_op jit(solution)/shard_map/ppermute | solution.py:469
  1723.8 31.8 %collective-permute-done.26 = bf16[512,2048]{1,0:T(8,128)(2,1)} collective-permute-done((bf16[512,2048]{1,0:T(8,128)(2,1)}, bf16[512,2048]{1,0:T(8,128)(2,1)}, u32[]{:S(2)}, u32[]{:S(2)}) %collective-permute-start.26) | collective-permute-done | bytes 2097184 | tf_op jit(solution)/shard_map/ppermute | solution.py:469
  1755.6 5.5 collective-permute-done.27
  1761.1 11.1 fusion.25
  1772.3 102.8 %all-reduce.2 = f32[32,72]{1,0:T(8,128)S(1)} all-reduce(f32[32,72]{1,0:T(8,128)S(1)} %pad_maximum_fusion.26), channel_id=12, replica_groups=mesh['row'=8,'col'=4] {'row','col'}, use_global_device_ids=true, to_apply=%region_30.31.clone | all-reduce | flops 2304 | bytes 18432
  1876.3 9.1 fusion.24
  (522 shorter events, 270.3 us)
Async XLA Ops:
  7.2 61.7 %all-reduce.6.cloned.1.call-start = ((), (), s32[]{:S(2)}) async-start(), calls=%async_computation.17 | async-start | bytes 282624
  14.0 114.8 %all-gather.10.cloned.1.call-start = ((), (), s32[]{:S(2)}) async-start(), calls=%async_computation.7 | async-start | bytes 5898240 | tf_op jit(solution)/shard_map/all_gather | solution.py:535
  16.9 229.6 %all-gather.14.cloned.1.call-start = ((), (), s32[]{:S(2)}) async-start(), calls=%async_computation.14 | async-start | bytes 9437184 | tf_op jit(solution)/shard_map/all_gather | solution.py:579
  16.9 120.3 %collective-permute-start.2 = (bf16[512,2048]{1,0:T(8,128)(2,1)}, bf16[512,2048]{1,0:T(8,128)(2,1)}, u32[]{:S(2)}, u32[]{:S(2)}) collective-permute-start(bf16[512,2048]{1,0:T(8,128)(2,1)} %bitcast.299), channel_id=1, source_target_pairs={{0,2},{1,3},{2,0},{3,1},{4,6},{5,7},{6,4},{7,5},{8,10},{9,11},{10,... | collective-permute-start | bytes 6291464 | tf_op jit(solution)/shard_map/ppermute | solution.py:469
  20.0 125.6 %collective-permute-start = (bf16[512,2048]{1,0:T(8,128)(2,1)}, bf16[512,2048]{1,0:T(8,128)(2,1)}, u32[]{:S(2)}, u32[]{:S(2)}) collective-permute-start(bf16[512,2048]{1,0:T(8,128)(2,1)} %bitcast.300), channel_id=1, source_target_pairs={{0,3},{1,2},{2,1},{3,0},{4,7},{5,6},{6,5},{7,4},{8,11},{9,10},{10,... | collective-permute-start | bytes 6291464 | tf_op jit(solution)/shard_map/ppermute | solution.py:469
  21.4 132.4 %collective-permute-start.1 = (bf16[512,2048]{1,0:T(8,128)(2,1)}, bf16[512,2048]{1,0:T(8,128)(2,1)S(1)}, u32[]{:S(2)}, u32[]{:S(2)}) collective-permute-start(bf16[512,2048]{1,0:T(8,128)(2,1)} %bitcast.301), channel_id=1, source_target_pairs={{0,1},{1,0},{2,3},{3,2},{4,5},{5,4},{6,7},{7,6},{8,9},{9,8},{10,11... | collective-permute-start | bytes 6291464 | tf_op jit(solution)/shard_map/ppermute | solution.py:469
  165.5 128.9 %all-gather.12.cloned.1.call-start = ((), (), s32[]{:S(2)}) async-start(), calls=%async_computation.8 | async-start | bytes 4718592 | tf_op jit(solution)/shard_map/all_gather | solution.py:580
  246.6 496.9 %all-gather.18.cloned.1.call-start = ((), (), s32[]{:S(2)}) async-start(), calls=%async_computation.16 | async-start | bytes 18874368 | tf_op jit(solution)/shard_map/all_gather | solution.py:581
  294.5 466.4 %all-gather.16.cloned.1.call-start = ((), (), s32[]{:S(2)}) async-start(), calls=%async_computation.15 | async-start | bytes 18874368 | tf_op jit(solution)/shard_map/all_gather | solution.py:591
  326.2 39.6 %collective-permute-start.3 = (bf16[512,2048]{1,0:T(8,128)(2,1)}, bf16[512,2048]{1,0:T(8,128)(2,1)}, u32[]{:S(2)}, u32[]{:S(2)}) collective-permute-start(bf16[512,2048]{1,0:T(8,128)(2,1)} %convolution_convert_fusion.5), channel_id=1, source_target_pairs={{0,3},{1,2},{2,1},{3,0},{4,7},{5,6},{6,5},{7,4},{8,11},{9,10},{10,... | collective-permute-start | bytes 6291464 | tf_op jit(solution)/shard_map/ppermute | solution.py:469
  332.4 88.4 %collective-permute-start.4 = (bf16[512,2048]{1,0:T(8,128)(2,1)}, bf16[512,2048]{1,0:T(8,128)(2,1)}, u32[]{:S(2)}, u32[]{:S(2)}) collective-permute-start(bf16[512,2048]{1,0:T(8,128)(2,1)} %convolution_convert_fusion.4), channel_id=1, source_target_pairs={{0,2},{1,3},{2,0},{3,1},{4,6},{5,7},{6,4},{7,5},{8,10},{9,11},{10,... | collective-permute-start | bytes 6291464 | tf_op jit(solution)/shard_map/ppermute | solution.py:469
  336.6 84.2 %collective-permute-start.5 = (bf16[512,2048]{1,0:T(8,128)(2,1)}, bf16[512,2048]{1,0:T(8,128)(2,1)}, u32[]{:S(2)}, u32[]{:S(2)}) collective-permute-start(bf16[512,2048]{1,0:T(8,128)(2,1)} %convolution_convert_fusion.3), channel_id=1, source_target_pairs={{0,1},{1,0},{2,3},{3,2},{4,5},{5,4},{6,7},{7,6},{8,9},{9,8},{10,11... | collective-permute-start | bytes 6291464 | tf_op jit(solution)/shard_map/ppermute | solution.py:469
  337.0 815.5 %copy-start.72 = (f32[1,2,8,128]{3,1,2,0:T(2,128)}, f32[1,2,8,128]{3,1,2,0:T(2,128)S(1)}, u32[]{:S(2)}) copy-start(f32[1,2,8,128]{3,1,2,0:T(2,128)S(1)} %copy.115) | copy-start | bytes 24580
  337.0 83.7 %copy-start.25 = (bf16[1,512,2048]{2,1,0:T(8,128)(2,1)S(1)}, bf16[1,512,2048]{2,1,0:T(8,128)(2,1)}, u32[]{:S(2)}) copy-start(bf16[1,512,2048]{2,1,0:T(8,128)(2,1)} %param.15) | copy-start | bytes 6291460
  427.8 724.7 %copy-start.75 = (f32[512]{0:T(512)}, f32[512]{0:T(512)S(1)}, u32[]{:S(2)}) copy-start(f32[512]{0:T(512)S(1)} %add_rsqrt_fusion.1) | copy-start | bytes 6148
  431.5 74.5 %copy-start.74 = (s32[1,512,8]{1,2,0:T(8,128)S(1)}, s32[1,512,8]{1,2,0:T(8,128)}, u32[]{:S(2)}) copy-start(s32[1,512,8]{1,2,0:T(8,128)} %param.17) | copy-start | bytes 49156
  431.6 716.3 %reduce-scatter.6.cloned.1.call-start = ((), (), s32[]{:S(2)}) async-start(), calls=%async_computation.9 | async-start | bytes 18874368 | tf_op jit(solution)/shard_map/reduce_scatter | solution.py:629
  431.6 71.2 %collective-permute-start.6 = (bf16[1,2048,768]{2,1,0:T(8,128)(2,1)}, bf16[1,2048,768]{2,1,0:T(8,128)(2,1)S(1)}, u32[]{:S(2)}, u32[]{:S(2)}) collective-permute-start(bf16[1,2048,768]{2,1,0:T(8,128)(2,1)} %wg_ref), channel_id=1, source_target_pairs={{0,1},{1,0},{2,3},{3,2},{4,5},{5,4},{6,7},{7,6},{8,9},{9,8},{10,11... | collective-permute-start | bytes 9437192 | tf_op jit(solution)/shard_map/ppermute | solution.py:469
  433.3 71.3 %collective-permute-start.9 = (bf16[1,2048,768]{2,1,0:T(8,128)(2,1)}, bf16[1,2048,768]{2,1,0:T(8,128)(2,1)}, u32[]{:S(2)}, u32[]{:S(2)}) collective-permute-start(bf16[1,2048,768]{2,1,0:T(8,128)(2,1)} %wg_ref), channel_id=1, source_target_pairs={{0,2},{1,3},{2,0},{3,1},{4,6},{5,7},{6,4},{7,5},{8,10},{9,11},{10,... | collective-permute-start | bytes 9437192 | tf_op jit(solution)/shard_map/ppermute | solution.py:469
  434.8 138.1 %collective-permute-start.7 = (bf16[1,2048,768]{2,1,0:T(8,128)(2,1)}, bf16[1,2048,768]{2,1,0:T(8,128)(2,1)}, u32[]{:S(2)}, u32[]{:S(2)}) collective-permute-start(bf16[1,2048,768]{2,1,0:T(8,128)(2,1)} %wu_ref), channel_id=1, source_target_pairs={{0,1},{1,0},{2,3},{3,2},{4,5},{5,4},{6,7},{7,6},{8,9},{9,8},{10,11... | collective-permute-start | bytes 9437192 | tf_op jit(solution)/shard_map/ppermute | solution.py:469
  435.3 141.7 %collective-permute-start.10 = (bf16[1,2048,768]{2,1,0:T(8,128)(2,1)}, bf16[1,2048,768]{2,1,0:T(8,128)(2,1)}, u32[]{:S(2)}, u32[]{:S(2)}) collective-permute-start(bf16[1,2048,768]{2,1,0:T(8,128)(2,1)} %wu_ref), channel_id=1, source_target_pairs={{0,2},{1,3},{2,0},{3,1},{4,6},{5,7},{6,4},{7,5},{8,10},{9,11},{10,... | collective-permute-start | bytes 9437192 | tf_op jit(solution)/shard_map/ppermute | solution.py:469
  435.8 202.0 %collective-permute-start.8 = (bf16[1,768,2048]{2,1,0:T(8,128)(2,1)}, bf16[1,768,2048]{2,1,0:T(8,128)(2,1)}, u32[]{:S(2)}, u32[]{:S(2)}) collective-permute-start(bf16[1,768,2048]{2,1,0:T(8,128)(2,1)} %wd_ref), channel_id=1, source_target_pairs={{0,1},{1,0},{2,3},{3,2},{4,5},{5,4},{6,7},{7,6},{8,9},{9,8},{10,11... | collective-permute-start | bytes 9437192 | tf_op jit(solution)/shard_map/ppermute | solution.py:469
  502.8 140.2 %collective-permute-start.11 = (bf16[1,768,2048]{2,1,0:T(8,128)(2,1)}, bf16[1,768,2048]{2,1,0:T(8,128)(2,1)}, u32[]{:S(2)}, u32[]{:S(2)}) collective-permute-start(bf16[1,768,2048]{2,1,0:T(8,128)(2,1)} %wd_ref), channel_id=1, source_target_pairs={{0,2},{1,3},{2,0},{3,1},{4,6},{5,7},{6,4},{7,5},{8,10},{9,11},{10,... | collective-permute-start | bytes 9437192 | tf_op jit(solution)/shard_map/ppermute | solution.py:469
  504.6 168.5 %collective-permute-start.12 = (bf16[1,1024,768]{2,1,0:T(8,128)(2,1)S(1)}, bf16[1,1024,768]{2,1,0:T(8,128)(2,1)}, u32[]{:S(2)}, u32[]{:S(2)}) collective-permute-start(bf16[1,1024,768]{2,1,0:T(8,128)(2,1)S(1)} %slice.331), channel_id=1, source_target_pairs={{0,2},{1,3},{2,0},{3,1},{4,6},{5,7},{6,4},{7,5},{8,10},{9,11},{10,... | collective-permute-start | bytes 4718600 | tf_op jit(solution)/shard_map/ppermute | solution.py:469
  572.9 112.1 %collective-permute-start.13 = (bf16[1,1024,768]{2,1,0:T(8,128)(2,1)}, bf16[1,1024,768]{2,1,0:T(8,128)(2,1)}, u32[]{:S(2)}, u32[]{:S(2)}) collective-permute-start(bf16[1,1024,768]{2,1,0:T(8,128)(2,1)} %slice.332), channel_id=1, source_target_pairs={{0,1},{1,0},{2,3},{3,2},{4,5},{5,4},{6,7},{7,6},{8,9},{9,8},{10,11... | collective-permute-start | bytes 4718600 | tf_op jit(solution)/shard_map/ppermute | solution.py:469
  577.1 129.7 %collective-permute-start.14 = (bf16[1,1024,768]{2,1,0:T(8,128)(2,1)}, bf16[1,1024,768]{2,1,0:T(8,128)(2,1)}, u32[]{:S(2)}, u32[]{:S(2)}) collective-permute-start(bf16[1,1024,768]{2,1,0:T(8,128)(2,1)} %slice.333), channel_id=1, source_target_pairs={{0,2},{1,3},{2,0},{3,1},{4,6},{5,7},{6,4},{7,5},{8,10},{9,11},{10,... | collective-permute-start | bytes 4718600 | tf_op jit(solution)/shard_map/ppermute | solution.py:469
  637.8 69.0 %collective-permute-start.15 = (bf16[1,1024,768]{2,1,0:T(8,128)(2,1)}, bf16[1,1024,768]{2,1,0:T(8,128)(2,1)}, u32[]{:S(2)}, u32[]{:S(2)}) collective-permute-start(bf16[1,1024,768]{2,1,0:T(8,128)(2,1)} %slice.334), channel_id=1, source_target_pairs={{0,1},{1,0},{2,3},{3,2},{4,5},{5,4},{6,7},{7,6},{8,9},{9,8},{10,11... | collective-permute-start | bytes 4718600 | tf_op jit(solution)/shard_map/ppermute | solution.py:469
  643.0 96.5 %collective-permute-start.16 = (bf16[1,384,2048]{2,1,0:T(8,128)(2,1)}, bf16[1,384,2048]{2,1,0:T(8,128)(2,1)}, u32[]{:S(2)}, u32[]{:S(2)}) collective-permute-start(bf16[1,384,2048]{2,1,0:T(8,128)(2,1)} %slice.335), channel_id=1, source_target_pairs={{0,2},{1,3},{2,0},{3,1},{4,6},{5,7},{6,4},{7,5},{8,10},{9,11},{10,... | collective-permute-start | bytes 4718600 | tf_op jit(solution)/shard_map/ppermute | solution.py:469
  673.1 66.4 %collective-permute-start.17 = (bf16[1,384,2048]{2,1,0:T(8,128)(2,1)}, bf16[1,384,2048]{2,1,0:T(8,128)(2,1)}, u32[]{:S(2)}, u32[]{:S(2)}) collective-permute-start(bf16[1,384,2048]{2,1,0:T(8,128)(2,1)} %slice.336), channel_id=1, source_target_pairs={{0,1},{1,0},{2,3},{3,2},{4,5},{5,4},{6,7},{7,6},{8,9},{9,8},{10,11... | collective-permute-start | bytes 4718600 | tf_op jit(solution)/shard_map/ppermute | solution.py:469
  939.1 4.7 collective-permute-start.18
  943.8 51.0 %collective-permute-start.19 = (f32[2,32]{1,0:T(2,128)S(1)}, f32[2,32]{1,0:T(2,128)S(1)}, u32[]{:S(2)}, u32[]{:S(2)}) collective-permute-start(f32[2,32]{1,0:T(2,128)S(1)} %fusion.71), channel_id=1, source_target_pairs={{0,2},{1,3},{2,0},{3,1},{4,6},{5,7},{6,4},{7,5},{8,10},{9,11},{10,... | collective-permute-start | bytes 776 | tf_op jit(solution)/shard_map/ppermute | solution.py:469
  948.3 53.4 %all-to-all-start = ((f32[8,4,512]{2,1,0:T(4,128)}), f32[8,4,512]{2,1,0:T(4,128)S(1)}, u32[]{:S(2)}, u32[]{:S(2)}) async-start(f32[8,4,512]{2,1,0:T(4,128)} %copy.100), calls=%async_computation.2 | async-start | bytes 131072 | tf_op jit(solution)/shard_map/all_to_all | solution.py:632
  994.8 458.9 %reduce-scatter.10.cloned.1.call-start = ((), (), s32[]{:S(2)}) async-start(), calls=%async_computation.11 | async-start | bytes 4718592 | tf_op jit(solution)/shard_map/reduce_scatter | solution.py:690
  1154.6 48.6 %collective-permute-start.20 = (bf16[512,2048]{1,0:T(8,128)(2,1)S(1)}, bf16[512,2048]{1,0:T(8,128)(2,1)S(1)}, u32[]{:S(2)}, u32[]{:S(2)}) collective-permute-start(bf16[512,2048]{1,0:T(8,128)(2,1)S(1)} %fusion.77), channel_id=1, source_target_pairs={{0,1},{1,0},{2,3},{3,2},{4,5},{5,4},{6,7},{7,6},{8,9},{9,8},{10,11... | collective-permute-start | bytes 6291464 | tf_op jit(solution)/shard_map/ppermute | solution.py:469
  1156.1 90.0 %collective-permute-start.21 = (bf16[512,2048]{1,0:T(8,128)(2,1)S(1)}, bf16[512,2048]{1,0:T(8,128)(2,1)}, u32[]{:S(2)}, u32[]{:S(2)}) collective-permute-start(bf16[512,2048]{1,0:T(8,128)(2,1)S(1)} %fusion.77), channel_id=1, source_target_pairs={{0,2},{1,3},{2,0},{3,1},{4,6},{5,7},{6,4},{7,5},{8,10},{9,11},{10,... | collective-permute-start | bytes 6291464 | tf_op jit(solution)/shard_map/ppermute | solution.py:469
  1157.6 111.9 %collective-permute-start.22 = (bf16[512,2048]{1,0:T(8,128)(2,1)S(1)}, bf16[512,2048]{1,0:T(8,128)(2,1)}, u32[]{:S(2)}, u32[]{:S(2)}) collective-permute-start(bf16[512,2048]{1,0:T(8,128)(2,1)S(1)} %fusion.77), channel_id=1, source_target_pairs={{0,3},{1,2},{2,1},{3,0},{4,7},{5,6},{6,5},{7,4},{8,11},{9,10},{10,... | collective-permute-start | bytes 6291464 | tf_op jit(solution)/shard_map/ppermute | solution.py:469
  1296.0 387.6 %all-reduce.8.cloned.1.call-start = ((), (), s32[]{:S(2)}) async-start(), calls=%async_computation.18 | async-start | bytes 557056
  1298.2 389.1 %reduce-scatter.14.cloned.1.call-start = ((), (), s32[]{:S(2)}) async-start(), calls=%async_computation.13 | async-start | bytes 4718592 | tf_op jit(solution)/shard_map/reduce_scatter | solution.py:732
  1314.1 562.1 %reduce-scatter.8.cloned.1.call-start = ((), (), s32[]{:S(2)}) async-start(), calls=%async_computation.10 | async-start | bytes 18874368 | tf_op jit(solution)/shard_map/reduce_scatter | solution.py:635
  1336.6 548.8 %reduce-scatter.12.cloned.1.call-start = ((), (), s32[]{:S(2)}) async-start(), calls=%async_computation.12 | async-start | bytes 5898240 | tf_op jit(solution)/shard_map/reduce_scatter | solution.py:725
  1355.3 81.2 %collective-permute-start.36 = (bf16[384,2048]{1,0:T(8,128)(2,1)}, bf16[384,2048]{1,0:T(8,128)(2,1)}, u32[]{:S(2)}, u32[]{:S(2)}) collective-permute-start(bf16[384,2048]{1,0:T(8,128)(2,1)} %get-tuple-element.238), channel_id=1, source_target_pairs={{0,2},{1,3},{2,0},{3,1},{4,6},{5,7},{6,4},{7,5},{8,10},{9,11},{10,... | collective-permute-start | bytes 4718600 | tf_op jit(solution)/shard_map/ppermute | solution.py:469
  1361.8 80.2 %collective-permute-start.38 = (bf16[384,2048]{1,0:T(8,128)(2,1)}, bf16[384,2048]{1,0:T(8,128)(2,1)}, u32[]{:S(2)}, u32[]{:S(2)}) collective-permute-start(bf16[384,2048]{1,0:T(8,128)(2,1)} %get-tuple-element.239), channel_id=1, source_target_pairs={{0,1},{1,0},{2,3},{3,2},{4,5},{5,4},{6,7},{7,6},{8,9},{9,8},{10,11... | collective-permute-start | bytes 4718600 | tf_op jit(solution)/shard_map/ppermute | solution.py:469
  1386.1 61.5 %collective-permute-start.32 = (bf16[1024,768]{1,0:T(8,128)(2,1)}, bf16[1024,768]{1,0:T(8,128)(2,1)}, u32[]{:S(2)}, u32[]{:S(2)}) collective-permute-start(bf16[1024,768]{1,0:T(8,128)(2,1)} %get-tuple-element.240), channel_id=1, source_target_pairs={{0,2},{1,3},{2,0},{3,1},{4,6},{5,7},{6,4},{7,5},{8,10},{9,11},{10,... | collective-permute-start | bytes 4718600 | tf_op jit(solution)/shard_map/ppermute | solution.py:469
  1393.2 58.4 %collective-permute-start.34 = (bf16[1024,768]{1,0:T(8,128)(2,1)}, bf16[1024,768]{1,0:T(8,128)(2,1)}, u32[]{:S(2)}, u32[]{:S(2)}) collective-permute-start(bf16[1024,768]{1,0:T(8,128)(2,1)} %get-tuple-element.241), channel_id=1, source_target_pairs={{0,1},{1,0},{2,3},{3,2},{4,5},{5,4},{6,7},{7,6},{8,9},{9,8},{10,11... | collective-permute-start | bytes 4718600 | tf_op jit(solution)/shard_map/ppermute | solution.py:469
  1405.9 52.7 %collective-permute-start.28 = (bf16[1024,768]{1,0:T(8,128)(2,1)}, bf16[1024,768]{1,0:T(8,128)(2,1)}, u32[]{:S(2)}, u32[]{:S(2)}) collective-permute-start(bf16[1024,768]{1,0:T(8,128)(2,1)} %get-tuple-element.242), channel_id=1, source_target_pairs={{0,2},{1,3},{2,0},{3,1},{4,6},{5,7},{6,4},{7,5},{8,10},{9,11},{10,... | collective-permute-start | bytes 4718600 | tf_op jit(solution)/shard_map/ppermute | solution.py:469
  1436.6 52.4 %collective-permute-start.30 = (bf16[1024,768]{1,0:T(8,128)(2,1)}, bf16[1024,768]{1,0:T(8,128)(2,1)}, u32[]{:S(2)}, u32[]{:S(2)}) collective-permute-start(bf16[1024,768]{1,0:T(8,128)(2,1)} %get-tuple-element.243), channel_id=1, source_target_pairs={{0,1},{1,0},{2,3},{3,2},{4,5},{5,4},{6,7},{7,6},{8,9},{9,8},{10,11... | collective-permute-start | bytes 4718600 | tf_op jit(solution)/shard_map/ppermute | solution.py:469
  1442.0 101.1 %collective-permute-start.37 = (bf16[768,2048]{1,0:T(8,128)(2,1)}, bf16[768,2048]{1,0:T(8,128)(2,1)}, u32[]{:S(2)}, u32[]{:S(2)}) collective-permute-start(bf16[768,2048]{1,0:T(8,128)(2,1)} %pad_maximum_fusion.9), channel_id=1, source_target_pairs={{0,1},{1,0},{2,3},{3,2},{4,5},{5,4},{6,7},{7,6},{8,9},{9,8},{10,11... | collective-permute-start | bytes 9437192 | tf_op jit(solution)/shard_map/ppermute | solution.py:469
  1453.6 9.2 collective-permute-start.23
  1455.3 8.3 collective-permute-start.24
  1458.6 94.2 %collective-permute-start.39 = (bf16[768,2048]{1,0:T(8,128)(2,1)}, bf16[768,2048]{1,0:T(8,128)(2,1)}, u32[]{:S(2)}, u32[]{:S(2)}) collective-permute-start(bf16[768,2048]{1,0:T(8,128)(2,1)} %pad_maximum_fusion.10), channel_id=1, source_target_pairs={{0,2},{1,3},{2,0},{3,1},{4,6},{5,7},{6,4},{7,5},{8,10},{9,11},{10,... | collective-permute-start | bytes 9437192 | tf_op jit(solution)/shard_map/ppermute | solution.py:469
  1462.9 147.6 %collective-permute-start.33 = (bf16[2048,768]{1,0:T(8,128)(2,1)}, bf16[2048,768]{1,0:T(8,128)(2,1)}, u32[]{:S(2)}, u32[]{:S(2)}) collective-permute-start(bf16[2048,768]{1,0:T(8,128)(2,1)} %pad_maximum_fusion.7), channel_id=1, source_target_pairs={{0,1},{1,0},{2,3},{3,2},{4,5},{5,4},{6,7},{7,6},{8,9},{9,8},{10,11... | collective-permute-start | bytes 9437192 | tf_op jit(solution)/shard_map/ppermute | solution.py:469
  1463.7 148.3 %collective-permute-start.35 = (bf16[2048,768]{1,0:T(8,128)(2,1)}, bf16[2048,768]{1,0:T(8,128)(2,1)}, u32[]{:S(2)}, u32[]{:S(2)}) collective-permute-start(bf16[2048,768]{1,0:T(8,128)(2,1)} %pad_maximum_fusion.8), channel_id=1, source_target_pairs={{0,2},{1,3},{2,0},{3,1},{4,6},{5,7},{6,4},{7,5},{8,10},{9,11},{10,... | collective-permute-start | bytes 9437192 | tf_op jit(solution)/shard_map/ppermute | solution.py:469
  1489.0 188.8 %collective-permute-start.29 = (bf16[2048,768]{1,0:T(8,128)(2,1)}, bf16[2048,768]{1,0:T(8,128)(2,1)S(1)}, u32[]{:S(2)}, u32[]{:S(2)}) collective-permute-start(bf16[2048,768]{1,0:T(8,128)(2,1)} %pad_maximum_fusion.5), channel_id=1, source_target_pairs={{0,1},{1,0},{2,3},{3,2},{4,5},{5,4},{6,7},{7,6},{8,9},{9,8},{10,11... | collective-permute-start | bytes 9437192 | tf_op jit(solution)/shard_map/ppermute | solution.py:469
  1543.1 134.7 %collective-permute-start.31 = (bf16[2048,768]{1,0:T(8,128)(2,1)}, bf16[2048,768]{1,0:T(8,128)(2,1)}, u32[]{:S(2)}, u32[]{:S(2)}) collective-permute-start(bf16[2048,768]{1,0:T(8,128)(2,1)} %pad_maximum_fusion.6), channel_id=1, source_target_pairs={{0,2},{1,3},{2,0},{3,1},{4,6},{5,7},{6,4},{7,5},{8,10},{9,11},{10,... | collective-permute-start | bytes 9437192 | tf_op jit(solution)/shard_map/ppermute | solution.py:469
  1552.9 170.9 %collective-permute-start.25 = (bf16[512,2048]{1,0:T(8,128)(2,1)}, bf16[512,2048]{1,0:T(8,128)(2,1)}, u32[]{:S(2)}, u32[]{:S(2)}) collective-permute-start(bf16[512,2048]{1,0:T(8,128)(2,1)} %convolution_convert_fusion.8), channel_id=1, source_target_pairs={{0,3},{1,2},{2,1},{3,0},{4,7},{5,6},{6,5},{7,4},{8,11},{9,10},{10,... | collective-permute-start | bytes 6291464 | tf_op jit(solution)/shard_map/ppermute | solution.py:469
  1610.5 145.0 %collective-permute-start.26 = (bf16[512,2048]{1,0:T(8,128)(2,1)}, bf16[512,2048]{1,0:T(8,128)(2,1)}, u32[]{:S(2)}, u32[]{:S(2)}) collective-permute-start(bf16[512,2048]{1,0:T(8,128)(2,1)} %convolution_convert_fusion.7), channel_id=1, source_target_pairs={{0,2},{1,3},{2,0},{3,1},{4,6},{5,7},{6,4},{7,5},{8,10},{9,11},{10,... | collective-permute-start | bytes 6291464 | tf_op jit(solution)/shard_map/ppermute | solution.py:469
  1612.0 149.1 %collective-permute-start.27 = (bf16[512,2048]{1,0:T(8,128)(2,1)}, bf16[512,2048]{1,0:T(8,128)(2,1)}, u32[]{:S(2)}, u32[]{:S(2)}) collective-permute-start(bf16[512,2048]{1,0:T(8,128)(2,1)} %convolution_convert_fusion.6), channel_id=1, source_target_pairs={{0,1},{1,0},{2,3},{3,2},{4,5},{5,4},{6,7},{7,6},{8,9},{9,8},{10,11... | collective-permute-start | bytes 6291464 | tf_op jit(solution)/shard_map/ppermute | solution.py:469
  1626.7 134.3 %copy-start.79 = (f32[1,2,8,128]{3,1,2,0:T(2,128)S(1)}, f32[1,2,8,128]{3,1,2,0:T(2,128)}, u32[]{:S(2)}) copy-start(f32[1,2,8,128]{3,1,2,0:T(2,128)} %copy.117) | copy-start | bytes 24580
  1626.7 134.3 %copy-start.83 = (f32[512]{0:T(512)S(1)}, f32[512]{0:T(512)}, u32[]{:S(2)}) copy-start(f32[512]{0:T(512)} %add_rsqrt_fusion) | copy-start | bytes 6148
  1761.1 115.2 %copy-start.7 = (bf16[1,512,2048]{2,1,0:T(8,128)(2,1)S(1)}, bf16[1,512,2048]{2,1,0:T(8,128)(2,1)}, u32[]{:S(2)}) copy-start(bf16[1,512,2048]{2,1,0:T(8,128)(2,1)} %param.16) | copy-start | bytes 6291460
  1761.1 115.2 %copy-start.73 = (f32[1,2,8,128]{3,1,2,0:T(2,128)S(1)}, f32[1,2,8,128]{3,1,2,0:T(2,128)}, u32[]{:S(2)}) copy-start(f32[1,2,8,128]{3,1,2,0:T(2,128)} %copy-done.72) | copy-start | bytes 24580
  1761.1 115.2 %copy-start.76 = (f32[512]{0:T(512)S(1)}, f32[512]{0:T(512)}, u32[]{:S(2)}) copy-start(f32[512]{0:T(512)} %copy-done.75) | copy-start | bytes 6148
  1761.1 115.2 %copy-start.82 = (f32[512]{0:T(512)S(1)}, f32[512]{0:T(512)}, u32[]{:S(2)}) copy-start(f32[512]{0:T(512)} %copy-done.81) | copy-start | bytes 6148
  1887.0 9.0 all-to-all-start.1
  (115 other events, 1108.3 us)
Sparse Core Ops, SparseCore 0:
  14.1 54.7 all-reduce.5
  71.2 57.4 all-gather.9
  165.7 80.8 all-gather.13
  248.1 46.3 all-gather.11
  296.0 149.4 all-gather.17
  447.0 179.6 all-gather.15
  936.8 210.9 reduce-scatter.5
  1296.2 108.3 reduce-scatter.9
  1410.8 127.8 all-reduce.7
  1540.9 51.4 reduce-scatter.13
  1594.8 166.3 reduce-scatter.7
  1763.4 58.2 reduce-scatter.11

commit v2 on v1

--- a/solution.py
+++ b/solution.py
@@ -93,7 +93,7 @@
 
 def qkv(x, gain, w, cos, sin, qg, kg, heads):
     rows, width = x.shape
-    cols = w.shape[1]
+    cols = (heads + 2) * HEAD
     tile = 256
     whole = lambda i: (0, 0)
     row = lambda i: (i, 0)
@@ -141,7 +141,7 @@
     @pl.when((at == 0) & (part == 0))
     def _():
         for j in range(blocks):
-            vp_one[j * rows : (j + 1) * rows, :HEAD] = vp_ref[j, 0, 0]
+            vp_one[j * rows : (j + 1) * rows, :HEAD] = vp_ref[j, 0]
         vp_one[:, HEAD:] = jnp.ones((blocks * rows, HEAD), BF)
         vl_one[:, :HEAD] = kv_ref[1]
         vl_one[:, HEAD:] = jnp.ones((rows, HEAD), BF)
@@ -163,7 +163,7 @@
 
     @pl.loop(0, jnp.minimum(row, blocks))
     def _(j):
-        weights = jnp.exp2(dot_nt(q, kp_ref[j, 0, 0])).astype(BF)
+        weights = jnp.exp2(dot_nt(q, kp_ref[j, 0])).astype(BF)
         acc[...] += dot_nn(weights, vp_one[pl.ds(pl.multiple_of(j * rows, rows), rows), :])
 
     total = acc[:, HEAD:]
@@ -182,7 +182,7 @@
     l_ref[...] = held
 
 
-def attend(row, q, every, kv, slot, blocks):
+def attend(row, q, every, kv, blocks):
     heads, rows, _ = q.shape
     per = 2
     keys = blocks * rows
@@ -192,8 +192,8 @@
         (rows // CONT, heads // per),
         [
             pl.BlockSpec((per, CONT, HEAD), lambda i, h, s: (h, i, 0)),
-            pl.BlockSpec((blocks, 1, 1, rows, HEAD), lambda i, h, s: (0, slot, 0, 0, 0)),
-            pl.BlockSpec((blocks, 1, 1, rows, HEAD), lambda i, h, s: (0, slot, 1, 0, 0)),
+            pl.BlockSpec((blocks, 1, rows, HEAD), lambda i, h, s: (0, 0, 0, 0)),
+            pl.BlockSpec((blocks, 1, rows, HEAD), lambda i, h, s: (0, 1, 0, 0)),
             pl.BlockSpec((2, rows, HEAD), lambda i, h, s: (0, 0, 0)),
         ],
         [
@@ -276,7 +276,7 @@
 
     @pl.loop(0, jnp.minimum(row, blocks))
     def _(j):
-        a, b, c = block(kp_ref[j, 0, 0], vp_ref[j, 0, 0], None)
+        a, b, c = block(kp_ref[j, 0], vp_ref[j, 0], None)
         piece = pl.ds(pl.multiple_of(j * rows, rows), rows)
         dq[...] += a
         dkp[piece, :] += b
@@ -302,7 +302,7 @@
         dl_ref[0] = dl_ref[0] * LN2
 
 
-def attend_back(row, q, every, kv, slot, blocks, do, o, logs, scales, cos, sin, qg):
+def attend_back(row, q, every, kv, blocks, do, o, logs, scales, cos, sin, qg):
     heads, rows, _ = q.shape
     per = 2
     keys = blocks * rows
@@ -314,8 +314,8 @@
         (rows // CONT, heads // per),
         [
             pl.BlockSpec((per, CONT, HEAD), lambda i, h, s: (h, i, 0)),
-            pl.BlockSpec((blocks, 1, 1, rows, HEAD), lambda i, h, s: (0, slot, 0, 0, 0)),
-            pl.BlockSpec((blocks, 1, 1, rows, HEAD), lambda i, h, s: (0, slot, 1, 0, 0)),
+            pl.BlockSpec((blocks, 1, rows, HEAD), lambda i, h, s: (0, 0, 0, 0)),
+            pl.BlockSpec((blocks, 1, rows, HEAD), lambda i, h, s: (0, 1, 0, 0)),
             pl.BlockSpec((2, rows, HEAD), lambda i, h, s: (0, 0, 0)),
             pl.BlockSpec((CONT, per * HEAD), head),
             pl.BlockSpec((CONT, per * HEAD), head),
@@ -372,6 +372,85 @@
         flops=2 * sources * count * cap * tokens * width,
         moved=2 * sources * width * (tokens + count * cap),
     )(rank, rows)
+
+
+def route_body(count, cap, ids_ref, rank_ref, rows_ref, mask_ref, router_ref, out_ref, probs_ref, gate_ref):
+    tokens = rows_ref.shape[1]
+    rows = rows_ref[0]
+    logits = dot_nt(router_ref[...], rows)
+    weights = jnp.exp(logits - jnp.max(logits, axis=0, keepdims=True))
+    probs = weights / jnp.sum(weights, axis=0, keepdims=True)
+    probs_ref[0] = probs
+    picked = probs * mask_ref[0]
+    gates = picked / jnp.sum(picked, axis=0, keepdims=True)
+    expert_at = lax.broadcasted_iota(jnp.int32, gates.shape, 0)
+    slot = lax.broadcasted_iota(jnp.int32, (cap, tokens), 0)
+    for d in range(count):
+        here = rank_ref[0, d : d + 1, :] == slot
+        out_ref[d, 0] = dot_nn(here.astype(F32).astype(BF), rows).astype(BF)
+        mine = jnp.sum(jnp.where(expert_at == ids_ref[d], gates, 0.0), axis=0, keepdims=True)
+        gate_ref[d, 0] = jnp.sum(jnp.where(here, mine, 0.0), axis=1, keepdims=True)
+
+
+def route_dispatch(ids, rank, rows, mask, router, cap):
+    sources, count, tokens = rank.shape
+    width = rows.shape[2]
+    experts = router.shape[0]
+    return call(
+        partial(route_body, count, cap),
+        "route_dispatch",
+        (sources,),
+        [
+            pl.BlockSpec((1, count, tokens), lambda s, i: (s, 0, 0)),
+            pl.BlockSpec((1, tokens, width), lambda s, i: (s, 0, 0)),
+            pl.BlockSpec((1, experts, tokens), lambda s, i: (s, 0, 0)),
+            pl.BlockSpec((experts, width), lambda s, i: (0, 0)),
+        ],
+        [
+            pl.BlockSpec((count, 1, cap, width), lambda s, i: (0, s, 0, 0)),
+            pl.BlockSpec((1, experts, tokens), lambda s, i: (s, 0, 0)),
+            pl.BlockSpec((count, 1, cap, 1), lambda s, i: (0, s, 0, 0)),
+        ],
+        [
+            struct((count, sources, cap, width), BF),
+            struct((sources, experts, tokens), F32),
+            struct((count, sources, cap, 1), F32),
+        ],
+        flops=2 * sources * count * cap * tokens * width,
+        moved=2 * sources * width * (tokens + count * cap),
+        prefetch=1,
+    )(ids, rank, rows, mask, router)
+
+
+def share_body(g_ref, w_ref, a_ref, out_ref, sum_ref):
+    share = dot_nt(g_ref[...], w_ref[...])
+    out_ref[...] = share.astype(out_ref.dtype)
+
+    @pl.when(pl.program_id(0) == 0)
+    def _():
+        sum_ref[...] = jnp.zeros_like(sum_ref)
+
+    sum_ref[0:1, :] += jnp.sum(share * a_ref[...].astype(F32), axis=0, keepdims=True)
+
+
+def input_share(grads, w, normed, dtype):
+    rows, cols = grads.shape
+    width = w.shape[0]
+    tile = 256
+    return call(
+        share_body,
+        "input_share",
+        (rows // tile,),
+        [
+            pl.BlockSpec((tile, cols), lambda i: (i, 0)),
+            pl.BlockSpec((width, cols), lambda i: (0, 0)),
+            pl.BlockSpec((tile, width), lambda i: (i, 0)),
+        ],
+        [pl.BlockSpec((tile, width), lambda i: (i, 0)), pl.BlockSpec((8, width), lambda i: (0, 0))],
+        [struct((rows, width), dtype), struct((8, width), F32)],
+        flops=2 * rows * width * cols,
+        moved=2 * (2 * rows * width + width * cols + rows * cols),
+    )(grads, w, normed)
 
 
 def combine_body(count, cap, rank_ref, *refs):
@@ -498,6 +577,11 @@
     return lax.optimization_barrier((value,) + earlier)[0]
 
 
+def norm_back(grad, hat, spread, gain):
+    scaled = grad * gain
+    return spread * (scaled - hat * jnp.mean(scaled * hat, axis=-1, keepdims=True))
+
+
 def per_device(
     layer_input, out_grad, routes, positions, w_q, key_value_weight, w_out, router,
     ln_attn, ln_moe, q_gain, k_gain, w_gate, w_up, w_down,
@@ -514,51 +598,54 @@
     sharing = QUERY_HEADS // KEY_VALUE_HEADS // heads
     blocks = PROMPT_TOKENS // rows
     slots = range(col_count)
+    others = list(slots[1:])
     members = [col_at ^ d for d in slots]
     row_word = row_at.astype(jnp.int32).reshape(1)
 
     x_own = layer_input[0]
     up_own = out_grad[0]
 
-    key_head = col_at // sharing
     kv_cols = KEY_VALUE_HEADS * HEAD
-    wkv_mine = jnp.concatenate(
-        [
-            lax.dynamic_slice_in_dim(key_value_weight, key_head * HEAD, HEAD, 1),
-            lax.dynamic_slice_in_dim(key_value_weight, kv_cols + key_head * HEAD, HEAD, 1),
-        ],
-        axis=1,
-    )
-    wide = jnp.concatenate([w_q, wkv_mine], axis=1)
-    small = jnp.concatenate([ln_attn, ln_moe, q_gain, k_gain, router.reshape(-1)])
-    small_all = lax.all_gather(small, "row", axis=0)
-    wqkv = lax.all_gather(wide, "row", axis=0, tiled=True)
+
+    def kv_pick(weight, member):
+        head = member // sharing
+        return [
+            lax.dynamic_slice_in_dim(weight, head * HEAD, HEAD, 1),
+            lax.dynamic_slice_in_dim(weight, kv_cols + head * HEAD, HEAD, 1),
+        ]
+
+    cols = (heads + 2) * HEAD
     piece, head_piece = ln_attn.shape[0], q_gain.shape[0]
-    cuts = [0, piece, 2 * piece, 2 * piece + head_piece, 2 * piece + 2 * head_piece, small.shape[0]]
-    gain_one, gain_two, gain_q, gain_k, router_all = [
-        small_all[:, a:b].reshape(-1) for a, b in zip(cuts[:-1], cuts[1:])
-    ]
-    gain_one, gain_two = gain_one.astype(F32)[None], gain_two.astype(F32)[None]
-    gain_q, gain_k = gain_q.astype(F32)[None], gain_k.astype(F32)[None]
-    router_all = router_all.reshape(width, experts)
-
-    xs = [x_own] + [swap(x_own, d, col_count) for d in slots[1:]]
-    wg, wu, wd = after((w_gate, w_up, w_down), xs[-1])
-    wg_all, wu_all, wd_all = fetch(wg, col_count), fetch(wu, col_count), fetch(wd, col_count)
+    rest = [jnp.pad(g, (0, piece - head_piece))[:, None] for g in (q_gain, k_gain)]
+    rest = [router, ln_attn[:, None], ln_moe[:, None]] + rest
+    wide = jnp.concatenate([w_q] + kv_pick(key_value_weight, col_at) + rest, axis=1)
+    wide = jnp.pad(wide, ((0, 0), (0, -wide.shape[1] % HEAD)))
+    wide = lax.all_gather(wide, "row", axis=0, tiled=True)
+    extra = wide[:, cols:]
+    router_all = extra[:, :experts]
+    gain_one = extra[:, experts].astype(F32)[None]
+    gain_two = extra[:, experts + 1].astype(F32)[None]
+    head_gains = extra.reshape(row_count, piece, -1)[:, :head_piece].astype(F32)
+    gain_q = head_gains[:, :, experts + 2].reshape(1, HEAD)
+    gain_k = head_gains[:, :, experts + 3].reshape(1, HEAD)
+
+    xs = [v[0] for v in fetch(layer_input, col_count)]
+    out_all = lax.all_gather(after(w_out, xs[1]), "row", axis=1, tiled=True)
 
     routes_all = lax.all_gather(routes[0], "row", axis=0)
     expert_ids = jnp.arange(experts, dtype=jnp.int32)
-    flat_routes = routes_all.reshape(row_count * rows, TOPK).T
-    mask_all = jnp.any(flat_routes[:, None, :] == expert_ids[None, :, None], axis=0)
-    mine_ids = [row_at * col_count + m for m in members]
+    flat_routes = routes_all.transpose(0, 2, 1)
+    mask_all = jnp.any(flat_routes[:, :, None, :] == expert_ids[None, None, :, None], axis=1)
+    mine_ids = jnp.stack([row_at * col_count + m for m in members]).astype(jnp.int32)
     has = jnp.stack(
-        [lax.dynamic_index_in_dim(mask_all, e, 0, keepdims=False) for e in mine_ids], axis=0
-    ).reshape(col_count, row_count, rows)
+        [lax.dynamic_index_in_dim(mask_all, e, 1, keepdims=False) for e in mine_ids], axis=1
+    )
     place = jnp.arange(rows)
     before = (place[:, None] <= place[None, :]).astype(BF)
-    order = jnp.einsum("drt,tu->rdu", has.astype(BF), before, preferred_element_type=F32)
-    rank = jnp.where(has.transpose(1, 0, 2), order.astype(jnp.int32) - 1, -1)
+    order = jnp.einsum("rdt,tu->rdu", has.astype(BF), before, preferred_element_type=F32)
+    rank = jnp.where(has, order.astype(jnp.int32) - 1, -1)
     rank_t = rank.transpose(0, 2, 1)
+    mask_all = mask_all.astype(F32)
 
     inv_freq = THETA ** (-2.0 * jnp.arange(HEAD // 2, dtype=F32) / HEAD)
     coses, sines = [], []
@@ -569,38 +656,50 @@
         coses.append(jnp.concatenate([cos, cos], axis=1))
         sines.append(jnp.concatenate([-sin, sin], axis=1))
 
-    qs, kvs, normed, scales = [], [], [], []
-    for d in slots:
-        a, b, c, e = qkv(xs[d], gain_one, wqkv, coses[d], sines[d], gain_q, gain_k, heads)
-        qs.append(a)
-        kvs.append(b)
-        normed.append(c)
-        scales.append(e)
-    every = lax.all_gather(jnp.stack(kvs, axis=0), "row", axis=0)
-    out_all = lax.all_gather(after(w_out, every), "row", axis=1, tiled=True)
-    up_all = lax.all_gather(after(up_own, out_all), "row", axis=0)
+    qs, kvs, normed, scales, every = [[None] * col_count for _ in range(5)]
+    line = others + [0]
+    for d in line:
+        qs[d], kvs[d], normed[d], scales[d] = qkv(
+            xs[d], gain_one, wide, coses[d], sines[d], gain_q, gain_k, heads
+        )
+        every[d] = lax.all_gather(kvs[d], "row", axis=0)
+    wg_all = fetch(after(w_gate, xs[-1]), col_count)
     mixes, logs = [None] * col_count, [None] * col_count
     hidden = x_own.astype(F32)
-    for d in reversed(slots):
-        mixes[d], logs[d] = attend(row_word, qs[d], every, kvs[d], d, blocks)
+    for d in line:
+        mixes[d], logs[d] = attend(row_word, qs[d], every[d], kvs[d], blocks)
         share = jnp.dot(mixes[d], out_all, preferred_element_type=F32)
         hidden = hidden + (share if d == 0 else swap(share.astype(BF), d, col_count).astype(F32))
+    up_all = lax.all_gather(after(up_own, mixes[line[0]]), "row", axis=0)
 
     spread = lax.rsqrt(jnp.mean(hidden * hidden, axis=-1, keepdims=True) + EPS)
     second = (hidden * spread * gain_two).astype(BF)
     second_all = lax.all_gather(second, "row", axis=0)
-
-    def route(vectors, mask):
-        logits = lax.dot_general(
-            router_all, vectors, (((0,), (1,)), ((), ())), preferred_element_type=F32
-        )
-        probs = jax.nn.softmax(logits, axis=0)
-        picked = jnp.where(mask, probs, 0.0)
-        total = jnp.sum(picked, axis=0, keepdims=True)
-        return probs, total, picked / total
-
-    probs_all, _, gates_all = route(second_all.reshape(row_count * rows, width), mask_all)
-    sums = jnp.stack([jnp.sum(mask_all.astype(F32), axis=1), jnp.sum(probs_all, axis=1)])
+    wu, wd = after((w_up, w_down), second)
+    wu_all, wd_all = fetch(wu, col_count), fetch(wd, col_count)
+
+    expert_up = dispatch(rank, up_all, cap).reshape(col_count, row_count * cap, width)
+    router_t = router_all.T
+    expert_in, probs_all, gate_pairs = route_dispatch(
+        mine_ids, rank, second_all, mask_all, router_t, cap
+    )
+    expert_in = expert_in.reshape(col_count, row_count * cap, width)
+    gate_pairs = gate_pairs.reshape(col_count, row_count * cap, 1)
+    kv_all = lax.all_gather(after(key_value_weight, expert_in), "row", axis=0, tiled=True)
+    ys, dbs, ms, dus, dws, dgs = [], [], [], [], [], []
+    for d in slots:
+        got = expert(d, expert_in, expert_up, gate_pairs[d], wg_all[d], wu_all[d], wd_all[d])
+        for kept, value in zip((ys, dbs, ms, dus, dws, dgs), got):
+            kept.append(value)
+    cut = lambda parts: [p.reshape(row_count, cap, width) for p in parts]
+    db_sum = lax.psum_scatter(combine(rank_t, cut(dbs)), "row", scatter_dimension=0)
+
+    slot_ids = jnp.arange(cap, dtype=jnp.int32)
+    hot = rank[:, :, None, :] == slot_ids[None, None, :, None]
+    pair_scores = jnp.stack(dgs, axis=0).reshape(col_count, row_count, cap, 1).transpose(1, 0, 2, 3)
+    score_grads = jnp.sum(jnp.where(hot, pair_scores, 0.0), axis=2)
+    score_grads = lax.all_to_all(score_grads, "row", split_axis=0, concat_axis=0, tiled=True)
+    sums = jnp.stack([jnp.sum(mask_all, axis=(0, 2)), jnp.sum(probs_all, axis=(0, 2))])
     step = 1
     while step < col_count:
         sums = sums + swap(sums, step, col_count)
@@ -610,41 +709,25 @@
     aux_loss = experts * jnp.sum(load * mean_probs)
     expert_load = jnp.stack([experts * load, experts * mean_probs])
 
-    expert_in = dispatch(rank, second_all, cap)
-    expert_up = dispatch(rank, up_all, cap).reshape(col_count, row_count * cap, width)
-    gates_mine = jnp.stack(
-        [lax.dynamic_index_in_dim(gates_all, e, 0, keepdims=False) for e in mine_ids], axis=0
-    ).reshape(col_count, row_count, rows)
-    slot_ids = jnp.arange(cap, dtype=jnp.int32)
-    hot = rank.transpose(1, 0, 2)[:, :, None, :] == slot_ids[None, None, :, None]
-    gate_pairs = jnp.sum(jnp.where(hot, gates_mine[:, :, None, :], 0.0), axis=-1)
-    gate_pairs = gate_pairs.reshape(col_count, row_count * cap, 1)
-    expert_in = expert_in.reshape(col_count, row_count * cap, width)
-    ys, dbs, ms, dus, dws, dgs = [], [], [], [], [], []
-    for d in slots:
-        got = expert(d, expert_in, expert_up, gate_pairs[d], wg_all[d], wu_all[d], wd_all[d])
-        for kept, value in zip((ys, dbs, ms, dus, dws, dgs), got):
-            kept.append(value)
-    cut = lambda parts: [p.reshape(row_count, cap, width) for p in parts]
-    db_sum = lax.psum_scatter(combine(rank_t, cut(dbs)), "row", scatter_dimension=0)
-    pair_scores = jnp.stack(dgs, axis=0).reshape(col_count, row_count, cap, 1)
-    score_grads = jnp.sum(jnp.where(hot, pair_scores, 0.0), axis=2)
-    score_grads = lax.all_to_all(
-        score_grads.transpose(1, 0, 2), "row", split_axis=0, concat_axis=0, tiled=True
-    )
-    y_sum = lax.psum_scatter(
-        after(combine(rank_t, cut(ys)), db_sum), "row", scatter_dimension=0
-    )
+    grad_parts = [
+        [dot_tn(ms[d], expert_up[d]) for d in slots],
+        [dot_tn(expert_in[d], dus[d]) for d in slots],
+        [dot_tn(expert_in[d], dws[d]) for d in slots],
+    ]
+    y_part = combine(rank_t, cut(ys))
+    db_sum, grad_parts, y_part = lax.optimization_barrier((db_sum, grad_parts, y_part))
+    grad_down, grad_gate, grad_up = [deliver(parts, col_count) for parts in grad_parts]
+    y_sum = lax.psum_scatter(y_part, "row", scatter_dimension=0)
     layer_output = (hidden + y_sum.astype(F32)).astype(BF)
 
-    grad_down = deliver(
-        [dot_tn(ms[d], expert_up[d]) for d in slots], col_count
-    )
-    grad_gate = deliver([dot_tn(expert_in[d], dus[d]) for d in slots], col_count)
-    grad_up = deliver([dot_tn(expert_in[d], dws[d]) for d in slots], col_count)
-
     mask_own = jnp.any(routes[0].T[:, None, :] == expert_ids[None, :, None], axis=0)
-    probs, total, gates = route(second, mask_own)
+    logits = lax.dot_general(
+        router_all, second, (((0,), (1,)), ((), ())), preferred_element_type=F32
+    )
+    probs = jax.nn.softmax(logits, axis=0)
+    picked = jnp.where(mask_own, probs, 0.0)
+    total = jnp.sum(picked, axis=0, keepdims=True)
+    gates = picked / total
     to_member = jnp.stack(members)[:, None] == jnp.arange(col_count)[None, :]
     gate_grad = jnp.sum(
         jnp.where(to_member[None, :, :, None], score_grads[:, :, None, :], 0.0), axis=1
@@ -661,104 +744,98 @@
     second_grad = db_sum.astype(F32) + lax.dot_general(
         logit_low, router_all, (((0,), (1,)), ((), ())), preferred_element_type=F32
     )
-
-    def norm_back(grad, hat, spread, gain):
-        scaled = grad * gain
-        return spread * (scaled - hat * jnp.mean(scaled * hat, axis=-1, keepdims=True))
-
     hat = hidden * spread
     gain_two_grad = jnp.sum(second_grad * hat, axis=0)
     hidden_grad = up_own.astype(F32) + norm_back(second_grad, hat, spread, gain_two)
     branch = hidden_grad.astype(BF)
-    early = jnp.concatenate(
-        [grad_router.reshape(devices, -1), gain_two_grad.reshape(devices, -1)], axis=1
-    )
-    early = lax.psum_scatter(early, ("row", "col"), scatter_dimension=0)
-
-    branches = [branch] + [swap(branch, d, col_count) for d in slots[1:]]
-    grad_qs, grad_prompts, grad_locals, gain_q_grad = [], [], [], 0.0
+
+    branches = [v[0] for v in fetch(branch[None], col_count)]
+    grad_qs, grad_kvs, kv_moved = [], [], []
+    gain_q_grad, gain_k_grad, gain_one_grad, input_sum = 0.0, 0.0, 0.0, 0.0
+
+    def back_turn(v, cos, sin):
+        moved = v * sin
+        half = HEAD // 2
+        return v * cos + jnp.concatenate([moved[:, half:], moved[:, :half]], axis=1)
+
     for d in slots:
         mix_grad = dot_nt(branches[d], out_all).astype(BF)
-        a, b, c, e = attend_back(
-            row_word, qs[d], every, kvs[d], d, blocks, mix_grad, mixes[d], logs[d], scales[d],
+        grad_q, grad_prompt, pair, gain_part = attend_back(
+            row_word, qs[d], every[d], kvs[d], blocks, mix_grad, mixes[d], logs[d], scales[d],
             coses[d], sines[d], gain_q,
         )
-        grad_qs.append(a)
-        grad_prompts.append(b)
-        grad_locals.append(c)
-        gain_q_grad = gain_q_grad + e[0]
-    prompt = lax.psum_scatter(
-        jnp.stack(grad_prompts, axis=0), "row", scatter_dimension=2, tiled=True
-    )
-    chunk = prompt.shape[2]
-    prompt = jnp.concatenate(
-        [
-            lax.ppermute(prompt, "row", [(rows // chunk * i + a, i) for i in range(blocks)])
-            for a in range(rows // chunk)
-        ],
-        axis=2,
-    )
-    pair = jnp.stack(grad_locals, axis=0) + prompt.astype(F32)
-    cos, sin = jnp.stack(coses), jnp.stack(sines)
-
-    def back_turn(v):
-        moved = v * sin
-        half = HEAD // 2
-        return v * cos + jnp.concatenate([moved[..., half:], moved[..., :half]], axis=-1)
-
-    key_dy = back_turn(pair[:, 0])
-    key_hat = back_turn(jnp.stack([kv[0] for kv in kvs]).astype(F32)) / gain_k
-    gain_k_grad = jnp.sum(key_dy * key_hat, axis=(0, 1))
-    key_spread = jnp.stack([s[:, heads : heads + 1] for s in scales])
-    key_raw = norm_back(key_dy, key_hat, key_spread, gain_k)
-    all_grads = jnp.concatenate(
-        [jnp.stack(grad_qs, axis=0), key_raw.astype(BF), pair[:, 1].astype(BF)], axis=2
-    )
-    input_sum = None
-    for d in reversed(slots):
-        share = dot_nt(all_grads[d], wqkv)
-        share = share if d == 0 else swap(share.astype(BF), d, col_count).astype(F32)
-        input_sum = share if input_sum is None else input_sum + share
-    grad_wide = lax.dot_general(
-        jnp.stack(normed, axis=0), all_grads, (((0, 1), (0, 1)), ((), ())), preferred_element_type=F32
-    )
-    grad_wide = lax.psum_scatter(grad_wide.astype(BF), "row", scatter_dimension=0, tiled=True)
-    grad_out = lax.dot_general(
-        jnp.stack(mixes, axis=0),
-        jnp.stack(branches, axis=0),
-        (((0, 1), (0, 1)), ((), ())),
-        preferred_element_type=F32,
-    )
+        grad_qs.append(grad_q)
+        gain_q_grad = gain_q_grad + gain_part[0]
+        prompt = lax.psum_scatter(grad_prompt, "row", scatter_dimension=1, tiled=True)
+        share, sums_one = input_share(grad_q, wide, normed[d], F32 if d == 0 else BF)
+        gain_one_grad = gain_one_grad + sums_one[0]
+        input_sum = input_sum + (share if d == 0 else swap(share, d, col_count).astype(F32))
+        chunk = prompt.shape[1]
+        prompt = jnp.concatenate(
+            [
+                lax.ppermute(prompt, "row", [(rows // chunk * i + a, i) for i in range(blocks)])
+                for a in range(rows // chunk)
+            ],
+            axis=1,
+        )
+        pair = pair + prompt.astype(F32)
+        key_dy = back_turn(pair[0], coses[d], sines[d])
+        key_hat = back_turn(kvs[d][0].astype(F32), coses[d], sines[d]) / gain_k
+        gain_k_grad = gain_k_grad + jnp.sum(key_dy * key_hat, axis=0)
+        key_raw = norm_back(key_dy, key_hat, scales[d][:, heads : heads + 1], gain_k)
+        grad_kv = jnp.concatenate([key_raw.astype(BF), pair[1].astype(BF)], axis=1)
+        grad_kvs.append(grad_kv)
+        kv_moved.append(grad_kv if d == 0 else swap(grad_kv, d, col_count))
+    normed_all = jnp.stack(normed, axis=0)
+    over_tokens = lambda a, b: lax.dot_general(
+        a, b, (((0, 1), (0, 1)), ((), ())), preferred_element_type=F32
+    )
+    grad_q = over_tokens(normed_all, jnp.stack(grad_qs, axis=0))
+    grad_q = lax.psum_scatter(grad_q.astype(BF), "row", scatter_dimension=0, tiled=True)
+    grad_out = over_tokens(jnp.stack(mixes, axis=0), jnp.stack(branches, axis=0))
     grad_out = lax.psum_scatter(grad_out.astype(BF), "row", scatter_dimension=1, tiled=True)
+
+    kv_weight = jnp.concatenate([w for m in members for w in kv_pick(kv_all, m)], axis=1)
+    kv_share = dot_nt(jnp.concatenate(kv_moved, axis=1), kv_weight)
+    input_sum = input_sum + kv_share
     x_wide = x_own.astype(F32)
     x_spread = lax.rsqrt(jnp.mean(x_wide * x_wide, axis=-1, keepdims=True) + EPS)
     x_hat = x_wide * x_spread
-    gain_one_grad = jnp.sum(input_sum * x_hat, axis=0)
+    gain_one_grad = gain_one_grad / gain_one[0] + jnp.sum(kv_share * x_hat, axis=0)
     input_grad = hidden_grad + norm_back(input_sum, x_hat, x_spread, gain_one)
 
-    late = jnp.concatenate(
-        [v.reshape(devices, -1) for v in (gain_one_grad, gain_q_grad, gain_k_grad)], axis=1
-    )
-    late = lax.psum_scatter(late, ("row", "col"), scatter_dimension=0)
-    per_one, per_q = gain_one_grad.size // devices, gain_q_grad.size // devices
-
-    grad_kv = grad_wide[:, heads * HEAD :].astype(F32).reshape(col_count, -1, 2 * HEAD)
-    grad_kv = lax.all_to_all(grad_kv, "col", split_axis=0, concat_axis=0, tiled=True)
+    grad_kv = over_tokens(normed_all, jnp.stack(grad_kvs, axis=0)).astype(BF)
+    grad_kv = lax.all_to_all(
+        grad_kv.reshape(devices, -1, 2 * HEAD), ("row", "col"), split_axis=0, concat_axis=0, tiled=True
+    )
+    grad_kv = jnp.sum(grad_kv.astype(F32).reshape(row_count, col_count, -1, 2 * HEAD), axis=0)
     grad_kv = grad_kv.reshape(KEY_VALUE_HEADS, sharing, -1, 2, HEAD).sum(axis=1)
     grad_kv = grad_kv.transpose(1, 2, 0, 3).reshape(-1, 2 * kv_cols)
+    tail = [grad_router, gain_two_grad, gain_one_grad, gain_q_grad, gain_k_grad]
+    tail = [v.reshape(devices, -1) for v in tail]
+    cuts = [0]
+    for v in tail:
+        cuts.append(cuts[-1] + v.shape[1])
+    tail = lax.all_to_all(
+        jnp.concatenate(tail, axis=1), ("row", "col"), split_axis=0, concat_axis=0, tiled=True
+    )
+    tail = jnp.sum(tail, axis=0)
+    grad_router, gain_two_grad, gain_one_grad, gain_q_grad, gain_k_grad = [
+        tail[a:b] for a, b in zip(cuts[:-1], cuts[1:])
+    ]
 
     return (
         layer_output[None],
         aux_loss,
         input_grad[None],
-        grad_wide[:, : heads * HEAD].astype(F32),
+        grad_q.astype(F32),
         grad_kv,
         grad_out.astype(F32),
-        early[: -(width // devices)].reshape(width // devices, experts),
-        late[:per_one],
-        early[-(width // devices) :],
-        late[per_one : per_one + per_q],
-        late[per_one + per_q :],
+        grad_router.reshape(width // devices, experts),
+        gain_one_grad,
+        gain_two_grad,
+        gain_q_grad,
+        gain_k_grad,
         grad_gate[None],
         grad_up[None],
         grad_down[None],

time: 1910 us -> 1870 us (0.979)
  blocking collectives: 166 us -> 33.1 us
  starting transfers between devices: 93.9 us -> 155 us
  Pallas kernels: 338 us -> 377 us
  waiting for transfers between devices: 914 us -> 885 us
  local copies, waits for them, and re-layouts: 96.6 us -> 116 us
    unnamed x1 -> x0, blocking collectives: 103 us -> none
    reduce_scatter x3 -> x6, waiting for transfers between devices: 0.02 us -> 78.4 us  [the longest x1 78.3 us: per_device(): y_sum = lax.psum_scatter(y_part, 'row', scatter_dimension=0)]
    all_gather x4 -> x8, waiting for transfers between devices: 185 us -> 108 us  [the longest x1 53.6 us: per_device(): wide = lax.all_gather(wide, 'row', axis=0, tiled=True)]
    ppermute x2 -> x8, waiting for transfers between devices: 0.01 us -> 77.1 us  [per_device(): lax.ppermute(prompt, 'row', [(rows // chunk * i + a, i) for i in range(bl...]
    reduce_scatter x1, waiting for transfers between devices: 146 us -> 71 us  [per_device(): lax.psum_scatter(combine(rank_t, cut(dbs)), 'row', scatter_dimension=0)]
    pallas_call x0 -> x5, Pallas kernels: none -> 49.4 us  [the longest x4 27.4 us: input_share(): call(share_body, 'input_share', (rows // tile,), [pl.BlockSpec((tile, col...]
    all_to_all x2 -> x3, starting transfers between devices: 50 us -> 89.4 us  [the longest x1 46.8 us: per_device(): lax.all_to_all(jnp.concatenate(tail, axis=1), ('row', 'col'), split_axis=...]
    unnamed x14 -> x17, waiting for transfers between devices: 38.6 us -> 0.79 us
  transfers between devices with their start and end apart: 54 -> 71, of which waited for: 22 -> 33; matrix products, arithmetic and copies ran while one was open for 16% -> 20% of each run, Pallas kernels for 8% -> 11%
where the time goes in v2:
time: 1870 us; the launch traced here: 1860 us
  waiting for transfers between devices  885 us (47%)
  Pallas kernels  377 us (20%)
  matrix products  168 us (9%)
  starting transfers between devices  155 us (8%)
  local copies, waits for them, and re-layouts  116 us (6%)
  other arithmetic  110 us (6%)
  blocking collectives  33.1 us (2%)
    ppermute x43, waiting for transfers between devices, swap(): return lax.ppermute(v, 'col', [(i, i ^ step) for i in range(count)])  524 us
    pallas_call x4, Pallas kernels, expert(): call(expert_body, 'expert', (rows // tile,), [pl.BlockSpec((1, tile, widt...  119 us
    reduce_scatter x1, waiting for transfers between devices, per_device(): y_sum = lax.psum_scatter(y_part, 'row', scatter_dimension=0)  78.3 us
    ppermute x8, waiting for transfers between devices, per_device(): lax.ppermute(prompt, 'row', [(rows // chunk * i + a, i) for i in range(bl...  77.1 us
    reduce_scatter x1, waiting for transfers between devices, per_device(): lax.psum_scatter(combine(rank_t, cut(dbs)), 'row', scatter_dimension=0)  71 us
    dot_general x12, matrix products, dot_tn(): lax.dot_general(a, b, (((0,), (0,)), ((), ())), preferred_element_type=F32)  67.7 us
    pallas_call x4, Pallas kernels, attend_back(): call(partial(attend_back_body, heads, per, blocks, rows), 'attend_back',...  67.2 us
    all_gather x1, waiting for transfers between devices, per_device(): wide = lax.all_gather(wide, 'row', axis=0, tiled=True)  53.6 us
  transfers between devices with their start and end apart: 71, of which 33 were waited for; matrix products, arithmetic and copies ran while one was open for 20% of the time, Pallas kernels for 11%

profile of v2, /device:TPU:0, one launch (start us, length us, event | category | flops | bytes accessed | tf_op | source)
XLA Modules:
  0.0 1862.3 jit_solution(3001490381411389831)
XLA Ops:
  24.0 53.6 %all-gather.16.cloned.1.call-done.w_ref = bf16[2048,1408]{1,0:T(8,128)(2,1)} async-done(((bf16[256,1408]{1,0:T(8,128)(2,1)}), bf16[2048,1408]{1,0:T(8,128)(2,1)}) %all-gather.16.cloned.1.call-update) | async-done | bytes 5767184 | tf_op jit(solution)/shard_map/all_gather | solution.py:623
  84.2 8.3 qkv.4
  96.1 44.3 %collective-permute-done.2 = bf16[1,512,2048]{2,1,0:T(8,128)(2,1)S(1)} collective-permute-done((bf16[1,512,2048]{2,1,0:T(8,128)(2,1)S(1)}, bf16[1,512,2048]{2,1,0:T(8,128)(2,1)S(1)}, u32[]{:S(2)}, u32[]{:S(2)}) %collective-permute-start.2) | collective-permute-done | bytes 2097184 | tf_op jit(solution)/shard_map/ppermute | solution.py:548
  141.7 8.3 qkv.5
  157.3 19.2 %collective-permute-done.5 = bf16[1,256,2048]{2,1,0:T(8,128)(2,1)S(1)} collective-permute-done((bf16[1,256,2048]{2,1,0:T(8,128)(2,1)S(1)}, bf16[1,256,2048]{2,1,0:T(8,128)(2,1)S(1)}, u32[]{:S(2)}, u32[]{:S(2)}) %collective-permute-start.5) | collective-permute-done | bytes 1048608 | tf_op jit(solution)/shard_map/ppermute | solution.py:548
  180.6 8.2 qkv.6
  189.9 8.3 qkv.7
  198.6 9.1 attend.4
  207.8 9.1 attend.5
  217.0 9.8 all-gather.18.cloned.1.call-done
  234.4 21.2 %all-gather.26.cloned.1.call-done = bf16[16,512,128]{2,1,0:T(8,128)(2,1)} async-done(((bf16[2,512,128]{2,1,0:T(8,128)(2,1)}), bf16[16,512,128]{2,1,0:T(8,128)(2,1)}) %all-gather.26.cloned.1.call-update) | async-done | bytes 2097168 | tf_op jit(solution)/shard_map/all_gather | solution.py:665
  255.6 9.2 attend.6
  276.4 9.5 all-gather.28.cloned.1.call-done
  285.9 18.9 %attend.7 = (bf16[512,1024]{1,0:T(8,128)(2,1)}, f32[512,128]{1,0:T(8,128)}) custom-call(s32[1]{0:T(128)} %bitcast.1.row_ref, bf16[8,512,128]{2,1,0:T(8,128)(2,1)} %get-tuple-element.120.q_ref, bf16[8,2,512,128]{3,2,1,0:T(8,128)(2,1)} %bitcast.342, bf16[8,2,512,128]{3,2,1,0:T(8,128)(2,1)} %bitcast.343, bf16[2,512,128]{2,1,0:T(8,128)(2,1)} %get-tuple-element.121.kv_ref), custom_call_target="tpu_custom_call" | custom-call | flops 9663676416 | bytes 3145728 | tf_op jit(solution)/shard_map/attend/pallas_call | solution.py:189
  304.8 21.2 %collective-permute-done.3 = bf16[512,2048]{1,0:T(8,128)(2,1)} collective-permute-done((bf16[512,2048]{1,0:T(8,128)(2,1)}, bf16[512,2048]{1,0:T(8,128)(2,1)}, u32[]{:S(2)}, u32[]{:S(2)}) %collective-permute-start.3) | collective-permute-done | bytes 2097184 | tf_op jit(solution)/shard_map/ppermute | solution.py:548
  325.9 35.6 %collective-permute-done.1 = bf16[512,2048]{1,0:T(8,128)(2,1)} collective-permute-done((bf16[512,2048]{1,0:T(8,128)(2,1)}, bf16[512,2048]{1,0:T(8,128)(2,1)}, u32[]{:S(2)}, u32[]{:S(2)}) %collective-permute-start.1) | collective-permute-done | bytes 2097184 | tf_op jit(solution)/shard_map/ppermute | solution.py:548
  361.5 7.2 multiply_reduce_fusion.2
  378.0 64.4 %collective-permute-done.10.wg_ref = bf16[1,2048,768]{2,1,0:T(8,128)(2,1)S(1)} collective-permute-done((bf16[1,2048,768]{2,1,0:T(8,128)(2,1)S(1)}, bf16[1,2048,768]{2,1,0:T(8,128)(2,1)S(1)}, u32[]{:S(2)}, u32[]{:S(2)}) %collective-permute-start.10) | collective-permute-done | bytes 3145760 | tf_op jit(solution)/shard_map/ppermute | solution.py:548
  446.6 63.2 %collective-permute-done.11.wu_ref = bf16[1,2048,768]{2,1,0:T(8,128)(2,1)S(1)} collective-permute-done((bf16[1,2048,768]{2,1,0:T(8,128)(2,1)}, bf16[1,2048,768]{2,1,0:T(8,128)(2,1)S(1)}, u32[]{:S(2)}, u32[]{:S(2)}) %collective-permute-start.11) | collective-permute-done | bytes 3145760 | tf_op jit(solution)/shard_map/ppermute | solution.py:548
  514.5 62.6 %collective-permute-done.12.wd_ref = bf16[1,768,2048]{2,1,0:T(8,128)(2,1)S(1)} collective-permute-done((bf16[1,768,2048]{2,1,0:T(8,128)(2,1)}, bf16[1,768,2048]{2,1,0:T(8,128)(2,1)S(1)}, u32[]{:S(2)}, u32[]{:S(2)}) %collective-permute-start.12) | collective-permute-done | bytes 3145760 | tf_op jit(solution)/shard_map/ppermute | solution.py:548
  577.6 33.1 %all_gather.58 = s32[8,512,8]{1,2,0:T(8,128)S(1)} all-gather(s32[1,512,8]{1,2,0:T(8,128)S(1)} %copy-done.82), channel_id=1, replica_groups=mesh['row'=8,'col'=4] {'row'}, dimensions={0}, use_global_device_ids=true | all-gather | bytes 147456 | tf_op jit(solution)/shard_map/all_gather | solution.py:635
  635.6 9.8 collective-permute-done.16
  649.2 29.9 %collective-permute-done.18 = bf16[1,384,2048]{2,1,0:T(8,128)(2,1)} collective-permute-done((bf16[1,384,2048]{2,1,0:T(8,128)(2,1)}, bf16[1,384,2048]{2,1,0:T(8,128)(2,1)}, u32[]{:S(2)}, u32[]{:S(2)}) %collective-permute-start.18) | collective-permute-done | bytes 1572896 | tf_op jit(solution)/shard_map/ppermute | solution.py:548
  683.1 17.4 dispatch.1
  700.6 22.1 %route_dispatch.1 = (bf16[4,8,128,2048]{3,2,1,0:T(8,128)(2,1)}, f32[8,32,512]{2,1,0:T(8,128)}, f32[4,8,128,1]{3,2,1,0:T(8,128)}) custom-call(s32[4]{0:T(128)} %pad_add_fusion.2.ids_ref, s32[8,4,512]{2,1,0:T(4,128)} %copy.119.rank_ref, bf16[8,512,2048]{2,1,0:T(8,128)(2,1)} %bitcast.329, f32[8,32,512]{2,1,0:T(8,128)} %convert_element_type.341.mask_ref, ...), custom_call_target="tpu_custom_call" | custom-call | flops 8589934592 | bytes 33554432 | tf_op jit(solution)/shard_map/route_dispatch/pallas_call | solution.py:399
  725.5 29.6 %expert.4 = (bf16[1024,2048]{1,0:T(8,128)(2,1)}, bf16[1024,2048]{1,0:T(8,128)(2,1)}, bf16[1024,768]{1,0:T(8,128)(2,1)}, bf16[1024,768]{1,0:T(8,128)(2,1)}, bf16[1024,768]{1,0:T(8,128)(2,1)}, /*index=5*/f32[1024,1]{1,0:T(8,128)}) custom-call(bf16[4,1024,2048]{2,1,0:T(8,128)(2,1)} %bitcast.259, bf16[4,1024,2048]{2,1,0:T(8,128)(2,1)} %bitcast.246, ...), custom_call_target="tpu_custom_call" | custom-call | flops 19327352832 | bytes 30932992 | tf_op jit(solution)/shard_map/expert/pallas_call | solution.py:514
  755.2 30.1 %expert.7 = (bf16[1024,2048]{1,0:T(8,128)(2,1)}, bf16[1024,2048]{1,0:T(8,128)(2,1)}, bf16[1024,768]{1,0:T(8,128)(2,1)}, bf16[1024,768]{1,0:T(8,128)(2,1)}, bf16[1024,768]{1,0:T(8,128)(2,1)}, /*index=5*/f32[1024,1]{1,0:T(8,128)}) custom-call(bf16[4,1024,2048]{2,1,0:T(8,128)(2,1)} %bitcast.260, bf16[4,1024,2048]{2,1,0:T(8,128)(2,1)} %bitcast.247, ...), custom_call_target="tpu_custom_call" | custom-call | flops 19327352832 | bytes 30932992 | tf_op jit(solution)/shard_map/expert/pallas_call | solution.py:514
  785.3 29.7 %expert.5 = (bf16[1024,2048]{1,0:T(8,128)(2,1)}, bf16[1024,2048]{1,0:T(8,128)(2,1)}, bf16[1024,768]{1,0:T(8,128)(2,1)}, bf16[1024,768]{1,0:T(8,128)(2,1)}, bf16[1024,768]{1,0:T(8,128)(2,1)}, /*index=5*/f32[1024,1]{1,0:T(8,128)}) custom-call(bf16[4,1024,2048]{2,1,0:T(8,128)(2,1)} %bitcast.261, bf16[4,1024,2048]{2,1,0:T(8,128)(2,1)} %bitcast.248, ...), custom_call_target="tpu_custom_call" | custom-call | flops 19327352832 | bytes 30932992 | tf_op jit(solution)/shard_map/expert/pallas_call | solution.py:514
  814.9 29.8 %expert.6 = (bf16[1024,2048]{1,0:T(8,128)(2,1)}, bf16[1024,2048]{1,0:T(8,128)(2,1)}, bf16[1024,768]{1,0:T(8,128)(2,1)}, bf16[1024,768]{1,0:T(8,128)(2,1)}, bf16[1024,768]{1,0:T(8,128)(2,1)}, /*index=5*/f32[1024,1]{1,0:T(8,128)}) custom-call(bf16[4,1024,2048]{2,1,0:T(8,128)(2,1)} %bitcast.262, bf16[4,1024,2048]{2,1,0:T(8,128)(2,1)} %bitcast.249, ...), custom_call_target="tpu_custom_call" | custom-call | flops 19327352832 | bytes 30932992 | tf_op jit(solution)/shard_map/expert/pallas_call | solution.py:514
  844.8 22.3 %combine.2 = bf16[8,512,2048]{2,1,0:T(8,128)(2,1)} custom-call(s32[8,512,4]{2,1,0:T(8,128)} %bitcast.256, bf16[8,128,2048]{2,1,0:T(8,128)(2,1)} %bitcast.273, bf16[8,128,2048]{2,1,0:T(8,128)(2,1)} %bitcast.275, bf16[8,128,2048]{2,1,0:T(8,128)(2,1)} %bitcast.276, bf16[8,128,2048]{2,1,0:T(8,128)(2,1)} %bitcast.274), custom_call_target="tpu_custom_call" | custom-call | flops 8589934592 | bytes 33554432 | tf_op jit(solution)/shard_map/combine/pallas_call | solution.py:470
  867.1 12.6 fusion.112
  879.8 11.5 fusion.111
  901.4 8.6 fusion.140
  959.1 22.4 %combine.3 = bf16[8,512,2048]{2,1,0:T(8,128)(2,1)} custom-call(s32[8,512,4]{2,1,0:T(8,128)} %bitcast.257, bf16[8,128,2048]{2,1,0:T(8,128)(2,1)} %bitcast.269, bf16[8,128,2048]{2,1,0:T(8,128)(2,1)} %bitcast.271, bf16[8,128,2048]{2,1,0:T(8,128)(2,1)} %bitcast.272, bf16[8,128,2048]{2,1,0:T(8,128)(2,1)} %bitcast.270), custom_call_target="tpu_custom_call" | custom-call | flops 8589934592 | bytes 33554432 | tf_op jit(solution)/shard_map/combine/pallas_call | solution.py:470
  981.5 71.0 %reduce-scatter.9.cloned.1.call-done = bf16[1,512,2048]{2,1,0:T(8,128)(2,1)} async-done(((bf16[8,512,2048]{2,1,0:T(8,128)(2,1)}), bf16[1,512,2048]{2,1,0:T(8,128)(2,1)}) %reduce-scatter.9.cloned.1.call-update) | async-done | bytes 2097168 | tf_op jit(solution)/shard_map/reduce_scatter | solution.py:695
  1087.2 13.6 all-gather.20.cloned.1.call-done
  1129.8 12.4 collective-permute-done.47
  1145.0 44.3 %collective-permute-done.49 = bf16[384,2048]{1,0:T(8,128)(2,1)S(1)} collective-permute-done((bf16[384,2048]{1,0:T(8,128)(2,1)S(1)}, bf16[384,2048]{1,0:T(8,128)(2,1)S(1)}, u32[]{:S(2)}, u32[]{:S(2)}) %collective-permute-start.49) | collective-permute-done | bytes 1572896 | tf_op jit(solution)/shard_map/ppermute | solution.py:548
  1191.9 78.3 %reduce-scatter.11.cloned.1.call-done = bf16[1,512,2048]{2,1,0:T(8,128)(2,1)} async-done(((bf16[8,512,2048]{2,1,0:T(8,128)(2,1)}), bf16[1,512,2048]{2,1,0:T(8,128)(2,1)}) %reduce-scatter.11.cloned.1.call-update) | async-done | bytes 2097168 | tf_op jit(solution)/shard_map/reduce_scatter | solution.py:720
  1270.2 7.0 convert_bitcast_fusion
  1283.5 16.8 attend_back.4
  1300.4 22.2 %collective-permute-done.23 = bf16[1,512,2048]{2,1,0:T(8,128)(2,1)S(1)} collective-permute-done((bf16[1,512,2048]{2,1,0:T(8,128)(2,1)}, bf16[1,512,2048]{2,1,0:T(8,128)(2,1)S(1)}, u32[]{:S(2)}, u32[]{:S(2)}) %collective-permute-start.23) | collective-permute-done | bytes 2097184 | tf_op jit(solution)/shard_map/ppermute | solution.py:548
  1334.6 16.8 attend_back.6
  1357.9 16.9 attend_back.5
  1381.1 16.7 attend_back.7
  1410.3 13.4 bitcast_convert_fusion
  1448.7 22.3 %collective-permute-done.48 = bf16[768,2048]{1,0:T(8,128)(2,1)} collective-permute-done((bf16[768,2048]{1,0:T(8,128)(2,1)}, bf16[768,2048]{1,0:T(8,128)(2,1)}, u32[]{:S(2)}, u32[]{:S(2)}) %collective-permute-start.48) | collective-permute-done | bytes 3145760 | tf_op jit(solution)/shard_map/ppermute | solution.py:548
  1470.9 7.2 add_bitcast_fusion
  1478.1 28.8 %collective-permute-done.46 = bf16[2048,768]{1,0:T(8,128)(2,1)} collective-permute-done((bf16[2048,768]{1,0:T(8,128)(2,1)}, bf16[2048,768]{1,0:T(8,128)(2,1)}, u32[]{:S(2)}, u32[]{:S(2)}) %collective-permute-start.46) | collective-permute-done | bytes 3145760 | tf_op jit(solution)/shard_map/ppermute | solution.py:548
  1507.0 31.4 %collective-permute-done.44 = bf16[2048,768]{1,0:T(8,128)(2,1)} collective-permute-done((bf16[2048,768]{1,0:T(8,128)(2,1)}, bf16[2048,768]{1,0:T(8,128)(2,1)}, u32[]{:S(2)}, u32[]{:S(2)}) %collective-permute-start.44) | collective-permute-done | bytes 3145760 | tf_op jit(solution)/shard_map/ppermute | solution.py:548
  1538.3 7.0 add_bitcast_fusion.1
  1545.3 7.1 input_share.4
  1562.7 6.8 input_share.6
  1574.5 6.8 input_share.7
  1585.8 15.1 bitcast_convert_fusion.1
  1602.7 19.6 %collective-permute-done.34 = bf16[2,256,128]{2,1,0:T(8,128)(2,1)S(1)} collective-permute-done((bf16[2,256,128]{2,1,0:T(8,128)(2,1)}, bf16[2,256,128]{2,1,0:T(8,128)(2,1)S(1)}, u32[]{:S(2)}, u32[]{:S(2)}) %collective-permute-start.34) | collective-permute-done | bytes 131104 | tf_op jit(solution)/shard_map/ppermute | solution.py:776
  1627.0 34.9 %collective-permute-done.31 = bf16[2,256,128]{2,1,0:T(8,128)(2,1)S(1)} collective-permute-done((bf16[2,256,128]{2,1,0:T(8,128)(2,1)}, bf16[2,256,128]{2,1,0:T(8,128)(2,1)S(1)}, u32[]{:S(2)}, u32[]{:S(2)}) %collective-permute-start.31) | collective-permute-done | bytes 131104 | tf_op jit(solution)/shard_map/ppermute | solution.py:776
  1665.7 21.1 %collective-permute-done.37 = bf16[2,256,128]{2,1,0:T(8,128)(2,1)S(1)} collective-permute-done((bf16[2,256,128]{2,1,0:T(8,128)(2,1)}, bf16[2,256,128]{2,1,0:T(8,128)(2,1)S(1)}, u32[]{:S(2)}, u32[]{:S(2)}) %collective-permute-start.37) | collective-permute-done | bytes 131104 | tf_op jit(solution)/shard_map/ppermute | solution.py:776
  1706.9 12.5 fusion.18
  1720.6 46.8 %all-to-all-start.2 = ((f32[32,1,2184]{2,1,0:T(1,128)}), f32[32,1,2184]{2,1,0:T(1,128)S(1)}, u32[]{:S(2)}, u32[]{:S(2)}) async-start(f32[32,1,2184]{2,1,0:T(1,128)} %copy.131), calls=%async_computation.10 | async-start | bytes 589824 | tf_op jit(solution)/shard_map/all_to_all | solution.py:819
  1773.2 10.0 all-to-all-done.2
  1783.3 39.2 %all-to-all-start.1 = ((bf16[32,64,256]{2,1,0:T(8,128)(2,1)}), bf16[32,64,256]{2,1,0:T(8,128)(2,1)S(1)}, u32[]{:S(2)}, u32[]{:S(2)}) async-start(bf16[32,64,256]{2,1,0:T(8,128)(2,1)} %bitcast.96), calls=%async_computation.8 | async-start | bytes 2097152 | tf_op jit(solution)/shard_map/all_to_all | solution.py:808
  1822.6 8.8 add_bitcast_fusion.2
  1837.5 11.4 all-to-all-done.1
  (599 shorter events, 378.3 us)
Async XLA Ops:
  7.2 70.4 %all-gather.16.cloned.1.call-start = ((), (), s32[]{:S(2)}) async-start(), calls=%async_computation.11 | async-start | bytes 6488064 | tf_op jit(solution)/shard_map/all_gather | solution.py:623
  14.4 184.2 %all-gather.22.cloned.1.call-start = ((), (), s32[]{:S(2)}) async-start(), calls=%async_computation.22 | async-start | bytes 2359296 | tf_op jit(solution)/shard_map/all_gather | solution.py:665
  14.4 69.7 %collective-permute-start = (bf16[1,512,2048]{2,1,0:T(8,128)(2,1)S(1)}, bf16[1,512,2048]{2,1,0:T(8,128)(2,1)}, u32[]{:S(2)}, u32[]{:S(2)}) collective-permute-start(bf16[1,512,2048]{2,1,0:T(8,128)(2,1)S(1)} %copy-done.32), channel_id=1, source_target_pairs={{0,1},{1,0},{2,3},{3,2},{4,5},{5,4},{6,7},{7,6},{8,9},{9,8},{10,11... | collective-permute-start | bytes 6291464 | tf_op jit(solution)/shard_map/ppermute | solution.py:548
  92.5 115.3 %all-gather.24.cloned.1.call-start = ((), (), s32[]{:S(2)}) async-start(), calls=%async_computation.23 | async-start | bytes 2359296 | tf_op jit(solution)/shard_map/all_gather | solution.py:665
  92.5 47.8 %collective-permute-start.2 = (bf16[1,512,2048]{2,1,0:T(8,128)(2,1)S(1)}, bf16[1,512,2048]{2,1,0:T(8,128)(2,1)S(1)}, u32[]{:S(2)}, u32[]{:S(2)}) collective-permute-start(bf16[1,512,2048]{2,1,0:T(8,128)(2,1)S(1)} %copy-done.32), channel_id=1, source_target_pairs={{0,2},{1,3},{2,0},{3,1},{4,6},{5,7},{6,4},{7,5},{8,10},{9,11},{10,... | collective-permute-start | bytes 6291464 | tf_op jit(solution)/shard_map/ppermute | solution.py:548
  150.0 76.7 %all-gather.18.cloned.1.call-start = ((), (), s32[]{:S(2)}) async-start(), calls=%async_computation.12 | async-start | bytes 4718592 | tf_op jit(solution)/shard_map/all_gather | solution.py:633
  150.6 105.0 %all-gather.26.cloned.1.call-start = ((), (), s32[]{:S(2)}) async-start(), calls=%async_computation.24 | async-start | bytes 2359296 | tf_op jit(solution)/shard_map/all_gather | solution.py:665
  151.9 24.6 %collective-permute-start.5 = (bf16[1,256,2048]{2,1,0:T(8,128)(2,1)S(1)}, bf16[1,256,2048]{2,1,0:T(8,128)(2,1)S(1)}, u32[]{:S(2)}, u32[]{:S(2)}) collective-permute-start(bf16[1,256,2048]{2,1,0:T(8,128)(2,1)S(1)} %slice.405), channel_id=1, source_target_pairs={{0,1},{1,0},{2,3},{3,2},{4,5},{5,4},{6,7},{7,6},{8,9},{9,8},{10,11... | collective-permute-start | bytes 3145736 | tf_op jit(solution)/shard_map/ppermute | solution.py:548
  154.8 24.3 %collective-permute-start.4 = (bf16[1,256,2048]{2,1,0:T(8,128)(2,1)S(1)}, bf16[1,256,2048]{2,1,0:T(8,128)(2,1)S(1)}, u32[]{:S(2)}, u32[]{:S(2)}) collective-permute-start(bf16[1,256,2048]{2,1,0:T(8,128)(2,1)S(1)} %slice.404), channel_id=1, source_target_pairs={{0,2},{1,3},{2,0},{3,1},{4,6},{5,7},{6,4},{7,5},{8,10},{9,11},{10,... | collective-permute-start | bytes 3145736 | tf_op jit(solution)/shard_map/ppermute | solution.py:548
  188.9 97.0 %all-gather.28.cloned.1.call-start = ((), (), s32[]{:S(2)}) async-start(), calls=%async_computation.25 | async-start | bytes 2359296 | tf_op jit(solution)/shard_map/all_gather | solution.py:665
  198.2 484.9 %all-gather.32.cloned.1.call-start = ((), (), s32[]{:S(2)}) async-start(), calls=%async_computation.27 | async-start | bytes 18874368 | tf_op jit(solution)/shard_map/all_gather | solution.py:673
  207.7 492.9 %all-gather.30.cloned.1.call-start = ((), (), s32[]{:S(2)}) async-start(), calls=%async_computation.26 | async-start | bytes 18874368 | tf_op jit(solution)/shard_map/all_gather | solution.py:677
  232.9 93.1 %collective-permute-start.3 = (bf16[512,2048]{1,0:T(8,128)(2,1)}, bf16[512,2048]{1,0:T(8,128)(2,1)}, u32[]{:S(2)}, u32[]{:S(2)}) collective-permute-start(bf16[512,2048]{1,0:T(8,128)(2,1)} %convolution_convert_fusion.1), channel_id=1, source_target_pairs={{0,2},{1,3},{2,0},{3,1},{4,6},{5,7},{6,4},{7,5},{8,10},{9,11},{10,... | collective-permute-start | bytes 6291464 | tf_op jit(solution)/shard_map/ppermute | solution.py:548
  269.7 56.2 %collective-permute-start.6 = (bf16[512,2048]{1,0:T(8,128)(2,1)}, bf16[512,2048]{1,0:T(8,128)(2,1)}, u32[]{:S(2)}, u32[]{:S(2)}) collective-permute-start(bf16[512,2048]{1,0:T(8,128)(2,1)} %convolution_convert_fusion), channel_id=1, source_target_pairs={{0,3},{1,2},{2,1},{3,0},{4,7},{5,6},{6,5},{7,4},{8,11},{9,10},{10,... | collective-permute-start | bytes 6291464 | tf_op jit(solution)/shard_map/ppermute | solution.py:548
  275.7 85.8 %collective-permute-start.1 = (bf16[512,2048]{1,0:T(8,128)(2,1)}, bf16[512,2048]{1,0:T(8,128)(2,1)}, u32[]{:S(2)}, u32[]{:S(2)}) collective-permute-start(bf16[512,2048]{1,0:T(8,128)(2,1)} %convolution_convert_fusion.2), channel_id=1, source_target_pairs={{0,1},{1,0},{2,3},{3,2},{4,5},{5,4},{6,7},{7,6},{8,9},{9,8},{10,11... | collective-permute-start | bytes 6291464 | tf_op jit(solution)/shard_map/ppermute | solution.py:548
  372.5 680.0 %reduce-scatter.9.cloned.1.call-start = ((), (), s32[]{:S(2)}) async-start(), calls=%async_computation.13 | async-start | bytes 18874368 | tf_op jit(solution)/shard_map/reduce_scatter | solution.py:695
  373.4 68.9 %collective-permute-start.10 = (bf16[1,2048,768]{2,1,0:T(8,128)(2,1)S(1)}, bf16[1,2048,768]{2,1,0:T(8,128)(2,1)S(1)}, u32[]{:S(2)}, u32[]{:S(2)}) collective-permute-start(bf16[1,2048,768]{2,1,0:T(8,128)(2,1)S(1)} %copy-done.109), channel_id=1, source_target_pairs={{0,2},{1,3},{2,0},{3,1},{4,6},{5,7},{6,4},{7,5},{8,10},{9,11},{10,... | collective-permute-start | bytes 9437192 | tf_op jit(solution)/shard_map/ppermute | solution.py:548
  373.9 70.1 %collective-permute-start.7 = (bf16[1,2048,768]{2,1,0:T(8,128)(2,1)S(1)}, bf16[1,2048,768]{2,1,0:T(8,128)(2,1)S(1)}, u32[]{:S(2)}, u32[]{:S(2)}) collective-permute-start(bf16[1,2048,768]{2,1,0:T(8,128)(2,1)S(1)} %copy-done.109), channel_id=1, source_target_pairs={{0,1},{1,0},{2,3},{3,2},{4,5},{5,4},{6,7},{7,6},{8,9},{9,8},{10,11... | collective-permute-start | bytes 9437192 | tf_op jit(solution)/shard_map/ppermute | solution.py:548
  375.4 134.3 %collective-permute-start.11 = (bf16[1,2048,768]{2,1,0:T(8,128)(2,1)}, bf16[1,2048,768]{2,1,0:T(8,128)(2,1)S(1)}, u32[]{:S(2)}, u32[]{:S(2)}) collective-permute-start(bf16[1,2048,768]{2,1,0:T(8,128)(2,1)} %wu_ref), channel_id=1, source_target_pairs={{0,2},{1,3},{2,0},{3,1},{4,6},{5,7},{6,4},{7,5},{8,10},{9,11},{10,... | collective-permute-start | bytes 9437192 | tf_op jit(solution)/shard_map/ppermute | solution.py:548
  376.8 135.0 %collective-permute-start.8 = (bf16[1,2048,768]{2,1,0:T(8,128)(2,1)}, bf16[1,2048,768]{2,1,0:T(8,128)(2,1)S(1)}, u32[]{:S(2)}, u32[]{:S(2)}) collective-permute-start(bf16[1,2048,768]{2,1,0:T(8,128)(2,1)} %wu_ref), channel_id=1, source_target_pairs={{0,1},{1,0},{2,3},{3,2},{4,5},{5,4},{6,7},{7,6},{8,9},{9,8},{10,11... | collective-permute-start | bytes 9437192 | tf_op jit(solution)/shard_map/ppermute | solution.py:548
  377.5 199.7 %collective-permute-start.12 = (bf16[1,768,2048]{2,1,0:T(8,128)(2,1)}, bf16[1,768,2048]{2,1,0:T(8,128)(2,1)S(1)}, u32[]{:S(2)}, u32[]{:S(2)}) collective-permute-start(bf16[1,768,2048]{2,1,0:T(8,128)(2,1)} %wd_ref), channel_id=1, source_target_pairs={{0,2},{1,3},{2,0},{3,1},{4,6},{5,7},{6,4},{7,5},{8,10},{9,11},{10,... | collective-permute-start | bytes 9437192 | tf_op jit(solution)/shard_map/ppermute | solution.py:548
  442.3 169.7 %collective-permute-start.9 = (bf16[1,768,2048]{2,1,0:T(8,128)(2,1)}, bf16[1,768,2048]{2,1,0:T(8,128)(2,1)S(1)}, u32[]{:S(2)}, u32[]{:S(2)}) collective-permute-start(bf16[1,768,2048]{2,1,0:T(8,128)(2,1)} %wd_ref), channel_id=1, source_target_pairs={{0,1},{1,0},{2,3},{3,2},{4,5},{5,4},{6,7},{7,6},{8,9},{9,8},{10,11... | collective-permute-start | bytes 9437192 | tf_op jit(solution)/shard_map/ppermute | solution.py:548
  444.0 170.8 %collective-permute-start.14 = (bf16[1,1024,768]{2,1,0:T(8,128)(2,1)S(1)}, bf16[1,1024,768]{2,1,0:T(8,128)(2,1)S(1)}, u32[]{:S(2)}, u32[]{:S(2)}) collective-permute-start(bf16[1,1024,768]{2,1,0:T(8,128)(2,1)S(1)} %slice.409), channel_id=1, source_target_pairs={{0,1},{1,0},{2,3},{3,2},{4,5},{5,4},{6,7},{7,6},{8,9},{9,8},{10,11... | collective-permute-start | bytes 4718600 | tf_op jit(solution)/shard_map/ppermute | solution.py:548
  509.8 120.2 %collective-permute-start.13 = (bf16[1,1024,768]{2,1,0:T(8,128)(2,1)}, bf16[1,1024,768]{2,1,0:T(8,128)(2,1)}, u32[]{:S(2)}, u32[]{:S(2)}) collective-permute-start(bf16[1,1024,768]{2,1,0:T(8,128)(2,1)} %slice.408), channel_id=1, source_target_pairs={{0,2},{1,3},{2,0},{3,1},{4,6},{5,7},{6,4},{7,5},{8,10},{9,11},{10,... | collective-permute-start | bytes 4718600 | tf_op jit(solution)/shard_map/ppermute | solution.py:548
  511.8 133.6 %collective-permute-start.16 = (bf16[1,1024,768]{2,1,0:T(8,128)(2,1)}, bf16[1,1024,768]{2,1,0:T(8,128)(2,1)}, u32[]{:S(2)}, u32[]{:S(2)}) collective-permute-start(bf16[1,1024,768]{2,1,0:T(8,128)(2,1)} %slice.411), channel_id=1, source_target_pairs={{0,1},{1,0},{2,3},{3,2},{4,5},{5,4},{6,7},{7,6},{8,9},{9,8},{10,11... | collective-permute-start | bytes 4718600 | tf_op jit(solution)/shard_map/ppermute | solution.py:548
  577.2 68.2 %collective-permute-start.15 = (bf16[1,1024,768]{2,1,0:T(8,128)(2,1)}, bf16[1,1024,768]{2,1,0:T(8,128)(2,1)}, u32[]{:S(2)}, u32[]{:S(2)}) collective-permute-start(bf16[1,1024,768]{2,1,0:T(8,128)(2,1)} %slice.410), channel_id=1, source_target_pairs={{0,2},{1,3},{2,0},{3,1},{4,6},{5,7},{6,4},{7,5},{8,10},{9,11},{10,... | collective-permute-start | bytes 4718600 | tf_op jit(solution)/shard_map/ppermute | solution.py:548
  612.0 67.1 %collective-permute-start.18 = (bf16[1,384,2048]{2,1,0:T(8,128)(2,1)}, bf16[1,384,2048]{2,1,0:T(8,128)(2,1)}, u32[]{:S(2)}, u32[]{:S(2)}) collective-permute-start(bf16[1,384,2048]{2,1,0:T(8,128)(2,1)} %slice.413), channel_id=1, source_target_pairs={{0,1},{1,0},{2,3},{3,2},{4,5},{5,4},{6,7},{7,6},{8,9},{9,8},{10,11... | collective-permute-start | bytes 4718600 | tf_op jit(solution)/shard_map/ppermute | solution.py:548
  614.8 64.3 %collective-permute-start.17 = (bf16[1,384,2048]{2,1,0:T(8,128)(2,1)}, bf16[1,384,2048]{2,1,0:T(8,128)(2,1)}, u32[]{:S(2)}, u32[]{:S(2)}) collective-permute-start(bf16[1,384,2048]{2,1,0:T(8,128)(2,1)} %slice.412), channel_id=1, source_target_pairs={{0,2},{1,3},{2,0},{3,1},{4,6},{5,7},{6,4},{7,5},{8,10},{9,11},{10,... | collective-permute-start | bytes 4718600 | tf_op jit(solution)/shard_map/ppermute | solution.py:548
  867.1 233.8 %all-gather.20.cloned.1.call-start = ((), (), s32[]{:S(2)}) async-start(), calls=%async_computation.19 | async-start | bytes 4718592 | tf_op jit(solution)/shard_map/all_gather | solution.py:688
  901.3 368.9 %reduce-scatter.11.cloned.1.call-start = ((), (), s32[]{:S(2)}) async-start(), calls=%async_computation.14 | async-start | bytes 18874368 | tf_op jit(solution)/shard_map/reduce_scatter | solution.py:720
  1077.3 482.6 %reduce-scatter.13.cloned.1.call-start = ((), (), s32[]{:S(2)}) async-start(), calls=%async_computation.15 | async-start | bytes 1179648 | tf_op jit(solution)/shard_map/reduce_scatter | solution.py:769
  1105.0 37.3 %collective-permute-start.47 = (bf16[384,2048]{1,0:T(8,128)(2,1)S(1)}, bf16[384,2048]{1,0:T(8,128)(2,1)S(1)}, u32[]{:S(2)}, u32[]{:S(2)}) collective-permute-start(bf16[384,2048]{1,0:T(8,128)(2,1)S(1)} %get-tuple-element.305), channel_id=1, source_target_pairs={{0,2},{1,3},{2,0},{3,1},{4,6},{5,7},{6,4},{7,5},{8,10},{9,11},{10,... | collective-permute-start | bytes 4718600 | tf_op jit(solution)/shard_map/ppermute | solution.py:548
  1118.5 310.7 %collective-permute-start.39 = (bf16[1024,768]{1,0:T(8,128)(2,1)}, bf16[1024,768]{1,0:T(8,128)(2,1)}, u32[]{:S(2)}, u32[]{:S(2)}) collective-permute-start(bf16[1024,768]{1,0:T(8,128)(2,1)} %get-tuple-element.309), channel_id=1, source_target_pairs={{0,2},{1,3},{2,0},{3,1},{4,6},{5,7},{6,4},{7,5},{8,10},{9,11},{10,... | collective-permute-start | bytes 4718600 | tf_op jit(solution)/shard_map/ppermute | solution.py:548
  1119.4 324.1 %collective-permute-start.41 = (bf16[1024,768]{1,0:T(8,128)(2,1)}, bf16[1024,768]{1,0:T(8,128)(2,1)}, u32[]{:S(2)}, u32[]{:S(2)}) collective-permute-start(bf16[1024,768]{1,0:T(8,128)(2,1)} %get-tuple-element.310), channel_id=1, source_target_pairs={{0,1},{1,0},{2,3},{3,2},{4,5},{5,4},{6,7},{7,6},{8,9},{9,8},{10,11... | collective-permute-start | bytes 4718600 | tf_op jit(solution)/shard_map/ppermute | solution.py:548
  1122.8 301.3 %collective-permute-start.43 = (bf16[1024,768]{1,0:T(8,128)(2,1)}, bf16[1024,768]{1,0:T(8,128)(2,1)}, u32[]{:S(2)}, u32[]{:S(2)}) collective-permute-start(bf16[1024,768]{1,0:T(8,128)(2,1)} %get-tuple-element.307), channel_id=1, source_target_pairs={{0,2},{1,3},{2,0},{3,1},{4,6},{5,7},{6,4},{7,5},{8,10},{9,11},{10,... | collective-permute-start | bytes 4718600 | tf_op jit(solution)/shard_map/ppermute | solution.py:548
  1123.9 65.4 %collective-permute-start.49 = (bf16[384,2048]{1,0:T(8,128)(2,1)S(1)}, bf16[384,2048]{1,0:T(8,128)(2,1)S(1)}, u32[]{:S(2)}, u32[]{:S(2)}) collective-permute-start(bf16[384,2048]{1,0:T(8,128)(2,1)S(1)} %get-tuple-element.306), channel_id=1, source_target_pairs={{0,1},{1,0},{2,3},{3,2},{4,5},{5,4},{6,7},{7,6},{8,9},{9,8},{10,11... | collective-permute-start | bytes 4718600 | tf_op jit(solution)/shard_map/ppermute | solution.py:548
  1277.2 45.4 %collective-permute-start.23 = (bf16[1,512,2048]{2,1,0:T(8,128)(2,1)}, bf16[1,512,2048]{2,1,0:T(8,128)(2,1)S(1)}, u32[]{:S(2)}, u32[]{:S(2)}) collective-permute-start(bf16[1,512,2048]{2,1,0:T(8,128)(2,1)} %get-tuple-element.286), channel_id=1, source_target_pairs={{0,2},{1,3},{2,0},{3,1},{4,6},{5,7},{6,4},{7,5},{8,10},{9,11},{10,... | collective-permute-start | bytes 6291464 | tf_op jit(solution)/shard_map/ppermute | solution.py:548
  1278.7 46.5 %collective-permute-start.21 = (bf16[1,512,2048]{2,1,0:T(8,128)(2,1)}, bf16[1,512,2048]{2,1,0:T(8,128)(2,1)}, u32[]{:S(2)}, u32[]{:S(2)}) collective-permute-start(bf16[1,512,2048]{2,1,0:T(8,128)(2,1)} %get-tuple-element.286), channel_id=1, source_target_pairs={{0,1},{1,0},{2,3},{3,2},{4,5},{5,4},{6,7},{7,6},{8,9},{9,8},{10,11... | collective-permute-start | bytes 6291464 | tf_op jit(solution)/shard_map/ppermute | solution.py:548
  1300.4 282.4 %reduce-scatter.17.cloned.1.call-start = ((), (), s32[]{:S(2)}) async-start(), calls=%async_computation.17 | async-start | bytes 1179648 | tf_op jit(solution)/shard_map/reduce_scatter | solution.py:769
  1323.8 53.5 %collective-permute-start.26 = (bf16[1,256,2048]{2,1,0:T(8,128)(2,1)}, bf16[1,256,2048]{2,1,0:T(8,128)(2,1)S(1)}, u32[]{:S(2)}, u32[]{:S(2)}) collective-permute-start(bf16[1,256,2048]{2,1,0:T(8,128)(2,1)} %slice.419), channel_id=1, source_target_pairs={{0,1},{1,0},{2,3},{3,2},{4,5},{5,4},{6,7},{7,6},{8,9},{9,8},{10,11... | collective-permute-start | bytes 3145736 | tf_op jit(solution)/shard_map/ppermute | solution.py:548
  1327.6 47.2 %collective-permute-start.25 = (bf16[1,256,2048]{2,1,0:T(8,128)(2,1)}, bf16[1,256,2048]{2,1,0:T(8,128)(2,1)}, u32[]{:S(2)}, u32[]{:S(2)}) collective-permute-start(bf16[1,256,2048]{2,1,0:T(8,128)(2,1)} %slice.418), channel_id=1, source_target_pairs={{0,2},{1,3},{2,0},{3,1},{4,6},{5,7},{6,4},{7,5},{8,10},{9,11},{10,... | collective-permute-start | bytes 3145736 | tf_op jit(solution)/shard_map/ppermute | solution.py:548
  1351.5 251.2 %reduce-scatter.15.cloned.1.call-start = ((), (), s32[]{:S(2)}) async-start(), calls=%async_computation.16 | async-start | bytes 1179648 | tf_op jit(solution)/shard_map/reduce_scatter | solution.py:769
  1374.8 287.6 %reduce-scatter.19.cloned.1.call-start = ((), (), s32[]{:S(2)}) async-start(), calls=%async_computation.18 | async-start | bytes 1179648 | tf_op jit(solution)/shard_map/reduce_scatter | solution.py:769
  1374.8 27.8 %collective-permute-start.45 = (bf16[1024,768]{1,0:T(8,128)(2,1)S(1)}, bf16[1024,768]{1,0:T(8,128)(2,1)}, u32[]{:S(2)}, u32[]{:S(2)}) collective-permute-start(bf16[1024,768]{1,0:T(8,128)(2,1)S(1)} %copy-done.37), channel_id=1, source_target_pairs={{0,1},{1,0},{2,3},{3,2},{4,5},{5,4},{6,7},{7,6},{8,9},{9,8},{10,11... | collective-permute-start | bytes 4718600 | tf_op jit(solution)/shard_map/ppermute | solution.py:548
  1377.3 71.4 %collective-permute-start.50 = (bf16[768,2048]{1,0:T(8,128)(2,1)}, bf16[768,2048]{1,0:T(8,128)(2,1)}, u32[]{:S(2)}, u32[]{:S(2)}) collective-permute-start(bf16[768,2048]{1,0:T(8,128)(2,1)} %pad_maximum_fusion.9), channel_id=1, source_target_pairs={{0,2},{1,3},{2,0},{3,1},{4,6},{5,7},{6,4},{7,5},{8,10},{9,11},{10,... | collective-permute-start | bytes 9437192 | tf_op jit(solution)/shard_map/ppermute | solution.py:548
  1397.9 452.3 %reduce-scatter.23.cloned.1.call-start = ((), (), s32[]{:S(2)}) async-start(), calls=%async_computation.21 | async-start | bytes 4718592 | tf_op jit(solution)/shard_map/reduce_scatter | solution.py:796
  1402.6 68.3 %collective-permute-start.48 = (bf16[768,2048]{1,0:T(8,128)(2,1)}, bf16[768,2048]{1,0:T(8,128)(2,1)}, u32[]{:S(2)}, u32[]{:S(2)}) collective-permute-start(bf16[768,2048]{1,0:T(8,128)(2,1)} %pad_maximum_fusion.8), channel_id=1, source_target_pairs={{0,1},{1,0},{2,3},{3,2},{4,5},{5,4},{6,7},{7,6},{8,9},{9,8},{10,11... | collective-permute-start | bytes 9437192 | tf_op jit(solution)/shard_map/ppermute | solution.py:548
  1423.7 428.6 %reduce-scatter.21.cloned.1.call-start = ((), (), s32[]{:S(2)}) async-start(), calls=%async_computation.20 | async-start | bytes 4718592 | tf_op jit(solution)/shard_map/reduce_scatter | solution.py:794
  1424.1 82.8 %collective-permute-start.46 = (bf16[2048,768]{1,0:T(8,128)(2,1)}, bf16[2048,768]{1,0:T(8,128)(2,1)}, u32[]{:S(2)}, u32[]{:S(2)}) collective-permute-start(bf16[2048,768]{1,0:T(8,128)(2,1)} %pad_maximum_fusion.7), channel_id=1, source_target_pairs={{0,2},{1,3},{2,0},{3,1},{4,6},{5,7},{6,4},{7,5},{8,10},{9,11},{10,... | collective-permute-start | bytes 9437192 | tf_op jit(solution)/shard_map/ppermute | solution.py:548
  1429.1 109.2 %collective-permute-start.44 = (bf16[2048,768]{1,0:T(8,128)(2,1)}, bf16[2048,768]{1,0:T(8,128)(2,1)}, u32[]{:S(2)}, u32[]{:S(2)}) collective-permute-start(bf16[2048,768]{1,0:T(8,128)(2,1)} %pad_maximum_fusion.6), channel_id=1, source_target_pairs={{0,1},{1,0},{2,3},{3,2},{4,5},{5,4},{6,7},{7,6},{8,9},{9,8},{10,11... | collective-permute-start | bytes 9437192 | tf_op jit(solution)/shard_map/ppermute | solution.py:548
  1559.1 147.7 %collective-permute-start.22 = (bf16[512,2048]{1,0:T(8,128)(2,1)}, bf16[512,2048]{1,0:T(8,128)(2,1)}, u32[]{:S(2)}, u32[]{:S(2)}) collective-permute-start(bf16[512,2048]{1,0:T(8,128)(2,1)} %get-tuple-element.165), channel_id=1, source_target_pairs={{0,1},{1,0},{2,3},{3,2},{4,5},{5,4},{6,7},{7,6},{8,9},{9,8},{10,11... | collective-permute-start | bytes 6291464 | tf_op jit(solution)/shard_map/ppermute | solution.py:548
  1559.9 11.4 collective-permute-start.29
  1569.5 137.4 %collective-permute-start.24 = (bf16[512,2048]{1,0:T(8,128)(2,1)}, bf16[512,2048]{1,0:T(8,128)(2,1)}, u32[]{:S(2)}, u32[]{:S(2)}) collective-permute-start(bf16[512,2048]{1,0:T(8,128)(2,1)} %get-tuple-element.170), channel_id=1, source_target_pairs={{0,2},{1,3},{2,0},{3,1},{4,6},{5,7},{6,4},{7,5},{8,10},{9,11},{10,... | collective-permute-start | bytes 6291464 | tf_op jit(solution)/shard_map/ppermute | solution.py:548
  1581.3 125.5 %collective-permute-start.27 = (bf16[512,2048]{1,0:T(8,128)(2,1)}, bf16[512,2048]{1,0:T(8,128)(2,1)}, u32[]{:S(2)}, u32[]{:S(2)}) collective-permute-start(bf16[512,2048]{1,0:T(8,128)(2,1)} %get-tuple-element.175), channel_id=1, source_target_pairs={{0,3},{1,2},{2,1},{3,0},{4,7},{5,6},{6,5},{7,4},{8,11},{9,10},{10,... | collective-permute-start | bytes 6291464 | tf_op jit(solution)/shard_map/ppermute | solution.py:548
  1582.8 39.4 %collective-permute-start.34 = (bf16[2,256,128]{2,1,0:T(8,128)(2,1)}, bf16[2,256,128]{2,1,0:T(8,128)(2,1)S(1)}, u32[]{:S(2)}, u32[]{:S(2)}) collective-permute-start(bf16[2,256,128]{2,1,0:T(8,128)(2,1)} %reduce-scatter.17.cloned.1.call-done), channel_id=1, source_target_pairs={{4,0},{12,4},{20,8},{28,12},{5,1},{13,5},{21,9},{29,13},{6,2},{14,... | collective-permute-start | bytes 393224 | tf_op jit(solution)/shard_map/ppermute | solution.py:776
  1584.2 39.3 %collective-permute-start.33 = (bf16[2,256,128]{2,1,0:T(8,128)(2,1)}, bf16[2,256,128]{2,1,0:T(8,128)(2,1)S(1)}, u32[]{:S(2)}, u32[]{:S(2)}) collective-permute-start(bf16[2,256,128]{2,1,0:T(8,128)(2,1)} %reduce-scatter.17.cloned.1.call-done), channel_id=1, source_target_pairs={{0,0},{8,4},{16,8},{24,12},{1,1},{9,5},{17,9},{25,13},{2,2},{10,6}... | collective-permute-start | bytes 393224 | tf_op jit(solution)/shard_map/ppermute | solution.py:776
  1622.2 39.7 %collective-permute-start.31 = (bf16[2,256,128]{2,1,0:T(8,128)(2,1)}, bf16[2,256,128]{2,1,0:T(8,128)(2,1)S(1)}, u32[]{:S(2)}, u32[]{:S(2)}) collective-permute-start(bf16[2,256,128]{2,1,0:T(8,128)(2,1)} %reduce-scatter.15.cloned.1.call-done), channel_id=1, source_target_pairs={{4,0},{12,4},{20,8},{28,12},{5,1},{13,5},{21,9},{29,13},{6,2},{14,... | collective-permute-start | bytes 393224 | tf_op jit(solution)/shard_map/ppermute | solution.py:776
  1623.5 38.4 %collective-permute-start.30 = (bf16[2,256,128]{2,1,0:T(8,128)(2,1)}, bf16[2,256,128]{2,1,0:T(8,128)(2,1)S(1)}, u32[]{:S(2)}, u32[]{:S(2)}) collective-permute-start(bf16[2,256,128]{2,1,0:T(8,128)(2,1)} %reduce-scatter.15.cloned.1.call-done), channel_id=1, source_target_pairs={{0,0},{8,4},{16,8},{24,12},{1,1},{9,5},{17,9},{25,13},{2,2},{10,6}... | collective-permute-start | bytes 393224 | tf_op jit(solution)/shard_map/ppermute | solution.py:776
  1662.4 24.3 %collective-permute-start.37 = (bf16[2,256,128]{2,1,0:T(8,128)(2,1)}, bf16[2,256,128]{2,1,0:T(8,128)(2,1)S(1)}, u32[]{:S(2)}, u32[]{:S(2)}) collective-permute-start(bf16[2,256,128]{2,1,0:T(8,128)(2,1)} %reduce-scatter.19.cloned.1.call-done), channel_id=1, source_target_pairs={{4,0},{12,4},{20,8},{28,12},{5,1},{13,5},{21,9},{29,13},{6,2},{14,... | collective-permute-start | bytes 393224 | tf_op jit(solution)/shard_map/ppermute | solution.py:776
  1663.9 22.9 %collective-permute-start.36 = (bf16[2,256,128]{2,1,0:T(8,128)(2,1)}, bf16[2,256,128]{2,1,0:T(8,128)(2,1)S(1)}, u32[]{:S(2)}, u32[]{:S(2)}) collective-permute-start(bf16[2,256,128]{2,1,0:T(8,128)(2,1)} %reduce-scatter.19.cloned.1.call-done), channel_id=1, source_target_pairs={{0,0},{8,4},{16,8},{24,12},{1,1},{9,5},{17,9},{25,13},{2,2},{10,6}... | collective-permute-start | bytes 393224 | tf_op jit(solution)/shard_map/ppermute | solution.py:776
  1701.1 121.4 %collective-permute-start.42 = (bf16[2048,768]{1,0:T(8,128)(2,1)}, bf16[2048,768]{1,0:T(8,128)(2,1)}, u32[]{:S(2)}, u32[]{:S(2)}) collective-permute-start(bf16[2048,768]{1,0:T(8,128)(2,1)} %pad_maximum_fusion.5), channel_id=1, source_target_pairs={{0,2},{1,3},{2,0},{3,1},{4,6},{5,7},{6,4},{7,5},{8,10},{9,11},{10,... | collective-permute-start | bytes 9437192 | tf_op jit(solution)/shard_map/ppermute | solution.py:548
  1705.2 117.4 %collective-permute-start.40 = (bf16[2048,768]{1,0:T(8,128)(2,1)}, bf16[2048,768]{1,0:T(8,128)(2,1)}, u32[]{:S(2)}, u32[]{:S(2)}) collective-permute-start(bf16[2048,768]{1,0:T(8,128)(2,1)} %pad_maximum_fusion.4), channel_id=1, source_target_pairs={{0,1},{1,0},{2,3},{3,2},{4,5},{5,4},{6,7},{7,6},{8,9},{9,8},{10,11... | collective-permute-start | bytes 9437192 | tf_op jit(solution)/shard_map/ppermute | solution.py:548
  1720.6 62.7 %all-to-all-start.2 = ((f32[32,1,2184]{2,1,0:T(1,128)}), f32[32,1,2184]{2,1,0:T(1,128)S(1)}, u32[]{:S(2)}, u32[]{:S(2)}) async-start(f32[32,1,2184]{2,1,0:T(1,128)} %copy.131), calls=%async_computation.10 | async-start | bytes 589824 | tf_op jit(solution)/shard_map/all_to_all | solution.py:819
  1783.3 65.7 %all-to-all-start.1 = ((bf16[32,64,256]{2,1,0:T(8,128)(2,1)}), bf16[32,64,256]{2,1,0:T(8,128)(2,1)S(1)}, u32[]{:S(2)}, u32[]{:S(2)}) async-start(bf16[32,64,256]{2,1,0:T(8,128)(2,1)} %bitcast.96), calls=%async_computation.8 | async-start | bytes 2097152 | tf_op jit(solution)/shard_map/all_to_all | solution.py:808
  (139 other events, 2831.0 us)
Sparse Core Ops, SparseCore 0:
  14.5 63.1 all-gather.15
  92.6 27.7 all-gather.21
  150.1 27.7 all-gather.23
  179.4 47.2 all-gather.17
  228.2 27.3 all-gather.25
  257.0 28.8 all-gather.27
  287.5 150.4 all-gather.31
  439.6 149.2 all-gather.29
  867.2 185.2 reduce-scatter.8
  1053.9 46.8 all-gather.19
  1103.2 166.9 reduce-scatter.10
  1300.5 54.8 reduce-scatter.12
  1357.6 52.9 reduce-scatter.16
  1412.8 47.3 reduce-scatter.14
  1462.3 47.0 reduce-scatter.18
  1511.5 48.3 reduce-scatter.22
  1602.8 125.8 reduce-scatter.20

commit v3 on v2

--- a/solution.py
+++ b/solution.py
@@ -50,7 +50,9 @@
             scratch_shapes=list(scratch),
         ),
         out_shape=out_shape,
-        cost_estimate=pl.CostEstimate(flops=int(flops), bytes_accessed=int(moved), transcendentals=0),
+        cost_estimate=pl.CostEstimate(
+            flops=int(flops), bytes_accessed=int(moved), transcendentals=0
+        ),
         compiler_params=pltpu.CompilerParams(
             dimension_semantics=("arbitrary",) * len(grid), vmem_limit_bytes=VMEM
         ),
@@ -185,6 +187,7 @@
 def attend(row, q, every, kv, blocks):
     heads, rows, _ = q.shape
     per = 2
+    every, place = every
     keys = blocks * rows
     return call(
         partial(attend_body, heads, per, blocks, rows),
@@ -192,8 +195,8 @@
         (rows // CONT, heads // per),
         [
             pl.BlockSpec((per, CONT, HEAD), lambda i, h, s: (h, i, 0)),
-            pl.BlockSpec((blocks, 1, rows, HEAD), lambda i, h, s: (0, 0, 0, 0)),
-            pl.BlockSpec((blocks, 1, rows, HEAD), lambda i, h, s: (0, 1, 0, 0)),
+            pl.BlockSpec((blocks, 1, rows, HEAD), lambda i, h, s: (0, 2 * place, 0, 0)),
+            pl.BlockSpec((blocks, 1, rows, HEAD), lambda i, h, s: (0, 2 * place + 1, 0, 0)),
             pl.BlockSpec((2, rows, HEAD), lambda i, h, s: (0, 0, 0)),
         ],
         [
@@ -305,6 +308,7 @@
 def attend_back(row, q, every, kv, blocks, do, o, logs, scales, cos, sin, qg):
     heads, rows, _ = q.shape
     per = 2
+    every, place = every
     keys = blocks * rows
     tile = lambda i, h, s: (i, 0)
     head = lambda i, h, s: (i, h)
@@ -314,8 +318,8 @@
         (rows // CONT, heads // per),
         [
             pl.BlockSpec((per, CONT, HEAD), lambda i, h, s: (h, i, 0)),
-            pl.BlockSpec((blocks, 1, rows, HEAD), lambda i, h, s: (0, 0, 0, 0)),
-            pl.BlockSpec((blocks, 1, rows, HEAD), lambda i, h, s: (0, 1, 0, 0)),
+            pl.BlockSpec((blocks, 1, rows, HEAD), lambda i, h, s: (0, 2 * place, 0, 0)),
+            pl.BlockSpec((blocks, 1, rows, HEAD), lambda i, h, s: (0, 2 * place + 1, 0, 0)),
             pl.BlockSpec((2, rows, HEAD), lambda i, h, s: (0, 0, 0)),
             pl.BlockSpec((CONT, per * HEAD), head),
             pl.BlockSpec((CONT, per * HEAD), head),
@@ -348,12 +352,12 @@
     )(row, q, every, every, kv, do, o, logs, scales, cos, sin, qg)
 
 
-def dispatch_body(count, cap, rank_ref, rows_ref, out_ref):
+def dispatch_body(count, cap, rank_ref, rows_ref, *out_refs):
     tokens = rows_ref.shape[1]
     slot = lax.broadcasted_iota(jnp.int32, (cap, tokens), 0)
     for d in range(count):
         hot = (rank_ref[0, d : d + 1, :] == slot).astype(F32).astype(BF)
-        out_ref[d, 0] = dot_nn(hot, rows_ref[0]).astype(BF)
+        out_refs[d][0] = dot_nn(hot, rows_ref[0]).astype(BF)
 
 
 def dispatch(rank, rows, cap):
@@ -367,27 +371,26 @@
             pl.BlockSpec((1, count, tokens), lambda s: (s, 0, 0)),
             pl.BlockSpec((1, tokens, width), lambda s: (s, 0, 0)),
         ],
-        pl.BlockSpec((count, 1, cap, width), lambda s: (0, s, 0, 0)),
-        struct((count, sources, cap, width), BF),
+        [pl.BlockSpec((1, cap, width), lambda s: (s, 0, 0))] * count,
+        [struct((sources, cap, width), BF)] * count,
         flops=2 * sources * count * cap * tokens * width,
         moved=2 * sources * width * (tokens + count * cap),
     )(rank, rows)
 
 
-def route_body(count, cap, ids_ref, rank_ref, rows_ref, mask_ref, router_ref, out_ref, probs_ref, gate_ref):
+def route_body(count, cap, ids_ref, rank_ref, rows_ref, mask_ref, router_ref, gate_ref, *out_refs):
     tokens = rows_ref.shape[1]
     rows = rows_ref[0]
     logits = dot_nt(router_ref[...], rows)
     weights = jnp.exp(logits - jnp.max(logits, axis=0, keepdims=True))
     probs = weights / jnp.sum(weights, axis=0, keepdims=True)
-    probs_ref[0] = probs
     picked = probs * mask_ref[0]
     gates = picked / jnp.sum(picked, axis=0, keepdims=True)
     expert_at = lax.broadcasted_iota(jnp.int32, gates.shape, 0)
     slot = lax.broadcasted_iota(jnp.int32, (cap, tokens), 0)
     for d in range(count):
         here = rank_ref[0, d : d + 1, :] == slot
-        out_ref[d, 0] = dot_nn(here.astype(F32).astype(BF), rows).astype(BF)
+        out_refs[d][0] = dot_nn(here.astype(F32).astype(BF), rows).astype(BF)
         mine = jnp.sum(jnp.where(expert_at == ids_ref[d], gates, 0.0), axis=0, keepdims=True)
         gate_ref[d, 0] = jnp.sum(jnp.where(here, mine, 0.0), axis=1, keepdims=True)
 
@@ -407,33 +410,22 @@
             pl.BlockSpec((experts, width), lambda s, i: (0, 0)),
         ],
         [
-            pl.BlockSpec((count, 1, cap, width), lambda s, i: (0, s, 0, 0)),
-            pl.BlockSpec((1, experts, tokens), lambda s, i: (s, 0, 0)),
             pl.BlockSpec((count, 1, cap, 1), lambda s, i: (0, s, 0, 0)),
-        ],
-        [
-            struct((count, sources, cap, width), BF),
-            struct((sources, experts, tokens), F32),
-            struct((count, sources, cap, 1), F32),
-        ],
+        ]
+        + [pl.BlockSpec((1, cap, width), lambda s, i: (s, 0, 0))] * count,
+        [struct((count, sources, cap, 1), F32)]
+        + [struct((sources, cap, width), BF)] * count,
         flops=2 * sources * count * cap * tokens * width,
         moved=2 * sources * width * (tokens + count * cap),
         prefetch=1,
     )(ids, rank, rows, mask, router)
 
 
-def share_body(g_ref, w_ref, a_ref, out_ref, sum_ref):
-    share = dot_nt(g_ref[...], w_ref[...])
-    out_ref[...] = share.astype(out_ref.dtype)
-
-    @pl.when(pl.program_id(0) == 0)
-    def _():
-        sum_ref[...] = jnp.zeros_like(sum_ref)
-
-    sum_ref[0:1, :] += jnp.sum(share * a_ref[...].astype(F32), axis=0, keepdims=True)
-
-
-def input_share(grads, w, normed, dtype):
+def share_body(g_ref, w_ref, out_ref):
+    out_ref[...] = dot_nt(g_ref[...], w_ref[...]).astype(out_ref.dtype)
+
+
+def input_share(grads, w, dtype):
     rows, cols = grads.shape
     width = w.shape[0]
     tile = 256
@@ -444,133 +436,159 @@
         [
             pl.BlockSpec((tile, cols), lambda i: (i, 0)),
             pl.BlockSpec((width, cols), lambda i: (0, 0)),
-            pl.BlockSpec((tile, width), lambda i: (i, 0)),
-        ],
-        [pl.BlockSpec((tile, width), lambda i: (i, 0)), pl.BlockSpec((8, width), lambda i: (0, 0))],
-        [struct((rows, width), dtype), struct((8, width), F32)],
+        ],
+        pl.BlockSpec((tile, width), lambda i: (i, 0)),
+        struct((rows, width), dtype),
         flops=2 * rows * width * cols,
-        moved=2 * (2 * rows * width + width * cols + rows * cols),
-    )(grads, w, normed)
-
-
-def combine_body(count, cap, rank_ref, *refs):
+        moved=2 * (rows * width + width * cols + rows * cols),
+    )(grads, w)
+
+
+def combine_body(count, cap, scored, rank_ref, *refs):
     tokens = rank_ref.shape[1]
     slot = lax.broadcasted_iota(jnp.int32, (tokens, cap), 1)
+    out_ref = refs[count * (2 if scored else 1)]
     total = None
     for d in range(count):
         hot = (rank_ref[0, :, d : d + 1] == slot).astype(F32).astype(BF)
         piece = dot_nn(hot, refs[d][0])
         total = piece if total is None else total + piece
-    refs[-1][0] = total.astype(BF)
-
-
-def combine(rank_t, parts):
+        if scored:
+            score = dot_nn(hot, refs[count + d][0])
+            refs[-1][0, :, d : d + 1] = jnp.sum(score, axis=-1, keepdims=True)
+    out_ref[0] = total.astype(BF)
+
+
+def combine(rank_t, parts, scores=()):
     sources, tokens, count = rank_t.shape
-    _, cap, width = parts[0].shape
+    cap = parts[0].shape[0] // sources
+    width = parts[0].shape[1]
+    at = lambda s: (s, 0, 0)
+    cut = lambda v: v.reshape(sources, cap, v.shape[1])
+    out_specs = [pl.BlockSpec((1, tokens, width), at)]
+    out_shape = [struct((sources, tokens, width), BF)]
+    if scores:
+        out_specs.append(pl.BlockSpec((1, tokens, count), at))
+        out_shape.append(struct((sources, tokens, count), F32))
     return call(
-        partial(combine_body, count, cap),
+        partial(combine_body, count, cap, bool(scores)),
         "combine",
         (sources,),
-        [pl.BlockSpec((1, tokens, count), lambda s: (s, 0, 0))]
-        + [pl.BlockSpec((1, cap, width), lambda s: (s, 0, 0))] * count,
-        pl.BlockSpec((1, tokens, width), lambda s: (s, 0, 0)),
-        struct((sources, tokens, width), BF),
+        [pl.BlockSpec((1, tokens, count), at)]
+        + [pl.BlockSpec((1, cap, width), at)] * count
+        + [pl.BlockSpec((1, cap, HEAD), at)] * len(scores),
+        out_specs,
+        out_shape,
         flops=2 * sources * count * cap * tokens * width,
         moved=2 * sources * width * (tokens + count * cap),
-    )(rank_t, *parts)
+    )(rank_t, *[cut(p) for p in parts], *[cut(p) for p in scores])
 
 
 def expert_body(
-    x_ref, up_ref, gate_ref, wg_ref, wu_ref, wd_ref,
-    y_ref, db_ref, m_ref, du_ref, dw_ref, dg_ref,
+    x_ref, up_ref, gate_ref, wga_ref, wgb_ref, wua_ref, wub_ref, wda_ref, wdb_ref,
+    y_ref, db_ref, m_ref, duw_ref, dg_ref,
 ):
-    x = x_ref[0]
+    half = wga_ref.shape[1]
+    deep = wda_ref.shape[1]
+    hidden = wga_ref.shape[2]
+    xa, xb = x_ref[:, :half], x_ref[:, half:]
     gate = gate_ref[...]
-    u = dot_nn(x, wg_ref[0])
-    w = dot_nn(x, wu_ref[0])
+    u = dot_nn(xa, wga_ref[0]) + dot_nn(xb, wgb_ref[0])
+    w = dot_nn(xa, wua_ref[0]) + dot_nn(xb, wub_ref[0])
     sigma = 1.0 / (1.0 + jnp.exp(-u))
     silu = u * sigma
     inner = silu * w
     low = inner.astype(BF)
-    y_ref[...] = (dot_nn(low, wd_ref[0]) * gate).astype(BF)
+    y = dot_nn(low[:, :deep], wda_ref[0]) + dot_nn(low[:, deep:], wdb_ref[0])
+    y_ref[...] = (y * gate).astype(BF)
     m_ref[...] = (inner * gate).astype(BF)
-    back = dot_nt(up_ref[0], wd_ref[0])
-    dg_ref[...] = jnp.sum(low.astype(F32) * back, axis=-1, keepdims=True)
+    up = up_ref[...]
+    back = jnp.concatenate([dot_nt(up, wda_ref[0]), dot_nt(up, wdb_ref[0])], axis=1)
+    score = jnp.sum(low.astype(F32) * back, axis=-1, keepdims=True)
+    lane = lax.broadcasted_iota(jnp.int32, dg_ref.shape, 1)
+    high = score.astype(BF)
+    rest = score - high.astype(F32)
+    middle = rest.astype(BF)
+    last = (rest - middle.astype(F32)).astype(BF)
+    pieces = jnp.where(lane == 0, high.astype(F32), 0.0)
+    pieces = jnp.where(lane == 1, middle.astype(F32), pieces)
+    dg_ref[...] = jnp.where(lane == 2, last.astype(F32), pieces).astype(BF)
     back = back * gate
     du = (back * w * sigma * (1.0 + u * (1.0 - sigma))).astype(BF)
     dw = (back * silu).astype(BF)
-    du_ref[...] = du
-    dw_ref[...] = dw
-    db_ref[...] = (dot_nt(du, wg_ref[0]) + dot_nt(dw, wu_ref[0])).astype(BF)
-
-
-def expert(slot, x, up, gate, wg, wu, wd):
-    _, rows, width = x.shape
-    hidden = wg.shape[2]
+    duw_ref[:, :hidden] = du
+    duw_ref[:, hidden:] = dw
+    db_ref[:, :half] = (dot_nt(du, wga_ref[0]) + dot_nt(dw, wua_ref[0])).astype(BF)
+    db_ref[:, half:] = (dot_nt(du, wgb_ref[0]) + dot_nt(dw, wub_ref[0])).astype(BF)
+
+
+def expert(x, up, gate, weights):
+    rows, width = x.shape
+    hidden = weights[0][0].shape[2]
     tile = min(256, rows)
     at = lambda i: (i, 0)
-    mine = lambda i: (slot, i, 0)
-    whole = lambda i: (0, 0, 0)
+    specs, arrays = [], []
+    for parts in weights:
+        shape = (1, parts[0].shape[1] * len(parts) // 2, parts[0].shape[2])
+        for j in range(2):
+            place = j if len(parts) == 1 else 0
+            specs.append(pl.BlockSpec(shape, lambda i, place=place: (0, place, 0)))
+            arrays.append(parts[0] if len(parts) == 1 else parts[j])
     return call(
         expert_body,
         "expert",
         (rows // tile,),
         [
-            pl.BlockSpec((1, tile, width), mine),
-            pl.BlockSpec((1, tile, width), mine),
+            pl.BlockSpec((tile, width), at),
+            pl.BlockSpec((tile, width), at),
             pl.BlockSpec((tile, 1), at),
-            pl.BlockSpec((1, width, hidden), whole),
-            pl.BlockSpec((1, width, hidden), whole),
-            pl.BlockSpec((1, hidden, width), whole),
-        ],
+        ]
+        + specs,
         [
             pl.BlockSpec((tile, width), at),
             pl.BlockSpec((tile, width), at),
             pl.BlockSpec((tile, hidden), at),
-            pl.BlockSpec((tile, hidden), at),
-            pl.BlockSpec((tile, hidden), at),
-            pl.BlockSpec((tile, 1), at),
+            pl.BlockSpec((tile, 2 * hidden), at),
+            pl.BlockSpec((tile, HEAD), at),
         ],
         [
             struct((rows, width), BF),
             struct((rows, width), BF),
             struct((rows, hidden), BF),
-            struct((rows, hidden), BF),
-            struct((rows, hidden), BF),
-            struct((rows, 1), F32),
+            struct((rows, 2 * hidden), BF),
+            struct((rows, HEAD), BF),
         ],
         flops=12 * rows * width * hidden,
         moved=2 * (4 * rows * width + 3 * rows * hidden + 3 * width * hidden),
-    )(x, up, gate, wg, wu, wd)
+    )(x, up, gate, *arrays)
 
 
 def swap(v, step, count):
     return lax.ppermute(v, "col", [(i, i ^ step) for i in range(count)])
 
 
-def fetch(v, count):
-    if count != 4:
-        return [v] + [swap(v, d, count) for d in range(1, count)]
-    half = v.shape[1] // 2
-    one, two = swap(v, 1, count), swap(v, 2, count)
-    first = swap(one[:, :half], 2, count)
-    second = swap(two[:, half:], 1, count)
-    return [v, one, two, jnp.concatenate([first, second], axis=1)]
-
-
-def deliver(parts, count):
-    own = parts[0]
-    low = [None] + [p.astype(BF) for p in parts[1:]]
-    if count != 4:
-        for d in range(1, count):
-            own = own + swap(low[d], d, count).astype(F32)
-        return own
-    half = own.shape[0] // 2
-    to_two = swap(low[3][:half], 1, count)
-    to_one = swap(low[3][half:], 2, count)
-    one = jnp.concatenate([low[1][:half], (parts[1][half:] + to_one.astype(F32)).astype(BF)], axis=0)
-    two = jnp.concatenate([(parts[2][:half] + to_two.astype(F32)).astype(BF), low[2][half:]], axis=0)
-    return own + swap(one, 1, count).astype(F32) + swap(two, 2, count).astype(F32)
+def near(v, count):
+    return [swap(v, d, count) for d in ((1, 2) if count == 4 else range(1, count))]
+
+
+def far(one, two, count):
+    half = one.shape[1] // 2
+    return [swap(one[:, :half], 2, count), swap(two[:, half:], 1, count)]
+
+
+def halves(v):
+    return v[:, : v.shape[1] // 2], v[:, v.shape[1] // 2 :]
+
+
+def deliver_far(part, count):
+    half = part.shape[0] // 2
+    return swap(part[:half], 1, count), swap(part[half:], 2, count)
+
+
+def join(part, got, first):
+    half = part.shape[0] // 2
+    wide = jnp.pad(got.astype(F32), ((0, half) if first else (half, 0), (0, 0)))
+    return (part.astype(F32) + wide).astype(BF)
 
 
 def after(value, *earlier):
@@ -629,8 +647,8 @@
     gain_q = head_gains[:, :, experts + 2].reshape(1, HEAD)
     gain_k = head_gains[:, :, experts + 3].reshape(1, HEAD)
 
-    xs = [v[0] for v in fetch(layer_input, col_count)]
-    out_all = lax.all_gather(after(w_out, xs[1]), "row", axis=1, tiled=True)
+    four = col_count == 4
+    beside = near(layer_input, col_count)
 
     routes_all = lax.all_gather(routes[0], "row", axis=0)
     expert_ids = jnp.arange(experts, dtype=jnp.int32)
@@ -646,6 +664,15 @@
     rank = jnp.where(has, order.astype(jnp.int32) - 1, -1)
     rank_t = rank.transpose(0, 2, 1)
     mask_all = mask_all.astype(F32)
+
+    def over_col(v):
+        step = 1
+        while step < col_count:
+            v = v + swap(v, step, col_count)
+            step *= 2
+        return v
+
+    load = over_col(jnp.sum(mask_all, axis=(0, 2))) / (tokens * TOPK)
 
     inv_freq = THETA ** (-2.0 * jnp.arange(HEAD // 2, dtype=F32) / HEAD)
     coses, sines = [], []
@@ -656,70 +683,143 @@
         coses.append(jnp.concatenate([cos, cos], axis=1))
         sines.append(jnp.concatenate([-sin, sin], axis=1))
 
+    beside, rank, rank_t, mask_all, coses, sines, load = lax.optimization_barrier(
+        (beside, rank, rank_t, mask_all, coses, sines, load)
+    )
+    out_all = lax.all_gather(after(w_out, beside), "row", axis=1, tiled=True)
+    xs = [x_own] + [v[0] for v in beside]
+    if four:
+        xs.append(jnp.concatenate(far(*beside, col_count), axis=1)[0])
     qs, kvs, normed, scales, every = [[None] * col_count for _ in range(5)]
     line = others + [0]
-    for d in line:
-        qs[d], kvs[d], normed[d], scales[d] = qkv(
-            xs[d], gain_one, wide, coses[d], sines[d], gain_q, gain_k, heads
-        )
-        every[d] = lax.all_gather(kvs[d], "row", axis=0)
-    wg_all = fetch(after(w_gate, xs[-1]), col_count)
+    batch = max(1, col_count // 2)
+    for first in range(0, col_count, batch):
+        ahead = line[first : first + batch]
+        for d in ahead:
+            qs[d], kvs[d], normed[d], scales[d] = qkv(
+                xs[d], gain_one, wide, coses[d], sines[d], gain_q, gain_k, heads
+            )
+        got = jnp.concatenate([kvs[d] for d in ahead], axis=0)
+        if first == 0:
+            got, out_all, xs[-1] = lax.optimization_barrier((got, out_all, xs[-1]))
+        got = lax.all_gather(got, "row", axis=0)
+        for j, d in enumerate(ahead):
+            every[d] = (got, j)
+    gates, ups = after((w_gate, w_up), xs[-1])
+    if four:
+        gates_near, ups_near = [[near(v, col_count) for v in halves(w)] for w in (gates, ups)]
+    else:
+        gates_near, ups_near = [near(gates, col_count)], [near(ups, col_count)]
     mixes, logs = [None] * col_count, [None] * col_count
     hidden = x_own.astype(F32)
-    for d in line:
-        mixes[d], logs[d] = attend(row_word, qs[d], every[d], kvs[d], blocks)
-        share = jnp.dot(mixes[d], out_all, preferred_element_type=F32)
-        hidden = hidden + (share if d == 0 else swap(share.astype(BF), d, col_count).astype(F32))
+    share, sent = None, []
+    for at, d in enumerate(line):
+        q = qs[d]
+        if at > 0:
+            q = after(q, share)
+        else:
+            q, gates_near[0] = lax.optimization_barrier((q, gates_near[0]))
+        mixes[d], logs[d] = attend(row_word, q, every[d], kvs[d], blocks)
+        mix = mixes[d]
+        if at == 0:
+            mix, gates_near[-1] = lax.optimization_barrier((mix, gates_near[-1]))
+        elif at == 1:
+            mix, ups_near[0] = lax.optimization_barrier((mix, ups_near[0]))
+        elif d == 0:
+            mix, sent[: at - 1] = lax.optimization_barrier((mix, sent[: at - 1]))
+        share = jnp.dot(mix, out_all, preferred_element_type=F32)
+        if d != 0:
+            share = share.astype(BF)
+            sent.append(swap(share, d, col_count))
+    share, sent = lax.optimization_barrier((share, sent))
+    for got in sent:
+        hidden = hidden + got.astype(F32)
+    hidden = hidden + share
     up_all = lax.all_gather(after(up_own, mixes[line[0]]), "row", axis=0)
 
     spread = lax.rsqrt(jnp.mean(hidden * hidden, axis=-1, keepdims=True) + EPS)
     second = (hidden * spread * gain_two).astype(BF)
     second_all = lax.all_gather(second, "row", axis=0)
-    wu, wd = after((w_up, w_down), second)
-    wu_all, wd_all = fetch(wu, col_count), fetch(wd, col_count)
-
-    expert_up = dispatch(rank, up_all, cap).reshape(col_count, row_count * cap, width)
+
+    downs_near = near(after(w_down, share), col_count)
+    gate_all = [[w_gate]] + [list(v) for v in zip(*gates_near)]
+    up_w_all = [[w_up]] + [list(v) for v in zip(*ups_near)]
+    down_all = [[w_down]] + [[w] for w in downs_near]
+    if four:
+        rank, ups_near, down_all = lax.optimization_barrier((rank, ups_near, down_all))
+        up_w_all = [[w_up]] + [list(v) for v in zip(*ups_near)]
+        gates_near, _ = lax.optimization_barrier((gates_near, ups_near))
+        far_of = lambda one, two: [swap(one[0], 2, col_count), swap(two[1], 1, col_count)]
+        gate_all.append(far_of(*zip(*gates_near)))
+
+    expert_up = [v.reshape(row_count * cap, width) for v in dispatch(rank, up_all, cap)]
     router_t = router_all.T
-    expert_in, probs_all, gate_pairs = route_dispatch(
+    second_all, expert_up, gate_all = lax.optimization_barrier((second_all, expert_up, gate_all))
+    gate_pairs, *expert_in = route_dispatch(
         mine_ids, rank, second_all, mask_all, router_t, cap
     )
-    expert_in = expert_in.reshape(col_count, row_count * cap, width)
+    expert_in = [v.reshape(row_count * cap, width) for v in expert_in]
     gate_pairs = gate_pairs.reshape(col_count, row_count * cap, 1)
-    kv_all = lax.all_gather(after(key_value_weight, expert_in), "row", axis=0, tiled=True)
-    ys, dbs, ms, dus, dws, dgs = [], [], [], [], [], []
-    for d in slots:
-        got = expert(d, expert_in, expert_up, gate_pairs[d], wg_all[d], wu_all[d], wd_all[d])
-        for kept, value in zip((ys, dbs, ms, dus, dws, dgs), got):
-            kept.append(value)
-    cut = lambda parts: [p.reshape(row_count, cap, width) for p in parts]
-    db_sum = lax.psum_scatter(combine(rank_t, cut(dbs)), "row", scatter_dimension=0)
-
-    slot_ids = jnp.arange(cap, dtype=jnp.int32)
-    hot = rank[:, :, None, :] == slot_ids[None, None, :, None]
-    pair_scores = jnp.stack(dgs, axis=0).reshape(col_count, row_count, cap, 1).transpose(1, 0, 2, 3)
-    score_grads = jnp.sum(jnp.where(hot, pair_scores, 0.0), axis=2)
+    if four:
+        up_w_all.append(far_of(*zip(*ups_near)))
+        expert_in[0], up_w_all = lax.optimization_barrier((expert_in[0], up_w_all))
+        down_far = far_of(*[halves(v[0]) for v in down_all[1:3]])
+    kv_all = lax.all_gather(after(key_value_weight, expert_in[0]), "row", axis=0, tiled=True)
+    ys, dbs, ms, duws, dgs = [[None] * col_count for _ in range(5)]
+    grad_gu, grad_dn = [None] * col_count, [None] * col_count
+
+    def gate_up_grad(d):
+        grad_gu[d] = dot_tn(expert_in[d], duws[d]).astype(F32 if d == 0 else BF)
+
+    def down_grad(d):
+        grad_dn[d] = dot_tn(ms[d], expert_up[d]).astype(F32 if d == 0 else BF)
+
+    far_sent = []
+    order = [0, 3, 1, 2] if four else list(slots)
+    for at, d in enumerate(order):
+        if at > 0:
+            held = [g for g in grad_gu + grad_dn if g is not None]
+            expert_in[d] = after(expert_in[d], dgs[order[at - 1]], held)
+        if four and at == 1:
+            expert_in[d], down_far = lax.optimization_barrier((expert_in[d], down_far))
+            down_all.append(down_far)
+        weights = [gate_all[d], up_w_all[d], down_all[d]]
+        ys[d], dbs[d], ms[d], duws[d], dgs[d] = expert(
+            expert_in[d], expert_up[d], gate_pairs[d], weights
+        )
+        if four and at == 1:
+            gate_up_grad(d)
+            down_grad(d)
+            far_sent = [deliver_far(grad_gu[d], col_count), deliver_far(grad_dn[d], col_count)]
+    if four:
+        dbs[0], far_sent[0] = lax.optimization_barrier((dbs[0], far_sent[0]))
+    dbs[0], kv_all = lax.optimization_barrier((dbs[0], kv_all))
+    db_part, score_grads = combine(rank_t, dbs, dgs)
+    if four:
+        score_grads, far_sent[1] = lax.optimization_barrier((score_grads, far_sent[1]))
+    db_sum = lax.psum_scatter(db_part, "row", scatter_dimension=0)
+    duws, ms, ys, _ = lax.optimization_barrier((duws, ms, ys, db_part))
+    remaining = (1, 2) if four else range(1, col_count)
+    for d in remaining:
+        gate_up_grad(d)
+    exchange = lambda sends: [swap(v, d, col_count) for d, v in enumerate(sends, 1)]
+    gu_sends = grad_gu[1:]
+    if four:
+        gu_two, gu_one = far_sent[0]
+        gu_sends = [join(grad_gu[1], gu_one, False), join(grad_gu[2], gu_two, True)]
+    gu_got = exchange(gu_sends)
+    ms, gu_sends = lax.optimization_barrier((ms, gu_sends))
+    for d in remaining:
+        down_grad(d)
+    dn_sends = grad_dn[1:]
+    if four:
+        dn_two, dn_one = far_sent[1]
+        dn_sends = [join(grad_dn[1], dn_one, False), join(grad_dn[2], dn_two, True)]
+    gate_up_grad(0)
+    down_grad(0)
+    (y_part,) = combine(rank_t, ys)
+
     score_grads = lax.all_to_all(score_grads, "row", split_axis=0, concat_axis=0, tiled=True)
-    sums = jnp.stack([jnp.sum(mask_all, axis=(0, 2)), jnp.sum(probs_all, axis=(0, 2))])
-    step = 1
-    while step < col_count:
-        sums = sums + swap(sums, step, col_count)
-        step *= 2
-    load = sums[0] / (tokens * TOPK)
-    mean_probs = sums[1] / tokens
-    aux_loss = experts * jnp.sum(load * mean_probs)
-    expert_load = jnp.stack([experts * load, experts * mean_probs])
-
-    grad_parts = [
-        [dot_tn(ms[d], expert_up[d]) for d in slots],
-        [dot_tn(expert_in[d], dus[d]) for d in slots],
-        [dot_tn(expert_in[d], dws[d]) for d in slots],
-    ]
-    y_part = combine(rank_t, cut(ys))
-    db_sum, grad_parts, y_part = lax.optimization_barrier((db_sum, grad_parts, y_part))
-    grad_down, grad_gate, grad_up = [deliver(parts, col_count) for parts in grad_parts]
-    y_sum = lax.psum_scatter(y_part, "row", scatter_dimension=0)
-    layer_output = (hidden + y_sum.astype(F32)).astype(BF)
-
     mask_own = jnp.any(routes[0].T[:, None, :] == expert_ids[None, :, None], axis=0)
     logits = lax.dot_general(
         router_all, second, (((0,), (1,)), ((), ())), preferred_element_type=F32
@@ -730,8 +830,9 @@
     gates = picked / total
     to_member = jnp.stack(members)[:, None] == jnp.arange(col_count)[None, :]
     gate_grad = jnp.sum(
-        jnp.where(to_member[None, :, :, None], score_grads[:, :, None, :], 0.0), axis=1
-    ).reshape(experts, rows)
+        jnp.where(to_member, score_grads[..., None], 0.0), axis=2
+    )
+    gate_grad = gate_grad.transpose(0, 2, 1).reshape(experts, rows)
     weighted = jnp.sum(gate_grad * gates, axis=0, keepdims=True)
     prob_grad = (
         jnp.where(mask_own, (gate_grad - weighted) / total, 0.0)
@@ -741,78 +842,138 @@
     grad_router = lax.dot_general(
         second, logit_low, (((0,), (1,)), ((), ())), preferred_element_type=F32
     )
-    second_grad = db_sum.astype(F32) + lax.dot_general(
+    router_part = lax.dot_general(
         logit_low, router_all, (((0,), (1,)), ((), ())), preferred_element_type=F32
     )
+
+    kv_weight = jnp.concatenate([w for m in members for w in kv_pick(kv_all, m)], axis=1)
+    db_sum, gu_got, y_part, router_part, grad_router, kv_weight, own_grads, dn_sends = (
+        lax.optimization_barrier(
+            (
+                db_sum, gu_got, y_part, router_part, grad_router, kv_weight,
+                (grad_gu[0], grad_dn[0]), dn_sends,
+            )
+        )
+    )
+    y_sum = lax.psum_scatter(y_part, "row", scatter_dimension=0)
+    second_grad = db_sum.astype(F32) + router_part
     hat = hidden * spread
     gain_two_grad = jnp.sum(second_grad * hat, axis=0)
     hidden_grad = up_own.astype(F32) + norm_back(second_grad, hat, spread, gain_two)
     branch = hidden_grad.astype(BF)
 
-    branches = [v[0] for v in fetch(branch[None], col_count)]
-    grad_qs, grad_kvs, kv_moved = [], [], []
-    gain_q_grad, gain_k_grad, gain_one_grad, input_sum = 0.0, 0.0, 0.0, 0.0
+    beside = near(branch[None], col_count)
+    branches = [branch] + [v[0] for v in beside]
+    grad_qs, prompts, pairs, shares, sent, grad_kvs, kv_moved = [], [], [], [], [], [], []
+    gain_q_grad, gain_k_grad = 0.0, 0.0
 
     def back_turn(v, cos, sin):
         moved = v * sin
         half = HEAD // 2
         return v * cos + jnp.concatenate([moved[:, half:], moved[:, :half]], axis=1)
 
+    normed_all = jnp.stack(normed, axis=0)
+    over_tokens = lambda a, b: lax.dot_general(
+        a, b, (((0, 1), (0, 1)), ((), ())), preferred_element_type=F32
+    )
+    mixes_all = jnp.stack(mixes, axis=0)
+    grad_out = None
+
+    def to_owners(prompt):
+        chunk = prompt.shape[2]
+        return jnp.concatenate(
+            [
+                lax.ppermute(prompt, "row", [(rows // chunk * i + a, i) for i in range(blocks)])
+                for a in range(rows // chunk)
+            ],
+            axis=2,
+        )
+
     for d in slots:
+        if d == col_count - 1:
+            grad_out = jnp.stack(branches, axis=0)
+            grad_out, y_sum, _ = lax.optimization_barrier((grad_out, y_sum, shares[-1]))
+            grad_out = over_tokens(mixes_all, grad_out).astype(BF)
+        if d == 1:
+            beside, shares[0] = lax.optimization_barrier((beside, shares[0]))
+            branches = [branch] + [v[0] for v in beside]
+            if four:
+                branches.append(jnp.concatenate(far(*beside, col_count), axis=1)[0])
+            dn_sends, _ = lax.optimization_barrier((dn_sends, branches[-1]))
+            dn_got = exchange(dn_sends)
+        elif d > 1:
+            branches[d], shares[-1] = lax.optimization_barrier((branches[d], shares[-1]))
+        if d == 2 and four:
+            branches[2], branches[3] = lax.optimization_barrier((branches[2], branches[3]))
+        if d == col_count - 1:
+            early_prompt = lax.psum_scatter(
+                jnp.stack(prompts[:batch], axis=0), "row", scatter_dimension=2, tiled=True
+            )
+            branches[d], dn_got, grad_out, early_prompt = lax.optimization_barrier(
+                (branches[d], dn_got, grad_out, early_prompt)
+            )
+            early_prompt = to_owners(early_prompt)
+            grad_out = lax.psum_scatter(grad_out, "row", scatter_dimension=1, tiled=True)
         mix_grad = dot_nt(branches[d], out_all).astype(BF)
+        if d == 2:
+            sent[0] = swap(after(shares[1], mix_grad), 1, col_count)
         grad_q, grad_prompt, pair, gain_part = attend_back(
             row_word, qs[d], every[d], kvs[d], blocks, mix_grad, mixes[d], logs[d], scales[d],
             coses[d], sines[d], gain_q,
         )
         grad_qs.append(grad_q)
+        prompts.append(grad_prompt)
+        pairs.append(pair)
         gain_q_grad = gain_q_grad + gain_part[0]
-        prompt = lax.psum_scatter(grad_prompt, "row", scatter_dimension=1, tiled=True)
-        share, sums_one = input_share(grad_q, wide, normed[d], F32 if d == 0 else BF)
-        gain_one_grad = gain_one_grad + sums_one[0]
-        input_sum = input_sum + (share if d == 0 else swap(share, d, col_count).astype(F32))
-        chunk = prompt.shape[1]
-        prompt = jnp.concatenate(
-            [
-                lax.ppermute(prompt, "row", [(rows // chunk * i + a, i) for i in range(blocks)])
-                for a in range(rows // chunk)
-            ],
-            axis=1,
-        )
-        pair = pair + prompt.astype(F32)
-        key_dy = back_turn(pair[0], coses[d], sines[d])
-        key_hat = back_turn(kvs[d][0].astype(F32), coses[d], sines[d]) / gain_k
-        gain_k_grad = gain_k_grad + jnp.sum(key_dy * key_hat, axis=0)
-        key_raw = norm_back(key_dy, key_hat, scales[d][:, heads : heads + 1], gain_k)
-        grad_kv = jnp.concatenate([key_raw.astype(BF), pair[1].astype(BF)], axis=1)
-        grad_kvs.append(grad_kv)
-        kv_moved.append(grad_kv if d == 0 else swap(grad_kv, d, col_count))
-    normed_all = jnp.stack(normed, axis=0)
-    over_tokens = lambda a, b: lax.dot_general(
-        a, b, (((0, 1), (0, 1)), ((), ())), preferred_element_type=F32
-    )
-    grad_q = over_tokens(normed_all, jnp.stack(grad_qs, axis=0))
-    grad_q = lax.psum_scatter(grad_q.astype(BF), "row", scatter_dimension=0, tiled=True)
-    grad_out = over_tokens(jnp.stack(mixes, axis=0), jnp.stack(branches, axis=0))
-    grad_out = lax.psum_scatter(grad_out.astype(BF), "row", scatter_dimension=1, tiled=True)
-
-    kv_weight = jnp.concatenate([w for m in members for w in kv_pick(kv_all, m)], axis=1)
-    kv_share = dot_nt(jnp.concatenate(kv_moved, axis=1), kv_weight)
-    input_sum = input_sum + kv_share
-    x_wide = x_own.astype(F32)
-    x_spread = lax.rsqrt(jnp.mean(x_wide * x_wide, axis=-1, keepdims=True) + EPS)
-    x_hat = x_wide * x_spread
-    gain_one_grad = gain_one_grad / gain_one[0] + jnp.sum(kv_share * x_hat, axis=0)
-    input_grad = hidden_grad + norm_back(input_sum, x_hat, x_spread, gain_one)
-
-    grad_kv = over_tokens(normed_all, jnp.stack(grad_kvs, axis=0)).astype(BF)
+        if d == col_count - 1:
+            grad_q, prompts[-1], pairs[-1], sent, early_prompt, grad_out = lax.optimization_barrier(
+                (grad_q, prompts[-1], pairs[-1], sent, early_prompt, grad_out)
+            )
+        share = input_share(grad_q, wide, F32 if d == 0 else BF)
+        shares.append(share)
+        if d > 0:
+            sent.append(swap(share, d, col_count))
+    grad_q = over_tokens(normed_all, after(jnp.stack(grad_qs, axis=0), shares[-1]))
+    gain_one_grad = jnp.sum(grad_q * wide[:, : heads * HEAD].astype(F32), axis=1)
+    grad_q = grad_q.astype(BF)
+    late_prompt = lax.psum_scatter(
+        jnp.stack(prompts[batch:], axis=0), "row", scatter_dimension=2, tiled=True
+    )
+    early_prompt = after(early_prompt, shares[-1])
+    for first in range(0, col_count, batch):
+        prompt = early_prompt
+        if first > 0:
+            late_prompt, grad_q, _ = lax.optimization_barrier((late_prompt, grad_q, grad_kvs))
+            prompt = to_owners(late_prompt)
+        for d in range(first, first + batch):
+            pair = pairs[d] + prompt[d - first].astype(F32)
+            key_dy = back_turn(pair[0], coses[d], sines[d])
+            key_hat = back_turn(kvs[d][0].astype(F32), coses[d], sines[d]) / gain_k
+            gain_k_grad = gain_k_grad + jnp.sum(key_dy * key_hat, axis=0)
+            key_raw = norm_back(key_dy, key_hat, scales[d][:, heads : heads + 1], gain_k)
+            grad_kv = jnp.concatenate([key_raw.astype(BF), pair[1].astype(BF)], axis=1)
+            grad_kvs.append(grad_kv)
+            kv_moved.append(grad_kv if d == 0 else swap(grad_kv, d, col_count))
+    grad_q = lax.psum_scatter(grad_q, "row", scatter_dimension=0, tiled=True)
+
+    grad_kv = over_tokens(normed_all, jnp.stack(grad_kvs, axis=0))
+    gain_one_grad = gain_one_grad + jnp.sum(
+        grad_kv * wide[:, heads * HEAD : cols].astype(F32), axis=1
+    )
+    gain_one_grad = gain_one_grad / gain_one[0]
     grad_kv = lax.all_to_all(
-        grad_kv.reshape(devices, -1, 2 * HEAD), ("row", "col"), split_axis=0, concat_axis=0, tiled=True
+        grad_kv.astype(BF).reshape(devices, -1, 2 * HEAD),
+        ("row", "col"),
+        split_axis=0,
+        concat_axis=0,
+        tiled=True,
     )
     grad_kv = jnp.sum(grad_kv.astype(F32).reshape(row_count, col_count, -1, 2 * HEAD), axis=0)
     grad_kv = grad_kv.reshape(KEY_VALUE_HEADS, sharing, -1, 2, HEAD).sum(axis=1)
     grad_kv = grad_kv.transpose(1, 2, 0, 3).reshape(-1, 2 * kv_cols)
     tail = [grad_router, gain_two_grad, gain_one_grad, gain_q_grad, gain_k_grad]
     tail = [v.reshape(devices, -1) for v in tail]
+    tail.append(jnp.broadcast_to(jnp.sum(probs, axis=1)[None], (devices, experts)))
     cuts = [0]
     for v in tail:
         cuts.append(cuts[-1] + v.shape[1])
@@ -820,9 +981,28 @@
         jnp.concatenate(tail, axis=1), ("row", "col"), split_axis=0, concat_axis=0, tiled=True
     )
     tail = jnp.sum(tail, axis=0)
-    grad_router, gain_two_grad, gain_one_grad, gain_q_grad, gain_k_grad = [
+    grad_router, gain_two_grad, gain_one_grad, gain_q_grad, gain_k_grad, mean_probs = [
         tail[a:b] for a, b in zip(cuts[:-1], cuts[1:])
     ]
+    mean_probs = mean_probs / tokens
+    aux_loss = experts * jnp.sum(load * mean_probs)
+    expert_load = jnp.stack([experts * load, experts * mean_probs])
+
+    kv_share = dot_nt(jnp.concatenate(kv_moved, axis=1), kv_weight)
+    input_sum = shares[0] + kv_share
+    for got in sent:
+        input_sum = input_sum + got.astype(F32)
+    x_wide = x_own.astype(F32)
+    x_spread = lax.rsqrt(jnp.mean(x_wide * x_wide, axis=-1, keepdims=True) + EPS)
+    x_hat = x_wide * x_spread
+    input_grad = hidden_grad + norm_back(input_sum, x_hat, x_spread, gain_one)
+
+    own_grads, _ = lax.optimization_barrier((own_grads, shares[-1]))
+    ffe = w_gate.shape[2]
+    grad_gate = own_grads[0][:, :ffe] + sum(v[:, :ffe].astype(F32) for v in gu_got)
+    grad_up = own_grads[0][:, ffe:] + sum(v[:, ffe:].astype(F32) for v in gu_got)
+    grad_down = own_grads[1] + sum(v.astype(F32) for v in dn_got)
+    layer_output = (hidden + y_sum.astype(F32)).astype(BF)
 
     return (
         layer_output[None],

time: 1870 us -> 1360 us (0.73)
  waiting for transfers between devices: 885 us -> 505 us
  starting transfers between devices: 155 us -> 85.2 us
  local copies, waits for them, and re-layouts: 116 us -> 92 us
    ppermute x43, waiting for transfers between devices: 524 us -> 395 us  [swap(): return lax.ppermute(v, 'col', [(i, i ^ step) for i in range(count)])]
    ppermute x8 -> x4, waiting for transfers between devices: 77.1 us -> 0.01 us  [to_owners(): lax.ppermute(prompt, 'row', [(rows // chunk * i + a, i) for i in range(bl...]
    all_gather x6 -> x4, waiting for transfers between devices: 54.1 us -> 0.01 us  [the longest x2 0.01 us: per_device(): got = lax.all_gather(got, 'row', axis=0)]
    all_gather x1, waiting for transfers between devices: 53.6 us -> 0.01 us  [per_device(): wide = lax.all_gather(wide, 'row', axis=0, tiled=True)]
    reduce_scatter x7 -> x5, waiting for transfers between devices: 71 us -> 27.9 us  [the longest x1 23 us: per_device(): lax.psum_scatter(jnp.stack(prompts[:batch], axis=0), 'row', scatter_dimen...]
    reduce_scatter x1, waiting for transfers between devices: 78.3 us -> 35.7 us  [per_device(): y_sum = lax.psum_scatter(y_part, 'row', scatter_dimension=0)]
    slice x21 -> x10, local copies, waits for them, and re-layouts: 53.7 us -> 13 us  [the longest x4 5.76 us: halves(): return (v[:, :v.shape[1] // 2], v[:, v.shape[1] // 2:])]
    all_to_all x1, starting transfers between devices: 39.2 us -> 3.55 us  [per_device(): lax.all_to_all(grad_kv.astype(BF).reshape(devices, -1, 2 * HEAD), ('row',...]
  transfers between devices with their start and end apart: 71 -> 63, of which waited for: 33 -> 26; matrix products, arithmetic and copies ran while one was open for 20% -> 25% of each run, Pallas kernels for 11% -> 25%
where the time goes in v3:
time: 1360 us; the launch traced here: 1340 us
  waiting for transfers between devices  505 us (37%)
  Pallas kernels  368 us (27%)
  matrix products  154 us (11%)
  other arithmetic  106 us (8%)
  local copies, waits for them, and re-layouts  92 us (7%)
  starting transfers between devices  85.2 us (6%)
  between operations  17.5 us (1%)
  blocking collectives  14.6 us (1%)
    ppermute x43, waiting for transfers between devices, swap(): return lax.ppermute(v, 'col', [(i, i ^ step) for i in range(count)])  395 us
    pallas_call x4, Pallas kernels, expert(): call(expert_body, 'expert', (rows // tile,), [pl.BlockSpec((tile, width),...  118 us
    pallas_call x4, Pallas kernels, attend_back(): call(partial(attend_back_body, heads, per, blocks, rows), 'attend_back',...  68.1 us
    dot_general x8, matrix products, dot_tn(): lax.dot_general(a, b, (((0,), (0,)), ((), ())), preferred_element_type=F32)  62.3 us
    ppermute x43, starting transfers between devices, swap(): return lax.ppermute(v, 'col', [(i, i ^ step) for i in range(count)])  52.1 us
    pallas_call x2, Pallas kernels, combine(): call(partial(combine_body, count, cap, bool(scores)), 'combine', (sources...  47.4 us
    pallas_call x4, Pallas kernels, attend(): call(partial(attend_body, heads, per, blocks, rows), 'attend', (rows // C...  37.4 us
    unnamed x251, local copies, waits for them, and re-layouts  36.4 us
  transfers between devices with their start and end apart: 63, of which 26 were waited for; matrix products, arithmetic and copies ran while one was open for 25% of the time, Pallas kernels for 25%

profile of v3, /device:TPU:0, one launch (start us, length us, event | category | flops | bytes accessed | tf_op | source)
XLA Modules:
  0.0 1341.9 jit_solution(17134633735346110287)
XLA Ops:
  19.0 14.6 %all_gather.37 = s32[8,512,8]{1,2,0:T(8,128)S(1)} all-gather(s32[1,512,8]{1,2,0:T(8,128)S(1)} %copy-done.59), channel_id=1, replica_groups=mesh['row'=8,'col'=4] {'row'}, dimensions={0}, use_global_device_ids=true | all-gather | bytes 147456 | tf_op jit(solution)/shard_map/all_gather | solution.py:653
  51.3 11.9 collective-permute-done.2
  64.9 10.7 pad_maximum_fusion.16
  81.8 21.7 %collective-permute-done.4 = bf16[1,256,2048]{2,1,0:T(8,128)(2,1)S(1)} collective-permute-done((bf16[1,256,2048]{2,1,0:T(8,128)(2,1)S(1)}, bf16[1,256,2048]{2,1,0:T(8,128)(2,1)S(1)}, u32[]{:S(2)}, u32[]{:S(2)}) %collective-permute-start.4) | collective-permute-done | bytes 1048608 | tf_op jit(solution)/shard_map/ppermute | solution.py:567
  110.5 8.3 qkv.5
  118.8 8.4 qkv.6
  129.1 8.2 qkv.7
  137.3 8.8 qkv.4
  152.3 31.3 %collective-permute-done.6.wga_ref = bf16[1,1024,768]{2,1,0:T(8,128)(2,1)S(1)} collective-permute-done((bf16[1,1024,768]{2,1,0:T(8,128)(2,1)S(1)}, bf16[1,1024,768]{2,1,0:T(8,128)(2,1)S(1)}, u32[]{:S(2)}, u32[]{:S(2)}) %collective-permute-start.6) | collective-permute-done | bytes 1572896 | tf_op jit(solution)/shard_map/ppermute | solution.py:567
  185.9 9.6 attend.4
  201.0 32.0 %collective-permute-done.8.wgb_ref = bf16[1,1024,768]{2,1,0:T(8,128)(2,1)S(1)} collective-permute-done((bf16[1,1024,768]{2,1,0:T(8,128)(2,1)}, bf16[1,1024,768]{2,1,0:T(8,128)(2,1)S(1)}, u32[]{:S(2)}, u32[]{:S(2)}) %collective-permute-start.8) | collective-permute-done | bytes 1572896 | tf_op jit(solution)/shard_map/ppermute | solution.py:567
  238.8 9.3 attend.5
  248.1 18.7 %collective-permute-done.10.wua_ref = bf16[1,1024,768]{2,1,0:T(8,128)(2,1)} collective-permute-done((bf16[1,1024,768]{2,1,0:T(8,128)(2,1)S(1)}, bf16[1,1024,768]{2,1,0:T(8,128)(2,1)}, u32[]{:S(2)}, u32[]{:S(2)}) %collective-permute-start.10) | collective-permute-done | bytes 1572896 | tf_op jit(solution)/shard_map/ppermute | solution.py:567
  266.9 6.3 convolution_convert_fusion.7
  273.9 9.4 attend.6
  290.1 9.1 attend.7
  299.2 66.0 %collective-permute-done.13 = bf16[512,2048]{1,0:T(8,128)(2,1)} collective-permute-done((bf16[512,2048]{1,0:T(8,128)(2,1)}, bf16[512,2048]{1,0:T(8,128)(2,1)}, u32[]{:S(2)}, u32[]{:S(2)}) %collective-permute-start.13) | collective-permute-done | bytes 2097184 | tf_op jit(solution)/shard_map/ppermute | solution.py:567
  382.5 98.4 %collective-permute-done.15.wub_ref = bf16[1,1024,768]{2,1,0:T(8,128)(2,1)} collective-permute-done((bf16[1,1024,768]{2,1,0:T(8,128)(2,1)}, bf16[1,1024,768]{2,1,0:T(8,128)(2,1)}, u32[]{:S(2)}, u32[]{:S(2)}) %collective-permute-start.15) | collective-permute-done | bytes 1572896 | tf_op jit(solution)/shard_map/ppermute | solution.py:567
  493.4 16.8 %dispatch.1 = (bf16[8,128,2048]{2,1,0:T(8,128)(2,1)}, bf16[8,128,2048]{2,1,0:T(8,128)(2,1)}, bf16[8,128,2048]{2,1,0:T(8,128)(2,1)}, bf16[8,128,2048]{2,1,0:T(8,128)(2,1)}) custom-call(s32[8,4,512]{2,1,0:T(4,128)} %copy.122.rank_ref, bf16[8,512,2048]{2,1,0:T(8,128)(2,1)} %bitcast.292), custom_call_target="tpu_custom_call" | custom-call | flops 8589934592 | bytes 33554432 | tf_op jit(solution)/shard_map/dispatch/pallas_call | solution.py:366
  510.2 9.5 collective-permute-done.19.wga_ref
  520.3 15.6 %all-gather.22.cloned.1.call-done = bf16[4096,2048]{1,0:T(8,128)(2,1)} async-done(((bf16[512,2048]{1,0:T(8,128)(2,1)}), bf16[4096,2048]{1,0:T(8,128)(2,1)}) %all-gather.22.cloned.1.call-update) | async-done | bytes 16777232 | tf_op jit(solution)/shard_map/all_gather | solution.py:742
  535.9 21.9 %route_dispatch.1 = (f32[4,8,128,1]{3,2,1,0:T(8,128)}, bf16[8,128,2048]{2,1,0:T(8,128)(2,1)}, bf16[8,128,2048]{2,1,0:T(8,128)(2,1)}, bf16[8,128,2048]{2,1,0:T(8,128)(2,1)}, bf16[8,128,2048]{2,1,0:T(8,128)(2,1)}) custom-call(s32[4]{0:T(128)} %pad_add_fusion.2.ids_ref, s32[8,4,512]{2,1,0:T(4,128)} %copy.122.rank_ref, bf16[8,512,2048]{2,1,0:T(8,128)(2,1)} %bitcast.293, ...), custom_call_target="tpu_custom_call" | custom-call | flops 8589934592 | bytes 33554432 | tf_op jit(solution)/shard_map/route_dispatch/pallas_call | solution.py:402
  560.7 29.3 %expert.4 = (bf16[1024,2048]{1,0:T(8,128)(2,1)}, bf16[1024,2048]{1,0:T(8,128)(2,1)}, bf16[1024,768]{1,0:T(8,128)(2,1)}, bf16[1024,1536]{1,0:T(8,128)(2,1)}, bf16[1024,128]{1,0:T(8,128)(2,1)}) custom-call(bf16[1024,2048]{1,0:T(8,128)(2,1)} %bitcast.314, bf16[1024,2048]{1,0:T(8,128)(2,1)} %bitcast.257, f32[1024,1]{1,0:T(8,128)} %bitcast.281, ...), custom_call_target="tpu_custom_call" | custom-call | flops 19327352832 | bytes 30932992 | tf_op jit(solution)/shard_map/expert/pallas_call | solution.py:537
  590.3 29.4 %expert.5 = (bf16[1024,2048]{1,0:T(8,128)(2,1)}, bf16[1024,2048]{1,0:T(8,128)(2,1)}, bf16[1024,768]{1,0:T(8,128)(2,1)}, bf16[1024,1536]{1,0:T(8,128)(2,1)}, bf16[1024,128]{1,0:T(8,128)(2,1)}) custom-call(bf16[1024,2048]{1,0:T(8,128)(2,1)} %bitcast.324, bf16[1024,2048]{1,0:T(8,128)(2,1)} %bitcast.321, f32[1024,1]{1,0:T(8,128)} %bitcast.280, ...), custom_call_target="tpu_custom_call" | custom-call | flops 19327352832 | bytes 30932992 | tf_op jit(solution)/shard_map/expert/pallas_call | solution.py:537
  619.8 6.5 convolution_convert_fusion.5
  626.4 7.4 convolution_convert_fusion.2
  637.2 29.5 %expert.6 = (bf16[1024,2048]{1,0:T(8,128)(2,1)}, bf16[1024,2048]{1,0:T(8,128)(2,1)}, bf16[1024,768]{1,0:T(8,128)(2,1)}, bf16[1024,1536]{1,0:T(8,128)(2,1)}, bf16[1024,128]{1,0:T(8,128)(2,1)}) custom-call(bf16[1024,2048]{1,0:T(8,128)(2,1)} %bitcast.316, bf16[1024,2048]{1,0:T(8,128)(2,1)} %bitcast.310, f32[1024,1]{1,0:T(8,128)} %bitcast.279, ...), custom_call_target="tpu_custom_call" | custom-call | flops 19327352832 | bytes 30932992 | tf_op jit(solution)/shard_map/expert/pallas_call | solution.py:537
  666.7 29.3 %expert.7 = (bf16[1024,2048]{1,0:T(8,128)(2,1)}, bf16[1024,2048]{1,0:T(8,128)(2,1)}, bf16[1024,768]{1,0:T(8,128)(2,1)}, bf16[1024,1536]{1,0:T(8,128)(2,1)}, bf16[1024,128]{1,0:T(8,128)(2,1)}) custom-call(bf16[1024,2048]{1,0:T(8,128)(2,1)} %bitcast.318, bf16[1024,2048]{1,0:T(8,128)(2,1)} %bitcast.312, f32[1024,1]{1,0:T(8,128)} %bitcast.278, ...), custom_call_target="tpu_custom_call" | custom-call | flops 19327352832 | bytes 30932992 | tf_op jit(solution)/shard_map/expert/pallas_call | solution.py:537
  696.0 8.6 collective-permute-done.25
  705.8 25.0 %combine.2 = (bf16[8,512,2048]{2,1,0:T(8,128)(2,1)}, f32[8,512,4]{2,1,0:T(8,128)}) custom-call(s32[8,512,4]{2,1,0:T(8,128)} %bitcast.253, bf16[8,128,2048]{2,1,0:T(8,128)(2,1)} %bitcast.320, bf16[8,128,2048]{2,1,0:T(8,128)(2,1)} %bitcast.326, bf16[8,128,2048]{2,1,0:T(8,128)(2,1)} %bitcast.327, bf16[8,128,2048]{2,1,0:T(8,128)(2,1)} %bitcast.323, ...), custom_call_target="tpu_custom_call" | custom-call | flops 8589934592 | bytes 33554432 | tf_op jit(solution)/shard_map/combine/pallas_call | solution.py:473
  739.7 10.6 add_convert_fusion
  750.8 9.2 add_convert_fusion.1
  761.5 13.5 %collective-permute-done.29 = bf16[384,2048]{1,0:T(8,128)(2,1)S(1)} collective-permute-done((bf16[384,2048]{1,0:T(8,128)(2,1)S(1)}, bf16[384,2048]{1,0:T(8,128)(2,1)S(1)}, u32[]{:S(2)}, u32[]{:S(2)}) %collective-permute-start.29) | collective-permute-done | bytes 1572896 | tf_op jit(solution)/shard_map/ppermute | solution.py:567
  802.9 22.4 %combine.3 = bf16[8,512,2048]{2,1,0:T(8,128)(2,1)} custom-call(s32[8,512,4]{2,1,0:T(8,128)} %bitcast.254, bf16[8,128,2048]{2,1,0:T(8,128)(2,1)} %bitcast.259, bf16[8,128,2048]{2,1,0:T(8,128)(2,1)} %bitcast.261, bf16[8,128,2048]{2,1,0:T(8,128)(2,1)} %bitcast.262, bf16[8,128,2048]{2,1,0:T(8,128)(2,1)} %bitcast.260), custom_call_target="tpu_custom_call" | custom-call | flops 8589934592 | bytes 33554432 | tf_op jit(solution)/shard_map/combine/pallas_call | solution.py:473
  825.3 8.5 add_convert_fusion.2
  838.8 9.5 fusion.103
  855.5 52.6 %collective-permute-done.28 = bf16[2048,1536]{1,0:T(8,128)(2,1)} collective-permute-done((bf16[2048,1536]{1,0:T(8,128)(2,1)}, bf16[2048,1536]{1,0:T(8,128)(2,1)}, u32[]{:S(2)}, u32[]{:S(2)}) %collective-permute-start.28) | collective-permute-done | bytes 6291488 | tf_op jit(solution)/shard_map/ppermute | solution.py:567
  909.7 5.5 multiply_reduce_fusion.1
  925.8 16.9 %attend_back.4 = (bf16[512,1024]{1,0:T(8,128)(2,1)}, bf16[2,2048,128]{2,1,0:T(8,128)(2,1)}, f32[2,512,128]{2,1,0:T(8,128)}, f32[8,128]{1,0:T(8,128)}) custom-call(s32[1]{0:T(128)} %bitcast.1.row_ref, bf16[8,512,128]{2,1,0:T(8,128)(2,1)} %get-tuple-element.259.q_ref, bf16[8,4,512,128]{3,2,1,0:T(8,128)(2,1)} %bitcast.298, bf16[8,4,512,128]{3,2,1,0:T(8,128)(2,1)} %bitcast.299, ...), custom_call_target="tpu_custom_call" | custom-call | flops 24159191040 | bytes 6291456 | tf_op jit(solution)/shard_map/attend_back/pallas_call | solution.py:315
  942.7 6.3 input_share.4
  949.0 16.0 %collective-permute-done.31 = bf16[1,512,2048]{2,1,0:T(8,128)(2,1)S(1)} collective-permute-done((bf16[1,512,2048]{2,1,0:T(8,128)(2,1)S(1)}, bf16[1,512,2048]{2,1,0:T(8,128)(2,1)S(1)}, u32[]{:S(2)}, u32[]{:S(2)}) %collective-permute-start.31) | collective-permute-done | bytes 2097184 | tf_op jit(solution)/shard_map/ppermute | solution.py:567
  969.6 5.6 fusion.22.do_ref
  975.2 17.3 %attend_back.5 = (bf16[512,1024]{1,0:T(8,128)(2,1)}, bf16[2,2048,128]{2,1,0:T(8,128)(2,1)}, f32[2,512,128]{2,1,0:T(8,128)}, f32[8,128]{1,0:T(8,128)}) custom-call(s32[1]{0:T(128)} %bitcast.1.row_ref, bf16[8,512,128]{2,1,0:T(8,128)(2,1)} %get-tuple-element.246.q_ref, bf16[8,4,512,128]{3,2,1,0:T(8,128)(2,1)} %bitcast.306, bf16[8,4,512,128]{3,2,1,0:T(8,128)(2,1)} %bitcast.307, ...), custom_call_target="tpu_custom_call" | custom-call | flops 24159191040 | bytes 6291456 | tf_op jit(solution)/shard_map/attend_back/pallas_call | solution.py:315
  992.5 6.3 input_share.5
  1010.3 17.0 %attend_back.6 = (bf16[512,1024]{1,0:T(8,128)(2,1)}, bf16[2,2048,128]{2,1,0:T(8,128)(2,1)}, f32[2,512,128]{2,1,0:T(8,128)}, f32[8,128]{1,0:T(8,128)}) custom-call(s32[1]{0:T(128)} %bitcast.1.row_ref, bf16[8,512,128]{2,1,0:T(8,128)(2,1)} %get-tuple-element.251.q_ref, bf16[8,4,512,128]{3,2,1,0:T(8,128)(2,1)} %bitcast.308, bf16[8,4,512,128]{3,2,1,0:T(8,128)(2,1)} %bitcast.309, ...), custom_call_target="tpu_custom_call" | custom-call | flops 24159191040 | bytes 6291456 | tf_op jit(solution)/shard_map/attend_back/pallas_call | solution.py:315
  1027.3 6.1 input_share.6
  1033.3 5.8 pad_maximum_fusion
  1039.1 35.7 %reduce-scatter.9.cloned.1.call-done = bf16[1,512,2048]{2,1,0:T(8,128)(2,1)} async-done(((bf16[8,512,2048]{2,1,0:T(8,128)(2,1)}), bf16[1,512,2048]{2,1,0:T(8,128)(2,1)}) %reduce-scatter.9.cloned.1.call-update) | async-done | bytes 2097168 | tf_op jit(solution)/shard_map/reduce_scatter | solution.py:858
  1074.8 13.7 %bitcast_convert_fusion = bf16[1024,2048]{1,0:T(8,128)(2,1)} fusion(bf16[4,512,2048]{2,1,0:T(8,128)(2,1)} %pad_maximum_fusion, bf16[1,512,1024]{2,1,0:T(8,128)(2,1)S(1)} %bitcast.336, bf16[1,512,1024]{2,1,0:T(8,128)(2,1)} %bitcast.338, bf16[1,512,1024]{2,1,0:T(8,128)(2,1)} %bitcast.337, bf16[1,512,1024]{2,1,0:T(8,128)(2,1)} %bitcast.339), kind=kOutput, calls=%fused_computation.4 | convolution fusion | flops 8598323200 | bytes 16777216 | tf_op jit(solution)/shard_map/dot_general | solution.py:876
  1088.6 23.0 %reduce-scatter.11.cloned.1.call-done = bf16[2,2,256,128]{3,2,1,0:T(8,128)(2,1)} async-done(((bf16[2,2,2048,128]{3,2,1,0:T(8,128)(2,1)}), bf16[2,2,256,128]{3,2,1,0:T(8,128)(2,1)}) %reduce-scatter.11.cloned.1.call-update) | async-done | bytes 262160 | tf_op jit(solution)/shard_map/reduce_scatter | solution.py:909
  1124.5 5.6 convolution_convert_fusion.9.do_ref
  1130.0 17.0 %attend_back.7 = (bf16[512,1024]{1,0:T(8,128)(2,1)}, bf16[2,2048,128]{2,1,0:T(8,128)(2,1)}, f32[2,512,128]{2,1,0:T(8,128)}, f32[8,128]{1,0:T(8,128)}) custom-call(s32[1]{0:T(128)} %bitcast.1.row_ref, bf16[8,512,128]{2,1,0:T(8,128)(2,1)} %get-tuple-element.255.q_ref, bf16[8,4,512,128]{3,2,1,0:T(8,128)(2,1)} %bitcast.300, bf16[8,4,512,128]{3,2,1,0:T(8,128)(2,1)} %bitcast.301, ...), custom_call_target="tpu_custom_call" | custom-call | flops 24159191040 | bytes 6291456 | tf_op jit(solution)/shard_map/attend_back/pallas_call | solution.py:315
  1156.2 8.4 collective-permute-done.37
  1169.6 6.1 input_share.7
  1183.0 15.7 %fusion.100 = (bf16[2048,1024]{0,1:T(8,128)(2,1)}, f32[2048,1024]{0,1:T(8,128)}) fusion(bf16[4,512,1024]{2,1,0:T(8,128)(2,1)} %pad_maximum_fusion.2, bf16[1,512,2048]{2,1,0:T(8,128)(2,1)} %bitcast.332, bf16[1,512,2048]{2,1,0:T(8,128)(2,1)} %bitcast.330, bf16[1,512,2048]{2,1,0:T(8,128)(2,1)} %bitcast.328, bf16[1,512,2048]{2,1,0:T(8,128)(2,1)} %bitcast.334), kind=kOutput, calls=%fused_computation.261 | convolution fusion | flops 8604614656 | bytes 25165824 | tf_op jit(solution)/shard_map/dot_general | solution.py:876
  1198.7 9.4 copy.130
  1213.3 6.7 multiply_reduce_fusion
  1220.0 7.9 add_bitcast_fusion
  1227.8 8.8 add_bitcast_fusion.1
  1257.2 18.2 %all-to-all-start.1 = ((f32[32,1,2216]{2,1,0:T(1,128)}), f32[32,1,2216]{2,1,0:T(1,128)S(1)}, u32[]{:S(2)}, u32[]{:S(2)}) async-start(f32[32,1,2216]{2,1,0:T(1,128)} %copy.132), calls=%async_computation.6 | async-start | bytes 589824 | tf_op jit(solution)/shard_map/all_to_all | solution.py:980
  1275.5 6.8 fusion.105
  1282.2 8.3 all-to-all-done.1
  1294.1 6.8 fusion.2
  1307.9 22.6 %all-to-all-done.2 = bf16[32,64,256]{2,1,0:T(8,128)(2,1)S(1)} async-done(((bf16[32,64,256]{2,1,0:T(8,128)(2,1)}), bf16[32,64,256]{2,1,0:T(8,128)(2,1)S(1)}, u32[]{:S(2)}, u32[]{:S(2)}) %all-to-all-start.2) | async-done | bytes 1048608 | tf_op jit(solution)/shard_map/all_to_all | solution.py:964
  (522 shorter events, 263.3 us)
Async XLA Ops:
  7.2 98.2 %all-gather.12.cloned.1.call-start = ((), (), s32[]{:S(2)}) async-start(), calls=%async_computation.9 | async-start | bytes 6488064 | tf_op jit(solution)/shard_map/all_gather | solution.py:641
  14.4 114.6 %all-gather.14.cloned.1.call-start = ((), (), s32[]{:S(2)}) async-start(), calls=%async_computation.10 | async-start | bytes 4718592 | tf_op jit(solution)/shard_map/all_gather | solution.py:689
  14.4 62.6 %collective-permute-start = (bf16[1,512,2048]{2,1,0:T(8,128)(2,1)S(1)}, bf16[1,512,2048]{2,1,0:T(8,128)(2,1)}, u32[]{:S(2)}, u32[]{:S(2)}) collective-permute-start(bf16[1,512,2048]{2,1,0:T(8,128)(2,1)S(1)} %copy-done.4), channel_id=1, source_target_pairs={{0,1},{1,0},{2,3},{3,2},{4,5},{5,4},{6,7},{7,6},{8,9},{9,8},{10,11... | collective-permute-start | bytes 6291464 | tf_op jit(solution)/shard_map/ppermute | solution.py:567
  17.4 59.6 %collective-permute-start.1 = (bf16[1,512,2048]{2,1,0:T(8,128)(2,1)S(1)}, bf16[1,512,2048]{2,1,0:T(8,128)(2,1)}, u32[]{:S(2)}, u32[]{:S(2)}) collective-permute-start(bf16[1,512,2048]{2,1,0:T(8,128)(2,1)S(1)} %copy-done.4), channel_id=1, source_target_pairs={{0,2},{1,3},{2,0},{3,1},{4,6},{5,7},{6,4},{7,5},{8,10},{9,11},{10,... | collective-permute-start | bytes 6291464 | tf_op jit(solution)/shard_map/ppermute | solution.py:567
  34.6 28.6 %collective-permute-start.2 = (f32[32]{0:T(128)S(1)}, f32[32]{0:T(128)S(1)}, u32[]{:S(2)}, u32[]{:S(2)}) collective-permute-start(f32[32]{0:T(128)S(1)} %convert_reduce_fusion.3), channel_id=1, source_target_pairs={{0,1},{1,0},{2,3},{3,2},{4,5},{5,4},{6,7},{7,6},{8,9},{9,8},{10,11... | collective-permute-start | bytes 392 | tf_op jit(solution)/shard_map/ppermute | solution.py:567
  63.2 13.4 collective-permute-start.3
  77.1 108.8 %all-gather.18.cloned.1.call-start = ((), (), s32[]{:S(2)}) async-start(), calls=%async_computation.18 | async-start | bytes 4718592 | tf_op jit(solution)/shard_map/all_gather | solution.py:705
  79.8 23.8 %collective-permute-start.4 = (bf16[1,256,2048]{2,1,0:T(8,128)(2,1)S(1)}, bf16[1,256,2048]{2,1,0:T(8,128)(2,1)S(1)}, u32[]{:S(2)}, u32[]{:S(2)}) collective-permute-start(bf16[1,256,2048]{2,1,0:T(8,128)(2,1)S(1)} %slice.253), channel_id=1, source_target_pairs={{0,2},{1,3},{2,0},{3,1},{4,6},{5,7},{6,4},{7,5},{8,10},{9,11},{10,... | collective-permute-start | bytes 3145736 | tf_op jit(solution)/shard_map/ppermute | solution.py:567
  80.1 23.8 %collective-permute-start.5 = (bf16[1,256,2048]{2,1,0:T(8,128)(2,1)S(1)}, bf16[1,256,2048]{2,1,0:T(8,128)(2,1)S(1)}, u32[]{:S(2)}, u32[]{:S(2)}) collective-permute-start(bf16[1,256,2048]{2,1,0:T(8,128)(2,1)S(1)} %slice.254), channel_id=1, source_target_pairs={{0,1},{1,0},{2,3},{3,2},{4,5},{5,4},{6,7},{7,6},{8,9},{9,8},{10,11... | collective-permute-start | bytes 3145736 | tf_op jit(solution)/shard_map/ppermute | solution.py:567
  110.5 263.7 %copy-start.56 = (f32[2048]{0:T(1024)}, f32[2048]{0:T(1024)S(1)}, u32[]{:S(2)}) copy-start(f32[2048]{0:T(1024)S(1)} %get-tuple-element.516) | copy-start | bytes 24580
  129.0 144.9 %all-gather.20.cloned.1.call-start = ((), (), s32[]{:S(2)}) async-start(), calls=%async_computation.19 | async-start | bytes 4718592 | tf_op jit(solution)/shard_map/all_gather | solution.py:705
  147.9 345.5 %all-gather.24.cloned.1.call-start = ((), (), s32[]{:S(2)}) async-start(), calls=%async_computation.21 | async-start | bytes 18874368 | tf_op jit(solution)/shard_map/all_gather | solution.py:738
  149.3 34.3 %collective-permute-start.6 = (bf16[1,1024,768]{2,1,0:T(8,128)(2,1)S(1)}, bf16[1,1024,768]{2,1,0:T(8,128)(2,1)S(1)}, u32[]{:S(2)}, u32[]{:S(2)}) collective-permute-start(bf16[1,1024,768]{2,1,0:T(8,128)(2,1)S(1)} %get-tuple-element.555), channel_id=1, source_target_pairs={{0,1},{1,0},{2,3},{3,2},{4,5},{5,4},{6,7},{7,6},{8,9},{9,8},{10,11... | collective-permute-start | bytes 4718600 | tf_op jit(solution)/shard_map/ppermute | solution.py:567
  150.8 33.3 %collective-permute-start.7 = (bf16[1,1024,768]{2,1,0:T(8,128)(2,1)S(1)}, bf16[1,1024,768]{2,1,0:T(8,128)(2,1)S(1)}, u32[]{:S(2)}, u32[]{:S(2)}) collective-permute-start(bf16[1,1024,768]{2,1,0:T(8,128)(2,1)S(1)} %get-tuple-element.555), channel_id=1, source_target_pairs={{0,2},{1,3},{2,0},{3,1},{4,6},{5,7},{6,4},{7,5},{8,10},{9,11},{10,... | collective-permute-start | bytes 4718600 | tf_op jit(solution)/shard_map/ppermute | solution.py:567
  195.5 340.4 %all-gather.22.cloned.1.call-start = ((), (), s32[]{:S(2)}) async-start(), calls=%async_computation.20 | async-start | bytes 18874368 | tf_op jit(solution)/shard_map/all_gather | solution.py:742
  195.6 37.5 %collective-permute-start.8 = (bf16[1,1024,768]{2,1,0:T(8,128)(2,1)}, bf16[1,1024,768]{2,1,0:T(8,128)(2,1)S(1)}, u32[]{:S(2)}, u32[]{:S(2)}) collective-permute-start(bf16[1,1024,768]{2,1,0:T(8,128)(2,1)} %get-tuple-element.554), channel_id=1, source_target_pairs={{0,1},{1,0},{2,3},{3,2},{4,5},{5,4},{6,7},{7,6},{8,9},{9,8},{10,11... | collective-permute-start | bytes 4718600 | tf_op jit(solution)/shard_map/ppermute | solution.py:567
  196.2 37.5 %collective-permute-start.9 = (bf16[1,1024,768]{2,1,0:T(8,128)(2,1)}, bf16[1,1024,768]{2,1,0:T(8,128)(2,1)S(1)}, u32[]{:S(2)}, u32[]{:S(2)}) collective-permute-start(bf16[1,1024,768]{2,1,0:T(8,128)(2,1)} %get-tuple-element.554), channel_id=1, source_target_pairs={{0,2},{1,3},{2,0},{3,1},{4,6},{5,7},{6,4},{7,5},{8,10},{9,11},{10,... | collective-permute-start | bytes 4718600 | tf_op jit(solution)/shard_map/ppermute | solution.py:567
  199.0 67.9 %collective-permute-start.10 = (bf16[1,1024,768]{2,1,0:T(8,128)(2,1)S(1)}, bf16[1,1024,768]{2,1,0:T(8,128)(2,1)}, u32[]{:S(2)}, u32[]{:S(2)}) collective-permute-start(bf16[1,1024,768]{2,1,0:T(8,128)(2,1)S(1)} %get-tuple-element.553), channel_id=1, source_target_pairs={{0,1},{1,0},{2,3},{3,2},{4,5},{5,4},{6,7},{7,6},{8,9},{9,8},{10,11... | collective-permute-start | bytes 4718600 | tf_op jit(solution)/shard_map/ppermute | solution.py:567
  199.6 67.3 %collective-permute-start.11 = (bf16[1,1024,768]{2,1,0:T(8,128)(2,1)S(1)}, bf16[1,1024,768]{2,1,0:T(8,128)(2,1)}, u32[]{:S(2)}, u32[]{:S(2)}) collective-permute-start(bf16[1,1024,768]{2,1,0:T(8,128)(2,1)S(1)} %get-tuple-element.553), channel_id=1, source_target_pairs={{0,2},{1,3},{2,0},{3,1},{4,6},{5,7},{6,4},{7,5},{8,10},{9,11},{10,... | collective-permute-start | bytes 4718600 | tf_op jit(solution)/shard_map/ppermute | solution.py:567
  237.4 127.8 %collective-permute-start.12 = (bf16[512,2048]{1,0:T(8,128)(2,1)}, bf16[512,2048]{1,0:T(8,128)(2,1)S(1)}, u32[]{:S(2)}, u32[]{:S(2)}) collective-permute-start(bf16[512,2048]{1,0:T(8,128)(2,1)} %convolution_convert_fusion.8), channel_id=1, source_target_pairs={{0,1},{1,0},{2,3},{3,2},{4,5},{5,4},{6,7},{7,6},{8,9},{9,8},{10,11... | collective-permute-start | bytes 6291464 | tf_op jit(solution)/shard_map/ppermute | solution.py:567
  273.1 92.0 %collective-permute-start.13 = (bf16[512,2048]{1,0:T(8,128)(2,1)}, bf16[512,2048]{1,0:T(8,128)(2,1)}, u32[]{:S(2)}, u32[]{:S(2)}) collective-permute-start(bf16[512,2048]{1,0:T(8,128)(2,1)} %convolution_convert_fusion.7), channel_id=1, source_target_pairs={{0,2},{1,3},{2,0},{3,1},{4,6},{5,7},{6,4},{7,5},{8,10},{9,11},{10,... | collective-permute-start | bytes 6291464 | tf_op jit(solution)/shard_map/ppermute | solution.py:567
  288.1 82.0 %collective-permute-start.14 = (bf16[512,2048]{1,0:T(8,128)(2,1)}, bf16[512,2048]{1,0:T(8,128)(2,1)S(1)}, u32[]{:S(2)}, u32[]{:S(2)}) collective-permute-start(bf16[512,2048]{1,0:T(8,128)(2,1)} %convolution_convert_fusion.6), channel_id=1, source_target_pairs={{0,3},{1,2},{2,1},{3,0},{4,7},{5,6},{6,5},{7,4},{8,11},{9,10},{10,... | collective-permute-start | bytes 6291464 | tf_op jit(solution)/shard_map/ppermute | solution.py:567
  377.9 327.9 %all-gather.16.cloned.1.call-start = ((), (), s32[]{:S(2)}) async-start(), calls=%async_computation.11 | async-start | bytes 4718592 | tf_op jit(solution)/shard_map/all_gather | solution.py:767
  378.4 103.7 %collective-permute-start.17 = (bf16[1,768,2048]{2,1,0:T(8,128)(2,1)}, bf16[1,768,2048]{2,1,0:T(8,128)(2,1)}, u32[]{:S(2)}, u32[]{:S(2)}) collective-permute-start(bf16[1,768,2048]{2,1,0:T(8,128)(2,1)} %wdb_ref), channel_id=1, source_target_pairs={{0,1},{1,0},{2,3},{3,2},{4,5},{5,4},{6,7},{7,6},{8,9},{9,8},{10,11... | collective-permute-start | bytes 9437192 | tf_op jit(solution)/shard_map/ppermute | solution.py:567
  379.9 102.3 %collective-permute-start.18 = (bf16[1,768,2048]{2,1,0:T(8,128)(2,1)}, bf16[1,768,2048]{2,1,0:T(8,128)(2,1)}, u32[]{:S(2)}, u32[]{:S(2)}) collective-permute-start(bf16[1,768,2048]{2,1,0:T(8,128)(2,1)} %wdb_ref), channel_id=1, source_target_pairs={{0,2},{1,3},{2,0},{3,1},{4,6},{5,7},{6,4},{7,5},{8,10},{9,11},{10,... | collective-permute-start | bytes 9437192 | tf_op jit(solution)/shard_map/ppermute | solution.py:567
  380.2 100.6 %collective-permute-start.15 = (bf16[1,1024,768]{2,1,0:T(8,128)(2,1)}, bf16[1,1024,768]{2,1,0:T(8,128)(2,1)}, u32[]{:S(2)}, u32[]{:S(2)}) collective-permute-start(bf16[1,1024,768]{2,1,0:T(8,128)(2,1)} %get-tuple-element.552), channel_id=1, source_target_pairs={{0,1},{1,0},{2,3},{3,2},{4,5},{5,4},{6,7},{7,6},{8,9},{9,8},{10,11... | collective-permute-start | bytes 4718600 | tf_op jit(solution)/shard_map/ppermute | solution.py:567
  380.8 101.3 %collective-permute-start.16 = (bf16[1,1024,768]{2,1,0:T(8,128)(2,1)}, bf16[1,1024,768]{2,1,0:T(8,128)(2,1)}, u32[]{:S(2)}, u32[]{:S(2)}) collective-permute-start(bf16[1,1024,768]{2,1,0:T(8,128)(2,1)} %get-tuple-element.552), channel_id=1, source_target_pairs={{0,2},{1,3},{2,0},{3,1},{4,6},{5,7},{6,4},{7,5},{8,10},{9,11},{10,... | collective-permute-start | bytes 4718600 | tf_op jit(solution)/shard_map/ppermute | solution.py:567
  482.1 37.6 %collective-permute-start.19 = (bf16[1,1024,768]{2,1,0:T(8,128)(2,1)}, bf16[1,1024,768]{2,1,0:T(8,128)(2,1)}, u32[]{:S(2)}, u32[]{:S(2)}) collective-permute-start(bf16[1,1024,768]{2,1,0:T(8,128)(2,1)} %copy-done.88), channel_id=1, source_target_pairs={{0,2},{1,3},{2,0},{3,1},{4,6},{5,7},{6,4},{7,5},{8,10},{9,11},{10,... | collective-permute-start | bytes 4718600 | tf_op jit(solution)/shard_map/ppermute | solution.py:567
  482.4 37.8 %collective-permute-start.20 = (bf16[1,1024,768]{2,1,0:T(8,128)(2,1)}, bf16[1,1024,768]{2,1,0:T(8,128)(2,1)}, u32[]{:S(2)}, u32[]{:S(2)}) collective-permute-start(bf16[1,1024,768]{2,1,0:T(8,128)(2,1)} %copy-done.89), channel_id=1, source_target_pairs={{0,1},{1,0},{2,3},{3,2},{4,5},{5,4},{6,7},{7,6},{8,9},{9,8},{10,11... | collective-permute-start | bytes 4718600 | tf_op jit(solution)/shard_map/ppermute | solution.py:567
  485.5 72.4 %collective-permute-start.21 = (bf16[1,1024,768]{2,1,0:T(8,128)(2,1)}, bf16[1,1024,768]{2,1,0:T(8,128)(2,1)}, u32[]{:S(2)}, u32[]{:S(2)}) collective-permute-start(bf16[1,1024,768]{2,1,0:T(8,128)(2,1)} %collective-permute-done.10.wua_ref), channel_id=1, source_target_pairs={{0,2},{1,3},{2,0},{3,1},{4,6},{5,7},{6,4},{7,5},{8,10},{9,11},{10,... | collective-permute-start | bytes 4718600 | tf_op jit(solution)/shard_map/ppermute | solution.py:567
  487.2 70.7 %collective-permute-start.22 = (bf16[1,1024,768]{2,1,0:T(8,128)(2,1)}, bf16[1,1024,768]{2,1,0:T(8,128)(2,1)}, u32[]{:S(2)}, u32[]{:S(2)}) collective-permute-start(bf16[1,1024,768]{2,1,0:T(8,128)(2,1)} %collective-permute-done.16.wub_ref), channel_id=1, source_target_pairs={{0,1},{1,0},{2,3},{3,2},{4,5},{5,4},{6,7},{7,6},{8,9},{9,8},{10,11... | collective-permute-start | bytes 4718600 | tf_op jit(solution)/shard_map/ppermute | solution.py:567
  491.5 98.6 %collective-permute-start.23 = (bf16[1,384,2048]{2,1,0:T(8,128)(2,1)S(1)}, bf16[1,384,2048]{2,1,0:T(8,128)(2,1)}, u32[]{:S(2)}, u32[]{:S(2)}) collective-permute-start(bf16[1,384,2048]{2,1,0:T(8,128)(2,1)S(1)} %slice.262), channel_id=1, source_target_pairs={{0,2},{1,3},{2,0},{3,1},{4,6},{5,7},{6,4},{7,5},{8,10},{9,11},{10,... | collective-permute-start | bytes 4718600 | tf_op jit(solution)/shard_map/ppermute | solution.py:567
  519.8 70.3 %collective-permute-start.24 = (bf16[1,384,2048]{2,1,0:T(8,128)(2,1)S(1)}, bf16[1,384,2048]{2,1,0:T(8,128)(2,1)}, u32[]{:S(2)}, u32[]{:S(2)}) collective-permute-start(bf16[1,384,2048]{2,1,0:T(8,128)(2,1)S(1)} %slice.263), channel_id=1, source_target_pairs={{0,1},{1,0},{2,3},{3,2},{4,5},{5,4},{6,7},{7,6},{8,9},{9,8},{10,11... | collective-permute-start | bytes 4718600 | tf_op jit(solution)/shard_map/ppermute | solution.py:567
  590.1 318.0 %reduce-scatter.7.cloned.1.call-start = ((), (), s32[]{:S(2)}) async-start(), calls=%async_computation.12 | async-start | bytes 18874368 | tf_op jit(solution)/shard_map/reduce_scatter | solution.py:800
  634.2 70.4 %collective-permute-start.25 = (bf16[1024,1536]{1,0:T(8,128)(2,1)S(1)}, bf16[1024,1536]{1,0:T(8,128)(2,1)}, u32[]{:S(2)}, u32[]{:S(2)}) collective-permute-start(bf16[1024,1536]{1,0:T(8,128)(2,1)S(1)} %get-tuple-element.549), channel_id=1, source_target_pairs={{0,1},{1,0},{2,3},{3,2},{4,5},{5,4},{6,7},{7,6},{8,9},{9,8},{10,11... | collective-permute-start | bytes 9437192 | tf_op jit(solution)/shard_map/ppermute | solution.py:567
  635.7 70.1 %collective-permute-start.26 = (bf16[1024,1536]{1,0:T(8,128)(2,1)S(1)}, bf16[1024,1536]{1,0:T(8,128)(2,1)}, u32[]{:S(2)}, u32[]{:S(2)}) collective-permute-start(bf16[1024,1536]{1,0:T(8,128)(2,1)S(1)} %get-tuple-element.548), channel_id=1, source_target_pairs={{0,2},{1,3},{2,0},{3,1},{4,6},{5,7},{6,4},{7,5},{8,10},{9,11},{10,... | collective-permute-start | bytes 9437192 | tf_op jit(solution)/shard_map/ppermute | solution.py:567
  737.5 37.4 %collective-permute-start.29 = (bf16[384,2048]{1,0:T(8,128)(2,1)S(1)}, bf16[384,2048]{1,0:T(8,128)(2,1)S(1)}, u32[]{:S(2)}, u32[]{:S(2)}) collective-permute-start(bf16[384,2048]{1,0:T(8,128)(2,1)S(1)} %get-tuple-element.551), channel_id=1, source_target_pairs={{0,1},{1,0},{2,3},{3,2},{4,5},{5,4},{6,7},{7,6},{8,9},{9,8},{10,11... | collective-permute-start | bytes 4718600 | tf_op jit(solution)/shard_map/ppermute | solution.py:567
  738.2 37.3 %collective-permute-start.30 = (bf16[384,2048]{1,0:T(8,128)(2,1)S(1)}, bf16[384,2048]{1,0:T(8,128)(2,1)S(1)}, u32[]{:S(2)}, u32[]{:S(2)}) collective-permute-start(bf16[384,2048]{1,0:T(8,128)(2,1)S(1)} %get-tuple-element.550), channel_id=1, source_target_pairs={{0,2},{1,3},{2,0},{3,1},{4,6},{5,7},{6,4},{7,5},{8,10},{9,11},{10,... | collective-permute-start | bytes 4718600 | tf_op jit(solution)/shard_map/ppermute | solution.py:567
  750.3 157.8 %collective-permute-start.28 = (bf16[2048,1536]{1,0:T(8,128)(2,1)}, bf16[2048,1536]{1,0:T(8,128)(2,1)}, u32[]{:S(2)}, u32[]{:S(2)}) collective-permute-start(bf16[2048,1536]{1,0:T(8,128)(2,1)} %add_convert_fusion), channel_id=1, source_target_pairs={{0,2},{1,3},{2,0},{3,1},{4,6},{5,7},{6,4},{7,5},{8,10},{9,11},{10,... | collective-permute-start | bytes 18874376 | tf_op jit(solution)/shard_map/ppermute | solution.py:567
  760.1 148.0 %collective-permute-start.27 = (bf16[2048,1536]{1,0:T(8,128)(2,1)}, bf16[2048,1536]{1,0:T(8,128)(2,1)}, u32[]{:S(2)}, u32[]{:S(2)}) collective-permute-start(bf16[2048,1536]{1,0:T(8,128)(2,1)} %add_convert_fusion.1), channel_id=1, source_target_pairs={{0,1},{1,0},{2,3},{3,2},{4,5},{5,4},{6,7},{7,6},{8,9},{9,8},{10,11... | collective-permute-start | bytes 18874376 | tf_op jit(solution)/shard_map/ppermute | solution.py:567
  780.1 70.2 %all-to-all-start = ((f32[8,512,4]{1,2,0:T(4,128)}), f32[8,512,4]{1,2,0:T(4,128)S(1)}, u32[]{:S(2)}, u32[]{:S(2)}) async-start(f32[8,512,4]{1,2,0:T(4,128)} %copy.124), calls=%async_computation.1 | async-start | bytes 131072 | tf_op jit(solution)/shard_map/all_to_all | solution.py:822
  783.4 291.4 %reduce-scatter.9.cloned.1.call-start = ((), (), s32[]{:S(2)}) async-start(), calls=%async_computation.13 | async-start | bytes 18874368 | tf_op jit(solution)/shard_map/reduce_scatter | solution.py:858
  908.1 203.4 %reduce-scatter.11.cloned.1.call-start = ((), (), s32[]{:S(2)}) async-start(), calls=%async_computation.14 | async-start | bytes 2359296 | tf_op jit(solution)/shard_map/reduce_scatter | solution.py:909
  919.3 45.8 %collective-permute-start.31 = (bf16[1,512,2048]{2,1,0:T(8,128)(2,1)S(1)}, bf16[1,512,2048]{2,1,0:T(8,128)(2,1)S(1)}, u32[]{:S(2)}, u32[]{:S(2)}) collective-permute-start(bf16[1,512,2048]{2,1,0:T(8,128)(2,1)S(1)} %get-tuple-element.542), channel_id=1, source_target_pairs={{0,1},{1,0},{2,3},{3,2},{4,5},{5,4},{6,7},{7,6},{8,9},{9,8},{10,11... | collective-permute-start | bytes 6291464 | tf_op jit(solution)/shard_map/ppermute | solution.py:567
  921.0 45.5 %collective-permute-start.32 = (bf16[1,512,2048]{2,1,0:T(8,128)(2,1)S(1)}, bf16[1,512,2048]{2,1,0:T(8,128)(2,1)S(1)}, u32[]{:S(2)}, u32[]{:S(2)}) collective-permute-start(bf16[1,512,2048]{2,1,0:T(8,128)(2,1)S(1)} %get-tuple-element.542), channel_id=1, source_target_pairs={{0,2},{1,3},{2,0},{3,1},{4,6},{5,7},{6,4},{7,5},{8,10},{9,11},{10,... | collective-permute-start | bytes 6291464 | tf_op jit(solution)/shard_map/ppermute | solution.py:567
  966.6 33.8 %collective-permute-start.33 = (bf16[1,256,2048]{2,1,0:T(8,128)(2,1)S(1)}, bf16[1,256,2048]{2,1,0:T(8,128)(2,1)}, u32[]{:S(2)}, u32[]{:S(2)}) collective-permute-start(bf16[1,256,2048]{2,1,0:T(8,128)(2,1)S(1)} %slice.271), channel_id=1, source_target_pairs={{0,2},{1,3},{2,0},{3,1},{4,6},{5,7},{6,4},{7,5},{8,10},{9,11},{10,... | collective-permute-start | bytes 3145736 | tf_op jit(solution)/shard_map/ppermute | solution.py:567
  969.2 31.2 %collective-permute-start.34 = (bf16[1,256,2048]{2,1,0:T(8,128)(2,1)}, bf16[1,256,2048]{2,1,0:T(8,128)(2,1)}, u32[]{:S(2)}, u32[]{:S(2)}) collective-permute-start(bf16[1,256,2048]{2,1,0:T(8,128)(2,1)} %slice.272), channel_id=1, source_target_pairs={{0,1},{1,0},{2,3},{3,2},{4,5},{5,4},{6,7},{7,6},{8,9},{9,8},{10,11... | collective-permute-start | bytes 3145736 | tf_op jit(solution)/shard_map/ppermute | solution.py:567
  1000.3 169.3 %reduce-scatter.13.cloned.1.call-start = ((), (), s32[]{:S(2)}) async-start(), calls=%async_computation.15 | async-start | bytes 4718592 | tf_op jit(solution)/shard_map/reduce_scatter | solution.py:916
  1008.2 103.3 %collective-permute-start.35 = (bf16[768,2048]{1,0:T(8,128)(2,1)}, bf16[768,2048]{1,0:T(8,128)(2,1)}, u32[]{:S(2)}, u32[]{:S(2)}) collective-permute-start(bf16[768,2048]{1,0:T(8,128)(2,1)} %add_convert_fusion.3), channel_id=1, source_target_pairs={{0,1},{1,0},{2,3},{3,2},{4,5},{5,4},{6,7},{7,6},{8,9},{9,8},{10,11... | collective-permute-start | bytes 9437192 | tf_op jit(solution)/shard_map/ppermute | solution.py:567
  1009.9 101.7 %collective-permute-start.36 = (bf16[768,2048]{1,0:T(8,128)(2,1)}, bf16[768,2048]{1,0:T(8,128)(2,1)}, u32[]{:S(2)}, u32[]{:S(2)}) collective-permute-start(bf16[768,2048]{1,0:T(8,128)(2,1)} %add_convert_fusion.2), channel_id=1, source_target_pairs={{0,2},{1,3},{2,0},{3,1},{4,6},{5,7},{6,4},{7,5},{8,10},{9,11},{10,... | collective-permute-start | bytes 9437192 | tf_op jit(solution)/shard_map/ppermute | solution.py:567
  1111.5 125.1 %reduce-scatter.15.cloned.1.call-start = ((), (), s32[]{:S(2)}) async-start(), calls=%async_computation.16 | async-start | bytes 2359296 | tf_op jit(solution)/shard_map/reduce_scatter | solution.py:939
  1118.3 46.3 %collective-permute-start.38 = (bf16[512,2048]{1,0:T(8,128)(2,1)}, bf16[512,2048]{1,0:T(8,128)(2,1)}, u32[]{:S(2)}, u32[]{:S(2)}) collective-permute-start(bf16[512,2048]{1,0:T(8,128)(2,1)} %input_share.6), channel_id=1, source_target_pairs={{0,2},{1,3},{2,0},{3,1},{4,6},{5,7},{6,4},{7,5},{8,10},{9,11},{10,... | collective-permute-start | bytes 6291464 | tf_op jit(solution)/shard_map/ppermute | solution.py:567
  1119.9 44.7 %collective-permute-start.37 = (bf16[512,2048]{1,0:T(8,128)(2,1)}, bf16[512,2048]{1,0:T(8,128)(2,1)}, u32[]{:S(2)}, u32[]{:S(2)}) collective-permute-start(bf16[512,2048]{1,0:T(8,128)(2,1)} %input_share.5), channel_id=1, source_target_pairs={{0,1},{1,0},{2,3},{3,2},{4,5},{5,4},{6,7},{7,6},{8,9},{9,8},{10,11... | collective-permute-start | bytes 6291464 | tf_op jit(solution)/shard_map/ppermute | solution.py:567
  1121.4 33.9 %collective-permute-start.39 = (bf16[2,2,256,128]{3,2,1,0:T(8,128)(2,1)}, bf16[2,2,256,128]{3,2,1,0:T(8,128)(2,1)S(1)}, u32[]{:S(2)}, u32[]{:S(2)}) collective-permute-start(bf16[2,2,256,128]{3,2,1,0:T(8,128)(2,1)} %reduce-scatter.11.cloned.1.call-done), channel_id=1, source_target_pairs={{0,0},{8,4},{16,8},{24,12},{1,1},{9,5},{17,9},{25,13},{2,2},{10,6}... | collective-permute-start | bytes 786440 | tf_op jit(solution)/shard_map/ppermute | solution.py:886
  1123.0 32.3 %collective-permute-start.40 = (bf16[2,2,256,128]{3,2,1,0:T(8,128)(2,1)}, bf16[2,2,256,128]{3,2,1,0:T(8,128)(2,1)}, u32[]{:S(2)}, u32[]{:S(2)}) collective-permute-start(bf16[2,2,256,128]{3,2,1,0:T(8,128)(2,1)} %reduce-scatter.11.cloned.1.call-done), channel_id=1, source_target_pairs={{4,0},{12,4},{20,8},{28,12},{5,1},{13,5},{21,9},{29,13},{6,2},{14,... | collective-permute-start | bytes 786440 | tf_op jit(solution)/shard_map/ppermute | solution.py:886
  1175.7 118.5 %collective-permute-start.46 = (bf16[512,2048]{1,0:T(8,128)(2,1)}, bf16[512,2048]{1,0:T(8,128)(2,1)}, u32[]{:S(2)}, u32[]{:S(2)}) collective-permute-start(bf16[512,2048]{1,0:T(8,128)(2,1)} %input_share.7), channel_id=1, source_target_pairs={{0,3},{1,2},{2,1},{3,0},{4,7},{5,6},{6,5},{7,4},{8,11},{9,10},{10,... | collective-permute-start | bytes 6291464 | tf_op jit(solution)/shard_map/ppermute | solution.py:567
  1182.5 149.3 %reduce-scatter.17.cloned.1.call-start = ((), (), s32[]{:S(2)}) async-start(), calls=%async_computation.17 | async-start | bytes 4718592 | tf_op jit(solution)/shard_map/reduce_scatter | solution.py:957
  1211.5 32.1 %collective-permute-start.43 = (bf16[512,256]{1,0:T(8,128)(2,1)}, bf16[512,256]{1,0:T(8,128)(2,1)}, u32[]{:S(2)}, u32[]{:S(2)}) collective-permute-start(bf16[512,256]{1,0:T(8,128)(2,1)} %get-tuple-element.580), channel_id=1, source_target_pairs={{0,1},{1,0},{2,3},{3,2},{4,5},{5,4},{6,7},{7,6},{8,9},{9,8},{10,11... | collective-permute-start | bytes 786440 | tf_op jit(solution)/shard_map/ppermute | solution.py:567
  1236.7 8.7 collective-permute-start.41
  1239.1 6.3 collective-permute-start.42
  1247.6 27.8 %collective-permute-start.44 = (bf16[512,256]{1,0:T(8,128)(2,1)S(1)}, bf16[512,256]{1,0:T(8,128)(2,1)S(1)}, u32[]{:S(2)}, u32[]{:S(2)}) collective-permute-start(bf16[512,256]{1,0:T(8,128)(2,1)S(1)} %get-tuple-element.571), channel_id=1, source_target_pairs={{0,2},{1,3},{2,0},{3,1},{4,6},{5,7},{6,4},{7,5},{8,10},{9,11},{10,... | collective-permute-start | bytes 786440 | tf_op jit(solution)/shard_map/ppermute | solution.py:567
  1248.2 27.2 %collective-permute-start.45 = (bf16[512,256]{1,0:T(8,128)(2,1)S(1)}, bf16[512,256]{1,0:T(8,128)(2,1)S(1)}, u32[]{:S(2)}, u32[]{:S(2)}) collective-permute-start(bf16[512,256]{1,0:T(8,128)(2,1)S(1)} %get-tuple-element.569), channel_id=1, source_target_pairs={{0,3},{1,2},{2,1},{3,0},{4,7},{5,6},{6,5},{7,4},{8,11},{9,10},{10,... | collective-permute-start | bytes 786440 | tf_op jit(solution)/shard_map/ppermute | solution.py:567
  1257.2 33.4 %all-to-all-start.1 = ((f32[32,1,2216]{2,1,0:T(1,128)}), f32[32,1,2216]{2,1,0:T(1,128)S(1)}, u32[]{:S(2)}, u32[]{:S(2)}) async-start(f32[32,1,2216]{2,1,0:T(1,128)} %copy.132), calls=%async_computation.6 | async-start | bytes 589824 | tf_op jit(solution)/shard_map/all_to_all | solution.py:980
  1290.5 40.0 %all-to-all-start.2 = ((bf16[32,64,256]{2,1,0:T(8,128)(2,1)}), bf16[32,64,256]{2,1,0:T(8,128)(2,1)S(1)}, u32[]{:S(2)}, u32[]{:S(2)}) async-start(bf16[32,64,256]{2,1,0:T(8,128)(2,1)} %bitcast.270), calls=%async_computation.8 | async-start | bytes 2097152 | tf_op jit(solution)/shard_map/all_to_all | solution.py:964
  (115 other events, 1115.5 us)
Sparse Core Ops, SparseCore 0:
  14.5 63.5 all-gather.11
  79.6 46.2 all-gather.13
  129.1 48.1 all-gather.17
  179.3 46.1 all-gather.19
  227.0 149.8 all-gather.23
  378.8 157.0 all-gather.21
  590.2 50.1 all-gather.15
  731.0 166.6 reduce-scatter.6
  908.2 166.5 reduce-scatter.8
  1077.5 33.9 reduce-scatter.10
  1114.4 55.1 reduce-scatter.12
  1182.6 44.8 reduce-scatter.14
  1245.5 69.9 reduce-scatter.16

commit v4 on v3

--- a/solution.py
+++ b/solution.py
@@ -163,10 +163,16 @@
                 weights = jnp.exp2(dot_nt(q, kv_ref[0, piece, :])).astype(BF)
                 acc[...] += dot_nn(weights, vl_one[piece, :])
 
-    @pl.loop(0, jnp.minimum(row, blocks))
-    def _(j):
-        weights = jnp.exp2(dot_nt(q, kp_ref[j, 0])).astype(BF)
-        acc[...] += dot_nn(weights, vp_one[pl.ds(pl.multiple_of(j * rows, rows), rows), :])
+        @pl.loop(0, row)
+        def _(j):
+            weights = jnp.exp2(dot_nt(q, kp_ref[j, 0])).astype(BF)
+            acc[...] += dot_nn(weights, vp_one[pl.ds(pl.multiple_of(j * rows, rows), rows), :])
+
+    @pl.when(row >= blocks)
+    def _():
+        keys = kp_ref[...].reshape(blocks * rows, HEAD)
+        weights = jnp.exp2(dot_nt(q, keys)).astype(BF)
+        acc[...] += dot_nn(weights, vp_one[...])
 
     total = acc[:, HEAD:]
     out = (acc[:, :HEAD] / total).astype(BF)
@@ -186,7 +192,7 @@
 
 def attend(row, q, every, kv, blocks):
     heads, rows, _ = q.shape
-    per = 2
+    per = min(4, heads)
     every, place = every
     keys = blocks * rows
     return call(
@@ -234,33 +240,33 @@
 
     q = q_ref[...].reshape(per * CONT, HEAD)
     lane = lax.broadcasted_iota(jnp.int32, (CONT, HEAD), 1)
+    line = lax.broadcasted_iota(jnp.int32, (HEAD, CONT), 0)
+    logs_t = l_ref[...].T
     do_parts, logs, centers, scales = [], [], [], []
     for p in range(per):
         do_part = do_ref[:, p * HEAD : (p + 1) * HEAD]
         do_parts.append(do_part)
-        centers.append(
-            jnp.sum(
-                do_part.astype(F32) * o_ref[:, p * HEAD : (p + 1) * HEAD].astype(F32),
-                axis=-1,
-                keepdims=True,
-            )
-        )
-        pick = lane == part * per + p
-        logs.append(jnp.sum(jnp.where(pick, l_ref[...], 0.0), axis=-1, keepdims=True))
-        scales.append(jnp.sum(jnp.where(pick, r_ref[...], 0.0), axis=-1, keepdims=True))
+        both = do_part.astype(F32) * o_ref[:, p * HEAD : (p + 1) * HEAD].astype(F32)
+        centers.append(jnp.sum(both.T, axis=0, keepdims=True))
+        head = part * per + p
+        logs.append(jnp.sum(jnp.where(line == head, logs_t, 0.0), axis=0, keepdims=True))
+        scales.append(jnp.sum(jnp.where(lane == head, r_ref[...], 0.0), axis=-1, keepdims=True))
     do = jnp.concatenate(do_parts, axis=0)
-    center = jnp.concatenate(centers, axis=0)
-    log = jnp.concatenate(logs, axis=0)
+    center = jnp.concatenate(centers, axis=1)
+    log = jnp.concatenate(logs, axis=1)
 
     def block(k, v, mask):
-        probs = jnp.exp2(dot_nt(q, k) - log)
+        probs = jnp.exp2(dot_nt(k, q) - log)
         if mask is not None:
             probs = jnp.where(mask, probs, 0.0)
-        ds = (probs * (dot_nt(do, v) - center)).astype(BF)
-        return dot_nn(ds, k), dot_tn(ds, q), dot_tn(probs.astype(BF), do)
-
+        ds = (probs * (dot_nt(v, do) - center)).astype(BF)
+        return dot_tn(ds, k), dot_nn(ds, q), dot_nn(probs.astype(BF), do)
+
+    k_at = lax.broadcasted_iota(jnp.int32, (CONT, CONT), 0)
+    q_at = lax.broadcasted_iota(jnp.int32, (CONT, CONT), 1)
+    seen = jnp.concatenate([k_at <= q_at] * per, axis=1)
     here = pl.ds(pl.multiple_of(at * CONT, CONT), CONT)
-    a, b, c = block(kv_ref[0, here, :], kv_ref[1, here, :], causal(per))
+    a, b, c = block(kv_ref[0, here, :], kv_ref[1, here, :], seen)
     dq[...] = a
     dl_ref[0, here, :] += b
     dl_ref[1, here, :] += c
@@ -307,7 +313,7 @@
 
 def attend_back(row, q, every, kv, blocks, do, o, logs, scales, cos, sin, qg):
     heads, rows, _ = q.shape
-    per = 2
+    per = min(8, heads)
     every, place = every
     keys = blocks * rows
     tile = lambda i, h, s: (i, 0)
@@ -447,16 +453,22 @@
 def combine_body(count, cap, scored, rank_ref, *refs):
     tokens = rank_ref.shape[1]
     slot = lax.broadcasted_iota(jnp.int32, (tokens, cap), 1)
-    out_ref = refs[count * (2 if scored else 1)]
-    total = None
-    for d in range(count):
-        hot = (rank_ref[0, :, d : d + 1] == slot).astype(F32).astype(BF)
-        piece = dot_nn(hot, refs[d][0])
-        total = piece if total is None else total + piece
-        if scored:
-            score = dot_nn(hot, refs[count + d][0])
-            refs[-1][0, :, d : d + 1] = jnp.sum(score, axis=-1, keepdims=True)
-    out_ref[0] = total.astype(BF)
+    hots = [(rank_ref[0, :, d : d + 1] == slot).astype(F32).astype(BF) for d in range(count)]
+
+    def gathered(parts):
+        if cap % HEAD:
+            return sum(dot_nn(hot, part[0]) for hot, part in zip(hots, parts))
+        return dot_nn(
+            jnp.concatenate(hots, axis=1), jnp.concatenate([p[0] for p in parts], axis=0)
+        )
+
+    refs[count * (2 if scored else 1)][0] = gathered(refs[:count]).astype(BF)
+    if scored:
+        scores = gathered(refs[count : 2 * count])
+        lane = lax.broadcasted_iota(jnp.int32, scores.shape, 1)
+        for d in range(count):
+            mine = jnp.where(lane // 4 == d, scores, 0.0)
+            refs[-1][0, :, d : d + 1] = jnp.sum(mine, axis=-1, keepdims=True)
 
 
 def combine(rank_t, parts, scores=()):
@@ -479,17 +491,14 @@
         + [pl.BlockSpec((1, cap, HEAD), at)] * len(scores),
         out_specs,
         out_shape,
-        flops=2 * sources * count * cap * tokens * width,
-        moved=2 * sources * width * (tokens + count * cap),
     )(rank_t, *[cut(p) for p in parts], *[cut(p) for p in scores])
 
 
 def expert_body(
-    x_ref, up_ref, gate_ref, wga_ref, wgb_ref, wua_ref, wub_ref, wda_ref, wdb_ref,
-    y_ref, db_ref, m_ref, duw_ref, dg_ref,
+    slot, x_ref, up_ref, gate_ref, wga_ref, wgb_ref, wua_ref, wub_ref, wda_ref, wdb_ref,
+    db_ref, m_ref, duw_ref, dg_ref,
 ):
     half = wga_ref.shape[1]
-    deep = wda_ref.shape[1]
     hidden = wga_ref.shape[2]
     xa, xb = x_ref[:, :half], x_ref[:, half:]
     gate = gate_ref[...]
@@ -499,8 +508,6 @@
     silu = u * sigma
     inner = silu * w
     low = inner.astype(BF)
-    y = dot_nn(low[:, :deep], wda_ref[0]) + dot_nn(low[:, deep:], wdb_ref[0])
-    y_ref[...] = (y * gate).astype(BF)
     m_ref[...] = (inner * gate).astype(BF)
     up = up_ref[...]
     back = jnp.concatenate([dot_nt(up, wda_ref[0]), dot_nt(up, wdb_ref[0])], axis=1)
@@ -510,9 +517,9 @@
     rest = score - high.astype(F32)
     middle = rest.astype(BF)
     last = (rest - middle.astype(F32)).astype(BF)
-    pieces = jnp.where(lane == 0, high.astype(F32), 0.0)
-    pieces = jnp.where(lane == 1, middle.astype(F32), pieces)
-    dg_ref[...] = jnp.where(lane == 2, last.astype(F32), pieces).astype(BF)
+    pieces = jnp.where(lane == 4 * slot, high.astype(F32), 0.0)
+    pieces = jnp.where(lane == 4 * slot + 1, middle.astype(F32), pieces)
+    dg_ref[...] = jnp.where(lane == 4 * slot + 2, last.astype(F32), pieces).astype(BF)
     back = back * gate
     du = (back * w * sigma * (1.0 + u * (1.0 - sigma))).astype(BF)
     dw = (back * silu).astype(BF)
@@ -522,7 +529,7 @@
     db_ref[:, half:] = (dot_nt(du, wgb_ref[0]) + dot_nt(dw, wub_ref[0])).astype(BF)
 
 
-def expert(x, up, gate, weights):
+def expert(slot, x, up, gate, weights):
     rows, width = x.shape
     hidden = weights[0][0].shape[2]
     tile = min(256, rows)
@@ -535,7 +542,7 @@
             specs.append(pl.BlockSpec(shape, lambda i, place=place: (0, place, 0)))
             arrays.append(parts[0] if len(parts) == 1 else parts[j])
     return call(
-        expert_body,
+        partial(expert_body, slot),
         "expert",
         (rows // tile,),
         [
@@ -546,20 +553,18 @@
         + specs,
         [
             pl.BlockSpec((tile, width), at),
-            pl.BlockSpec((tile, width), at),
             pl.BlockSpec((tile, hidden), at),
             pl.BlockSpec((tile, 2 * hidden), at),
             pl.BlockSpec((tile, HEAD), at),
         ],
         [
-            struct((rows, width), BF),
             struct((rows, width), BF),
             struct((rows, hidden), BF),
             struct((rows, 2 * hidden), BF),
             struct((rows, HEAD), BF),
         ],
-        flops=12 * rows * width * hidden,
-        moved=2 * (4 * rows * width + 3 * rows * hidden + 3 * width * hidden),
+        flops=10 * rows * width * hidden,
+        moved=2 * (3 * rows * width + 3 * rows * hidden + 3 * width * hidden),
     )(x, up, gate, *arrays)
 
 
@@ -578,6 +583,10 @@
 
 def halves(v):
     return v[:, : v.shape[1] // 2], v[:, v.shape[1] // 2 :]
+
+
+def whole(parts):
+    return parts[0] if len(parts) == 1 else jnp.concatenate(parts, axis=1)
 
 
 def deliver_far(part, count):
@@ -765,7 +774,7 @@
         expert_in[0], up_w_all = lax.optimization_barrier((expert_in[0], up_w_all))
         down_far = far_of(*[halves(v[0]) for v in down_all[1:3]])
     kv_all = lax.all_gather(after(key_value_weight, expert_in[0]), "row", axis=0, tiled=True)
-    ys, dbs, ms, duws, dgs = [[None] * col_count for _ in range(5)]
+    dbs, ms, duws, dgs = [[None] * col_count for _ in range(4)]
     grad_gu, grad_dn = [None] * col_count, [None] * col_count
 
     def gate_up_grad(d):
@@ -784,8 +793,8 @@
             expert_in[d], down_far = lax.optimization_barrier((expert_in[d], down_far))
             down_all.append(down_far)
         weights = [gate_all[d], up_w_all[d], down_all[d]]
-        ys[d], dbs[d], ms[d], duws[d], dgs[d] = expert(
-            expert_in[d], expert_up[d], gate_pairs[d], weights
+        dbs[d], ms[d], duws[d], dgs[d] = expert(
+            d, expert_in[d], expert_up[d], gate_pairs[d], weights
         )
         if four and at == 1:
             gate_up_grad(d)
@@ -795,10 +804,8 @@
         dbs[0], far_sent[0] = lax.optimization_barrier((dbs[0], far_sent[0]))
     dbs[0], kv_all = lax.optimization_barrier((dbs[0], kv_all))
     db_part, score_grads = combine(rank_t, dbs, dgs)
-    if four:
-        score_grads, far_sent[1] = lax.optimization_barrier((score_grads, far_sent[1]))
     db_sum = lax.psum_scatter(db_part, "row", scatter_dimension=0)
-    duws, ms, ys, _ = lax.optimization_barrier((duws, ms, ys, db_part))
+    duws, ms, _ = lax.optimization_barrier((duws, ms, db_part))
     remaining = (1, 2) if four else range(1, col_count)
     for d in remaining:
         gate_up_grad(d)
@@ -807,6 +814,8 @@
     if four:
         gu_two, gu_one = far_sent[0]
         gu_sends = [join(grad_gu[1], gu_one, False), join(grad_gu[2], gu_two, True)]
+    if four:
+        gu_sends, far_sent[1] = lax.optimization_barrier((gu_sends, far_sent[1]))
     gu_got = exchange(gu_sends)
     ms, gu_sends = lax.optimization_barrier((ms, gu_sends))
     for d in remaining:
@@ -817,6 +826,7 @@
         dn_sends = [join(grad_dn[1], dn_one, False), join(grad_dn[2], dn_two, True)]
     gate_up_grad(0)
     down_grad(0)
+    ys = [dot_nn(m, whole(w)[0]).astype(BF) for m, w in zip(ms, down_all)]
     (y_part,) = combine(rank_t, ys)
 
     score_grads = lax.all_to_all(score_grads, "row", split_axis=0, concat_axis=0, tiled=True)
@@ -892,8 +902,7 @@
     for d in slots:
         if d == col_count - 1:
             grad_out = jnp.stack(branches, axis=0)
-            grad_out, y_sum, _ = lax.optimization_barrier((grad_out, y_sum, shares[-1]))
-            grad_out = over_tokens(mixes_all, grad_out).astype(BF)
+            grad_out = over_tokens(mixes_all, after(grad_out, shares[-1])).astype(BF)
         if d == 1:
             beside, shares[0] = lax.optimization_barrier((beside, shares[0]))
             branches = [branch] + [v[0] for v in beside]
@@ -909,14 +918,11 @@
             early_prompt = lax.psum_scatter(
                 jnp.stack(prompts[:batch], axis=0), "row", scatter_dimension=2, tiled=True
             )
-            branches[d], dn_got, grad_out, early_prompt = lax.optimization_barrier(
-                (branches[d], dn_got, grad_out, early_prompt)
+            branches[d], dn_got, grad_out, y_sum = lax.optimization_barrier(
+                (branches[d], dn_got, grad_out, y_sum)
             )
-            early_prompt = to_owners(early_prompt)
             grad_out = lax.psum_scatter(grad_out, "row", scatter_dimension=1, tiled=True)
         mix_grad = dot_nt(branches[d], out_all).astype(BF)
-        if d == 2:
-            sent[0] = swap(after(shares[1], mix_grad), 1, col_count)
         grad_q, grad_prompt, pair, gain_part = attend_back(
             row_word, qs[d], every[d], kvs[d], blocks, mix_grad, mixes[d], logs[d], scales[d],
             coses[d], sines[d], gain_q,
@@ -931,6 +937,8 @@
             )
         share = input_share(grad_q, wide, F32 if d == 0 else BF)
         shares.append(share)
+        if d == 2:
+            sent[0] = swap(after(shares[1], share), 1, col_count)
         if d > 0:
             sent.append(swap(share, d, col_count))
     grad_q = over_tokens(normed_all, after(jnp.stack(grad_qs, axis=0), shares[-1]))
@@ -939,11 +947,11 @@
     late_prompt = lax.psum_scatter(
         jnp.stack(prompts[batch:], axis=0), "row", scatter_dimension=2, tiled=True
     )
-    early_prompt = after(early_prompt, shares[-1])
+    early_prompt = to_owners(after(early_prompt, shares[-1]))
+    early_prompt, grad_q = lax.optimization_barrier((early_prompt, grad_q))
     for first in range(0, col_count, batch):
         prompt = early_prompt
         if first > 0:
-            late_prompt, grad_q, _ = lax.optimization_barrier((late_prompt, grad_q, grad_kvs))
             prompt = to_owners(late_prompt)
         for d in range(first, first + batch):
             pair = pairs[d] + prompt[d - first].astype(F32)
@@ -997,7 +1005,7 @@
     x_hat = x_wide * x_spread
     input_grad = hidden_grad + norm_back(input_sum, x_hat, x_spread, gain_one)
 
-    own_grads, _ = lax.optimization_barrier((own_grads, shares[-1]))
+    own_grads, _ = lax.optimization_barrier((own_grads, kv_share))
     ffe = w_gate.shape[2]
     grad_gate = own_grads[0][:, :ffe] + sum(v[:, :ffe].astype(F32) for v in gu_got)
     grad_up = own_grads[0][:, ffe:] + sum(v[:, ffe:].astype(F32) for v in gu_got)

time: 1360 us -> 1320 us (0.971)
  Pallas kernels: 368 us -> 306 us
  matrix products: 154 us -> 173 us
    ppermute x43, waiting for transfers between devices: 395 us -> 451 us  [swap(): return lax.ppermute(v, 'col', [(i, i ^ step) for i in range(count)])]
    reduce_scatter x1, waiting for transfers between devices: 4.95 us -> 38.5 us  [per_device(): lax.psum_scatter(grad_out, 'row', scatter_dimension=1, tiled=True)]
    reduce_scatter x1, waiting for transfers between devices: 35.7 us -> 8.04 us  [per_device(): y_sum = lax.psum_scatter(y_part, 'row', scatter_dimension=0)]
    dot_general x0 -> x4, matrix products: none -> 26.4 us  [dot_nn(): lax.dot_general(a, b, (((1,), (0,)), ((), ())), preferred_element_type=F32)]
    reduce_scatter x1, waiting for transfers between devices: 23 us -> 0.01 us  [per_device(): lax.psum_scatter(jnp.stack(prompts[:batch], axis=0), 'row', scatter_dimen...]
    pallas_call x4, Pallas kernels: 68.1 us -> 46 us  [attend_back(): call(partial(attend_back_body, heads, per, blocks, rows), 'attend_back',...]
    all_to_all x1, waiting for transfers between devices: 22.6 us -> 1.43 us  [per_device(): lax.all_to_all(grad_kv.astype(BF).reshape(devices, -1, 2 * HEAD), ('row',...]
    pallas_call x4, Pallas kernels: 118 us -> 98.5 us  [expert(): call(partial(expert_body, slot), 'expert', (rows // tile,), [pl.BlockSpec...]
  transfers between devices with their start and end apart: 63 -> 63, of which waited for: 26 -> 32; matrix products, arithmetic and copies ran while one was open for 25% -> 26% of each run, Pallas kernels for 25% -> 21%
where the time goes in v4:
time: 1320 us; the launch traced here: 1310 us
  waiting for transfers between devices  518 us (39%)
  Pallas kernels  306 us (23%)
  matrix products  173 us (13%)
  other arithmetic  96.7 us (7%)
  starting transfers between devices  93.8 us (7%)
  local copies, waits for them, and re-layouts  87.3 us (7%)
  between operations  17.8 us (1%)
  blocking collectives  14.6 us (1%)
    ppermute x43, waiting for transfers between devices, swap(): return lax.ppermute(v, 'col', [(i, i ^ step) for i in range(count)])  451 us
    pallas_call x4, Pallas kernels, expert(): call(partial(expert_body, slot), 'expert', (rows // tile,), [pl.BlockSpec...  98.5 us
    dot_general x8, matrix products, dot_tn(): lax.dot_general(a, b, (((0,), (0,)), ((), ())), preferred_element_type=F32)  59.6 us
    ppermute x43, starting transfers between devices, swap(): return lax.ppermute(v, 'col', [(i, i ^ step) for i in range(count)])  52.4 us
    pallas_call x4, Pallas kernels, attend_back(): call(partial(attend_back_body, heads, per, blocks, rows), 'attend_back',...  46 us
    reduce_scatter x1, waiting for transfers between devices, per_device(): lax.psum_scatter(grad_out, 'row', scatter_dimension=1, tiled=True)  38.5 us
    pallas_call x2, Pallas kernels, combine(): call(partial(combine_body, count, cap, bool(scores)), 'combine', (sources...  37.1 us
    pallas_call x4, Pallas kernels, qkv(): call(partial(qkv_body, heads), 'qkv', (rows // tile,), [pl.BlockSpec((til...  33.4 us
  transfers between devices with their start and end apart: 63, of which 32 were waited for; matrix products, arithmetic and copies ran while one was open for 26% of the time, Pallas kernels for 21%

profile of v4, /device:TPU:0, one launch (start us, length us, event | category | flops | bytes accessed | tf_op | source)
XLA Modules:
  0.0 1307.4 jit_solution(16343934819724520821)
XLA Ops:
  18.8 14.6 %all_gather.37 = s32[8,512,8]{1,2,0:T(8,128)S(1)} all-gather(s32[1,512,8]{1,2,0:T(8,128)S(1)} %copy-done.58), channel_id=1, replica_groups=mesh['row'=8,'col'=4] {'row'}, dimensions={0}, use_global_device_ids=true | all-gather | bytes 147456 | tf_op jit(solution)/shard_map/all_gather | solution.py:662
  49.9 13.3 %collective-permute-done.2 = f32[32]{0:T(128)S(1)} collective-permute-done((f32[32]{0:T(128)S(1)}, f32[32]{0:T(128)S(1)}, u32[]{:S(2)}, u32[]{:S(2)}) %collective-permute-start.2) | collective-permute-done | bytes 160 | tf_op jit(solution)/shard_map/ppermute | solution.py:572
  73.6 20.6 %collective-permute-done.4 = bf16[1,256,2048]{2,1,0:T(8,128)(2,1)S(1)} collective-permute-done((bf16[1,256,2048]{2,1,0:T(8,128)(2,1)S(1)}, bf16[1,256,2048]{2,1,0:T(8,128)(2,1)S(1)}, u32[]{:S(2)}, u32[]{:S(2)}) %collective-permute-start.4) | collective-permute-done | bytes 1048608 | tf_op jit(solution)/shard_map/ppermute | solution.py:572
  101.7 8.3 qkv.5
  110.0 8.3 qkv.6
  120.1 5.7 all-gather.14.cloned.1.call-done
  125.9 8.2 qkv.7
  134.1 8.5 qkv.4
  151.2 33.5 %collective-permute-done.6.wga_ref = bf16[1,1024,768]{2,1,0:T(8,128)(2,1)S(1)} collective-permute-done((bf16[1,1024,768]{2,1,0:T(8,128)(2,1)S(1)}, bf16[1,1024,768]{2,1,0:T(8,128)(2,1)S(1)}, u32[]{:S(2)}, u32[]{:S(2)}) %collective-permute-start.6) | collective-permute-done | bytes 1572896 | tf_op jit(solution)/shard_map/ppermute | solution.py:572
  187.1 6.8 attend.4
  201.7 28.4 %collective-permute-done.8.wgb_ref = bf16[1,1024,768]{2,1,0:T(8,128)(2,1)S(1)} collective-permute-done((bf16[1,1024,768]{2,1,0:T(8,128)(2,1)}, bf16[1,1024,768]{2,1,0:T(8,128)(2,1)S(1)}, u32[]{:S(2)}, u32[]{:S(2)}) %collective-permute-start.8) | collective-permute-done | bytes 1572896 | tf_op jit(solution)/shard_map/ppermute | solution.py:572
  236.1 6.9 attend.5
  243.0 20.8 %collective-permute-done.10.wua_ref = bf16[1,1024,768]{2,1,0:T(8,128)(2,1)} collective-permute-done((bf16[1,1024,768]{2,1,0:T(8,128)(2,1)S(1)}, bf16[1,1024,768]{2,1,0:T(8,128)(2,1)}, u32[]{:S(2)}, u32[]{:S(2)}) %collective-permute-start.10) | collective-permute-done | bytes 1572896 | tf_op jit(solution)/shard_map/ppermute | solution.py:572
  265.5 6.2 convolution_convert_fusion.11
  273.2 7.2 attend.6
  285.9 6.8 attend.7
  292.7 72.4 %collective-permute-done.13 = bf16[512,2048]{1,0:T(8,128)(2,1)} collective-permute-done((bf16[512,2048]{1,0:T(8,128)(2,1)}, bf16[512,2048]{1,0:T(8,128)(2,1)}, u32[]{:S(2)}, u32[]{:S(2)}) %collective-permute-start.13) | collective-permute-done | bytes 2097184 | tf_op jit(solution)/shard_map/ppermute | solution.py:572
  383.3 100.5 %collective-permute-done.15.wub_ref = bf16[1,1024,768]{2,1,0:T(8,128)(2,1)} collective-permute-done((bf16[1,1024,768]{2,1,0:T(8,128)(2,1)}, bf16[1,1024,768]{2,1,0:T(8,128)(2,1)}, u32[]{:S(2)}, u32[]{:S(2)}) %collective-permute-start.15) | collective-permute-done | bytes 1572896 | tf_op jit(solution)/shard_map/ppermute | solution.py:572
  496.5 16.8 %dispatch.1 = (bf16[8,128,2048]{2,1,0:T(8,128)(2,1)}, bf16[8,128,2048]{2,1,0:T(8,128)(2,1)}, bf16[8,128,2048]{2,1,0:T(8,128)(2,1)}, bf16[8,128,2048]{2,1,0:T(8,128)(2,1)}) custom-call(s32[8,4,512]{2,1,0:T(4,128)} %copy.122.rank_ref, bf16[8,512,2048]{2,1,0:T(8,128)(2,1)} %bitcast.312), custom_call_target="tpu_custom_call" | custom-call | flops 8589934592 | bytes 33554432 | tf_op jit(solution)/shard_map/dispatch/pallas_call | solution.py:372
  513.3 8.4 collective-permute-done.19.wga_ref
  523.2 10.4 all-gather.22.cloned.1.call-done
  533.6 22.0 %route_dispatch.1 = (f32[4,8,128,1]{3,2,1,0:T(8,128)}, bf16[8,128,2048]{2,1,0:T(8,128)(2,1)}, bf16[8,128,2048]{2,1,0:T(8,128)(2,1)}, bf16[8,128,2048]{2,1,0:T(8,128)(2,1)}, bf16[8,128,2048]{2,1,0:T(8,128)(2,1)}) custom-call(s32[4]{0:T(128)} %pad_add_fusion.2.ids_ref, s32[8,4,512]{2,1,0:T(4,128)} %copy.122.rank_ref, bf16[8,512,2048]{2,1,0:T(8,128)(2,1)} %bitcast.313, ...), custom_call_target="tpu_custom_call" | custom-call | flops 8589934592 | bytes 33554432 | tf_op jit(solution)/shard_map/route_dispatch/pallas_call | solution.py:408
  558.4 24.5 %expert.4 = (bf16[1024,2048]{1,0:T(8,128)(2,1)}, bf16[1024,768]{1,0:T(8,128)(2,1)}, bf16[1024,1536]{1,0:T(8,128)(2,1)}, bf16[1024,128]{1,0:T(8,128)(2,1)}) custom-call(bf16[1024,2048]{1,0:T(8,128)(2,1)} %bitcast.334, bf16[1024,2048]{1,0:T(8,128)(2,1)} %bitcast.270, f32[1024,1]{1,0:T(8,128)} %bitcast.297, bf16[1,2048,768]{2,1,0:T(8,128)(2,1)} %wgb_ref, ...), custom_call_target="tpu_custom_call" | custom-call | flops 16106127360 | bytes 26738688 | tf_op jit(solution)/shard_map/expert/pallas_call | solution.py:544
  589.4 24.8 %expert.5 = (bf16[1024,2048]{1,0:T(8,128)(2,1)}, bf16[1024,768]{1,0:T(8,128)(2,1)}, bf16[1024,1536]{1,0:T(8,128)(2,1)}, bf16[1024,128]{1,0:T(8,128)(2,1)}) custom-call(bf16[1024,2048]{1,0:T(8,128)(2,1)} %bitcast.342, bf16[1024,2048]{1,0:T(8,128)(2,1)} %bitcast.340, f32[1024,1]{1,0:T(8,128)} %bitcast.296, ...), custom_call_target="tpu_custom_call" | custom-call | flops 16106127360 | bytes 26738688 | tf_op jit(solution)/shard_map/expert/pallas_call | solution.py:544
  614.1 8.9 convolution_convert_fusion.2
  630.7 24.7 %expert.6 = (bf16[1024,2048]{1,0:T(8,128)(2,1)}, bf16[1024,768]{1,0:T(8,128)(2,1)}, bf16[1024,1536]{1,0:T(8,128)(2,1)}, bf16[1024,128]{1,0:T(8,128)(2,1)}) custom-call(bf16[1024,2048]{1,0:T(8,128)(2,1)} %bitcast.336, bf16[1024,2048]{1,0:T(8,128)(2,1)} %bitcast.330, f32[1024,1]{1,0:T(8,128)} %bitcast.295, bf16[1,1024,768]{2,1,0:T(8,128)(2,1)} %copy-done.76, ...), custom_call_target="tpu_custom_call" | custom-call | flops 16106127360 | bytes 26738688 | tf_op jit(solution)/shard_map/expert/pallas_call | solution.py:544
  655.5 24.5 %expert.7 = (bf16[1024,2048]{1,0:T(8,128)(2,1)}, bf16[1024,768]{1,0:T(8,128)(2,1)}, bf16[1024,1536]{1,0:T(8,128)(2,1)}, bf16[1024,128]{1,0:T(8,128)(2,1)}) custom-call(bf16[1024,2048]{1,0:T(8,128)(2,1)} %bitcast.338, bf16[1024,2048]{1,0:T(8,128)(2,1)} %bitcast.332, f32[1024,1]{1,0:T(8,128)} %bitcast.294, bf16[1,1024,768]{2,1,0:T(8,128)(2,1)} %copy-done.75, ...), custom_call_target="tpu_custom_call" | custom-call | flops 16106127360 | bytes 26738688 | tf_op jit(solution)/shard_map/expert/pallas_call | solution.py:544
  679.9 12.5 collective-permute-done.25
  692.6 19.5 %combine.2 = (bf16[8,512,2048]{2,1,0:T(8,128)(2,1)}, f32[8,512,4]{2,1,0:T(8,128)}) custom-call(s32[8,512,4]{2,1,0:T(8,128)} %bitcast.263, bf16[8,128,2048]{2,1,0:T(8,128)(2,1)} %bitcast.272, bf16[8,128,2048]{2,1,0:T(8,128)(2,1)} %bitcast.274, bf16[8,128,2048]{2,1,0:T(8,128)(2,1)} %bitcast.275, bf16[8,128,2048]{2,1,0:T(8,128)(2,1)} %bitcast.273, ...), custom_call_target="tpu_custom_call" | custom-call | tf_op jit(solution)/shard_map/combine/pallas_call | solution.py:485
  720.4 11.3 add_convert_fusion
  731.8 9.2 add_convert_fusion.1
  741.0 11.2 collective-permute-done.27
  758.3 7.4 all-to-all-start
  772.3 7.2 convolution_convert_fusion.4
  779.5 7.1 convolution_convert_fusion.5
  791.7 7.0 convolution_convert_fusion.3
  814.0 9.9 fusion.108
  826.3 17.7 %combine.3 = bf16[8,512,2048]{2,1,0:T(8,128)(2,1)} custom-call(s32[8,512,4]{2,1,0:T(8,128)} %bitcast.264, bf16[8,128,2048]{2,1,0:T(8,128)(2,1)} %bitcast.278, bf16[8,128,2048]{2,1,0:T(8,128)(2,1)} %bitcast.277, bf16[8,128,2048]{2,1,0:T(8,128)(2,1)} %bitcast.276, bf16[8,128,2048]{2,1,0:T(8,128)(2,1)} %bitcast.279), custom_call_target="tpu_custom_call" | custom-call | tf_op jit(solution)/shard_map/combine/pallas_call | solution.py:485
  849.1 38.8 %collective-permute-done.29 = bf16[2048,1536]{1,0:T(8,128)(2,1)} collective-permute-done((bf16[2048,1536]{1,0:T(8,128)(2,1)}, bf16[2048,1536]{1,0:T(8,128)(2,1)}, u32[]{:S(2)}, u32[]{:S(2)}) %collective-permute-start.29) | collective-permute-done | bytes 6291488 | tf_op jit(solution)/shard_map/ppermute | solution.py:572
  905.0 11.4 attend_back.4
  916.4 6.5 input_share.4
  922.9 19.9 %collective-permute-done.31 = bf16[1,512,2048]{2,1,0:T(8,128)(2,1)S(1)} collective-permute-done((bf16[1,512,2048]{2,1,0:T(8,128)(2,1)S(1)}, bf16[1,512,2048]{2,1,0:T(8,128)(2,1)S(1)}, u32[]{:S(2)}, u32[]{:S(2)}) %collective-permute-start.31) | collective-permute-done | bytes 2097184 | tf_op jit(solution)/shard_map/ppermute | solution.py:572
  949.0 5.7 fusion.27.do_ref
  954.7 11.5 attend_back.5
  966.2 6.3 input_share.5
  985.1 11.5 attend_back.6
  996.6 6.2 input_share.6
  1006.1 11.4 bitcast_convert_fusion
  1017.5 33.1 %collective-permute-done.35 = bf16[768,2048]{1,0:T(8,128)(2,1)} collective-permute-done((bf16[768,2048]{1,0:T(8,128)(2,1)}, bf16[768,2048]{1,0:T(8,128)(2,1)}, u32[]{:S(2)}, u32[]{:S(2)}) %collective-permute-start.35) | collective-permute-done | bytes 3145760 | tf_op jit(solution)/shard_map/ppermute | solution.py:572
  1051.4 8.0 reduce-scatter.9.cloned.1.call-done
  1064.5 5.7 convolution_convert_fusion.13.do_ref
  1070.2 11.7 attend_back.7
  1089.6 18.7 %collective-permute-done.37 = bf16[512,2048]{1,0:T(8,128)(2,1)} collective-permute-done((bf16[512,2048]{1,0:T(8,128)(2,1)}, bf16[512,2048]{1,0:T(8,128)(2,1)}, u32[]{:S(2)}, u32[]{:S(2)}) %collective-permute-start.37) | collective-permute-done | bytes 2097184 | tf_op jit(solution)/shard_map/ppermute | solution.py:572
  1108.3 38.5 %reduce-scatter.13.cloned.1.call-done = bf16[1024,256]{1,0:T(8,128)(2,1)} async-done(((bf16[1024,2048]{1,0:T(8,128)(2,1)}), bf16[1024,256]{1,0:T(8,128)(2,1)}) %reduce-scatter.13.cloned.1.call-update) | async-done | bytes 524304 | tf_op jit(solution)/shard_map/reduce_scatter | solution.py:924
  1146.8 6.1 input_share.7
  1159.0 15.9 %fusion.105 = (bf16[2048,1024]{0,1:T(8,128)(2,1)}, f32[2048,1024]{0,1:T(8,128)}) fusion(bf16[4,512,1024]{2,1,0:T(8,128)(2,1)} %pad_maximum_fusion.2, bf16[1,512,2048]{2,1,0:T(8,128)(2,1)} %bitcast.348, bf16[1,512,2048]{2,1,0:T(8,128)(2,1)} %bitcast.346, bf16[1,512,2048]{2,1,0:T(8,128)(2,1)S(1)} %bitcast.344, bf16[1,512,2048]{2,1,0:T(8,128)(2,1)} %bitcast.350), kind=kOutput, calls=%fused_computation.271 | convolution fusion | flops 8604614656 | bytes 25165824 | tf_op jit(solution)/shard_map/dot_general | solution.py:886
  1175.0 9.3 copy.130
  1184.3 5.7 multiply_reduce_fusion
  1217.9 21.7 %all-to-all-start.1 = ((f32[32,1,2216]{2,1,0:T(1,128)}), f32[32,1,2216]{2,1,0:T(1,128)S(1)}, u32[]{:S(2)}, u32[]{:S(2)}) async-start(f32[32,1,2216]{2,1,0:T(1,128)} %copy.132), calls=%async_computation.6 | async-start | bytes 589824 | tf_op jit(solution)/shard_map/all_to_all | solution.py:988
  1249.9 7.4 add_bitcast_fusion
  1257.3 5.9 fusion.2
  1263.2 6.1 all-to-all-start.2
  1269.3 7.0 fusion.6
  1276.3 14.0 %add_bitcast_fusion.1 = (f32[1,2048,768]{2,1,0:T(8,128)}, f32[1,2048,768]{2,1,0:T(8,128)}) fusion(f32[2048,1536]{1,0:T(8,128)} %fusion.108, bf16[2048,1536]{1,0:T(8,128)(2,1)} %collective-permute-done.30, bf16[2048,1536]{1,0:T(8,128)(2,1)} %collective-permute-done.29), kind=kLoop, calls=%fused_computation.10 | loop fusion | flops 12582912 | bytes 37748736 | tf_op jit(solution)/shard_map/broadcast_in_dim | solution.py:1028
  (512 shorter events, 283.7 us)
Async XLA Ops:
  7.2 89.5 %all-gather.12.cloned.1.call-start = ((), (), s32[]{:S(2)}) async-start(), calls=%async_computation.9 | async-start | bytes 6488064 | tf_op jit(solution)/shard_map/all_gather | solution.py:650
  14.2 111.6 %all-gather.14.cloned.1.call-start = ((), (), s32[]{:S(2)}) async-start(), calls=%async_computation.10 | async-start | bytes 4718592 | tf_op jit(solution)/shard_map/all_gather | solution.py:698
  14.3 53.4 %collective-permute-start = (bf16[1,512,2048]{2,1,0:T(8,128)(2,1)}, bf16[1,512,2048]{2,1,0:T(8,128)(2,1)}, u32[]{:S(2)}, u32[]{:S(2)}) collective-permute-start(bf16[1,512,2048]{2,1,0:T(8,128)(2,1)} %param.15), channel_id=1, source_target_pairs={{0,1},{1,0},{2,3},{3,2},{4,5},{5,4},{6,7},{7,6},{8,9},{9,8},{10,11... | collective-permute-start | bytes 6291464 | tf_op jit(solution)/shard_map/ppermute | solution.py:572
  17.3 50.4 %collective-permute-start.1 = (bf16[1,512,2048]{2,1,0:T(8,128)(2,1)}, bf16[1,512,2048]{2,1,0:T(8,128)(2,1)}, u32[]{:S(2)}, u32[]{:S(2)}) collective-permute-start(bf16[1,512,2048]{2,1,0:T(8,128)(2,1)} %param.15), channel_id=1, source_target_pairs={{0,2},{1,3},{2,0},{3,1},{4,6},{5,7},{6,4},{7,5},{8,10},{9,11},{10,... | collective-permute-start | bytes 6291464 | tf_op jit(solution)/shard_map/ppermute | solution.py:572
  34.4 28.8 %collective-permute-start.2 = (f32[32]{0:T(128)S(1)}, f32[32]{0:T(128)S(1)}, u32[]{:S(2)}, u32[]{:S(2)}) collective-permute-start(f32[32]{0:T(128)S(1)} %convert_reduce_fusion.3), channel_id=1, source_target_pairs={{0,1},{1,0},{2,3},{3,2},{4,5},{5,4},{6,7},{7,6},{8,9},{9,8},{10,11... | collective-permute-start | bytes 392 | tf_op jit(solution)/shard_map/ppermute | solution.py:572
  48.8 442.0 %copy-start.5 = (s32[8,4,512]{1,2,0:T(8,128)}, s32[8,4,512]{1,2,0:T(8,128)S(1)}, u32[]{:S(2)}) copy-start(s32[8,4,512]{1,2,0:T(8,128)S(1)} %add_select_fusion) | copy-start | bytes 196612
  63.2 3.9 collective-permute-start.3
  67.7 119.4 %all-gather.18.cloned.1.call-start = ((), (), s32[]{:S(2)}) async-start(), calls=%async_computation.18 | async-start | bytes 4718592 | tf_op jit(solution)/shard_map/all_gather | solution.py:714
  70.4 23.8 %collective-permute-start.4 = (bf16[1,256,2048]{2,1,0:T(8,128)(2,1)S(1)}, bf16[1,256,2048]{2,1,0:T(8,128)(2,1)S(1)}, u32[]{:S(2)}, u32[]{:S(2)}) collective-permute-start(bf16[1,256,2048]{2,1,0:T(8,128)(2,1)S(1)} %slice.253), channel_id=1, source_target_pairs={{0,2},{1,3},{2,0},{3,1},{4,6},{5,7},{6,4},{7,5},{8,10},{9,11},{10,... | collective-permute-start | bytes 3145736 | tf_op jit(solution)/shard_map/ppermute | solution.py:572
  72.1 23.0 %collective-permute-start.5 = (bf16[1,256,2048]{2,1,0:T(8,128)(2,1)S(1)}, bf16[1,256,2048]{2,1,0:T(8,128)(2,1)S(1)}, u32[]{:S(2)}, u32[]{:S(2)}) collective-permute-start(bf16[1,256,2048]{2,1,0:T(8,128)(2,1)S(1)} %slice.254), channel_id=1, source_target_pairs={{0,1},{1,0},{2,3},{3,2},{4,5},{5,4},{6,7},{7,6},{8,9},{9,8},{10,11... | collective-permute-start | bytes 3145736 | tf_op jit(solution)/shard_map/ppermute | solution.py:572
  125.8 147.4 %all-gather.20.cloned.1.call-start = ((), (), s32[]{:S(2)}) async-start(), calls=%async_computation.19 | async-start | bytes 4718592 | tf_op jit(solution)/shard_map/all_gather | solution.py:714
  144.5 352.1 %all-gather.24.cloned.1.call-start = ((), (), s32[]{:S(2)}) async-start(), calls=%async_computation.21 | async-start | bytes 18874368 | tf_op jit(solution)/shard_map/all_gather | solution.py:747
  148.2 36.5 %collective-permute-start.6 = (bf16[1,1024,768]{2,1,0:T(8,128)(2,1)S(1)}, bf16[1,1024,768]{2,1,0:T(8,128)(2,1)S(1)}, u32[]{:S(2)}, u32[]{:S(2)}) collective-permute-start(bf16[1,1024,768]{2,1,0:T(8,128)(2,1)S(1)} %get-tuple-element.543), channel_id=1, source_target_pairs={{0,1},{1,0},{2,3},{3,2},{4,5},{5,4},{6,7},{7,6},{8,9},{9,8},{10,11... | collective-permute-start | bytes 4718600 | tf_op jit(solution)/shard_map/ppermute | solution.py:572
  149.7 36.2 %collective-permute-start.7 = (bf16[1,1024,768]{2,1,0:T(8,128)(2,1)S(1)}, bf16[1,1024,768]{2,1,0:T(8,128)(2,1)S(1)}, u32[]{:S(2)}, u32[]{:S(2)}) collective-permute-start(bf16[1,1024,768]{2,1,0:T(8,128)(2,1)S(1)} %get-tuple-element.543), channel_id=1, source_target_pairs={{0,2},{1,3},{2,0},{3,1},{4,6},{5,7},{6,4},{7,5},{8,10},{9,11},{10,... | collective-permute-start | bytes 4718600 | tf_op jit(solution)/shard_map/ppermute | solution.py:572
  193.9 339.6 %all-gather.22.cloned.1.call-start = ((), (), s32[]{:S(2)}) async-start(), calls=%async_computation.20 | async-start | bytes 18874368 | tf_op jit(solution)/shard_map/all_gather | solution.py:751
  194.0 36.1 %collective-permute-start.8 = (bf16[1,1024,768]{2,1,0:T(8,128)(2,1)}, bf16[1,1024,768]{2,1,0:T(8,128)(2,1)S(1)}, u32[]{:S(2)}, u32[]{:S(2)}) collective-permute-start(bf16[1,1024,768]{2,1,0:T(8,128)(2,1)} %get-tuple-element.542), channel_id=1, source_target_pairs={{0,1},{1,0},{2,3},{3,2},{4,5},{5,4},{6,7},{7,6},{8,9},{9,8},{10,11... | collective-permute-start | bytes 4718600 | tf_op jit(solution)/shard_map/ppermute | solution.py:572
  195.5 36.2 %collective-permute-start.9 = (bf16[1,1024,768]{2,1,0:T(8,128)(2,1)}, bf16[1,1024,768]{2,1,0:T(8,128)(2,1)S(1)}, u32[]{:S(2)}, u32[]{:S(2)}) collective-permute-start(bf16[1,1024,768]{2,1,0:T(8,128)(2,1)} %get-tuple-element.542), channel_id=1, source_target_pairs={{0,2},{1,3},{2,0},{3,1},{4,6},{5,7},{6,4},{7,5},{8,10},{9,11},{10,... | collective-permute-start | bytes 4718600 | tf_op jit(solution)/shard_map/ppermute | solution.py:572
  200.2 63.7 %collective-permute-start.10 = (bf16[1,1024,768]{2,1,0:T(8,128)(2,1)S(1)}, bf16[1,1024,768]{2,1,0:T(8,128)(2,1)}, u32[]{:S(2)}, u32[]{:S(2)}) collective-permute-start(bf16[1,1024,768]{2,1,0:T(8,128)(2,1)S(1)} %get-tuple-element.541), channel_id=1, source_target_pairs={{0,1},{1,0},{2,3},{3,2},{4,5},{5,4},{6,7},{7,6},{8,9},{9,8},{10,11... | collective-permute-start | bytes 4718600 | tf_op jit(solution)/shard_map/ppermute | solution.py:572
  200.8 64.7 %collective-permute-start.11 = (bf16[1,1024,768]{2,1,0:T(8,128)(2,1)S(1)}, bf16[1,1024,768]{2,1,0:T(8,128)(2,1)}, u32[]{:S(2)}, u32[]{:S(2)}) collective-permute-start(bf16[1,1024,768]{2,1,0:T(8,128)(2,1)S(1)} %get-tuple-element.541), channel_id=1, source_target_pairs={{0,2},{1,3},{2,0},{3,1},{4,6},{5,7},{6,4},{7,5},{8,10},{9,11},{10,... | collective-permute-start | bytes 4718600 | tf_op jit(solution)/shard_map/ppermute | solution.py:572
  235.4 129.7 %collective-permute-start.12 = (bf16[512,2048]{1,0:T(8,128)(2,1)}, bf16[512,2048]{1,0:T(8,128)(2,1)}, u32[]{:S(2)}, u32[]{:S(2)}) collective-permute-start(bf16[512,2048]{1,0:T(8,128)(2,1)} %convolution_convert_fusion.12), channel_id=1, source_target_pairs={{0,1},{1,0},{2,3},{3,2},{4,5},{5,4},{6,7},{7,6},{8,9},{9,8},{10,11... | collective-permute-start | bytes 6291464 | tf_op jit(solution)/shard_map/ppermute | solution.py:572
  271.7 93.4 %collective-permute-start.13 = (bf16[512,2048]{1,0:T(8,128)(2,1)}, bf16[512,2048]{1,0:T(8,128)(2,1)}, u32[]{:S(2)}, u32[]{:S(2)}) collective-permute-start(bf16[512,2048]{1,0:T(8,128)(2,1)} %convolution_convert_fusion.11), channel_id=1, source_target_pairs={{0,2},{1,3},{2,0},{3,1},{4,6},{5,7},{6,4},{7,5},{8,10},{9,11},{10,... | collective-permute-start | bytes 6291464 | tf_op jit(solution)/shard_map/ppermute | solution.py:572
  285.2 84.7 %collective-permute-start.14 = (bf16[512,2048]{1,0:T(8,128)(2,1)}, bf16[512,2048]{1,0:T(8,128)(2,1)S(1)}, u32[]{:S(2)}, u32[]{:S(2)}) collective-permute-start(bf16[512,2048]{1,0:T(8,128)(2,1)} %convolution_convert_fusion.10), channel_id=1, source_target_pairs={{0,3},{1,2},{2,1},{3,0},{4,7},{5,6},{6,5},{7,4},{8,11},{9,10},{10,... | collective-permute-start | bytes 6291464 | tf_op jit(solution)/shard_map/ppermute | solution.py:572
  379.1 313.4 %all-gather.16.cloned.1.call-start = ((), (), s32[]{:S(2)}) async-start(), calls=%async_computation.11 | async-start | bytes 4718592 | tf_op jit(solution)/shard_map/all_gather | solution.py:776
  379.2 105.0 %collective-permute-start.17 = (bf16[1,768,2048]{2,1,0:T(8,128)(2,1)}, bf16[1,768,2048]{2,1,0:T(8,128)(2,1)}, u32[]{:S(2)}, u32[]{:S(2)}) collective-permute-start(bf16[1,768,2048]{2,1,0:T(8,128)(2,1)} %wdb_ref), channel_id=1, source_target_pairs={{0,1},{1,0},{2,3},{3,2},{4,5},{5,4},{6,7},{7,6},{8,9},{9,8},{10,11... | collective-permute-start | bytes 9437192 | tf_op jit(solution)/shard_map/ppermute | solution.py:572
  379.2 104.9 %collective-permute-start.18 = (bf16[1,768,2048]{2,1,0:T(8,128)(2,1)}, bf16[1,768,2048]{2,1,0:T(8,128)(2,1)}, u32[]{:S(2)}, u32[]{:S(2)}) collective-permute-start(bf16[1,768,2048]{2,1,0:T(8,128)(2,1)} %wdb_ref), channel_id=1, source_target_pairs={{0,2},{1,3},{2,0},{3,1},{4,6},{5,7},{6,4},{7,5},{8,10},{9,11},{10,... | collective-permute-start | bytes 9437192 | tf_op jit(solution)/shard_map/ppermute | solution.py:572
  380.7 103.0 %collective-permute-start.15 = (bf16[1,1024,768]{2,1,0:T(8,128)(2,1)}, bf16[1,1024,768]{2,1,0:T(8,128)(2,1)}, u32[]{:S(2)}, u32[]{:S(2)}) collective-permute-start(bf16[1,1024,768]{2,1,0:T(8,128)(2,1)} %get-tuple-element.540), channel_id=1, source_target_pairs={{0,1},{1,0},{2,3},{3,2},{4,5},{5,4},{6,7},{7,6},{8,9},{9,8},{10,11... | collective-permute-start | bytes 4718600 | tf_op jit(solution)/shard_map/ppermute | solution.py:572
  382.7 101.5 %collective-permute-start.16 = (bf16[1,1024,768]{2,1,0:T(8,128)(2,1)}, bf16[1,1024,768]{2,1,0:T(8,128)(2,1)}, u32[]{:S(2)}, u32[]{:S(2)}) collective-permute-start(bf16[1,1024,768]{2,1,0:T(8,128)(2,1)} %get-tuple-element.540), channel_id=1, source_target_pairs={{0,2},{1,3},{2,0},{3,1},{4,6},{5,7},{6,4},{7,5},{8,10},{9,11},{10,... | collective-permute-start | bytes 4718600 | tf_op jit(solution)/shard_map/ppermute | solution.py:572
  484.2 37.6 %collective-permute-start.19 = (bf16[1,1024,768]{2,1,0:T(8,128)(2,1)}, bf16[1,1024,768]{2,1,0:T(8,128)(2,1)}, u32[]{:S(2)}, u32[]{:S(2)}) collective-permute-start(bf16[1,1024,768]{2,1,0:T(8,128)(2,1)} %copy-done.76), channel_id=1, source_target_pairs={{0,2},{1,3},{2,0},{3,1},{4,6},{5,7},{6,4},{7,5},{8,10},{9,11},{10,... | collective-permute-start | bytes 4718600 | tf_op jit(solution)/shard_map/ppermute | solution.py:572
  485.6 37.6 %collective-permute-start.20 = (bf16[1,1024,768]{2,1,0:T(8,128)(2,1)}, bf16[1,1024,768]{2,1,0:T(8,128)(2,1)}, u32[]{:S(2)}, u32[]{:S(2)}) collective-permute-start(bf16[1,1024,768]{2,1,0:T(8,128)(2,1)} %copy-done.77), channel_id=1, source_target_pairs={{0,1},{1,0},{2,3},{3,2},{4,5},{5,4},{6,7},{7,6},{8,9},{9,8},{10,11... | collective-permute-start | bytes 4718600 | tf_op jit(solution)/shard_map/ppermute | solution.py:572
  489.5 68.9 %collective-permute-start.21 = (bf16[1,1024,768]{2,1,0:T(8,128)(2,1)}, bf16[1,1024,768]{2,1,0:T(8,128)(2,1)}, u32[]{:S(2)}, u32[]{:S(2)}) collective-permute-start(bf16[1,1024,768]{2,1,0:T(8,128)(2,1)} %collective-permute-done.10.wua_ref), channel_id=1, source_target_pairs={{0,2},{1,3},{2,0},{3,1},{4,6},{5,7},{6,4},{7,5},{8,10},{9,11},{10,... | collective-permute-start | bytes 4718600 | tf_op jit(solution)/shard_map/ppermute | solution.py:572
  490.1 68.4 %collective-permute-start.22 = (bf16[1,1024,768]{2,1,0:T(8,128)(2,1)}, bf16[1,1024,768]{2,1,0:T(8,128)(2,1)}, u32[]{:S(2)}, u32[]{:S(2)}) collective-permute-start(bf16[1,1024,768]{2,1,0:T(8,128)(2,1)} %collective-permute-done.16.wub_ref), channel_id=1, source_target_pairs={{0,1},{1,0},{2,3},{3,2},{4,5},{5,4},{6,7},{7,6},{8,9},{9,8},{10,11... | collective-permute-start | bytes 4718600 | tf_op jit(solution)/shard_map/ppermute | solution.py:572
  493.5 94.7 %collective-permute-start.23 = (bf16[1,384,2048]{2,1,0:T(8,128)(2,1)S(1)}, bf16[1,384,2048]{2,1,0:T(8,128)(2,1)}, u32[]{:S(2)}, u32[]{:S(2)}) collective-permute-start(bf16[1,384,2048]{2,1,0:T(8,128)(2,1)S(1)} %slice.262), channel_id=1, source_target_pairs={{0,2},{1,3},{2,0},{3,1},{4,6},{5,7},{6,4},{7,5},{8,10},{9,11},{10,... | collective-permute-start | bytes 4718600 | tf_op jit(solution)/shard_map/ppermute | solution.py:572
  521.7 67.5 %collective-permute-start.24 = (bf16[1,384,2048]{2,1,0:T(8,128)(2,1)S(1)}, bf16[1,384,2048]{2,1,0:T(8,128)(2,1)}, u32[]{:S(2)}, u32[]{:S(2)}) collective-permute-start(bf16[1,384,2048]{2,1,0:T(8,128)(2,1)S(1)} %slice.263), channel_id=1, source_target_pairs={{0,1},{1,0},{2,3},{3,2},{4,5},{5,4},{6,7},{7,6},{8,9},{9,8},{10,11... | collective-permute-start | bytes 4718600 | tf_op jit(solution)/shard_map/ppermute | solution.py:572
  589.3 299.8 %reduce-scatter.7.cloned.1.call-start = ((), (), s32[]{:S(2)}) async-start(), calls=%async_computation.12 | async-start | bytes 18874368 | tf_op jit(solution)/shard_map/reduce_scatter | solution.py:807
  623.5 68.9 %collective-permute-start.25 = (bf16[1024,1536]{1,0:T(8,128)(2,1)S(1)}, bf16[1024,1536]{1,0:T(8,128)(2,1)}, u32[]{:S(2)}, u32[]{:S(2)}) collective-permute-start(bf16[1024,1536]{1,0:T(8,128)(2,1)S(1)} %get-tuple-element.537), channel_id=1, source_target_pairs={{0,1},{1,0},{2,3},{3,2},{4,5},{5,4},{6,7},{7,6},{8,9},{9,8},{10,11... | collective-permute-start | bytes 9437192 | tf_op jit(solution)/shard_map/ppermute | solution.py:572
  624.4 68.1 %collective-permute-start.26 = (bf16[1024,1536]{1,0:T(8,128)(2,1)S(1)}, bf16[1024,1536]{1,0:T(8,128)(2,1)}, u32[]{:S(2)}, u32[]{:S(2)}) collective-permute-start(bf16[1024,1536]{1,0:T(8,128)(2,1)S(1)} %get-tuple-element.536), channel_id=1, source_target_pairs={{0,2},{1,3},{2,0},{3,1},{4,6},{5,7},{6,4},{7,5},{8,10},{9,11},{10,... | collective-permute-start | bytes 9437192 | tf_op jit(solution)/shard_map/ppermute | solution.py:572
  718.1 34.1 %collective-permute-start.27 = (bf16[384,2048]{1,0:T(8,128)(2,1)S(1)}, bf16[384,2048]{1,0:T(8,128)(2,1)S(1)}, u32[]{:S(2)}, u32[]{:S(2)}) collective-permute-start(bf16[384,2048]{1,0:T(8,128)(2,1)S(1)} %get-tuple-element.539), channel_id=1, source_target_pairs={{0,1},{1,0},{2,3},{3,2},{4,5},{5,4},{6,7},{7,6},{8,9},{9,8},{10,11... | collective-permute-start | bytes 4718600 | tf_op jit(solution)/shard_map/ppermute | solution.py:572
  719.8 33.6 %collective-permute-start.28 = (bf16[384,2048]{1,0:T(8,128)(2,1)S(1)}, bf16[384,2048]{1,0:T(8,128)(2,1)S(1)}, u32[]{:S(2)}, u32[]{:S(2)}) collective-permute-start(bf16[384,2048]{1,0:T(8,128)(2,1)S(1)} %get-tuple-element.538), channel_id=1, source_target_pairs={{0,2},{1,3},{2,0},{3,1},{4,6},{5,7},{6,4},{7,5},{8,10},{9,11},{10,... | collective-permute-start | bytes 4718600 | tf_op jit(solution)/shard_map/ppermute | solution.py:572
  753.4 134.6 %collective-permute-start.29 = (bf16[2048,1536]{1,0:T(8,128)(2,1)}, bf16[2048,1536]{1,0:T(8,128)(2,1)}, u32[]{:S(2)}, u32[]{:S(2)}) collective-permute-start(bf16[2048,1536]{1,0:T(8,128)(2,1)} %add_convert_fusion.1), channel_id=1, source_target_pairs={{0,1},{1,0},{2,3},{3,2},{4,5},{5,4},{6,7},{7,6},{8,9},{9,8},{10,11... | collective-permute-start | bytes 18874376 | tf_op jit(solution)/shard_map/ppermute | solution.py:572
  754.8 134.3 %collective-permute-start.30 = (bf16[2048,1536]{1,0:T(8,128)(2,1)}, bf16[2048,1536]{1,0:T(8,128)(2,1)}, u32[]{:S(2)}, u32[]{:S(2)}) collective-permute-start(bf16[2048,1536]{1,0:T(8,128)(2,1)} %add_convert_fusion), channel_id=1, source_target_pairs={{0,2},{1,3},{2,0},{3,1},{4,6},{5,7},{6,4},{7,5},{8,10},{9,11},{10,... | collective-permute-start | bytes 18874376 | tf_op jit(solution)/shard_map/ppermute | solution.py:572
  758.3 85.6 %all-to-all-start = ((f32[8,512,4]{1,2,0:T(4,128)}), f32[8,512,4]{1,2,0:T(4,128)S(1)}, u32[]{:S(2)}, u32[]{:S(2)}) async-start(f32[8,512,4]{1,2,0:T(4,128)} %copy.124), calls=%async_computation.1 | async-start | bytes 131072 | tf_op jit(solution)/shard_map/all_to_all | solution.py:832
  765.7 293.8 %reduce-scatter.9.cloned.1.call-start = ((), (), s32[]{:S(2)}) async-start(), calls=%async_computation.13 | async-start | bytes 18874368 | tf_op jit(solution)/shard_map/reduce_scatter | solution.py:868
  889.2 219.2 %reduce-scatter.11.cloned.1.call-start = ((), (), s32[]{:S(2)}) async-start(), calls=%async_computation.14 | async-start | bytes 2359296 | tf_op jit(solution)/shard_map/reduce_scatter | solution.py:918
  899.6 43.2 %collective-permute-start.31 = (bf16[1,512,2048]{2,1,0:T(8,128)(2,1)S(1)}, bf16[1,512,2048]{2,1,0:T(8,128)(2,1)S(1)}, u32[]{:S(2)}, u32[]{:S(2)}) collective-permute-start(bf16[1,512,2048]{2,1,0:T(8,128)(2,1)S(1)} %get-tuple-element.530), channel_id=1, source_target_pairs={{0,1},{1,0},{2,3},{3,2},{4,5},{5,4},{6,7},{7,6},{8,9},{9,8},{10,11... | collective-permute-start | bytes 6291464 | tf_op jit(solution)/shard_map/ppermute | solution.py:572
  900.9 45.5 %collective-permute-start.32 = (bf16[1,512,2048]{2,1,0:T(8,128)(2,1)S(1)}, bf16[1,512,2048]{2,1,0:T(8,128)(2,1)S(1)}, u32[]{:S(2)}, u32[]{:S(2)}) collective-permute-start(bf16[1,512,2048]{2,1,0:T(8,128)(2,1)S(1)} %get-tuple-element.530), channel_id=1, source_target_pairs={{0,2},{1,3},{2,0},{3,1},{4,6},{5,7},{6,4},{7,5},{8,10},{9,11},{10,... | collective-permute-start | bytes 6291464 | tf_op jit(solution)/shard_map/ppermute | solution.py:572
  946.5 27.6 %collective-permute-start.33 = (bf16[1,256,2048]{2,1,0:T(8,128)(2,1)S(1)}, bf16[1,256,2048]{2,1,0:T(8,128)(2,1)}, u32[]{:S(2)}, u32[]{:S(2)}) collective-permute-start(bf16[1,256,2048]{2,1,0:T(8,128)(2,1)S(1)} %slice.271), channel_id=1, source_target_pairs={{0,2},{1,3},{2,0},{3,1},{4,6},{5,7},{6,4},{7,5},{8,10},{9,11},{10,... | collective-permute-start | bytes 3145736 | tf_op jit(solution)/shard_map/ppermute | solution.py:572
  948.4 25.8 %collective-permute-start.34 = (bf16[1,256,2048]{2,1,0:T(8,128)(2,1)}, bf16[1,256,2048]{2,1,0:T(8,128)(2,1)}, u32[]{:S(2)}, u32[]{:S(2)}) collective-permute-start(bf16[1,256,2048]{2,1,0:T(8,128)(2,1)} %slice.272), channel_id=1, source_target_pairs={{0,1},{1,0},{2,3},{3,2},{4,5},{5,4},{6,7},{7,6},{8,9},{9,8},{10,11... | collective-permute-start | bytes 3145736 | tf_op jit(solution)/shard_map/ppermute | solution.py:572
  974.1 172.7 %reduce-scatter.13.cloned.1.call-start = ((), (), s32[]{:S(2)}) async-start(), calls=%async_computation.15 | async-start | bytes 4718592 | tf_op jit(solution)/shard_map/reduce_scatter | solution.py:924
  982.4 68.3 %collective-permute-start.35 = (bf16[768,2048]{1,0:T(8,128)(2,1)}, bf16[768,2048]{1,0:T(8,128)(2,1)}, u32[]{:S(2)}, u32[]{:S(2)}) collective-permute-start(bf16[768,2048]{1,0:T(8,128)(2,1)} %add_convert_fusion.3), channel_id=1, source_target_pairs={{0,1},{1,0},{2,3},{3,2},{4,5},{5,4},{6,7},{7,6},{8,9},{9,8},{10,11... | collective-permute-start | bytes 9437192 | tf_op jit(solution)/shard_map/ppermute | solution.py:572
  983.8 67.6 %collective-permute-start.36 = (bf16[768,2048]{1,0:T(8,128)(2,1)}, bf16[768,2048]{1,0:T(8,128)(2,1)}, u32[]{:S(2)}, u32[]{:S(2)}) collective-permute-start(bf16[768,2048]{1,0:T(8,128)(2,1)} %add_convert_fusion.2), channel_id=1, source_target_pairs={{0,2},{1,3},{2,0},{3,1},{4,6},{5,7},{6,4},{7,5},{8,10},{9,11},{10,... | collective-permute-start | bytes 9437192 | tf_op jit(solution)/shard_map/ppermute | solution.py:572
  1059.5 135.4 %reduce-scatter.15.cloned.1.call-start = ((), (), s32[]{:S(2)}) async-start(), calls=%async_computation.16 | async-start | bytes 2359296 | tf_op jit(solution)/shard_map/reduce_scatter | solution.py:947
  1061.6 46.7 %collective-permute-start.38 = (bf16[512,2048]{1,0:T(8,128)(2,1)}, bf16[512,2048]{1,0:T(8,128)(2,1)}, u32[]{:S(2)}, u32[]{:S(2)}) collective-permute-start(bf16[512,2048]{1,0:T(8,128)(2,1)} %input_share.6), channel_id=1, source_target_pairs={{0,2},{1,3},{2,0},{3,1},{4,6},{5,7},{6,4},{7,5},{8,10},{9,11},{10,... | collective-permute-start | bytes 6291464 | tf_op jit(solution)/shard_map/ppermute | solution.py:572
  1063.1 45.3 %collective-permute-start.37 = (bf16[512,2048]{1,0:T(8,128)(2,1)}, bf16[512,2048]{1,0:T(8,128)(2,1)}, u32[]{:S(2)}, u32[]{:S(2)}) collective-permute-start(bf16[512,2048]{1,0:T(8,128)(2,1)} %input_share.5), channel_id=1, source_target_pairs={{0,1},{1,0},{2,3},{3,2},{4,5},{5,4},{6,7},{7,6},{8,9},{9,8},{10,11... | collective-permute-start | bytes 6291464 | tf_op jit(solution)/shard_map/ppermute | solution.py:572
  1152.9 38.2 %collective-permute-start.39 = (bf16[2,2,256,128]{3,2,1,0:T(8,128)(2,1)S(1)}, bf16[2,2,256,128]{3,2,1,0:T(8,128)(2,1)S(1)}, u32[]{:S(2)}, u32[]{:S(2)}) collective-permute-start(bf16[2,2,256,128]{3,2,1,0:T(8,128)(2,1)S(1)} %copy-done.83), channel_id=1, source_target_pairs={{0,0},{8,4},{16,8},{24,12},{1,1},{9,5},{17,9},{25,13},{2,2},{10,6}... | collective-permute-start | bytes 786440 | tf_op jit(solution)/shard_map/ppermute | solution.py:896
  1153.7 37.4 %collective-permute-start.40 = (bf16[2,2,256,128]{3,2,1,0:T(8,128)(2,1)S(1)}, bf16[2,2,256,128]{3,2,1,0:T(8,128)(2,1)S(1)}, u32[]{:S(2)}, u32[]{:S(2)}) collective-permute-start(bf16[2,2,256,128]{3,2,1,0:T(8,128)(2,1)S(1)} %copy-done.83), channel_id=1, source_target_pairs={{4,0},{12,4},{20,8},{28,12},{5,1},{13,5},{21,9},{29,13},{6,2},{14,... | collective-permute-start | bytes 786440 | tf_op jit(solution)/shard_map/ppermute | solution.py:896
  1155.0 102.3 %collective-permute-start.46 = (bf16[512,2048]{1,0:T(8,128)(2,1)}, bf16[512,2048]{1,0:T(8,128)(2,1)}, u32[]{:S(2)}, u32[]{:S(2)}) collective-permute-start(bf16[512,2048]{1,0:T(8,128)(2,1)} %input_share.7), channel_id=1, source_target_pairs={{0,3},{1,2},{2,1},{3,0},{4,7},{5,6},{6,5},{7,4},{8,11},{9,10},{10,... | collective-permute-start | bytes 6291464 | tf_op jit(solution)/shard_map/ppermute | solution.py:572
  1159.0 138.0 %reduce-scatter.17.cloned.1.call-start = ((), (), s32[]{:S(2)}) async-start(), calls=%async_computation.17 | async-start | bytes 4718592 | tf_op jit(solution)/shard_map/reduce_scatter | solution.py:965
  1194.9 4.2 collective-permute-start.41
  1197.4 3.9 collective-permute-start.42
  1205.8 33.8 %collective-permute-start.43 = (bf16[512,256]{1,0:T(8,128)(2,1)S(1)}, bf16[512,256]{1,0:T(8,128)(2,1)}, u32[]{:S(2)}, u32[]{:S(2)}) collective-permute-start(bf16[512,256]{1,0:T(8,128)(2,1)S(1)} %get-tuple-element.561), channel_id=1, source_target_pairs={{0,1},{1,0},{2,3},{3,2},{4,5},{5,4},{6,7},{7,6},{8,9},{9,8},{10,11... | collective-permute-start | bytes 786440 | tf_op jit(solution)/shard_map/ppermute | solution.py:572
  1206.7 34.6 %collective-permute-start.44 = (bf16[512,256]{1,0:T(8,128)(2,1)S(1)}, bf16[512,256]{1,0:T(8,128)(2,1)}, u32[]{:S(2)}, u32[]{:S(2)}) collective-permute-start(bf16[512,256]{1,0:T(8,128)(2,1)S(1)} %get-tuple-element.559), channel_id=1, source_target_pairs={{0,2},{1,3},{2,0},{3,1},{4,6},{5,7},{6,4},{7,5},{8,10},{9,11},{10,... | collective-permute-start | bytes 786440 | tf_op jit(solution)/shard_map/ppermute | solution.py:572
  1207.0 36.0 %collective-permute-start.45 = (bf16[512,256]{1,0:T(8,128)(2,1)S(1)}, bf16[512,256]{1,0:T(8,128)(2,1)}, u32[]{:S(2)}, u32[]{:S(2)}) collective-permute-start(bf16[512,256]{1,0:T(8,128)(2,1)S(1)} %get-tuple-element.557), channel_id=1, source_target_pairs={{0,3},{1,2},{2,1},{3,0},{4,7},{5,6},{6,5},{7,4},{8,11},{9,10},{10,... | collective-permute-start | bytes 786440 | tf_op jit(solution)/shard_map/ppermute | solution.py:572
  1217.9 45.2 %all-to-all-start.1 = ((f32[32,1,2216]{2,1,0:T(1,128)}), f32[32,1,2216]{2,1,0:T(1,128)S(1)}, u32[]{:S(2)}, u32[]{:S(2)}) async-start(f32[32,1,2216]{2,1,0:T(1,128)} %copy.132), calls=%async_computation.6 | async-start | bytes 589824 | tf_op jit(solution)/shard_map/all_to_all | solution.py:988
  1263.2 32.5 %all-to-all-start.2 = ((bf16[32,64,256]{2,1,0:T(8,128)(2,1)}), bf16[32,64,256]{2,1,0:T(8,128)(2,1)S(1)}, u32[]{:S(2)}, u32[]{:S(2)}) async-start(bf16[32,64,256]{2,1,0:T(8,128)(2,1)} %bitcast.112), calls=%async_computation.8 | async-start | bytes 2097152 | tf_op jit(solution)/shard_map/all_to_all | solution.py:972
  (109 other events, 1199.4 us)
Sparse Core Ops, SparseCore 0:
  14.3 63.5 all-gather.11
  79.5 46.2 all-gather.13
  128.0 45.3 all-gather.17
  175.4 45.8 all-gather.19
  222.8 149.8 all-gather.23
  379.2 154.2 all-gather.21
  589.4 48.8 all-gather.15
  712.2 171.7 reduce-scatter.6
  889.3 170.1 reduce-scatter.8
  1061.6 34.1 reduce-scatter.10
  1098.1 48.6 reduce-scatter.12
  1159.1 33.9 reduce-scatter.14
  1197.5 52.8 reduce-scatter.16

commit v5 on v4

--- a/solution.py
+++ b/solution.py
@@ -915,9 +915,6 @@
         if d == 2 and four:
             branches[2], branches[3] = lax.optimization_barrier((branches[2], branches[3]))
         if d == col_count - 1:
-            early_prompt = lax.psum_scatter(
-                jnp.stack(prompts[:batch], axis=0), "row", scatter_dimension=2, tiled=True
-            )
             branches[d], dn_got, grad_out, y_sum = lax.optimization_barrier(
                 (branches[d], dn_got, grad_out, y_sum)
             )
@@ -932,8 +929,8 @@
         pairs.append(pair)
         gain_q_grad = gain_q_grad + gain_part[0]
         if d == col_count - 1:
-            grad_q, prompts[-1], pairs[-1], sent, early_prompt, grad_out = lax.optimization_barrier(
-                (grad_q, prompts[-1], pairs[-1], sent, early_prompt, grad_out)
+            grad_q, prompts[-1], pairs[-1], sent, grad_out = lax.optimization_barrier(
+                (grad_q, prompts[-1], pairs[-1], sent, grad_out)
             )
         share = input_share(grad_q, wide, F32 if d == 0 else BF)
         shares.append(share)
@@ -944,24 +941,23 @@
     grad_q = over_tokens(normed_all, after(jnp.stack(grad_qs, axis=0), shares[-1]))
     gain_one_grad = jnp.sum(grad_q * wide[:, : heads * HEAD].astype(F32), axis=1)
     grad_q = grad_q.astype(BF)
-    late_prompt = lax.psum_scatter(
-        jnp.stack(prompts[batch:], axis=0), "row", scatter_dimension=2, tiled=True
-    )
-    early_prompt = to_owners(after(early_prompt, shares[-1]))
-    early_prompt, grad_q = lax.optimization_barrier((early_prompt, grad_q))
-    for first in range(0, col_count, batch):
-        prompt = early_prompt
-        if first > 0:
-            prompt = to_owners(late_prompt)
-        for d in range(first, first + batch):
-            pair = pairs[d] + prompt[d - first].astype(F32)
-            key_dy = back_turn(pair[0], coses[d], sines[d])
-            key_hat = back_turn(kvs[d][0].astype(F32), coses[d], sines[d]) / gain_k
-            gain_k_grad = gain_k_grad + jnp.sum(key_dy * key_hat, axis=0)
-            key_raw = norm_back(key_dy, key_hat, scales[d][:, heads : heads + 1], gain_k)
-            grad_kv = jnp.concatenate([key_raw.astype(BF), pair[1].astype(BF)], axis=1)
-            grad_kvs.append(grad_kv)
-            kv_moved.append(grad_kv if d == 0 else swap(grad_kv, d, col_count))
+    prompt = jnp.stack(prompts, axis=0)
+    prompt = lax.psum_scatter(prompt, "row", scatter_dimension=2, tiled=True)
+    ffe = w_gate.shape[2]
+    own_gu = after(own_grads[0], grad_q)
+    grad_gate = own_gu[:, :ffe] + sum(v[:, :ffe].astype(F32) for v in gu_got)
+    grad_up = own_gu[:, ffe:] + sum(v[:, ffe:].astype(F32) for v in gu_got)
+    prompt, grad_gate, grad_up, _ = lax.optimization_barrier((prompt, grad_gate, grad_up, grad_q))
+    prompt = to_owners(prompt)
+    for d in slots:
+        pair = pairs[d] + prompt[d].astype(F32)
+        key_dy = back_turn(pair[0], coses[d], sines[d])
+        key_hat = back_turn(kvs[d][0].astype(F32), coses[d], sines[d]) / gain_k
+        gain_k_grad = gain_k_grad + jnp.sum(key_dy * key_hat, axis=0)
+        key_raw = norm_back(key_dy, key_hat, scales[d][:, heads : heads + 1], gain_k)
+        grad_kv = jnp.concatenate([key_raw.astype(BF), pair[1].astype(BF)], axis=1)
+        grad_kvs.append(grad_kv)
+        kv_moved.append(grad_kv if d == 0 else swap(grad_kv, d, col_count))
     grad_q = lax.psum_scatter(grad_q, "row", scatter_dimension=0, tiled=True)
 
     grad_kv = over_tokens(normed_all, jnp.stack(grad_kvs, axis=0))
@@ -1005,11 +1001,7 @@
     x_hat = x_wide * x_spread
     input_grad = hidden_grad + norm_back(input_sum, x_hat, x_spread, gain_one)
 
-    own_grads, _ = lax.optimization_barrier((own_grads, kv_share))
-    ffe = w_gate.shape[2]
-    grad_gate = own_grads[0][:, :ffe] + sum(v[:, :ffe].astype(F32) for v in gu_got)
-    grad_up = own_grads[0][:, ffe:] + sum(v[:, ffe:].astype(F32) for v in gu_got)
-    grad_down = own_grads[1] + sum(v.astype(F32) for v in dn_got)
+    grad_down = after(own_grads[1], kv_share) + sum(v.astype(F32) for v in dn_got)
     layer_output = (hidden + y_sum.astype(F32)).astype(BF)
 
     return (

time: 1320 us -> 1330 us (level)
  waiting for transfers between devices: 518 us -> 542 us
    reduce_scatter x1, waiting for transfers between devices: 0.01 us -> 44.5 us  [per_device(): grad_q = lax.psum_scatter(grad_q, 'row', scatter_dimension=0, tiled=True)]
    reduce_scatter x1, waiting for transfers between devices: 38.5 us -> 4.95 us  [per_device(): lax.psum_scatter(grad_out, 'row', scatter_dimension=1, tiled=True)]
    all_to_all x1, starting transfers between devices: 21.7 us -> 7.64 us  [per_device(): lax.all_to_all(jnp.concatenate(tail, axis=1), ('row', 'col'), split_axis=...]
    broadcast_in_dim x1 -> x0, other arithmetic: 14 us -> none  [per_device(): grad_up[None]]
    add x2, other arithmetic: 2.65 us -> 16.1 us  [the longest x1 14.4 us: per_device(): grad_up = own_gu[:, ffe:] + sum((v[:, ffe:].astype(F32) for v in gu_got))]
    unnamed x239 -> x215, local copies, waits for them, and re-layouts: 32.6 us -> 33.4 us
  transfers between devices with their start and end apart: 63 -> 60, of which waited for: 32 -> 33; matrix products, arithmetic and copies ran while one was open for 26% -> 25% of each run, Pallas kernels for 21% -> 22%
where the time goes in v5:
time: 1330 us; the launch traced here: 1320 us
  waiting for transfers between devices  542 us (41%)
  Pallas kernels  307 us (23%)
  matrix products  172 us (13%)
  other arithmetic  98.3 us (7%)
  local copies, waits for them, and re-layouts  86.3 us (6%)
  starting transfers between devices  81.5 us (6%)
  between operations  18 us (1%)
  blocking collectives  14.6 us (1%)
    ppermute x43, waiting for transfers between devices, swap(): return lax.ppermute(v, 'col', [(i, i ^ step) for i in range(count)])  453 us
    pallas_call x4, Pallas kernels, expert(): call(partial(expert_body, slot), 'expert', (rows // tile,), [pl.BlockSpec...  98.5 us
    dot_general x8, matrix products, dot_tn(): lax.dot_general(a, b, (((0,), (0,)), ((), ())), preferred_element_type=F32)  59.4 us
    ppermute x43, starting transfers between devices, swap(): return lax.ppermute(v, 'col', [(i, i ^ step) for i in range(count)])  52.5 us
    pallas_call x4, Pallas kernels, attend_back(): call(partial(attend_back_body, heads, per, blocks, rows), 'attend_back',...  46 us
    reduce_scatter x1, waiting for transfers between devices, per_device(): grad_q = lax.psum_scatter(grad_q, 'row', scatter_dimension=0, tiled=True)  44.5 us
    pallas_call x2, Pallas kernels, combine(): call(partial(combine_body, count, cap, bool(scores)), 'combine', (sources...  37.3 us
    pallas_call x4, Pallas kernels, qkv(): call(partial(qkv_body, heads), 'qkv', (rows // tile,), [pl.BlockSpec((til...  33.5 us
  transfers between devices with their start and end apart: 60, of which 33 were waited for; matrix products, arithmetic and copies ran while one was open for 25% of the time, Pallas kernels for 22%

profile of v5, /device:TPU:0, one launch (start us, length us, event | category | flops | bytes accessed | tf_op | source)
XLA Modules:
  0.0 1319.1 jit_solution(5394586934798941742)
XLA Ops:
  18.8 14.6 %all_gather.37 = s32[8,512,8]{1,2,0:T(8,128)S(1)} all-gather(s32[1,512,8]{1,2,0:T(8,128)S(1)} %copy-done.47), channel_id=1, replica_groups=mesh['row'=8,'col'=4] {'row'}, dimensions={0}, use_global_device_ids=true | all-gather | bytes 147456 | tf_op jit(solution)/shard_map/all_gather | solution.py:662
  50.0 13.3 %collective-permute-done.2 = f32[32]{0:T(128)S(1)} collective-permute-done((f32[32]{0:T(128)S(1)}, f32[32]{0:T(128)S(1)}, u32[]{:S(2)}, u32[]{:S(2)}) %collective-permute-start.2) | collective-permute-done | bytes 160 | tf_op jit(solution)/shard_map/ppermute | solution.py:572
  73.6 20.6 %collective-permute-done.4 = bf16[1,256,2048]{2,1,0:T(8,128)(2,1)S(1)} collective-permute-done((bf16[1,256,2048]{2,1,0:T(8,128)(2,1)S(1)}, bf16[1,256,2048]{2,1,0:T(8,128)(2,1)S(1)}, u32[]{:S(2)}, u32[]{:S(2)}) %collective-permute-start.4) | collective-permute-done | bytes 1048608 | tf_op jit(solution)/shard_map/ppermute | solution.py:572
  101.7 8.4 qkv.5
  110.1 8.3 qkv.6
  120.2 5.6 all-gather.14.cloned.1.call-done
  125.9 8.2 qkv.7
  134.1 8.5 qkv.4
  151.2 33.5 %collective-permute-done.6.wga_ref = bf16[1,1024,768]{2,1,0:T(8,128)(2,1)S(1)} collective-permute-done((bf16[1,1024,768]{2,1,0:T(8,128)(2,1)S(1)}, bf16[1,1024,768]{2,1,0:T(8,128)(2,1)S(1)}, u32[]{:S(2)}, u32[]{:S(2)}) %collective-permute-start.6) | collective-permute-done | bytes 1572896 | tf_op jit(solution)/shard_map/ppermute | solution.py:572
  187.1 6.8 attend.4
  201.7 28.4 %collective-permute-done.8.wgb_ref = bf16[1,1024,768]{2,1,0:T(8,128)(2,1)S(1)} collective-permute-done((bf16[1,1024,768]{2,1,0:T(8,128)(2,1)}, bf16[1,1024,768]{2,1,0:T(8,128)(2,1)S(1)}, u32[]{:S(2)}, u32[]{:S(2)}) %collective-permute-start.8) | collective-permute-done | bytes 1572896 | tf_op jit(solution)/shard_map/ppermute | solution.py:572
  236.1 6.9 attend.5
  243.0 20.9 %collective-permute-done.10.wua_ref = bf16[1,1024,768]{2,1,0:T(8,128)(2,1)} collective-permute-done((bf16[1,1024,768]{2,1,0:T(8,128)(2,1)S(1)}, bf16[1,1024,768]{2,1,0:T(8,128)(2,1)}, u32[]{:S(2)}, u32[]{:S(2)}) %collective-permute-start.10) | collective-permute-done | bytes 1572896 | tf_op jit(solution)/shard_map/ppermute | solution.py:572
  265.5 6.2 convolution_convert_fusion.11
  273.2 7.1 attend.6
  285.9 6.8 attend.7
  292.7 72.4 %collective-permute-done.13 = bf16[512,2048]{1,0:T(8,128)(2,1)} collective-permute-done((bf16[512,2048]{1,0:T(8,128)(2,1)}, bf16[512,2048]{1,0:T(8,128)(2,1)}, u32[]{:S(2)}, u32[]{:S(2)}) %collective-permute-start.13) | collective-permute-done | bytes 2097184 | tf_op jit(solution)/shard_map/ppermute | solution.py:572
  383.3 100.5 %collective-permute-done.15.wub_ref = bf16[1,1024,768]{2,1,0:T(8,128)(2,1)} collective-permute-done((bf16[1,1024,768]{2,1,0:T(8,128)(2,1)}, bf16[1,1024,768]{2,1,0:T(8,128)(2,1)}, u32[]{:S(2)}, u32[]{:S(2)}) %collective-permute-start.15) | collective-permute-done | bytes 1572896 | tf_op jit(solution)/shard_map/ppermute | solution.py:572
  496.6 16.9 %dispatch.1 = (bf16[8,128,2048]{2,1,0:T(8,128)(2,1)}, bf16[8,128,2048]{2,1,0:T(8,128)(2,1)}, bf16[8,128,2048]{2,1,0:T(8,128)(2,1)}, bf16[8,128,2048]{2,1,0:T(8,128)(2,1)}) custom-call(s32[8,4,512]{2,1,0:T(4,128)} %copy.122.rank_ref, bf16[8,512,2048]{2,1,0:T(8,128)(2,1)} %bitcast.316), custom_call_target="tpu_custom_call" | custom-call | flops 8589934592 | bytes 33554432 | tf_op jit(solution)/shard_map/dispatch/pallas_call | solution.py:372
  513.5 8.3 collective-permute-done.19.wga_ref
  523.2 10.4 all-gather.22.cloned.1.call-done
  533.6 21.9 %route_dispatch.1 = (f32[4,8,128,1]{3,2,1,0:T(8,128)}, bf16[8,128,2048]{2,1,0:T(8,128)(2,1)}, bf16[8,128,2048]{2,1,0:T(8,128)(2,1)}, bf16[8,128,2048]{2,1,0:T(8,128)(2,1)}, bf16[8,128,2048]{2,1,0:T(8,128)(2,1)}) custom-call(s32[4]{0:T(128)} %pad_add_fusion.2.ids_ref, s32[8,4,512]{2,1,0:T(4,128)} %copy.122.rank_ref, bf16[8,512,2048]{2,1,0:T(8,128)(2,1)} %bitcast.317, ...), custom_call_target="tpu_custom_call" | custom-call | flops 8589934592 | bytes 33554432 | tf_op jit(solution)/shard_map/route_dispatch/pallas_call | solution.py:408
  558.4 24.5 %expert.4 = (bf16[1024,2048]{1,0:T(8,128)(2,1)}, bf16[1024,768]{1,0:T(8,128)(2,1)}, bf16[1024,1536]{1,0:T(8,128)(2,1)}, bf16[1024,128]{1,0:T(8,128)(2,1)}) custom-call(bf16[1024,2048]{1,0:T(8,128)(2,1)} %bitcast.338, bf16[1024,2048]{1,0:T(8,128)(2,1)} %bitcast.274, f32[1024,1]{1,0:T(8,128)} %bitcast.301, bf16[1,2048,768]{2,1,0:T(8,128)(2,1)} %wgb_ref, ...), custom_call_target="tpu_custom_call" | custom-call | flops 16106127360 | bytes 26738688 | tf_op jit(solution)/shard_map/expert/pallas_call | solution.py:544
  589.4 24.8 %expert.5 = (bf16[1024,2048]{1,0:T(8,128)(2,1)}, bf16[1024,768]{1,0:T(8,128)(2,1)}, bf16[1024,1536]{1,0:T(8,128)(2,1)}, bf16[1024,128]{1,0:T(8,128)(2,1)}) custom-call(bf16[1024,2048]{1,0:T(8,128)(2,1)} %bitcast.346, bf16[1024,2048]{1,0:T(8,128)(2,1)} %bitcast.344, f32[1024,1]{1,0:T(8,128)} %bitcast.300, ...), custom_call_target="tpu_custom_call" | custom-call | flops 16106127360 | bytes 26738688 | tf_op jit(solution)/shard_map/expert/pallas_call | solution.py:544
  614.2 8.9 convolution_convert_fusion.2
  630.7 24.8 %expert.6 = (bf16[1024,2048]{1,0:T(8,128)(2,1)}, bf16[1024,768]{1,0:T(8,128)(2,1)}, bf16[1024,1536]{1,0:T(8,128)(2,1)}, bf16[1024,128]{1,0:T(8,128)(2,1)}) custom-call(bf16[1024,2048]{1,0:T(8,128)(2,1)} %bitcast.340, bf16[1024,2048]{1,0:T(8,128)(2,1)} %bitcast.334, f32[1024,1]{1,0:T(8,128)} %bitcast.299, bf16[1,1024,768]{2,1,0:T(8,128)(2,1)} %copy-done.65, ...), custom_call_target="tpu_custom_call" | custom-call | flops 16106127360 | bytes 26738688 | tf_op jit(solution)/shard_map/expert/pallas_call | solution.py:544
  655.5 24.5 %expert.7 = (bf16[1024,2048]{1,0:T(8,128)(2,1)}, bf16[1024,768]{1,0:T(8,128)(2,1)}, bf16[1024,1536]{1,0:T(8,128)(2,1)}, bf16[1024,128]{1,0:T(8,128)(2,1)}) custom-call(bf16[1024,2048]{1,0:T(8,128)(2,1)} %bitcast.342, bf16[1024,2048]{1,0:T(8,128)(2,1)} %bitcast.336, f32[1024,1]{1,0:T(8,128)} %bitcast.298, bf16[1,1024,768]{2,1,0:T(8,128)(2,1)} %copy-done.64, ...), custom_call_target="tpu_custom_call" | custom-call | flops 16106127360 | bytes 26738688 | tf_op jit(solution)/shard_map/expert/pallas_call | solution.py:544
  680.0 12.5 collective-permute-done.25
  692.6 19.6 %combine.2 = (bf16[8,512,2048]{2,1,0:T(8,128)(2,1)}, f32[8,512,4]{2,1,0:T(8,128)}) custom-call(s32[8,512,4]{2,1,0:T(8,128)} %bitcast.265, bf16[8,128,2048]{2,1,0:T(8,128)(2,1)} %bitcast.276, bf16[8,128,2048]{2,1,0:T(8,128)(2,1)} %bitcast.278, bf16[8,128,2048]{2,1,0:T(8,128)(2,1)} %bitcast.279, bf16[8,128,2048]{2,1,0:T(8,128)(2,1)} %bitcast.277, ...), custom_call_target="tpu_custom_call" | custom-call | tf_op jit(solution)/shard_map/combine/pallas_call | solution.py:485
  720.6 11.3 add_convert_fusion
  731.9 9.2 add_convert_fusion.1
  741.2 11.2 collective-permute-done.27
  758.5 7.3 all-to-all-start
  772.4 7.3 convolution_convert_fusion.4
  779.6 7.2 convolution_convert_fusion.5
  791.9 7.0 convolution_convert_fusion.3
  798.9 5.6 fusion.109
  814.5 9.6 fusion.108
  826.3 17.7 %combine.3 = bf16[8,512,2048]{2,1,0:T(8,128)(2,1)} custom-call(s32[8,512,4]{2,1,0:T(8,128)} %bitcast.266, bf16[8,128,2048]{2,1,0:T(8,128)(2,1)} %bitcast.282, bf16[8,128,2048]{2,1,0:T(8,128)(2,1)} %bitcast.281, bf16[8,128,2048]{2,1,0:T(8,128)(2,1)} %bitcast.280, bf16[8,128,2048]{2,1,0:T(8,128)(2,1)} %bitcast.283), custom_call_target="tpu_custom_call" | custom-call | tf_op jit(solution)/shard_map/combine/pallas_call | solution.py:485
  850.0 38.1 %collective-permute-done.29 = bf16[2048,1536]{1,0:T(8,128)(2,1)} collective-permute-done((bf16[2048,1536]{1,0:T(8,128)(2,1)}, bf16[2048,1536]{1,0:T(8,128)(2,1)}, u32[]{:S(2)}, u32[]{:S(2)}) %collective-permute-start.29) | collective-permute-done | bytes 6291488 | tf_op jit(solution)/shard_map/ppermute | solution.py:572
  905.6 11.4 attend_back.4
  917.0 6.6 input_share.4
  923.6 19.9 %collective-permute-done.31 = bf16[1,512,2048]{2,1,0:T(8,128)(2,1)S(1)} collective-permute-done((bf16[1,512,2048]{2,1,0:T(8,128)(2,1)S(1)}, bf16[1,512,2048]{2,1,0:T(8,128)(2,1)S(1)}, u32[]{:S(2)}, u32[]{:S(2)}) %collective-permute-start.31) | collective-permute-done | bytes 2097184 | tf_op jit(solution)/shard_map/ppermute | solution.py:572
  955.3 11.4 attend_back.5
  966.7 6.1 input_share.5
  977.4 5.7 convolution_convert_fusion.14.do_ref
  983.1 11.4 attend_back.6
  994.6 5.9 input_share.6
  1003.7 11.4 bitcast_convert_fusion
  1015.2 27.6 %collective-permute-done.35 = bf16[768,2048]{1,0:T(8,128)(2,1)} collective-permute-done((bf16[768,2048]{1,0:T(8,128)(2,1)}, bf16[768,2048]{1,0:T(8,128)(2,1)}, u32[]{:S(2)}, u32[]{:S(2)}) %collective-permute-start.35) | collective-permute-done | bytes 3145760 | tf_op jit(solution)/shard_map/ppermute | solution.py:572
  1043.9 15.5 %reduce-scatter.8.cloned.1.call-done = bf16[1,512,2048]{2,1,0:T(8,128)(2,1)} async-done(((bf16[8,512,2048]{2,1,0:T(8,128)(2,1)}), bf16[1,512,2048]{2,1,0:T(8,128)(2,1)}) %reduce-scatter.8.cloned.1.call-update) | async-done | bytes 2097168 | tf_op jit(solution)/shard_map/reduce_scatter | solution.py:868
  1068.0 11.7 attend_back.7
  1079.7 26.5 %collective-permute-done.37 = bf16[512,2048]{1,0:T(8,128)(2,1)} collective-permute-done((bf16[512,2048]{1,0:T(8,128)(2,1)}, bf16[512,2048]{1,0:T(8,128)(2,1)}, u32[]{:S(2)}, u32[]{:S(2)}) %collective-permute-start.37) | collective-permute-done | bytes 2097184 | tf_op jit(solution)/shard_map/ppermute | solution.py:572
  1118.2 6.2 input_share.7
  1124.4 13.7 %fusion.105 = (bf16[2048,1024]{0,1:T(8,128)(2,1)}, f32[2048,1024]{0,1:T(8,128)}) fusion(bf16[4,512,1024]{2,1,0:T(8,128)(2,1)S(1)} %pad_maximum_fusion.2, bf16[1,512,2048]{2,1,0:T(8,128)(2,1)} %bitcast.352, bf16[1,512,2048]{2,1,0:T(8,128)(2,1)} %bitcast.350, bf16[1,512,2048]{2,1,0:T(8,128)(2,1)S(1)} %bitcast.348, bf16[1,512,2048]{2,1,0:T(8,128)(2,1)} %bitcast.354), kind=kOutput, calls=%fused_computation.271 | convolution fusion | flops 8604614656 | bytes 25165824 | tf_op jit(solution)/shard_map/dot_general | solution.py:886
  1149.5 9.4 copy.130
  1160.0 14.4 %add_add_fusion = (f32[2048,768]{1,0:T(8,128)}, f32[2048,768]{1,0:T(8,128)}) fusion(f32[2048,1536]{1,0:T(8,128)} %fusion.108, bf16[2048,1536]{1,0:T(8,128)(2,1)} %collective-permute-done.30, bf16[2048,1536]{1,0:T(8,128)(2,1)} %collective-permute-done.29), kind=kLoop, calls=%fused_computation.10 | loop fusion | flops 12582912 | bytes 37748736 | tf_op jit(solution)/shard_map/add | solution.py:949
  1187.1 44.5 %reduce-scatter.14.cloned.1.call-done = bf16[256,1024]{0,1:T(8,128)(2,1)} async-done(((bf16[2048,1024]{0,1:T(8,128)(2,1)}), bf16[256,1024]{0,1:T(8,128)(2,1)}) %reduce-scatter.14.cloned.1.call-update) | async-done | bytes 524304 | tf_op jit(solution)/shard_map/reduce_scatter | solution.py:961
  1253.1 7.6 all-to-all-start.1
  1270.9 5.9 fusion.2
  1276.8 6.1 all-to-all-start.2
  1283.0 7.1 fusion.6
  1290.1 7.2 add_bitcast_fusion
  1301.3 8.0 all-to-all-done.2
  (478 shorter events, 294.1 us)
Async XLA Ops:
  7.2 89.4 %all-gather.12.cloned.1.call-start = ((), (), s32[]{:S(2)}) async-start(), calls=%async_computation.8 | async-start | bytes 6488064 | tf_op jit(solution)/shard_map/all_gather | solution.py:650
  14.2 111.6 %all-gather.14.cloned.1.call-start = ((), (), s32[]{:S(2)}) async-start(), calls=%async_computation.9 | async-start | bytes 4718592 | tf_op jit(solution)/shard_map/all_gather | solution.py:698
  14.3 53.4 %collective-permute-start = (bf16[1,512,2048]{2,1,0:T(8,128)(2,1)}, bf16[1,512,2048]{2,1,0:T(8,128)(2,1)}, u32[]{:S(2)}, u32[]{:S(2)}) collective-permute-start(bf16[1,512,2048]{2,1,0:T(8,128)(2,1)} %param.15), channel_id=1, source_target_pairs={{0,1},{1,0},{2,3},{3,2},{4,5},{5,4},{6,7},{7,6},{8,9},{9,8},{10,11... | collective-permute-start | bytes 6291464 | tf_op jit(solution)/shard_map/ppermute | solution.py:572
  17.3 50.4 %collective-permute-start.1 = (bf16[1,512,2048]{2,1,0:T(8,128)(2,1)}, bf16[1,512,2048]{2,1,0:T(8,128)(2,1)}, u32[]{:S(2)}, u32[]{:S(2)}) collective-permute-start(bf16[1,512,2048]{2,1,0:T(8,128)(2,1)} %param.15), channel_id=1, source_target_pairs={{0,2},{1,3},{2,0},{3,1},{4,6},{5,7},{6,4},{7,5},{8,10},{9,11},{10,... | collective-permute-start | bytes 6291464 | tf_op jit(solution)/shard_map/ppermute | solution.py:572
  34.4 28.8 %collective-permute-start.2 = (f32[32]{0:T(128)S(1)}, f32[32]{0:T(128)S(1)}, u32[]{:S(2)}, u32[]{:S(2)}) collective-permute-start(f32[32]{0:T(128)S(1)} %convert_reduce_fusion.3), channel_id=1, source_target_pairs={{0,1},{1,0},{2,3},{3,2},{4,5},{5,4},{6,7},{7,6},{8,9},{9,8},{10,11... | collective-permute-start | bytes 392 | tf_op jit(solution)/shard_map/ppermute | solution.py:572
  48.8 442.1 %copy-start.4 = (s32[8,4,512]{1,2,0:T(8,128)}, s32[8,4,512]{1,2,0:T(8,128)S(1)}, u32[]{:S(2)}) copy-start(s32[8,4,512]{1,2,0:T(8,128)S(1)} %add_select_fusion) | copy-start | bytes 196612
  63.2 3.9 collective-permute-start.3
  67.7 119.4 %all-gather.18.cloned.1.call-start = ((), (), s32[]{:S(2)}) async-start(), calls=%async_computation.16 | async-start | bytes 4718592 | tf_op jit(solution)/shard_map/all_gather | solution.py:714
  70.4 23.8 %collective-permute-start.4 = (bf16[1,256,2048]{2,1,0:T(8,128)(2,1)S(1)}, bf16[1,256,2048]{2,1,0:T(8,128)(2,1)S(1)}, u32[]{:S(2)}, u32[]{:S(2)}) collective-permute-start(bf16[1,256,2048]{2,1,0:T(8,128)(2,1)S(1)} %slice.253), channel_id=1, source_target_pairs={{0,2},{1,3},{2,0},{3,1},{4,6},{5,7},{6,4},{7,5},{8,10},{9,11},{10,... | collective-permute-start | bytes 3145736 | tf_op jit(solution)/shard_map/ppermute | solution.py:572
  72.1 23.0 %collective-permute-start.5 = (bf16[1,256,2048]{2,1,0:T(8,128)(2,1)S(1)}, bf16[1,256,2048]{2,1,0:T(8,128)(2,1)S(1)}, u32[]{:S(2)}, u32[]{:S(2)}) collective-permute-start(bf16[1,256,2048]{2,1,0:T(8,128)(2,1)S(1)} %slice.254), channel_id=1, source_target_pairs={{0,1},{1,0},{2,3},{3,2},{4,5},{5,4},{6,7},{7,6},{8,9},{9,8},{10,11... | collective-permute-start | bytes 3145736 | tf_op jit(solution)/shard_map/ppermute | solution.py:572
  101.7 273.7 %copy-start.44 = (f32[2048]{0:T(1024)}, f32[2048]{0:T(1024)S(1)}, u32[]{:S(2)}) copy-start(f32[2048]{0:T(1024)S(1)} %get-tuple-element.502) | copy-start | bytes 24580
  125.8 147.4 %all-gather.20.cloned.1.call-start = ((), (), s32[]{:S(2)}) async-start(), calls=%async_computation.17 | async-start | bytes 4718592 | tf_op jit(solution)/shard_map/all_gather | solution.py:714
  144.5 352.1 %all-gather.24.cloned.1.call-start = ((), (), s32[]{:S(2)}) async-start(), calls=%async_computation.19 | async-start | bytes 18874368 | tf_op jit(solution)/shard_map/all_gather | solution.py:747
  148.2 36.5 %collective-permute-start.6 = (bf16[1,1024,768]{2,1,0:T(8,128)(2,1)S(1)}, bf16[1,1024,768]{2,1,0:T(8,128)(2,1)S(1)}, u32[]{:S(2)}, u32[]{:S(2)}) collective-permute-start(bf16[1,1024,768]{2,1,0:T(8,128)(2,1)S(1)} %get-tuple-element.541), channel_id=1, source_target_pairs={{0,1},{1,0},{2,3},{3,2},{4,5},{5,4},{6,7},{7,6},{8,9},{9,8},{10,11... | collective-permute-start | bytes 4718600 | tf_op jit(solution)/shard_map/ppermute | solution.py:572
  149.8 36.2 %collective-permute-start.7 = (bf16[1,1024,768]{2,1,0:T(8,128)(2,1)S(1)}, bf16[1,1024,768]{2,1,0:T(8,128)(2,1)S(1)}, u32[]{:S(2)}, u32[]{:S(2)}) collective-permute-start(bf16[1,1024,768]{2,1,0:T(8,128)(2,1)S(1)} %get-tuple-element.541), channel_id=1, source_target_pairs={{0,2},{1,3},{2,0},{3,1},{4,6},{5,7},{6,4},{7,5},{8,10},{9,11},{10,... | collective-permute-start | bytes 4718600 | tf_op jit(solution)/shard_map/ppermute | solution.py:572
  193.9 339.6 %all-gather.22.cloned.1.call-start = ((), (), s32[]{:S(2)}) async-start(), calls=%async_computation.18 | async-start | bytes 18874368 | tf_op jit(solution)/shard_map/all_gather | solution.py:751
  194.0 36.1 %collective-permute-start.8 = (bf16[1,1024,768]{2,1,0:T(8,128)(2,1)}, bf16[1,1024,768]{2,1,0:T(8,128)(2,1)S(1)}, u32[]{:S(2)}, u32[]{:S(2)}) collective-permute-start(bf16[1,1024,768]{2,1,0:T(8,128)(2,1)} %get-tuple-element.540), channel_id=1, source_target_pairs={{0,1},{1,0},{2,3},{3,2},{4,5},{5,4},{6,7},{7,6},{8,9},{9,8},{10,11... | collective-permute-start | bytes 4718600 | tf_op jit(solution)/shard_map/ppermute | solution.py:572
  195.5 36.2 %collective-permute-start.9 = (bf16[1,1024,768]{2,1,0:T(8,128)(2,1)}, bf16[1,1024,768]{2,1,0:T(8,128)(2,1)S(1)}, u32[]{:S(2)}, u32[]{:S(2)}) collective-permute-start(bf16[1,1024,768]{2,1,0:T(8,128)(2,1)} %get-tuple-element.540), channel_id=1, source_target_pairs={{0,2},{1,3},{2,0},{3,1},{4,6},{5,7},{6,4},{7,5},{8,10},{9,11},{10,... | collective-permute-start | bytes 4718600 | tf_op jit(solution)/shard_map/ppermute | solution.py:572
  200.2 63.7 %collective-permute-start.10 = (bf16[1,1024,768]{2,1,0:T(8,128)(2,1)S(1)}, bf16[1,1024,768]{2,1,0:T(8,128)(2,1)}, u32[]{:S(2)}, u32[]{:S(2)}) collective-permute-start(bf16[1,1024,768]{2,1,0:T(8,128)(2,1)S(1)} %get-tuple-element.539), channel_id=1, source_target_pairs={{0,1},{1,0},{2,3},{3,2},{4,5},{5,4},{6,7},{7,6},{8,9},{9,8},{10,11... | collective-permute-start | bytes 4718600 | tf_op jit(solution)/shard_map/ppermute | solution.py:572
  200.8 64.7 %collective-permute-start.11 = (bf16[1,1024,768]{2,1,0:T(8,128)(2,1)S(1)}, bf16[1,1024,768]{2,1,0:T(8,128)(2,1)}, u32[]{:S(2)}, u32[]{:S(2)}) collective-permute-start(bf16[1,1024,768]{2,1,0:T(8,128)(2,1)S(1)} %get-tuple-element.539), channel_id=1, source_target_pairs={{0,2},{1,3},{2,0},{3,1},{4,6},{5,7},{6,4},{7,5},{8,10},{9,11},{10,... | collective-permute-start | bytes 4718600 | tf_op jit(solution)/shard_map/ppermute | solution.py:572
  235.4 129.7 %collective-permute-start.12 = (bf16[512,2048]{1,0:T(8,128)(2,1)}, bf16[512,2048]{1,0:T(8,128)(2,1)}, u32[]{:S(2)}, u32[]{:S(2)}) collective-permute-start(bf16[512,2048]{1,0:T(8,128)(2,1)} %convolution_convert_fusion.12), channel_id=1, source_target_pairs={{0,1},{1,0},{2,3},{3,2},{4,5},{5,4},{6,7},{7,6},{8,9},{9,8},{10,11... | collective-permute-start | bytes 6291464 | tf_op jit(solution)/shard_map/ppermute | solution.py:572
  271.7 93.4 %collective-permute-start.13 = (bf16[512,2048]{1,0:T(8,128)(2,1)}, bf16[512,2048]{1,0:T(8,128)(2,1)}, u32[]{:S(2)}, u32[]{:S(2)}) collective-permute-start(bf16[512,2048]{1,0:T(8,128)(2,1)} %convolution_convert_fusion.11), channel_id=1, source_target_pairs={{0,2},{1,3},{2,0},{3,1},{4,6},{5,7},{6,4},{7,5},{8,10},{9,11},{10,... | collective-permute-start | bytes 6291464 | tf_op jit(solution)/shard_map/ppermute | solution.py:572
  285.2 84.7 %collective-permute-start.14 = (bf16[512,2048]{1,0:T(8,128)(2,1)}, bf16[512,2048]{1,0:T(8,128)(2,1)S(1)}, u32[]{:S(2)}, u32[]{:S(2)}) collective-permute-start(bf16[512,2048]{1,0:T(8,128)(2,1)} %convolution_convert_fusion.10), channel_id=1, source_target_pairs={{0,3},{1,2},{2,1},{3,0},{4,7},{5,6},{6,5},{7,4},{8,11},{9,10},{10,... | collective-permute-start | bytes 6291464 | tf_op jit(solution)/shard_map/ppermute | solution.py:572
  379.1 313.4 %all-gather.16.cloned.1.call-start = ((), (), s32[]{:S(2)}) async-start(), calls=%async_computation.10 | async-start | bytes 4718592 | tf_op jit(solution)/shard_map/all_gather | solution.py:776
  379.2 105.0 %collective-permute-start.17 = (bf16[1,768,2048]{2,1,0:T(8,128)(2,1)}, bf16[1,768,2048]{2,1,0:T(8,128)(2,1)}, u32[]{:S(2)}, u32[]{:S(2)}) collective-permute-start(bf16[1,768,2048]{2,1,0:T(8,128)(2,1)} %wdb_ref), channel_id=1, source_target_pairs={{0,1},{1,0},{2,3},{3,2},{4,5},{5,4},{6,7},{7,6},{8,9},{9,8},{10,11... | collective-permute-start | bytes 9437192 | tf_op jit(solution)/shard_map/ppermute | solution.py:572
  379.3 104.9 %collective-permute-start.18 = (bf16[1,768,2048]{2,1,0:T(8,128)(2,1)}, bf16[1,768,2048]{2,1,0:T(8,128)(2,1)}, u32[]{:S(2)}, u32[]{:S(2)}) collective-permute-start(bf16[1,768,2048]{2,1,0:T(8,128)(2,1)} %wdb_ref), channel_id=1, source_target_pairs={{0,2},{1,3},{2,0},{3,1},{4,6},{5,7},{6,4},{7,5},{8,10},{9,11},{10,... | collective-permute-start | bytes 9437192 | tf_op jit(solution)/shard_map/ppermute | solution.py:572
  380.7 103.0 %collective-permute-start.15 = (bf16[1,1024,768]{2,1,0:T(8,128)(2,1)}, bf16[1,1024,768]{2,1,0:T(8,128)(2,1)}, u32[]{:S(2)}, u32[]{:S(2)}) collective-permute-start(bf16[1,1024,768]{2,1,0:T(8,128)(2,1)} %get-tuple-element.538), channel_id=1, source_target_pairs={{0,1},{1,0},{2,3},{3,2},{4,5},{5,4},{6,7},{7,6},{8,9},{9,8},{10,11... | collective-permute-start | bytes 4718600 | tf_op jit(solution)/shard_map/ppermute | solution.py:572
  382.7 101.5 %collective-permute-start.16 = (bf16[1,1024,768]{2,1,0:T(8,128)(2,1)}, bf16[1,1024,768]{2,1,0:T(8,128)(2,1)}, u32[]{:S(2)}, u32[]{:S(2)}) collective-permute-start(bf16[1,1024,768]{2,1,0:T(8,128)(2,1)} %get-tuple-element.538), channel_id=1, source_target_pairs={{0,2},{1,3},{2,0},{3,1},{4,6},{5,7},{6,4},{7,5},{8,10},{9,11},{10,... | collective-permute-start | bytes 4718600 | tf_op jit(solution)/shard_map/ppermute | solution.py:572
  484.2 37.6 %collective-permute-start.19 = (bf16[1,1024,768]{2,1,0:T(8,128)(2,1)}, bf16[1,1024,768]{2,1,0:T(8,128)(2,1)}, u32[]{:S(2)}, u32[]{:S(2)}) collective-permute-start(bf16[1,1024,768]{2,1,0:T(8,128)(2,1)} %copy-done.65), channel_id=1, source_target_pairs={{0,2},{1,3},{2,0},{3,1},{4,6},{5,7},{6,4},{7,5},{8,10},{9,11},{10,... | collective-permute-start | bytes 4718600 | tf_op jit(solution)/shard_map/ppermute | solution.py:572
  485.6 37.6 %collective-permute-start.20 = (bf16[1,1024,768]{2,1,0:T(8,128)(2,1)}, bf16[1,1024,768]{2,1,0:T(8,128)(2,1)}, u32[]{:S(2)}, u32[]{:S(2)}) collective-permute-start(bf16[1,1024,768]{2,1,0:T(8,128)(2,1)} %copy-done.66), channel_id=1, source_target_pairs={{0,1},{1,0},{2,3},{3,2},{4,5},{5,4},{6,7},{7,6},{8,9},{9,8},{10,11... | collective-permute-start | bytes 4718600 | tf_op jit(solution)/shard_map/ppermute | solution.py:572
  489.6 68.8 %collective-permute-start.21 = (bf16[1,1024,768]{2,1,0:T(8,128)(2,1)}, bf16[1,1024,768]{2,1,0:T(8,128)(2,1)}, u32[]{:S(2)}, u32[]{:S(2)}) collective-permute-start(bf16[1,1024,768]{2,1,0:T(8,128)(2,1)} %collective-permute-done.10.wua_ref), channel_id=1, source_target_pairs={{0,2},{1,3},{2,0},{3,1},{4,6},{5,7},{6,4},{7,5},{8,10},{9,11},{10,... | collective-permute-start | bytes 4718600 | tf_op jit(solution)/shard_map/ppermute | solution.py:572
  490.1 68.3 %collective-permute-start.22 = (bf16[1,1024,768]{2,1,0:T(8,128)(2,1)}, bf16[1,1024,768]{2,1,0:T(8,128)(2,1)}, u32[]{:S(2)}, u32[]{:S(2)}) collective-permute-start(bf16[1,1024,768]{2,1,0:T(8,128)(2,1)} %collective-permute-done.16.wub_ref), channel_id=1, source_target_pairs={{0,1},{1,0},{2,3},{3,2},{4,5},{5,4},{6,7},{7,6},{8,9},{9,8},{10,11... | collective-permute-start | bytes 4718600 | tf_op jit(solution)/shard_map/ppermute | solution.py:572
  493.6 94.6 %collective-permute-start.23 = (bf16[1,384,2048]{2,1,0:T(8,128)(2,1)S(1)}, bf16[1,384,2048]{2,1,0:T(8,128)(2,1)}, u32[]{:S(2)}, u32[]{:S(2)}) collective-permute-start(bf16[1,384,2048]{2,1,0:T(8,128)(2,1)S(1)} %slice.262), channel_id=1, source_target_pairs={{0,2},{1,3},{2,0},{3,1},{4,6},{5,7},{6,4},{7,5},{8,10},{9,11},{10,... | collective-permute-start | bytes 4718600 | tf_op jit(solution)/shard_map/ppermute | solution.py:572
  521.8 67.5 %collective-permute-start.24 = (bf16[1,384,2048]{2,1,0:T(8,128)(2,1)S(1)}, bf16[1,384,2048]{2,1,0:T(8,128)(2,1)}, u32[]{:S(2)}, u32[]{:S(2)}) collective-permute-start(bf16[1,384,2048]{2,1,0:T(8,128)(2,1)S(1)} %slice.263), channel_id=1, source_target_pairs={{0,1},{1,0},{2,3},{3,2},{4,5},{5,4},{6,7},{7,6},{8,9},{9,8},{10,11... | collective-permute-start | bytes 4718600 | tf_op jit(solution)/shard_map/ppermute | solution.py:572
  589.3 300.0 %reduce-scatter.6.cloned.1.call-start = ((), (), s32[]{:S(2)}) async-start(), calls=%async_computation.11 | async-start | bytes 18874368 | tf_op jit(solution)/shard_map/reduce_scatter | solution.py:807
  623.5 68.9 %collective-permute-start.25 = (bf16[1024,1536]{1,0:T(8,128)(2,1)S(1)}, bf16[1024,1536]{1,0:T(8,128)(2,1)}, u32[]{:S(2)}, u32[]{:S(2)}) collective-permute-start(bf16[1024,1536]{1,0:T(8,128)(2,1)S(1)} %get-tuple-element.535), channel_id=1, source_target_pairs={{0,1},{1,0},{2,3},{3,2},{4,5},{5,4},{6,7},{7,6},{8,9},{9,8},{10,11... | collective-permute-start | bytes 9437192 | tf_op jit(solution)/shard_map/ppermute | solution.py:572
  624.4 68.1 %collective-permute-start.26 = (bf16[1024,1536]{1,0:T(8,128)(2,1)S(1)}, bf16[1024,1536]{1,0:T(8,128)(2,1)}, u32[]{:S(2)}, u32[]{:S(2)}) collective-permute-start(bf16[1024,1536]{1,0:T(8,128)(2,1)S(1)} %get-tuple-element.534), channel_id=1, source_target_pairs={{0,2},{1,3},{2,0},{3,1},{4,6},{5,7},{6,4},{7,5},{8,10},{9,11},{10,... | collective-permute-start | bytes 9437192 | tf_op jit(solution)/shard_map/ppermute | solution.py:572
  718.2 34.1 %collective-permute-start.27 = (bf16[384,2048]{1,0:T(8,128)(2,1)S(1)}, bf16[384,2048]{1,0:T(8,128)(2,1)S(1)}, u32[]{:S(2)}, u32[]{:S(2)}) collective-permute-start(bf16[384,2048]{1,0:T(8,128)(2,1)S(1)} %get-tuple-element.537), channel_id=1, source_target_pairs={{0,1},{1,0},{2,3},{3,2},{4,5},{5,4},{6,7},{7,6},{8,9},{9,8},{10,11... | collective-permute-start | bytes 4718600 | tf_op jit(solution)/shard_map/ppermute | solution.py:572
  719.9 33.6 %collective-permute-start.28 = (bf16[384,2048]{1,0:T(8,128)(2,1)S(1)}, bf16[384,2048]{1,0:T(8,128)(2,1)S(1)}, u32[]{:S(2)}, u32[]{:S(2)}) collective-permute-start(bf16[384,2048]{1,0:T(8,128)(2,1)S(1)} %get-tuple-element.536), channel_id=1, source_target_pairs={{0,2},{1,3},{2,0},{3,1},{4,6},{5,7},{6,4},{7,5},{8,10},{9,11},{10,... | collective-permute-start | bytes 4718600 | tf_op jit(solution)/shard_map/ppermute | solution.py:572
  753.5 134.6 %collective-permute-start.29 = (bf16[2048,1536]{1,0:T(8,128)(2,1)}, bf16[2048,1536]{1,0:T(8,128)(2,1)}, u32[]{:S(2)}, u32[]{:S(2)}) collective-permute-start(bf16[2048,1536]{1,0:T(8,128)(2,1)} %add_convert_fusion.1), channel_id=1, source_target_pairs={{0,1},{1,0},{2,3},{3,2},{4,5},{5,4},{6,7},{7,6},{8,9},{9,8},{10,11... | collective-permute-start | bytes 18874376 | tf_op jit(solution)/shard_map/ppermute | solution.py:572
  755.0 134.4 %collective-permute-start.30 = (bf16[2048,1536]{1,0:T(8,128)(2,1)}, bf16[2048,1536]{1,0:T(8,128)(2,1)}, u32[]{:S(2)}, u32[]{:S(2)}) collective-permute-start(bf16[2048,1536]{1,0:T(8,128)(2,1)} %add_convert_fusion), channel_id=1, source_target_pairs={{0,2},{1,3},{2,0},{3,1},{4,6},{5,7},{6,4},{7,5},{8,10},{9,11},{10,... | collective-permute-start | bytes 18874376 | tf_op jit(solution)/shard_map/ppermute | solution.py:572
  758.5 85.5 %all-to-all-start = ((f32[8,512,4]{1,2,0:T(4,128)}), f32[8,512,4]{1,2,0:T(4,128)S(1)}, u32[]{:S(2)}, u32[]{:S(2)}) async-start(f32[8,512,4]{1,2,0:T(4,128)} %copy.124), calls=%async_computation.1 | async-start | bytes 131072 | tf_op jit(solution)/shard_map/all_to_all | solution.py:832
  765.8 293.6 %reduce-scatter.8.cloned.1.call-start = ((), (), s32[]{:S(2)}) async-start(), calls=%async_computation.12 | async-start | bytes 18874368 | tf_op jit(solution)/shard_map/reduce_scatter | solution.py:868
  889.4 221.9 %reduce-scatter.10.cloned.1.call-start = ((), (), s32[]{:S(2)}) async-start(), calls=%async_computation.13 | async-start | bytes 4718592 | tf_op jit(solution)/shard_map/reduce_scatter | solution.py:921
  900.5 43.0 %collective-permute-start.31 = (bf16[1,512,2048]{2,1,0:T(8,128)(2,1)S(1)}, bf16[1,512,2048]{2,1,0:T(8,128)(2,1)S(1)}, u32[]{:S(2)}, u32[]{:S(2)}) collective-permute-start(bf16[1,512,2048]{2,1,0:T(8,128)(2,1)S(1)} %get-tuple-element.528), channel_id=1, source_target_pairs={{0,1},{1,0},{2,3},{3,2},{4,5},{5,4},{6,7},{7,6},{8,9},{9,8},{10,11... | collective-permute-start | bytes 6291464 | tf_op jit(solution)/shard_map/ppermute | solution.py:572
  901.5 45.5 %collective-permute-start.32 = (bf16[1,512,2048]{2,1,0:T(8,128)(2,1)S(1)}, bf16[1,512,2048]{2,1,0:T(8,128)(2,1)S(1)}, u32[]{:S(2)}, u32[]{:S(2)}) collective-permute-start(bf16[1,512,2048]{2,1,0:T(8,128)(2,1)S(1)} %get-tuple-element.528), channel_id=1, source_target_pairs={{0,2},{1,3},{2,0},{3,1},{4,6},{5,7},{6,4},{7,5},{8,10},{9,11},{10,... | collective-permute-start | bytes 6291464 | tf_op jit(solution)/shard_map/ppermute | solution.py:572
  947.1 25.7 %collective-permute-start.33 = (bf16[1,256,2048]{2,1,0:T(8,128)(2,1)S(1)}, bf16[1,256,2048]{2,1,0:T(8,128)(2,1)}, u32[]{:S(2)}, u32[]{:S(2)}) collective-permute-start(bf16[1,256,2048]{2,1,0:T(8,128)(2,1)S(1)} %slice.271), channel_id=1, source_target_pairs={{0,2},{1,3},{2,0},{3,1},{4,6},{5,7},{6,4},{7,5},{8,10},{9,11},{10,... | collective-permute-start | bytes 3145736 | tf_op jit(solution)/shard_map/ppermute | solution.py:572
  949.0 23.9 %collective-permute-start.34 = (bf16[1,256,2048]{2,1,0:T(8,128)(2,1)}, bf16[1,256,2048]{2,1,0:T(8,128)(2,1)}, u32[]{:S(2)}, u32[]{:S(2)}) collective-permute-start(bf16[1,256,2048]{2,1,0:T(8,128)(2,1)} %slice.272), channel_id=1, source_target_pairs={{0,1},{1,0},{2,3},{3,2},{4,5},{5,4},{6,7},{7,6},{8,9},{9,8},{10,11... | collective-permute-start | bytes 3145736 | tf_op jit(solution)/shard_map/ppermute | solution.py:572
  974.7 68.1 %collective-permute-start.35 = (bf16[768,2048]{1,0:T(8,128)(2,1)}, bf16[768,2048]{1,0:T(8,128)(2,1)}, u32[]{:S(2)}, u32[]{:S(2)}) collective-permute-start(bf16[768,2048]{1,0:T(8,128)(2,1)} %add_convert_fusion.3), channel_id=1, source_target_pairs={{0,1},{1,0},{2,3},{3,2},{4,5},{5,4},{6,7},{7,6},{8,9},{9,8},{10,11... | collective-permute-start | bytes 9437192 | tf_op jit(solution)/shard_map/ppermute | solution.py:572
  976.1 67.8 %collective-permute-start.36 = (bf16[768,2048]{1,0:T(8,128)(2,1)}, bf16[768,2048]{1,0:T(8,128)(2,1)}, u32[]{:S(2)}, u32[]{:S(2)}) collective-permute-start(bf16[768,2048]{1,0:T(8,128)(2,1)} %add_convert_fusion.2), channel_id=1, source_target_pairs={{0,2},{1,3},{2,0},{3,1},{4,6},{5,7},{6,4},{7,5},{8,10},{9,11},{10,... | collective-permute-start | bytes 9437192 | tf_op jit(solution)/shard_map/ppermute | solution.py:572
  1059.4 115.0 %reduce-scatter.12.cloned.1.call-start = ((), (), s32[]{:S(2)}) async-start(), calls=%async_computation.14 | async-start | bytes 4718592 | tf_op jit(solution)/shard_map/reduce_scatter | solution.py:945
  1059.5 46.8 %collective-permute-start.38 = (bf16[512,2048]{1,0:T(8,128)(2,1)}, bf16[512,2048]{1,0:T(8,128)(2,1)}, u32[]{:S(2)}, u32[]{:S(2)}) collective-permute-start(bf16[512,2048]{1,0:T(8,128)(2,1)} %input_share.6), channel_id=1, source_target_pairs={{0,2},{1,3},{2,0},{3,1},{4,6},{5,7},{6,4},{7,5},{8,10},{9,11},{10,... | collective-permute-start | bytes 6291464 | tf_op jit(solution)/shard_map/ppermute | solution.py:572
  1061.0 45.3 %collective-permute-start.37 = (bf16[512,2048]{1,0:T(8,128)(2,1)}, bf16[512,2048]{1,0:T(8,128)(2,1)}, u32[]{:S(2)}, u32[]{:S(2)}) collective-permute-start(bf16[512,2048]{1,0:T(8,128)(2,1)} %input_share.5), channel_id=1, source_target_pairs={{0,1},{1,0},{2,3},{3,2},{4,5},{5,4},{6,7},{7,6},{8,9},{9,8},{10,11... | collective-permute-start | bytes 6291464 | tf_op jit(solution)/shard_map/ppermute | solution.py:572
  1114.5 117.1 %reduce-scatter.14.cloned.1.call-start = ((), (), s32[]{:S(2)}) async-start(), calls=%async_computation.15 | async-start | bytes 4718592 | tf_op jit(solution)/shard_map/reduce_scatter | solution.py:961
  1147.0 123.9 %collective-permute-start.44 = (bf16[512,2048]{1,0:T(8,128)(2,1)S(1)}, bf16[512,2048]{1,0:T(8,128)(2,1)}, u32[]{:S(2)}, u32[]{:S(2)}) collective-permute-start(bf16[512,2048]{1,0:T(8,128)(2,1)S(1)} %copy-done.16), channel_id=1, source_target_pairs={{0,3},{1,2},{2,1},{3,0},{4,7},{5,6},{6,5},{7,4},{8,11},{9,10},{10,... | collective-permute-start | bytes 6291464 | tf_op jit(solution)/shard_map/ppermute | solution.py:572
  1174.4 61.7 %copy-start.36 = (f32[2,512,128]{2,1,0:T(8,128)S(1)}, f32[2,512,128]{2,1,0:T(8,128)}, u32[]{:S(2)}) copy-start(f32[2,512,128]{2,1,0:T(8,128)} %get-tuple-element.397) | copy-start | bytes 1572868
  1174.4 59.4 %collective-permute-start.39 = (bf16[4,2,256,128]{3,2,1,0:T(8,128)(2,1)}, bf16[4,2,256,128]{3,2,1,0:T(8,128)(2,1)}, u32[]{:S(2)}, u32[]{:S(2)}) collective-permute-start(bf16[4,2,256,128]{3,2,1,0:T(8,128)(2,1)} %reduce-scatter.12.cloned.1.call-done), channel_id=1, source_target_pairs={{0,0},{8,4},{16,8},{24,12},{1,1},{9,5},{17,9},{25,13},{2,2},{10,6}... | collective-permute-start | bytes 1572872 | tf_op jit(solution)/shard_map/ppermute | solution.py:896
  1180.0 55.0 %collective-permute-start.40 = (bf16[4,2,256,128]{3,2,1,0:T(8,128)(2,1)}, bf16[4,2,256,128]{3,2,1,0:T(8,128)(2,1)}, u32[]{:S(2)}, u32[]{:S(2)}) collective-permute-start(bf16[4,2,256,128]{3,2,1,0:T(8,128)(2,1)} %reduce-scatter.12.cloned.1.call-done), channel_id=1, source_target_pairs={{4,0},{12,4},{20,8},{28,12},{5,1},{13,5},{21,9},{29,13},{6,2},{14,... | collective-permute-start | bytes 1572872 | tf_op jit(solution)/shard_map/ppermute | solution.py:896
  1187.1 50.7 %copy-start.25 = (bf16[2,512,128]{2,1,0:T(8,128)(2,1)S(1)}, bf16[2,512,128]{2,1,0:T(8,128)(2,1)}, u32[]{:S(2)}) copy-start(bf16[2,512,128]{2,1,0:T(8,128)(2,1)} %get-tuple-element.226.kv_ref) | copy-start | bytes 786436
  1242.6 18.2 %collective-permute-start.41 = (bf16[512,256]{1,0:T(8,128)(2,1)S(1)}, bf16[512,256]{1,0:T(8,128)(2,1)}, u32[]{:S(2)}, u32[]{:S(2)}) collective-permute-start(bf16[512,256]{1,0:T(8,128)(2,1)S(1)} %get-tuple-element.559), channel_id=1, source_target_pairs={{0,1},{1,0},{2,3},{3,2},{4,5},{5,4},{6,7},{7,6},{8,9},{9,8},{10,11... | collective-permute-start | bytes 786440 | tf_op jit(solution)/shard_map/ppermute | solution.py:572
  1244.3 18.2 %collective-permute-start.42 = (bf16[512,256]{1,0:T(8,128)(2,1)S(1)}, bf16[512,256]{1,0:T(8,128)(2,1)}, u32[]{:S(2)}, u32[]{:S(2)}) collective-permute-start(bf16[512,256]{1,0:T(8,128)(2,1)S(1)} %get-tuple-element.557), channel_id=1, source_target_pairs={{0,2},{1,3},{2,0},{3,1},{4,6},{5,7},{6,4},{7,5},{8,10},{9,11},{10,... | collective-permute-start | bytes 786440 | tf_op jit(solution)/shard_map/ppermute | solution.py:572
  1245.7 18.4 %collective-permute-start.43 = (bf16[512,256]{1,0:T(8,128)(2,1)S(1)}, bf16[512,256]{1,0:T(8,128)(2,1)}, u32[]{:S(2)}, u32[]{:S(2)}) collective-permute-start(bf16[512,256]{1,0:T(8,128)(2,1)S(1)} %get-tuple-element.555), channel_id=1, source_target_pairs={{0,3},{1,2},{2,1},{3,0},{4,7},{5,6},{6,5},{7,4},{8,11},{9,10},{10,... | collective-permute-start | bytes 786440 | tf_op jit(solution)/shard_map/ppermute | solution.py:572
  1253.1 23.7 %all-to-all-start.1 = ((f32[32,1,2216]{2,1,0:T(1,128)}), f32[32,1,2216]{2,1,0:T(1,128)S(1)}, u32[]{:S(2)}, u32[]{:S(2)}) async-start(f32[32,1,2216]{2,1,0:T(1,128)} %copy.132), calls=%async_computation.5 | async-start | bytes 589824 | tf_op jit(solution)/shard_map/all_to_all | solution.py:984
  1276.8 32.6 %all-to-all-start.2 = ((bf16[32,64,256]{2,1,0:T(8,128)(2,1)}), bf16[32,64,256]{2,1,0:T(8,128)(2,1)S(1)}, u32[]{:S(2)}, u32[]{:S(2)}) async-start(bf16[32,64,256]{2,1,0:T(8,128)(2,1)} %bitcast.112), calls=%async_computation.7 | async-start | bytes 2097152 | tf_op jit(solution)/shard_map/all_to_all | solution.py:968
  (94 other events, 679.6 us)
Sparse Core Ops, SparseCore 0:
  14.3 63.5 all-gather.11
  79.5 46.2 all-gather.13
  128.0 45.3 all-gather.17
  175.4 45.8 all-gather.19
  222.8 149.8 all-gather.23
  379.2 154.2 all-gather.21
  589.4 48.8 all-gather.15
  712.3 171.7 reduce-scatter.5
  889.5 169.8 reduce-scatter.7
  1062.1 49.0 reduce-scatter.9
  1114.6 48.1 reduce-scatter.11
  1165.6 66.0 reduce-scatter.13

commit v6 on v5

--- a/solution.py
+++ b/solution.py
@@ -943,11 +943,7 @@
     grad_q = grad_q.astype(BF)
     prompt = jnp.stack(prompts, axis=0)
     prompt = lax.psum_scatter(prompt, "row", scatter_dimension=2, tiled=True)
-    ffe = w_gate.shape[2]
-    own_gu = after(own_grads[0], grad_q)
-    grad_gate = own_gu[:, :ffe] + sum(v[:, :ffe].astype(F32) for v in gu_got)
-    grad_up = own_gu[:, ffe:] + sum(v[:, ffe:].astype(F32) for v in gu_got)
-    prompt, grad_gate, grad_up, _ = lax.optimization_barrier((prompt, grad_gate, grad_up, grad_q))
+    prompt, grad_q = lax.optimization_barrier((prompt, grad_q))
     prompt = to_owners(prompt)
     for d in slots:
         pair = pairs[d] + prompt[d].astype(F32)
@@ -1001,7 +997,11 @@
     x_hat = x_wide * x_spread
     input_grad = hidden_grad + norm_back(input_sum, x_hat, x_spread, gain_one)
 
-    grad_down = after(own_grads[1], kv_share) + sum(v.astype(F32) for v in dn_got)
+    own_grads, _ = lax.optimization_barrier((own_grads, kv_share))
+    ffe = w_gate.shape[2]
+    grad_gate = own_grads[0][:, :ffe] + sum(v[:, :ffe].astype(F32) for v in gu_got)
+    grad_up = own_grads[0][:, ffe:] + sum(v[:, ffe:].astype(F32) for v in gu_got)
+    grad_down = own_grads[1] + sum(v.astype(F32) for v in dn_got)
     layer_output = (hidden + y_sum.astype(F32)).astype(BF)
 
     return (

time: 1330 us -> 1300 us (0.977)
  waiting for transfers between devices: 542 us -> 498 us
  starting transfers between devices: 81.5 us -> 100 us
    reduce_scatter x1, waiting for transfers between devices: 44.5 us -> 0.01 us  [per_device(): grad_q = lax.psum_scatter(grad_q, 'row', scatter_dimension=0, tiled=True)]
    all_to_all x1, starting transfers between devices: 7.64 us -> 27 us  [per_device(): lax.all_to_all(jnp.concatenate(tail, axis=1), ('row', 'col'), split_axis=...]
    add x1 -> x0, other arithmetic: 14.4 us -> none  [per_device(): grad_up = own_gu[:, ffe:] + sum((v[:, ffe:].astype(F32) for v in gu_got))]
    broadcast_in_dim x0 -> x1, other arithmetic: none -> 14 us  [per_device(): grad_up[None]]
    unnamed x215 -> x213, local copies, waits for them, and re-layouts: 33.4 us -> 33.1 us
where the time goes in v6:
time: 1300 us; the launch traced here: 1290 us
  waiting for transfers between devices  498 us (38%)
  Pallas kernels  306 us (24%)
  matrix products  172 us (13%)
  starting transfers between devices  100 us (8%)
  other arithmetic  95.8 us (7%)
  local copies, waits for them, and re-layouts  86.1 us (7%)
  between operations  18.1 us (1%)
  blocking collectives  14.6 us (1%)
    ppermute x43, waiting for transfers between devices, swap(): return lax.ppermute(v, 'col', [(i, i ^ step) for i in range(count)])  454 us
    pallas_call x4, Pallas kernels, expert(): call(partial(expert_body, slot), 'expert', (rows // tile,), [pl.BlockSpec...  98.5 us
    dot_general x8, matrix products, dot_tn(): lax.dot_general(a, b, (((0,), (0,)), ((), ())), preferred_element_type=F32)  59.2 us
    ppermute x43, starting transfers between devices, swap(): return lax.ppermute(v, 'col', [(i, i ^ step) for i in range(count)])  52.2 us
    pallas_call x4, Pallas kernels, attend_back(): call(partial(attend_back_body, heads, per, blocks, rows), 'attend_back',...  45.8 us
    pallas_call x2, Pallas kernels, combine(): call(partial(combine_body, count, cap, bool(scores)), 'combine', (sources...  37.2 us
    pallas_call x4, Pallas kernels, qkv(): call(partial(qkv_body, heads), 'qkv', (rows // tile,), [pl.BlockSpec((til...  33.5 us
    unnamed x213, local copies, waits for them, and re-layouts  33.1 us
  transfers between devices with their start and end apart: 60, of which 33 were waited for; matrix products, arithmetic and copies ran while one was open for 25% of the time, Pallas kernels for 22%

profile of v6, /device:TPU:0, one launch (start us, length us, event | category | flops | bytes accessed | tf_op | source)
XLA Modules:
  0.0 1290.1 jit_solution(13677721996220773598)
XLA Ops:
  18.8 14.6 %all_gather.37 = s32[8,512,8]{1,2,0:T(8,128)S(1)} all-gather(s32[1,512,8]{1,2,0:T(8,128)S(1)} %copy-done.47), channel_id=1, replica_groups=mesh['row'=8,'col'=4] {'row'}, dimensions={0}, use_global_device_ids=true | all-gather | bytes 147456 | tf_op jit(solution)/shard_map/all_gather | solution.py:662
  50.0 13.3 %collective-permute-done.2 = f32[32]{0:T(128)S(1)} collective-permute-done((f32[32]{0:T(128)S(1)}, f32[32]{0:T(128)S(1)}, u32[]{:S(2)}, u32[]{:S(2)}) %collective-permute-start.2) | collective-permute-done | bytes 160 | tf_op jit(solution)/shard_map/ppermute | solution.py:572
  73.5 20.6 %collective-permute-done.4 = bf16[1,256,2048]{2,1,0:T(8,128)(2,1)S(1)} collective-permute-done((bf16[1,256,2048]{2,1,0:T(8,128)(2,1)S(1)}, bf16[1,256,2048]{2,1,0:T(8,128)(2,1)S(1)}, u32[]{:S(2)}, u32[]{:S(2)}) %collective-permute-start.4) | collective-permute-done | bytes 1048608 | tf_op jit(solution)/shard_map/ppermute | solution.py:572
  101.7 8.3 qkv.5
  110.0 8.4 qkv.6
  120.2 5.6 all-gather.14.cloned.1.call-done
  125.9 8.2 qkv.7
  134.1 8.5 qkv.4
  151.2 33.5 %collective-permute-done.6.wga_ref = bf16[1,1024,768]{2,1,0:T(8,128)(2,1)S(1)} collective-permute-done((bf16[1,1024,768]{2,1,0:T(8,128)(2,1)S(1)}, bf16[1,1024,768]{2,1,0:T(8,128)(2,1)S(1)}, u32[]{:S(2)}, u32[]{:S(2)}) %collective-permute-start.6) | collective-permute-done | bytes 1572896 | tf_op jit(solution)/shard_map/ppermute | solution.py:572
  187.1 6.8 attend.4
  201.7 28.4 %collective-permute-done.8.wgb_ref = bf16[1,1024,768]{2,1,0:T(8,128)(2,1)S(1)} collective-permute-done((bf16[1,1024,768]{2,1,0:T(8,128)(2,1)}, bf16[1,1024,768]{2,1,0:T(8,128)(2,1)S(1)}, u32[]{:S(2)}, u32[]{:S(2)}) %collective-permute-start.8) | collective-permute-done | bytes 1572896 | tf_op jit(solution)/shard_map/ppermute | solution.py:572
  236.1 6.9 attend.5
  243.0 20.8 %collective-permute-done.10.wua_ref = bf16[1,1024,768]{2,1,0:T(8,128)(2,1)} collective-permute-done((bf16[1,1024,768]{2,1,0:T(8,128)(2,1)S(1)}, bf16[1,1024,768]{2,1,0:T(8,128)(2,1)}, u32[]{:S(2)}, u32[]{:S(2)}) %collective-permute-start.10) | collective-permute-done | bytes 1572896 | tf_op jit(solution)/shard_map/ppermute | solution.py:572
  265.5 6.2 convolution_convert_fusion.11
  273.2 7.1 attend.6
  285.9 6.7 attend.7
  292.7 72.4 %collective-permute-done.13 = bf16[512,2048]{1,0:T(8,128)(2,1)} collective-permute-done((bf16[512,2048]{1,0:T(8,128)(2,1)}, bf16[512,2048]{1,0:T(8,128)(2,1)}, u32[]{:S(2)}, u32[]{:S(2)}) %collective-permute-start.13) | collective-permute-done | bytes 2097184 | tf_op jit(solution)/shard_map/ppermute | solution.py:572
  383.3 100.5 %collective-permute-done.15.wub_ref = bf16[1,1024,768]{2,1,0:T(8,128)(2,1)} collective-permute-done((bf16[1,1024,768]{2,1,0:T(8,128)(2,1)}, bf16[1,1024,768]{2,1,0:T(8,128)(2,1)}, u32[]{:S(2)}, u32[]{:S(2)}) %collective-permute-start.15) | collective-permute-done | bytes 1572896 | tf_op jit(solution)/shard_map/ppermute | solution.py:572
  496.5 16.8 %dispatch.1 = (bf16[8,128,2048]{2,1,0:T(8,128)(2,1)}, bf16[8,128,2048]{2,1,0:T(8,128)(2,1)}, bf16[8,128,2048]{2,1,0:T(8,128)(2,1)}, bf16[8,128,2048]{2,1,0:T(8,128)(2,1)}) custom-call(s32[8,4,512]{2,1,0:T(4,128)} %copy.122.rank_ref, bf16[8,512,2048]{2,1,0:T(8,128)(2,1)} %bitcast.316), custom_call_target="tpu_custom_call" | custom-call | flops 8589934592 | bytes 33554432 | tf_op jit(solution)/shard_map/dispatch/pallas_call | solution.py:372
  513.3 8.4 collective-permute-done.19.wga_ref
  523.2 10.4 all-gather.22.cloned.1.call-done
  533.5 21.9 %route_dispatch.1 = (f32[4,8,128,1]{3,2,1,0:T(8,128)}, bf16[8,128,2048]{2,1,0:T(8,128)(2,1)}, bf16[8,128,2048]{2,1,0:T(8,128)(2,1)}, bf16[8,128,2048]{2,1,0:T(8,128)(2,1)}, bf16[8,128,2048]{2,1,0:T(8,128)(2,1)}) custom-call(s32[4]{0:T(128)} %pad_add_fusion.2.ids_ref, s32[8,4,512]{2,1,0:T(4,128)} %copy.122.rank_ref, bf16[8,512,2048]{2,1,0:T(8,128)(2,1)} %bitcast.317, ...), custom_call_target="tpu_custom_call" | custom-call | flops 8589934592 | bytes 33554432 | tf_op jit(solution)/shard_map/route_dispatch/pallas_call | solution.py:408
  558.4 24.5 %expert.4 = (bf16[1024,2048]{1,0:T(8,128)(2,1)}, bf16[1024,768]{1,0:T(8,128)(2,1)}, bf16[1024,1536]{1,0:T(8,128)(2,1)}, bf16[1024,128]{1,0:T(8,128)(2,1)}) custom-call(bf16[1024,2048]{1,0:T(8,128)(2,1)} %bitcast.338, bf16[1024,2048]{1,0:T(8,128)(2,1)} %bitcast.274, f32[1024,1]{1,0:T(8,128)} %bitcast.301, bf16[1,2048,768]{2,1,0:T(8,128)(2,1)} %wgb_ref, ...), custom_call_target="tpu_custom_call" | custom-call | flops 16106127360 | bytes 26738688 | tf_op jit(solution)/shard_map/expert/pallas_call | solution.py:544
  589.4 24.8 %expert.5 = (bf16[1024,2048]{1,0:T(8,128)(2,1)}, bf16[1024,768]{1,0:T(8,128)(2,1)}, bf16[1024,1536]{1,0:T(8,128)(2,1)}, bf16[1024,128]{1,0:T(8,128)(2,1)}) custom-call(bf16[1024,2048]{1,0:T(8,128)(2,1)} %bitcast.346, bf16[1024,2048]{1,0:T(8,128)(2,1)} %bitcast.344, f32[1024,1]{1,0:T(8,128)} %bitcast.300, ...), custom_call_target="tpu_custom_call" | custom-call | flops 16106127360 | bytes 26738688 | tf_op jit(solution)/shard_map/expert/pallas_call | solution.py:544
  614.2 8.9 convolution_convert_fusion.2
  630.8 24.7 %expert.6 = (bf16[1024,2048]{1,0:T(8,128)(2,1)}, bf16[1024,768]{1,0:T(8,128)(2,1)}, bf16[1024,1536]{1,0:T(8,128)(2,1)}, bf16[1024,128]{1,0:T(8,128)(2,1)}) custom-call(bf16[1024,2048]{1,0:T(8,128)(2,1)} %bitcast.340, bf16[1024,2048]{1,0:T(8,128)(2,1)} %bitcast.334, f32[1024,1]{1,0:T(8,128)} %bitcast.299, bf16[1,1024,768]{2,1,0:T(8,128)(2,1)} %copy-done.65, ...), custom_call_target="tpu_custom_call" | custom-call | flops 16106127360 | bytes 26738688 | tf_op jit(solution)/shard_map/expert/pallas_call | solution.py:544
  655.5 24.5 %expert.7 = (bf16[1024,2048]{1,0:T(8,128)(2,1)}, bf16[1024,768]{1,0:T(8,128)(2,1)}, bf16[1024,1536]{1,0:T(8,128)(2,1)}, bf16[1024,128]{1,0:T(8,128)(2,1)}) custom-call(bf16[1024,2048]{1,0:T(8,128)(2,1)} %bitcast.342, bf16[1024,2048]{1,0:T(8,128)(2,1)} %bitcast.336, f32[1024,1]{1,0:T(8,128)} %bitcast.298, bf16[1,1024,768]{2,1,0:T(8,128)(2,1)} %copy-done.64, ...), custom_call_target="tpu_custom_call" | custom-call | flops 16106127360 | bytes 26738688 | tf_op jit(solution)/shard_map/expert/pallas_call | solution.py:544
  680.0 12.5 collective-permute-done.25
  692.6 19.5 %combine.2 = (bf16[8,512,2048]{2,1,0:T(8,128)(2,1)}, f32[8,512,4]{2,1,0:T(8,128)}) custom-call(s32[8,512,4]{2,1,0:T(8,128)} %bitcast.267, bf16[8,128,2048]{2,1,0:T(8,128)(2,1)} %bitcast.276, bf16[8,128,2048]{2,1,0:T(8,128)(2,1)} %bitcast.278, bf16[8,128,2048]{2,1,0:T(8,128)(2,1)} %bitcast.279, bf16[8,128,2048]{2,1,0:T(8,128)(2,1)} %bitcast.277, ...), custom_call_target="tpu_custom_call" | custom-call | tf_op jit(solution)/shard_map/combine/pallas_call | solution.py:485
  720.5 11.3 add_convert_fusion
  731.9 9.2 add_convert_fusion.1
  741.1 11.2 collective-permute-done.27
  758.5 7.2 all-to-all-start
  772.3 7.2 convolution_convert_fusion.4
  779.5 7.1 convolution_convert_fusion.5
  791.7 7.1 convolution_convert_fusion.3
  814.1 9.5 fusion.108
  825.9 17.7 %combine.3 = bf16[8,512,2048]{2,1,0:T(8,128)(2,1)} custom-call(s32[8,512,4]{2,1,0:T(8,128)} %bitcast.268, bf16[8,128,2048]{2,1,0:T(8,128)(2,1)} %bitcast.282, bf16[8,128,2048]{2,1,0:T(8,128)(2,1)} %bitcast.281, bf16[8,128,2048]{2,1,0:T(8,128)(2,1)} %bitcast.280, bf16[8,128,2048]{2,1,0:T(8,128)(2,1)} %bitcast.283), custom_call_target="tpu_custom_call" | custom-call | tf_op jit(solution)/shard_map/combine/pallas_call | solution.py:485
  849.5 38.7 %collective-permute-done.29 = bf16[2048,1536]{1,0:T(8,128)(2,1)} collective-permute-done((bf16[2048,1536]{1,0:T(8,128)(2,1)}, bf16[2048,1536]{1,0:T(8,128)(2,1)}, u32[]{:S(2)}, u32[]{:S(2)}) %collective-permute-start.29) | collective-permute-done | bytes 6291488 | tf_op jit(solution)/shard_map/ppermute | solution.py:572
  905.6 11.4 attend_back.4
  917.0 6.5 input_share.4
  923.5 20.1 %collective-permute-done.31 = bf16[1,512,2048]{2,1,0:T(8,128)(2,1)S(1)} collective-permute-done((bf16[1,512,2048]{2,1,0:T(8,128)(2,1)S(1)}, bf16[1,512,2048]{2,1,0:T(8,128)(2,1)S(1)}, u32[]{:S(2)}, u32[]{:S(2)}) %collective-permute-start.31) | collective-permute-done | bytes 2097184 | tf_op jit(solution)/shard_map/ppermute | solution.py:572
  949.8 5.5 fusion.27.do_ref
  955.3 11.4 attend_back.5
  966.7 6.2 input_share.5
  977.5 5.7 convolution_convert_fusion.14.do_ref
  983.1 11.4 attend_back.6
  994.6 5.9 input_share.6
  1003.7 11.4 bitcast_convert_fusion
  1015.2 27.8 %collective-permute-done.35 = bf16[768,2048]{1,0:T(8,128)(2,1)} collective-permute-done((bf16[768,2048]{1,0:T(8,128)(2,1)}, bf16[768,2048]{1,0:T(8,128)(2,1)}, u32[]{:S(2)}, u32[]{:S(2)}) %collective-permute-start.35) | collective-permute-done | bytes 3145760 | tf_op jit(solution)/shard_map/ppermute | solution.py:572
  1044.0 15.3 %reduce-scatter.8.cloned.1.call-done = bf16[1,512,2048]{2,1,0:T(8,128)(2,1)} async-done(((bf16[8,512,2048]{2,1,0:T(8,128)(2,1)}), bf16[1,512,2048]{2,1,0:T(8,128)(2,1)}) %reduce-scatter.8.cloned.1.call-update) | async-done | bytes 2097168 | tf_op jit(solution)/shard_map/reduce_scatter | solution.py:868
  1062.5 5.5 convolution_convert_fusion.13.do_ref
  1068.0 11.7 attend_back.7
  1079.7 26.6 %collective-permute-done.37 = bf16[512,2048]{1,0:T(8,128)(2,1)} collective-permute-done((bf16[512,2048]{1,0:T(8,128)(2,1)}, bf16[512,2048]{1,0:T(8,128)(2,1)}, u32[]{:S(2)}, u32[]{:S(2)}) %collective-permute-start.37) | collective-permute-done | bytes 2097184 | tf_op jit(solution)/shard_map/ppermute | solution.py:572
  1123.9 6.0 input_share.7
  1132.5 14.1 %fusion.105 = (bf16[2048,1024]{0,1:T(8,128)(2,1)}, f32[2048,1024]{0,1:T(8,128)}) fusion(bf16[4,512,1024]{2,1,0:T(8,128)(2,1)S(1)} %pad_maximum_fusion.2, bf16[1,512,2048]{2,1,0:T(8,128)(2,1)} %bitcast.352, bf16[1,512,2048]{2,1,0:T(8,128)(2,1)} %bitcast.350, bf16[1,512,2048]{2,1,0:T(8,128)(2,1)} %bitcast.348, bf16[1,512,2048]{2,1,0:T(8,128)(2,1)} %bitcast.354), kind=kOutput, calls=%fused_computation.271 | convolution fusion | flops 8604614656 | bytes 25165824 | tf_op jit(solution)/shard_map/dot_general | solution.py:886
  1146.6 9.4 copy.130
  1157.0 5.8 reduce-scatter.12.cloned.1.call-done
  1195.3 27.0 %all-to-all-start.1 = ((f32[32,1,2216]{2,1,0:T(1,128)}), f32[32,1,2216]{2,1,0:T(1,128)S(1)}, u32[]{:S(2)}, u32[]{:S(2)}) async-start(f32[32,1,2216]{2,1,0:T(1,128)} %copy.132), calls=%async_computation.5 | async-start | bytes 589824 | tf_op jit(solution)/shard_map/all_to_all | solution.py:980
  1232.6 7.4 add_bitcast_fusion
  1239.9 5.8 fusion.2
  1245.7 5.9 all-to-all-start.2
  1251.7 7.0 fusion.6
  1258.7 14.0 %add_bitcast_fusion.1 = (f32[1,2048,768]{2,1,0:T(8,128)}, f32[1,2048,768]{2,1,0:T(8,128)}) fusion(f32[2048,1536]{1,0:T(8,128)} %fusion.108, bf16[2048,1536]{1,0:T(8,128)(2,1)} %collective-permute-done.30, bf16[2048,1536]{1,0:T(8,128)(2,1)} %collective-permute-done.29), kind=kLoop, calls=%fused_computation.10 | loop fusion | flops 12582912 | bytes 37748736 | tf_op jit(solution)/shard_map/broadcast_in_dim | solution.py:1020
  (476 shorter events, 287.2 us)
Async XLA Ops:
  7.2 89.4 %all-gather.12.cloned.1.call-start = ((), (), s32[]{:S(2)}) async-start(), calls=%async_computation.8 | async-start | bytes 6488064 | tf_op jit(solution)/shard_map/all_gather | solution.py:650
  14.2 111.6 %all-gather.14.cloned.1.call-start = ((), (), s32[]{:S(2)}) async-start(), calls=%async_computation.9 | async-start | bytes 4718592 | tf_op jit(solution)/shard_map/all_gather | solution.py:698
  14.3 53.3 %collective-permute-start = (bf16[1,512,2048]{2,1,0:T(8,128)(2,1)}, bf16[1,512,2048]{2,1,0:T(8,128)(2,1)}, u32[]{:S(2)}, u32[]{:S(2)}) collective-permute-start(bf16[1,512,2048]{2,1,0:T(8,128)(2,1)} %param.15), channel_id=1, source_target_pairs={{0,1},{1,0},{2,3},{3,2},{4,5},{5,4},{6,7},{7,6},{8,9},{9,8},{10,11... | collective-permute-start | bytes 6291464 | tf_op jit(solution)/shard_map/ppermute | solution.py:572
  17.3 50.3 %collective-permute-start.1 = (bf16[1,512,2048]{2,1,0:T(8,128)(2,1)}, bf16[1,512,2048]{2,1,0:T(8,128)(2,1)}, u32[]{:S(2)}, u32[]{:S(2)}) collective-permute-start(bf16[1,512,2048]{2,1,0:T(8,128)(2,1)} %param.15), channel_id=1, source_target_pairs={{0,2},{1,3},{2,0},{3,1},{4,6},{5,7},{6,4},{7,5},{8,10},{9,11},{10,... | collective-permute-start | bytes 6291464 | tf_op jit(solution)/shard_map/ppermute | solution.py:572
  34.4 28.8 %collective-permute-start.2 = (f32[32]{0:T(128)S(1)}, f32[32]{0:T(128)S(1)}, u32[]{:S(2)}, u32[]{:S(2)}) collective-permute-start(f32[32]{0:T(128)S(1)} %convert_reduce_fusion.3), channel_id=1, source_target_pairs={{0,1},{1,0},{2,3},{3,2},{4,5},{5,4},{6,7},{7,6},{8,9},{9,8},{10,11... | collective-permute-start | bytes 392 | tf_op jit(solution)/shard_map/ppermute | solution.py:572
  48.8 441.9 %copy-start.5 = (s32[8,4,512]{1,2,0:T(8,128)}, s32[8,4,512]{1,2,0:T(8,128)S(1)}, u32[]{:S(2)}) copy-start(s32[8,4,512]{1,2,0:T(8,128)S(1)} %add_select_fusion) | copy-start | bytes 196612
  63.2 3.8 collective-permute-start.3
  67.6 119.5 %all-gather.18.cloned.1.call-start = ((), (), s32[]{:S(2)}) async-start(), calls=%async_computation.16 | async-start | bytes 4718592 | tf_op jit(solution)/shard_map/all_gather | solution.py:714
  70.3 23.8 %collective-permute-start.4 = (bf16[1,256,2048]{2,1,0:T(8,128)(2,1)S(1)}, bf16[1,256,2048]{2,1,0:T(8,128)(2,1)S(1)}, u32[]{:S(2)}, u32[]{:S(2)}) collective-permute-start(bf16[1,256,2048]{2,1,0:T(8,128)(2,1)S(1)} %slice.253), channel_id=1, source_target_pairs={{0,2},{1,3},{2,0},{3,1},{4,6},{5,7},{6,4},{7,5},{8,10},{9,11},{10,... | collective-permute-start | bytes 3145736 | tf_op jit(solution)/shard_map/ppermute | solution.py:572
  72.0 23.0 %collective-permute-start.5 = (bf16[1,256,2048]{2,1,0:T(8,128)(2,1)S(1)}, bf16[1,256,2048]{2,1,0:T(8,128)(2,1)S(1)}, u32[]{:S(2)}, u32[]{:S(2)}) collective-permute-start(bf16[1,256,2048]{2,1,0:T(8,128)(2,1)S(1)} %slice.254), channel_id=1, source_target_pairs={{0,1},{1,0},{2,3},{3,2},{4,5},{5,4},{6,7},{7,6},{8,9},{9,8},{10,11... | collective-permute-start | bytes 3145736 | tf_op jit(solution)/shard_map/ppermute | solution.py:572
  101.7 273.6 %copy-start.44 = (f32[2048]{0:T(1024)}, f32[2048]{0:T(1024)S(1)}, u32[]{:S(2)}) copy-start(f32[2048]{0:T(1024)S(1)} %get-tuple-element.500) | copy-start | bytes 24580
  125.8 147.3 %all-gather.20.cloned.1.call-start = ((), (), s32[]{:S(2)}) async-start(), calls=%async_computation.17 | async-start | bytes 4718592 | tf_op jit(solution)/shard_map/all_gather | solution.py:714
  144.4 352.0 %all-gather.24.cloned.1.call-start = ((), (), s32[]{:S(2)}) async-start(), calls=%async_computation.19 | async-start | bytes 18874368 | tf_op jit(solution)/shard_map/all_gather | solution.py:747
  148.2 36.5 %collective-permute-start.6 = (bf16[1,1024,768]{2,1,0:T(8,128)(2,1)S(1)}, bf16[1,1024,768]{2,1,0:T(8,128)(2,1)S(1)}, u32[]{:S(2)}, u32[]{:S(2)}) collective-permute-start(bf16[1,1024,768]{2,1,0:T(8,128)(2,1)S(1)} %get-tuple-element.539), channel_id=1, source_target_pairs={{0,1},{1,0},{2,3},{3,2},{4,5},{5,4},{6,7},{7,6},{8,9},{9,8},{10,11... | collective-permute-start | bytes 4718600 | tf_op jit(solution)/shard_map/ppermute | solution.py:572
  149.7 36.2 %collective-permute-start.7 = (bf16[1,1024,768]{2,1,0:T(8,128)(2,1)S(1)}, bf16[1,1024,768]{2,1,0:T(8,128)(2,1)S(1)}, u32[]{:S(2)}, u32[]{:S(2)}) collective-permute-start(bf16[1,1024,768]{2,1,0:T(8,128)(2,1)S(1)} %get-tuple-element.539), channel_id=1, source_target_pairs={{0,2},{1,3},{2,0},{3,1},{4,6},{5,7},{6,4},{7,5},{8,10},{9,11},{10,... | collective-permute-start | bytes 4718600 | tf_op jit(solution)/shard_map/ppermute | solution.py:572
  193.9 339.6 %all-gather.22.cloned.1.call-start = ((), (), s32[]{:S(2)}) async-start(), calls=%async_computation.18 | async-start | bytes 18874368 | tf_op jit(solution)/shard_map/all_gather | solution.py:751
  194.0 36.1 %collective-permute-start.8 = (bf16[1,1024,768]{2,1,0:T(8,128)(2,1)}, bf16[1,1024,768]{2,1,0:T(8,128)(2,1)S(1)}, u32[]{:S(2)}, u32[]{:S(2)}) collective-permute-start(bf16[1,1024,768]{2,1,0:T(8,128)(2,1)} %get-tuple-element.538), channel_id=1, source_target_pairs={{0,1},{1,0},{2,3},{3,2},{4,5},{5,4},{6,7},{7,6},{8,9},{9,8},{10,11... | collective-permute-start | bytes 4718600 | tf_op jit(solution)/shard_map/ppermute | solution.py:572
  195.5 36.2 %collective-permute-start.9 = (bf16[1,1024,768]{2,1,0:T(8,128)(2,1)}, bf16[1,1024,768]{2,1,0:T(8,128)(2,1)S(1)}, u32[]{:S(2)}, u32[]{:S(2)}) collective-permute-start(bf16[1,1024,768]{2,1,0:T(8,128)(2,1)} %get-tuple-element.538), channel_id=1, source_target_pairs={{0,2},{1,3},{2,0},{3,1},{4,6},{5,7},{6,4},{7,5},{8,10},{9,11},{10,... | collective-permute-start | bytes 4718600 | tf_op jit(solution)/shard_map/ppermute | solution.py:572
  200.2 63.7 %collective-permute-start.10 = (bf16[1,1024,768]{2,1,0:T(8,128)(2,1)S(1)}, bf16[1,1024,768]{2,1,0:T(8,128)(2,1)}, u32[]{:S(2)}, u32[]{:S(2)}) collective-permute-start(bf16[1,1024,768]{2,1,0:T(8,128)(2,1)S(1)} %get-tuple-element.537), channel_id=1, source_target_pairs={{0,1},{1,0},{2,3},{3,2},{4,5},{5,4},{6,7},{7,6},{8,9},{9,8},{10,11... | collective-permute-start | bytes 4718600 | tf_op jit(solution)/shard_map/ppermute | solution.py:572
  200.8 64.7 %collective-permute-start.11 = (bf16[1,1024,768]{2,1,0:T(8,128)(2,1)S(1)}, bf16[1,1024,768]{2,1,0:T(8,128)(2,1)}, u32[]{:S(2)}, u32[]{:S(2)}) collective-permute-start(bf16[1,1024,768]{2,1,0:T(8,128)(2,1)S(1)} %get-tuple-element.537), channel_id=1, source_target_pairs={{0,2},{1,3},{2,0},{3,1},{4,6},{5,7},{6,4},{7,5},{8,10},{9,11},{10,... | collective-permute-start | bytes 4718600 | tf_op jit(solution)/shard_map/ppermute | solution.py:572
  235.4 129.7 %collective-permute-start.12 = (bf16[512,2048]{1,0:T(8,128)(2,1)}, bf16[512,2048]{1,0:T(8,128)(2,1)}, u32[]{:S(2)}, u32[]{:S(2)}) collective-permute-start(bf16[512,2048]{1,0:T(8,128)(2,1)} %convolution_convert_fusion.12), channel_id=1, source_target_pairs={{0,1},{1,0},{2,3},{3,2},{4,5},{5,4},{6,7},{7,6},{8,9},{9,8},{10,11... | collective-permute-start | bytes 6291464 | tf_op jit(solution)/shard_map/ppermute | solution.py:572
  271.7 93.4 %collective-permute-start.13 = (bf16[512,2048]{1,0:T(8,128)(2,1)}, bf16[512,2048]{1,0:T(8,128)(2,1)}, u32[]{:S(2)}, u32[]{:S(2)}) collective-permute-start(bf16[512,2048]{1,0:T(8,128)(2,1)} %convolution_convert_fusion.11), channel_id=1, source_target_pairs={{0,2},{1,3},{2,0},{3,1},{4,6},{5,7},{6,4},{7,5},{8,10},{9,11},{10,... | collective-permute-start | bytes 6291464 | tf_op jit(solution)/shard_map/ppermute | solution.py:572
  285.2 84.7 %collective-permute-start.14 = (bf16[512,2048]{1,0:T(8,128)(2,1)}, bf16[512,2048]{1,0:T(8,128)(2,1)S(1)}, u32[]{:S(2)}, u32[]{:S(2)}) collective-permute-start(bf16[512,2048]{1,0:T(8,128)(2,1)} %convolution_convert_fusion.10), channel_id=1, source_target_pairs={{0,3},{1,2},{2,1},{3,0},{4,7},{5,6},{6,5},{7,4},{8,11},{9,10},{10,... | collective-permute-start | bytes 6291464 | tf_op jit(solution)/shard_map/ppermute | solution.py:572
  379.1 313.5 %all-gather.16.cloned.1.call-start = ((), (), s32[]{:S(2)}) async-start(), calls=%async_computation.10 | async-start | bytes 4718592 | tf_op jit(solution)/shard_map/all_gather | solution.py:776
  379.1 105.0 %collective-permute-start.17 = (bf16[1,768,2048]{2,1,0:T(8,128)(2,1)}, bf16[1,768,2048]{2,1,0:T(8,128)(2,1)}, u32[]{:S(2)}, u32[]{:S(2)}) collective-permute-start(bf16[1,768,2048]{2,1,0:T(8,128)(2,1)} %wdb_ref), channel_id=1, source_target_pairs={{0,1},{1,0},{2,3},{3,2},{4,5},{5,4},{6,7},{7,6},{8,9},{9,8},{10,11... | collective-permute-start | bytes 9437192 | tf_op jit(solution)/shard_map/ppermute | solution.py:572
  379.2 105.0 %collective-permute-start.18 = (bf16[1,768,2048]{2,1,0:T(8,128)(2,1)}, bf16[1,768,2048]{2,1,0:T(8,128)(2,1)}, u32[]{:S(2)}, u32[]{:S(2)}) collective-permute-start(bf16[1,768,2048]{2,1,0:T(8,128)(2,1)} %wdb_ref), channel_id=1, source_target_pairs={{0,2},{1,3},{2,0},{3,1},{4,6},{5,7},{6,4},{7,5},{8,10},{9,11},{10,... | collective-permute-start | bytes 9437192 | tf_op jit(solution)/shard_map/ppermute | solution.py:572
  380.7 103.1 %collective-permute-start.15 = (bf16[1,1024,768]{2,1,0:T(8,128)(2,1)}, bf16[1,1024,768]{2,1,0:T(8,128)(2,1)}, u32[]{:S(2)}, u32[]{:S(2)}) collective-permute-start(bf16[1,1024,768]{2,1,0:T(8,128)(2,1)} %get-tuple-element.536), channel_id=1, source_target_pairs={{0,1},{1,0},{2,3},{3,2},{4,5},{5,4},{6,7},{7,6},{8,9},{9,8},{10,11... | collective-permute-start | bytes 4718600 | tf_op jit(solution)/shard_map/ppermute | solution.py:572
  382.6 101.6 %collective-permute-start.16 = (bf16[1,1024,768]{2,1,0:T(8,128)(2,1)}, bf16[1,1024,768]{2,1,0:T(8,128)(2,1)}, u32[]{:S(2)}, u32[]{:S(2)}) collective-permute-start(bf16[1,1024,768]{2,1,0:T(8,128)(2,1)} %get-tuple-element.536), channel_id=1, source_target_pairs={{0,2},{1,3},{2,0},{3,1},{4,6},{5,7},{6,4},{7,5},{8,10},{9,11},{10,... | collective-permute-start | bytes 4718600 | tf_op jit(solution)/shard_map/ppermute | solution.py:572
  484.2 37.6 %collective-permute-start.19 = (bf16[1,1024,768]{2,1,0:T(8,128)(2,1)}, bf16[1,1024,768]{2,1,0:T(8,128)(2,1)}, u32[]{:S(2)}, u32[]{:S(2)}) collective-permute-start(bf16[1,1024,768]{2,1,0:T(8,128)(2,1)} %copy-done.65), channel_id=1, source_target_pairs={{0,2},{1,3},{2,0},{3,1},{4,6},{5,7},{6,4},{7,5},{8,10},{9,11},{10,... | collective-permute-start | bytes 4718600 | tf_op jit(solution)/shard_map/ppermute | solution.py:572
  485.6 37.6 %collective-permute-start.20 = (bf16[1,1024,768]{2,1,0:T(8,128)(2,1)}, bf16[1,1024,768]{2,1,0:T(8,128)(2,1)}, u32[]{:S(2)}, u32[]{:S(2)}) collective-permute-start(bf16[1,1024,768]{2,1,0:T(8,128)(2,1)} %copy-done.66), channel_id=1, source_target_pairs={{0,1},{1,0},{2,3},{3,2},{4,5},{5,4},{6,7},{7,6},{8,9},{9,8},{10,11... | collective-permute-start | bytes 4718600 | tf_op jit(solution)/shard_map/ppermute | solution.py:572
  489.5 68.9 %collective-permute-start.21 = (bf16[1,1024,768]{2,1,0:T(8,128)(2,1)}, bf16[1,1024,768]{2,1,0:T(8,128)(2,1)}, u32[]{:S(2)}, u32[]{:S(2)}) collective-permute-start(bf16[1,1024,768]{2,1,0:T(8,128)(2,1)} %collective-permute-done.10.wua_ref), channel_id=1, source_target_pairs={{0,2},{1,3},{2,0},{3,1},{4,6},{5,7},{6,4},{7,5},{8,10},{9,11},{10,... | collective-permute-start | bytes 4718600 | tf_op jit(solution)/shard_map/ppermute | solution.py:572
  490.0 68.4 %collective-permute-start.22 = (bf16[1,1024,768]{2,1,0:T(8,128)(2,1)}, bf16[1,1024,768]{2,1,0:T(8,128)(2,1)}, u32[]{:S(2)}, u32[]{:S(2)}) collective-permute-start(bf16[1,1024,768]{2,1,0:T(8,128)(2,1)} %collective-permute-done.16.wub_ref), channel_id=1, source_target_pairs={{0,1},{1,0},{2,3},{3,2},{4,5},{5,4},{6,7},{7,6},{8,9},{9,8},{10,11... | collective-permute-start | bytes 4718600 | tf_op jit(solution)/shard_map/ppermute | solution.py:572
  493.5 94.7 %collective-permute-start.23 = (bf16[1,384,2048]{2,1,0:T(8,128)(2,1)S(1)}, bf16[1,384,2048]{2,1,0:T(8,128)(2,1)}, u32[]{:S(2)}, u32[]{:S(2)}) collective-permute-start(bf16[1,384,2048]{2,1,0:T(8,128)(2,1)S(1)} %slice.262), channel_id=1, source_target_pairs={{0,2},{1,3},{2,0},{3,1},{4,6},{5,7},{6,4},{7,5},{8,10},{9,11},{10,... | collective-permute-start | bytes 4718600 | tf_op jit(solution)/shard_map/ppermute | solution.py:572
  521.8 67.6 %collective-permute-start.24 = (bf16[1,384,2048]{2,1,0:T(8,128)(2,1)S(1)}, bf16[1,384,2048]{2,1,0:T(8,128)(2,1)}, u32[]{:S(2)}, u32[]{:S(2)}) collective-permute-start(bf16[1,384,2048]{2,1,0:T(8,128)(2,1)S(1)} %slice.263), channel_id=1, source_target_pairs={{0,1},{1,0},{2,3},{3,2},{4,5},{5,4},{6,7},{7,6},{8,9},{9,8},{10,11... | collective-permute-start | bytes 4718600 | tf_op jit(solution)/shard_map/ppermute | solution.py:572
  589.3 300.0 %reduce-scatter.6.cloned.1.call-start = ((), (), s32[]{:S(2)}) async-start(), calls=%async_computation.11 | async-start | bytes 18874368 | tf_op jit(solution)/shard_map/reduce_scatter | solution.py:807
  623.5 69.0 %collective-permute-start.25 = (bf16[1024,1536]{1,0:T(8,128)(2,1)S(1)}, bf16[1024,1536]{1,0:T(8,128)(2,1)}, u32[]{:S(2)}, u32[]{:S(2)}) collective-permute-start(bf16[1024,1536]{1,0:T(8,128)(2,1)S(1)} %get-tuple-element.533), channel_id=1, source_target_pairs={{0,1},{1,0},{2,3},{3,2},{4,5},{5,4},{6,7},{7,6},{8,9},{9,8},{10,11... | collective-permute-start | bytes 9437192 | tf_op jit(solution)/shard_map/ppermute | solution.py:572
  624.4 68.2 %collective-permute-start.26 = (bf16[1024,1536]{1,0:T(8,128)(2,1)S(1)}, bf16[1024,1536]{1,0:T(8,128)(2,1)}, u32[]{:S(2)}, u32[]{:S(2)}) collective-permute-start(bf16[1024,1536]{1,0:T(8,128)(2,1)S(1)} %get-tuple-element.532), channel_id=1, source_target_pairs={{0,2},{1,3},{2,0},{3,1},{4,6},{5,7},{6,4},{7,5},{8,10},{9,11},{10,... | collective-permute-start | bytes 9437192 | tf_op jit(solution)/shard_map/ppermute | solution.py:572
  718.2 34.1 %collective-permute-start.27 = (bf16[384,2048]{1,0:T(8,128)(2,1)S(1)}, bf16[384,2048]{1,0:T(8,128)(2,1)S(1)}, u32[]{:S(2)}, u32[]{:S(2)}) collective-permute-start(bf16[384,2048]{1,0:T(8,128)(2,1)S(1)} %get-tuple-element.535), channel_id=1, source_target_pairs={{0,1},{1,0},{2,3},{3,2},{4,5},{5,4},{6,7},{7,6},{8,9},{9,8},{10,11... | collective-permute-start | bytes 4718600 | tf_op jit(solution)/shard_map/ppermute | solution.py:572
  719.9 33.6 %collective-permute-start.28 = (bf16[384,2048]{1,0:T(8,128)(2,1)S(1)}, bf16[384,2048]{1,0:T(8,128)(2,1)S(1)}, u32[]{:S(2)}, u32[]{:S(2)}) collective-permute-start(bf16[384,2048]{1,0:T(8,128)(2,1)S(1)} %get-tuple-element.534), channel_id=1, source_target_pairs={{0,2},{1,3},{2,0},{3,1},{4,6},{5,7},{6,4},{7,5},{8,10},{9,11},{10,... | collective-permute-start | bytes 4718600 | tf_op jit(solution)/shard_map/ppermute | solution.py:572
  753.5 134.6 %collective-permute-start.29 = (bf16[2048,1536]{1,0:T(8,128)(2,1)}, bf16[2048,1536]{1,0:T(8,128)(2,1)}, u32[]{:S(2)}, u32[]{:S(2)}) collective-permute-start(bf16[2048,1536]{1,0:T(8,128)(2,1)} %add_convert_fusion.1), channel_id=1, source_target_pairs={{0,1},{1,0},{2,3},{3,2},{4,5},{5,4},{6,7},{7,6},{8,9},{9,8},{10,11... | collective-permute-start | bytes 18874376 | tf_op jit(solution)/shard_map/ppermute | solution.py:572
  755.0 134.4 %collective-permute-start.30 = (bf16[2048,1536]{1,0:T(8,128)(2,1)}, bf16[2048,1536]{1,0:T(8,128)(2,1)}, u32[]{:S(2)}, u32[]{:S(2)}) collective-permute-start(bf16[2048,1536]{1,0:T(8,128)(2,1)} %add_convert_fusion), channel_id=1, source_target_pairs={{0,2},{1,3},{2,0},{3,1},{4,6},{5,7},{6,4},{7,5},{8,10},{9,11},{10,... | collective-permute-start | bytes 18874376 | tf_op jit(solution)/shard_map/ppermute | solution.py:572
  758.5 85.1 %all-to-all-start = ((f32[8,512,4]{1,2,0:T(4,128)}), f32[8,512,4]{1,2,0:T(4,128)S(1)}, u32[]{:S(2)}, u32[]{:S(2)}) async-start(f32[8,512,4]{1,2,0:T(4,128)} %copy.124), calls=%async_computation.1 | async-start | bytes 131072 | tf_op jit(solution)/shard_map/all_to_all | solution.py:832
  765.7 293.7 %reduce-scatter.8.cloned.1.call-start = ((), (), s32[]{:S(2)}) async-start(), calls=%async_computation.12 | async-start | bytes 18874368 | tf_op jit(solution)/shard_map/reduce_scatter | solution.py:868
  889.4 221.7 %reduce-scatter.10.cloned.1.call-start = ((), (), s32[]{:S(2)}) async-start(), calls=%async_computation.13 | async-start | bytes 4718592 | tf_op jit(solution)/shard_map/reduce_scatter | solution.py:921
  900.6 42.9 %collective-permute-start.31 = (bf16[1,512,2048]{2,1,0:T(8,128)(2,1)S(1)}, bf16[1,512,2048]{2,1,0:T(8,128)(2,1)S(1)}, u32[]{:S(2)}, u32[]{:S(2)}) collective-permute-start(bf16[1,512,2048]{2,1,0:T(8,128)(2,1)S(1)} %get-tuple-element.526), channel_id=1, source_target_pairs={{0,1},{1,0},{2,3},{3,2},{4,5},{5,4},{6,7},{7,6},{8,9},{9,8},{10,11... | collective-permute-start | bytes 6291464 | tf_op jit(solution)/shard_map/ppermute | solution.py:572
  901.6 45.5 %collective-permute-start.32 = (bf16[1,512,2048]{2,1,0:T(8,128)(2,1)S(1)}, bf16[1,512,2048]{2,1,0:T(8,128)(2,1)S(1)}, u32[]{:S(2)}, u32[]{:S(2)}) collective-permute-start(bf16[1,512,2048]{2,1,0:T(8,128)(2,1)S(1)} %get-tuple-element.526), channel_id=1, source_target_pairs={{0,2},{1,3},{2,0},{3,1},{4,6},{5,7},{6,4},{7,5},{8,10},{9,11},{10,... | collective-permute-start | bytes 6291464 | tf_op jit(solution)/shard_map/ppermute | solution.py:572
  947.2 25.7 %collective-permute-start.33 = (bf16[1,256,2048]{2,1,0:T(8,128)(2,1)S(1)}, bf16[1,256,2048]{2,1,0:T(8,128)(2,1)}, u32[]{:S(2)}, u32[]{:S(2)}) collective-permute-start(bf16[1,256,2048]{2,1,0:T(8,128)(2,1)S(1)} %slice.271), channel_id=1, source_target_pairs={{0,2},{1,3},{2,0},{3,1},{4,6},{5,7},{6,4},{7,5},{8,10},{9,11},{10,... | collective-permute-start | bytes 3145736 | tf_op jit(solution)/shard_map/ppermute | solution.py:572
  949.0 23.9 %collective-permute-start.34 = (bf16[1,256,2048]{2,1,0:T(8,128)(2,1)}, bf16[1,256,2048]{2,1,0:T(8,128)(2,1)}, u32[]{:S(2)}, u32[]{:S(2)}) collective-permute-start(bf16[1,256,2048]{2,1,0:T(8,128)(2,1)} %slice.272), channel_id=1, source_target_pairs={{0,1},{1,0},{2,3},{3,2},{4,5},{5,4},{6,7},{7,6},{8,9},{9,8},{10,11... | collective-permute-start | bytes 3145736 | tf_op jit(solution)/shard_map/ppermute | solution.py:572
  974.7 68.3 %collective-permute-start.35 = (bf16[768,2048]{1,0:T(8,128)(2,1)}, bf16[768,2048]{1,0:T(8,128)(2,1)}, u32[]{:S(2)}, u32[]{:S(2)}) collective-permute-start(bf16[768,2048]{1,0:T(8,128)(2,1)} %add_convert_fusion.3), channel_id=1, source_target_pairs={{0,1},{1,0},{2,3},{3,2},{4,5},{5,4},{6,7},{7,6},{8,9},{9,8},{10,11... | collective-permute-start | bytes 9437192 | tf_op jit(solution)/shard_map/ppermute | solution.py:572
  976.1 67.9 %collective-permute-start.36 = (bf16[768,2048]{1,0:T(8,128)(2,1)}, bf16[768,2048]{1,0:T(8,128)(2,1)}, u32[]{:S(2)}, u32[]{:S(2)}) collective-permute-start(bf16[768,2048]{1,0:T(8,128)(2,1)} %add_convert_fusion.2), channel_id=1, source_target_pairs={{0,2},{1,3},{2,0},{3,1},{4,6},{5,7},{6,4},{7,5},{8,10},{9,11},{10,... | collective-permute-start | bytes 9437192 | tf_op jit(solution)/shard_map/ppermute | solution.py:572
  1059.4 103.5 %reduce-scatter.12.cloned.1.call-start = ((), (), s32[]{:S(2)}) async-start(), calls=%async_computation.14 | async-start | bytes 4718592 | tf_op jit(solution)/shard_map/reduce_scatter | solution.py:945
  1059.4 46.8 %collective-permute-start.38 = (bf16[512,2048]{1,0:T(8,128)(2,1)}, bf16[512,2048]{1,0:T(8,128)(2,1)}, u32[]{:S(2)}, u32[]{:S(2)}) collective-permute-start(bf16[512,2048]{1,0:T(8,128)(2,1)} %input_share.6), channel_id=1, source_target_pairs={{0,2},{1,3},{2,0},{3,1},{4,6},{5,7},{6,4},{7,5},{8,10},{9,11},{10,... | collective-permute-start | bytes 6291464 | tf_op jit(solution)/shard_map/ppermute | solution.py:572
  1061.0 45.3 %collective-permute-start.37 = (bf16[512,2048]{1,0:T(8,128)(2,1)}, bf16[512,2048]{1,0:T(8,128)(2,1)}, u32[]{:S(2)}, u32[]{:S(2)}) collective-permute-start(bf16[512,2048]{1,0:T(8,128)(2,1)} %input_share.5), channel_id=1, source_target_pairs={{0,1},{1,0},{2,3},{3,2},{4,5},{5,4},{6,7},{7,6},{8,9},{9,8},{10,11... | collective-permute-start | bytes 6291464 | tf_op jit(solution)/shard_map/ppermute | solution.py:572
  1068.0 43.2 %copy-start.34 = (bf16[2,2048,128]{2,1,0:T(8,128)(2,1)S(1)}, bf16[2,2048,128]{2,1,0:T(8,128)(2,1)}, u32[]{:S(2)}) copy-start(bf16[2,2048,128]{2,1,0:T(8,128)(2,1)} %get-tuple-element.398) | copy-start | bytes 3145732
  1068.0 43.2 %copy-start.35 = (bf16[2,2048,128]{2,1,0:T(8,128)(2,1)S(1)}, bf16[2,2048,128]{2,1,0:T(8,128)(2,1)}, u32[]{:S(2)}) copy-start(bf16[2,2048,128]{2,1,0:T(8,128)(2,1)} %get-tuple-element.399) | copy-start | bytes 3145732
  1114.6 164.8 %reduce-scatter.14.cloned.1.call-start = ((), (), s32[]{:S(2)}) async-start(), calls=%async_computation.15 | async-start | bytes 4718592 | tf_op jit(solution)/shard_map/reduce_scatter | solution.py:957
  1129.9 110.0 %collective-permute-start.44 = (bf16[512,2048]{1,0:T(8,128)(2,1)}, bf16[512,2048]{1,0:T(8,128)(2,1)S(1)}, u32[]{:S(2)}, u32[]{:S(2)}) collective-permute-start(bf16[512,2048]{1,0:T(8,128)(2,1)} %input_share.7), channel_id=1, source_target_pairs={{0,3},{1,2},{2,1},{3,0},{4,7},{5,6},{6,5},{7,4},{8,11},{9,10},{10,... | collective-permute-start | bytes 6291464 | tf_op jit(solution)/shard_map/ppermute | solution.py:572
  1162.9 12.4 collective-permute-start.39
  1168.2 8.3 collective-permute-start.40
  1182.6 39.7 %collective-permute-start.41 = (bf16[512,256]{1,0:T(8,128)(2,1)S(1)}, bf16[512,256]{1,0:T(8,128)(2,1)}, u32[]{:S(2)}, u32[]{:S(2)}) collective-permute-start(bf16[512,256]{1,0:T(8,128)(2,1)S(1)} %get-tuple-element.557), channel_id=1, source_target_pairs={{0,1},{1,0},{2,3},{3,2},{4,5},{5,4},{6,7},{7,6},{8,9},{9,8},{10,11... | collective-permute-start | bytes 786440 | tf_op jit(solution)/shard_map/ppermute | solution.py:572
  1184.3 39.7 %collective-permute-start.42 = (bf16[512,256]{1,0:T(8,128)(2,1)S(1)}, bf16[512,256]{1,0:T(8,128)(2,1)}, u32[]{:S(2)}, u32[]{:S(2)}) collective-permute-start(bf16[512,256]{1,0:T(8,128)(2,1)S(1)} %get-tuple-element.555), channel_id=1, source_target_pairs={{0,2},{1,3},{2,0},{3,1},{4,6},{5,7},{6,4},{7,5},{8,10},{9,11},{10,... | collective-permute-start | bytes 786440 | tf_op jit(solution)/shard_map/ppermute | solution.py:572
  1186.6 39.1 %collective-permute-start.43 = (bf16[512,256]{1,0:T(8,128)(2,1)}, bf16[512,256]{1,0:T(8,128)(2,1)}, u32[]{:S(2)}, u32[]{:S(2)}) collective-permute-start(bf16[512,256]{1,0:T(8,128)(2,1)} %get-tuple-element.553), channel_id=1, source_target_pairs={{0,3},{1,2},{2,1},{3,0},{4,7},{5,6},{6,5},{7,4},{8,11},{9,10},{10,... | collective-permute-start | bytes 786440 | tf_op jit(solution)/shard_map/ppermute | solution.py:572
  1195.3 50.4 %all-to-all-start.1 = ((f32[32,1,2216]{2,1,0:T(1,128)}), f32[32,1,2216]{2,1,0:T(1,128)S(1)}, u32[]{:S(2)}, u32[]{:S(2)}) async-start(f32[32,1,2216]{2,1,0:T(1,128)} %copy.132), calls=%async_computation.5 | async-start | bytes 589824 | tf_op jit(solution)/shard_map/all_to_all | solution.py:980
  1245.7 32.4 %all-to-all-start.2 = ((bf16[32,64,256]{2,1,0:T(8,128)(2,1)}), bf16[32,64,256]{2,1,0:T(8,128)(2,1)S(1)}, u32[]{:S(2)}, u32[]{:S(2)}) async-start(bf16[32,64,256]{2,1,0:T(8,128)(2,1)} %bitcast.112), calls=%async_computation.7 | async-start | bytes 2097152 | tf_op jit(solution)/shard_map/all_to_all | solution.py:964
  (93 other events, 558.3 us)
Sparse Core Ops, SparseCore 0:
  14.3 63.5 all-gather.11
  79.5 46.2 all-gather.13
  128.0 45.3 all-gather.17
  175.4 45.8 all-gather.19
  222.8 149.8 all-gather.23
  379.2 154.2 all-gather.21
  589.5 48.7 all-gather.15
  712.3 171.6 reduce-scatter.5
  889.5 169.7 reduce-scatter.7
  1062.1 48.9 reduce-scatter.9
  1114.7 48.1 reduce-scatter.11
  1175.4 48.9 reduce-scatter.13
